TPU v7x, 32 devices: a whole 2x2x4 slice. The times are simulated.
32 devices in a mesh: seq: 8 (over z, y), enc: 4 (over x, core).
Axes of the slice: x: 2, y: 2, z: 4, core: 2. Of those that a mesh axis runs over, the one named last changes fastest.
Arguments:
- source_ids: int32 [8, 1024], P('seq', 'enc'), may hold values from 0 to 25599
- target_ids: int32 [8, 1024], P('seq', 'enc'), may hold values from 0 to 25599
- labels: int32 [8, 1024], P('seq', 'enc'), may hold values from 0 to 25599
- lengths: int32 [8, 2], P('seq'), may hold values from 170 to 1024, as said below
- embedding: bfloat16 [25600, 1024], P('enc'), may hold values from -0.375 to 0.375
- positions: bfloat16 [2, 1024, 1024], P(None, 'enc'), may hold values from -0.375 to 0.375
- attention_in: bfloat16 [3, 1024, 3072], P(None, ('seq', 'enc')), may hold values from -0.1875 to 0.1875
- attention_out: bfloat16 [3, 1024, 1024], P(None, ('seq', 'enc')), may hold values from -6 to 6
- feed_in: bfloat16 [2, 1024, 4096], P(None, ('seq', 'enc')), may hold values from -0.1875 to 0.1875
- feed_out: bfloat16 [2, 4096, 1024], P(None, ('seq', 'enc')), may hold values from -0.09375 to 0.09375
- adapter_down: float32 [2, 1024, 512], P(None, ('seq', 'enc')), may hold values from -0.1875 to 0.1875
- adapter_up: float32 [2, 512, 1024], P(None, ('seq', 'enc')), may hold values from -0.25 to 0.25
- norm_params: float32 [2, 7, 1024], P(None, None, ('seq', 'enc')), may hold values from -0.9 to 2.25
- down_moment: float32 [2, 1024, 512], P(None, ('seq', 'enc')), may hold values from -0.00030517578 to 0.00030517578
- down_second: float32 [2, 1024, 512], P(None, ('seq', 'enc')), may hold values from 2.959998e-11 to 1.1839991e-10
- up_moment: float32 [2, 512, 1024], P(None, ('seq', 'enc')), may hold values from -0.00030517578 to 0.00030517578
- up_second: float32 [2, 512, 1024], P(None, ('seq', 'enc')), may hold values from 2.959998e-11 to 1.1839991e-10
- norm_moment: float32 [2, 7, 1024], P(None, None, ('seq', 'enc')), may hold values from -0.0008544922 to 0.0008544922
- norm_second: float32 [2, 7, 1024], P(None, None, ('seq', 'enc')), may hold values from 2.6521582e-10 to 1.0655993e-09
Outputs:
- loss_sum: float32 [], replicated
- token_count: float32 [], replicated
- grad_norm: float32 [], replicated
- moment_down: float32 [2, 1024, 512], P(None, ('seq', 'enc'))
- second_down: float32 [2, 1024, 512], P(None, ('seq', 'enc'))
- updated_down: float32 [2, 1024, 512], P(None, ('seq', 'enc'))
- moment_up: float32 [2, 512, 1024], P(None, ('seq', 'enc'))
- second_up: float32 [2, 512, 1024], P(None, ('seq', 'enc'))
- updated_up: float32 [2, 512, 1024], P(None, ('seq', 'enc'))
- moment_norms: float32 [2, 7, 1024], P(None, None, ('seq', 'enc'))
- second_norms: float32 [2, 7, 1024], P(None, None, ('seq', 'enc'))
- updated_norms: float32 [2, 7, 1024], P(None, None, ('seq', 'enc'))
Inputs may be any that keep to these rules, and one draw needn't show every extreme that they name: Group g lies in bucket b = 3 g // 8; both of its lengths lie in 1024 (2 b + 1) // 6 to 1024 (2 b + 2) // 6, except in one group drawn from the seed whose two lengths are both 1024.
All inputs are finite; a program needn't handle non-finite values.
Results may differ from a plain program's by a relative error of at most 0.005.
The roundings to bfloat16 on the way count: a program that leaves them out, or rounds other values in their place, can miss the bound.
Values may be sent and summed in bfloat16 or wider, within the bound.
No kernel may reach another device: no remote copies, remote signals or barrier semaphores. Data moves between devices by JAX's collectives and lax.ppermute only.
A program may use at most 640 MiB of HBM per device.

v0:
```python
import jax
import jax.numpy as jnp
from jax import lax
from jax.sharding import PartitionSpec as P

HEAD_DIM = 64
STEP = 10


EPSILON = 1e-05
ADAPTER_SCALE = 4.0
CLIP_NORM = 0.25
RATE_ADAPTER = 0.05
RATE_NORMS = 0.5
BETA_FIRST = 0.9
BETA_SECOND = 0.999
ADAM_EPSILON = 1e-08
DECAY_ADAPTER = 0.01
MASKED_SCORE = -1000000000.0


def merged(value, axis, join):
    pieces = jax.tree.map(lambda part: lax.all_gather(part, axis), value)
    head = jax.tree.map(lambda part: part[0], pieces)
    tail = jax.tree.map(lambda part: part[1:], pieces)
    running, _ = lax.scan(lambda running, piece: (join(running, piece), None), head, tail)
    return running


def dense(left, right):
    return jnp.dot(left, right, preferred_element_type=jnp.float32)


def dense_back(left, right):
    return lax.dot_general(
        left, right, (((1,), (1,)), ((), ())), preferred_element_type=jnp.float32
    )


def inner_rows(left, right):
    return lax.dot_general(
        left, right, (((0,), (0,)), ((), ())), preferred_element_type=jnp.float32
    )


def smooth(values):
    return jax.nn.gelu(values, approximate=False)


def layer_norm(values, gain, shift):
    middle = jnp.mean(values, -1, keepdims=True)
    centred = values - middle
    variance = jnp.mean(centred * centred, -1, keepdims=True)
    return centred * lax.rsqrt(variance + EPSILON) * gain + shift


def norm_forward(values, norms_low, index):
    return jax.vjp(
        layer_norm,
        values,
        norms_low[0, index].astype(jnp.float32),
        norms_low[1, index].astype(jnp.float32),
    )


def key_pairs(rows_low, weights):
    pairs = dense(rows_low, weights).astype(jnp.bfloat16)
    return lax.all_gather(pairs, "enc", axis=0, tiled=True)


def head_split(matrix):
    return matrix.reshape(matrix.shape[0], matrix.shape[1] // HEAD_DIM, HEAD_DIM)


def score_table(queries, pairs, allowed):
    feature_width = queries.shape[1]
    raw = (
        jnp.einsum(
            "rhd,lhd->hrl",
            head_split(queries),
            head_split(pairs[:, :feature_width]),
            preferred_element_type=jnp.float32,
        )
        * 0.125
    )
    return jnp.where(allowed[None], raw, MASKED_SCORE)


def attend_forward(rows_low, pairs, query_weights, out_weights, allowed):
    feature_width = rows_low.shape[1]
    queries = dense(rows_low, query_weights).astype(jnp.bfloat16)
    scores = score_table(queries, pairs, allowed)
    highest = jnp.max(scores, -1, keepdims=True)
    exponent = jnp.exp(scores - highest)
    summed = jnp.sum(exponent, -1, keepdims=True)
    soft_weights = (exponent / summed).astype(jnp.bfloat16)
    context = jnp.einsum(
        "hrl,lhd->rhd",
        soft_weights,
        head_split(pairs[:, feature_width:]),
        preferred_element_type=jnp.float32,
    )
    context = context.reshape(rows_low.shape[0], feature_width).astype(jnp.bfloat16)
    return (dense(context, out_weights), (queries, highest + jnp.log(summed)))


def attend_back(grad_out, kept, pairs, out_weights, allowed):
    queries, log_total = kept
    feature_width = queries.shape[1]
    own_rows = queries.shape[0]
    grad_context = dense_back(grad_out.astype(jnp.bfloat16), out_weights).astype(jnp.bfloat16)
    soft_weights = jnp.exp(score_table(queries, pairs, allowed) - log_total)
    value_heads = head_split(pairs[:, feature_width:])
    grad_soft = jnp.einsum(
        "rhd,lhd->hrl", head_split(grad_context), value_heads, preferred_element_type=jnp.float32
    )
    weighted = jnp.sum(soft_weights * grad_soft, -1, keepdims=True)
    grad_scores = (soft_weights * (grad_soft - weighted)).astype(jnp.bfloat16)
    grad_query = (
        jnp.einsum(
            "hrl,lhd->rhd",
            grad_scores,
            head_split(pairs[:, :feature_width]),
            preferred_element_type=jnp.float32,
        )
        * 0.125
    )
    grad_key = (
        jnp.einsum(
            "hrl,rhd->lhd", grad_scores, head_split(queries), preferred_element_type=jnp.float32
        )
        * 0.125
    )
    grad_value = jnp.einsum(
        "hrl,rhd->lhd",
        soft_weights.astype(jnp.bfloat16),
        head_split(grad_context),
        preferred_element_type=jnp.float32,
    )
    key_rows = pairs.shape[0]
    grad_pairs = jnp.concatenate(
        [grad_key.reshape(key_rows, feature_width), grad_value.reshape(key_rows, feature_width)], 1
    )
    grad_pairs = lax.psum_scatter(
        grad_pairs.astype(jnp.bfloat16), "enc", scatter_dimension=0, tiled=True
    ).astype(jnp.float32)
    return (
        grad_query.reshape(own_rows, feature_width).astype(jnp.bfloat16),
        grad_pairs.astype(jnp.bfloat16),
    )


def branch_forward(rows, expand_weights, reduce_weights, down_weights, up_weights):
    rows_low = rows.astype(jnp.bfloat16)
    expanded = dense(rows_low, expand_weights)
    hidden = smooth(expanded).astype(jnp.bfloat16)
    adapter_pre = dense(rows_low, down_weights)
    adapted = smooth(adapter_pre).astype(jnp.bfloat16)
    result = dense(hidden, reduce_weights) + ADAPTER_SCALE * dense(adapted, up_weights)
    return (result, (rows_low, expanded, adapter_pre, adapted))


def branch_back(grad_out, kept, expand_weights, reduce_weights, down_weights, up_weights):
    rows_low, expanded, adapter_pre, adapted = kept
    grad_hidden = dense_back(grad_out.astype(jnp.bfloat16), reduce_weights)
    grad_expanded = jax.vjp(smooth, expanded)[1](grad_hidden)[0].astype(jnp.bfloat16)
    grad_adapter = (ADAPTER_SCALE * grad_out).astype(jnp.bfloat16)
    grad_up = inner_rows(adapted, grad_adapter)
    grad_adapted = dense_back(grad_adapter, up_weights)
    grad_pre = jax.vjp(smooth, adapter_pre)[1](grad_adapted)[0].astype(jnp.bfloat16)
    grad_down = inner_rows(rows_low, grad_pre)
    grad_rows = dense_back(grad_expanded, expand_weights) + dense_back(grad_pre, down_weights)
    return (grad_rows, grad_down, grad_up)


def adamw(grad, moment, second, weight, rate, decay):
    moment = BETA_FIRST * moment + (1.0 - BETA_FIRST) * grad
    second = BETA_SECOND * second + (1.0 - BETA_SECOND) * grad * grad
    corrected = moment / (1.0 - BETA_FIRST**STEP)
    scale_two = jnp.sqrt(second / (1.0 - BETA_SECOND**STEP))
    return (
        moment,
        second,
        weight - rate * (corrected / (scale_two + ADAM_EPSILON) + decay * weight),
    )


def shards(
    source_ids,
    target_ids,
    labels,
    lengths,
    embedding,
    positions,
    attention_in,
    attention_out,
    feed_in,
    feed_out,
    adapter_down,
    adapter_up,
    norm_params,
    down_moment,
    down_second,
    up_moment,
    up_second,
    norm_moment,
    norm_second,
):
    row_count = source_ids.shape[1]
    feature_width = embedding.shape[1]
    vocab_shard = embedding.shape[0]
    shard_index = lax.axis_index("enc")
    full_length = row_count * lax.axis_size("enc")
    source_length = lengths[0, 0]
    target_length = lengths[0, 1]
    count_own = jnp.clip(target_length - shard_index * row_count, 0, row_count).astype(jnp.float32)
    token_total = lax.psum(count_own, ("seq", "enc"))
    attend_in, attend_out, expand_weights, reduce_weights, down_low, up_low, norms_low = (
        lax.all_gather(attention_in, ("seq", "enc"), axis=1, tiled=True),
        lax.all_gather(attention_out, ("seq", "enc"), axis=1, tiled=True),
        lax.all_gather(feed_in, ("seq", "enc"), axis=1, tiled=True),
        lax.all_gather(feed_out, ("seq", "enc"), axis=1, tiled=True),
        lax.all_gather(adapter_down.astype(jnp.bfloat16), ("seq", "enc"), axis=1, tiled=True),
        lax.all_gather(adapter_up.astype(jnp.bfloat16), ("seq", "enc"), axis=1, tiled=True),
        lax.all_gather(norm_params.astype(jnp.bfloat16), ("seq", "enc"), axis=2, tiled=True),
    )
    source_all, target_all, label_all = (
        lax.all_gather(source_ids, "enc", axis=1, tiled=True),
        lax.all_gather(target_ids, "enc", axis=1, tiled=True),
        lax.all_gather(labels, "enc", axis=1, tiled=True),
    )
    local_ids = jnp.concatenate([source_all, target_all], 0) - shard_index * vocab_shard
    inside = (local_ids >= 0) & (local_ids < vocab_shard)
    looked_up = jnp.take(embedding, jnp.clip(local_ids, 0, vocab_shard - 1), axis=0)
    looked_up = jnp.where(inside[:, :, None], looked_up, jnp.zeros((), jnp.bfloat16))
    embedded = lax.psum_scatter(looked_up, "enc", scatter_dimension=1, tiled=True).astype(
        jnp.float32
    ) + positions.astype(jnp.float32)
    spots_all = jnp.arange(full_length)
    own_spots = shard_index * row_count + jnp.arange(row_count)
    source_mask = jnp.broadcast_to(spots_all[None, :] < source_length, (row_count, full_length))
    causal_mask = (spots_all[None, :] <= own_spots[:, None]) & (spots_all[None, :] < target_length)
    encoder_in, pull_zero = norm_forward(embedded[0], norms_low, 0)
    encoder_low = encoder_in.astype(jnp.bfloat16)
    pairs_encoder = key_pairs(encoder_low, attend_in[0][:, feature_width:])
    attended, kept_encoder = attend_forward(
        encoder_low, pairs_encoder, attend_in[0][:, :feature_width], attend_out[0], source_mask
    )
    after_self, pull_one = norm_forward(encoder_in + attended, norms_low, 1)
    branched, kept_branch_enc = branch_forward(
        after_self, expand_weights[0], reduce_weights[0], down_low[0], up_low[0]
    )
    encoded, pull_two = norm_forward(after_self + branched, norms_low, 2)
    encoded_low = encoded.astype(jnp.bfloat16)
    decoder_in, pull_three = norm_forward(embedded[1], norms_low, 3)
    decoder_low = decoder_in.astype(jnp.bfloat16)
    pairs_decoder = key_pairs(decoder_low, attend_in[1][:, feature_width:])
    attended, kept_decoder = attend_forward(
        decoder_low, pairs_decoder, attend_in[1][:, :feature_width], attend_out[1], causal_mask
    )
    after_causal, pull_four = norm_forward(decoder_in + attended, norms_low, 4)
    pairs_cross = key_pairs(encoded_low, attend_in[2][:, feature_width:])
    attended, kept_cross = attend_forward(
        after_causal.astype(jnp.bfloat16),
        pairs_cross,
        attend_in[2][:, :feature_width],
        attend_out[2],
        source_mask,
    )
    after_cross, pull_five = norm_forward(after_causal + attended, norms_low, 5)
    branched, kept_branch_dec = branch_forward(
        after_cross, expand_weights[1], reduce_weights[1], down_low[1], up_low[1]
    )
    decoded, pull_six = norm_forward(after_cross + branched, norms_low, 6)
    head_input = lax.all_gather(decoded.astype(jnp.bfloat16), "enc", axis=0, tiled=True)
    block_rows = min(512, full_length)
    offset = shard_index * vocab_shard
    columns = jnp.arange(vocab_shard)
    label_line = label_all[0]

    def logit_block(pair_item):
        piece, marks = pair_item
        logits = dense_back(piece, embedding)
        highest = jnp.max(logits, -1)
        summed = jnp.sum(jnp.exp(logits - highest[:, None]), -1)
        picked = jnp.sum(jnp.where(columns[None, :] == (marks - offset)[:, None], logits, 0.0), -1)
        return (logits, highest, summed, picked)

    logits, highest, summed, picked = lax.map(
        logit_block,
        (head_input.reshape(-1, block_rows, feature_width), label_line.reshape(-1, block_rows)),
    )
    logits = logits.reshape(full_length, vocab_shard)

    def combine(first, second):
        peak = jnp.maximum(first[0], second[0])
        return (
            peak,
            first[1] * jnp.exp(first[0] - peak) + second[1] * jnp.exp(second[0] - peak),
            first[2] + second[2],
        )

    highest, summed, picked = merged(
        (highest.reshape(-1), summed.reshape(-1), picked.reshape(-1)), "enc", combine
    )
    log_total = highest + jnp.log(summed)
    valid = (spots_all < target_length).astype(jnp.float32)
    loss_own = jnp.sum(
        lax.dynamic_slice_in_dim((log_total - picked) * valid, shard_index * row_count, row_count)
    )
    piece = logits
    marks = label_line
    onehot = (columns[None, :] == (marks - offset)[:, None]).astype(jnp.float32)
    grad_logits = ((jnp.exp(piece - log_total[:, None]) - onehot) * valid[:, None]).astype(
        jnp.bfloat16
    )
    grad_decoded = lax.psum_scatter(
        dense(grad_logits, embedding).astype(jnp.bfloat16), "enc", scatter_dimension=0, tiled=True
    ).astype(jnp.float32)
    grad_res, gain_six, shift_six = pull_six(grad_decoded)
    grad_rows, down_dec, up_dec = branch_back(
        grad_res, kept_branch_dec, expand_weights[1], reduce_weights[1], down_low[1], up_low[1]
    )
    grad_res, gain_five, shift_five = pull_five(grad_res + grad_rows)
    grad_query, grad_pairs = attend_back(
        grad_res, kept_cross, pairs_cross, attend_out[2], source_mask
    )
    grad_encoded = dense_back(grad_pairs, attend_in[2][:, feature_width:])
    grad_causal = grad_res + dense_back(grad_query, attend_in[2][:, :feature_width])
    grad_res, gain_four, shift_four = pull_four(grad_causal)
    grad_query, grad_pairs = attend_back(
        grad_res, kept_decoder, pairs_decoder, attend_out[1], causal_mask
    )
    grad_decoder = grad_res + dense_back(jnp.concatenate([grad_query, grad_pairs], 1), attend_in[1])
    grad_unused, gain_three, shift_three = pull_three(grad_decoder)
    grad_res, gain_two, shift_two = pull_two(grad_encoded)
    grad_rows, down_enc, up_enc = branch_back(
        grad_res, kept_branch_enc, expand_weights[0], reduce_weights[0], down_low[0], up_low[0]
    )
    grad_res, gain_one, shift_one = pull_one(grad_res + grad_rows)
    grad_query, grad_pairs = attend_back(
        grad_res, kept_encoder, pairs_encoder, attend_out[0], source_mask
    )
    grad_encoder = grad_res + dense_back(jnp.concatenate([grad_query, grad_pairs], 1), attend_in[0])
    grad_unused, gain_zero, shift_zero = pull_zero(grad_encoder)
    grad_norms = jnp.stack(
        [
            jnp.stack([gain_zero, gain_one, gain_two, gain_three, gain_four, gain_five, gain_six]),
            jnp.stack(
                [shift_zero, shift_one, shift_two, shift_three, shift_four, shift_five, shift_six]
            ),
        ]
    )
    grad_down, grad_up, grad_norms = (
        lax.psum_scatter(
            jnp.stack([down_enc, down_dec]), ("seq", "enc"), scatter_dimension=1, tiled=True
        ),
        lax.psum_scatter(
            jnp.stack([up_enc, up_dec]), ("seq", "enc"), scatter_dimension=1, tiled=True
        ),
        lax.psum_scatter(grad_norms, ("seq", "enc"), scatter_dimension=2, tiled=True),
    )
    squares = (
        jnp.sum(grad_down * grad_down)
        + jnp.sum(grad_up * grad_up)
        + jnp.sum(grad_norms * grad_norms)
    )
    loss_sum, squares = lax.psum((loss_own, squares), ("seq", "enc"))
    grad_norm = jnp.sqrt(squares) / token_total
    factor = jnp.minimum(1.0, CLIP_NORM / grad_norm) / token_total
    moment_down, second_down, updated_down = adamw(
        grad_down * factor, down_moment, down_second, adapter_down, RATE_ADAPTER, DECAY_ADAPTER
    )
    moment_up, second_up, updated_up = adamw(
        grad_up * factor, up_moment, up_second, adapter_up, RATE_ADAPTER, DECAY_ADAPTER
    )
    moment_norms, second_norms, updated_norms = adamw(
        grad_norms * factor, norm_moment, norm_second, norm_params, RATE_NORMS, 0.0
    )
    return (
        loss_sum,
        token_total,
        grad_norm,
        moment_down,
        second_down,
        updated_down,
        moment_up,
        second_up,
        updated_up,
        moment_norms,
        second_norms,
        updated_norms,
    )


def solution(mesh):
    return jax.shard_map(
        shards,
        mesh=mesh,
        in_specs=(
            P("seq", "enc"),
            P("seq", "enc"),
            P("seq", "enc"),
            P("seq", None),
            P("enc", None),
            P(None, "enc", None),
            P(None, ("seq", "enc"), None),
            P(None, ("seq", "enc"), None),
            P(None, ("seq", "enc"), None),
            P(None, ("seq", "enc"), None),
            P(None, ("seq", "enc"), None),
            P(None, ("seq", "enc"), None),
            P(None, None, ("seq", "enc")),
            P(None, ("seq", "enc"), None),
            P(None, ("seq", "enc"), None),
            P(None, ("seq", "enc"), None),
            P(None, ("seq", "enc"), None),
            P(None, None, ("seq", "enc")),
            P(None, None, ("seq", "enc")),
        ),
        out_specs=(
            P(),
            P(),
            P(),
            P(None, ("seq", "enc"), None),
            P(None, ("seq", "enc"), None),
            P(None, ("seq", "enc"), None),
            P(None, ("seq", "enc"), None),
            P(None, ("seq", "enc"), None),
            P(None, ("seq", "enc"), None),
            P(None, None, ("seq", "enc")),
            P(None, None, ("seq", "enc")),
            P(None, None, ("seq", "enc")),
        ),
        check_vma=False,
    )
```

profile of v0, /device:TPU:0, one launch (start us, length us, event | category | flops | bytes accessed | tf_op | source)
XLA Modules:
  0.0 1688.1 jit_solution(15796110584412093589)
XLA Ops:
  8.1 6.3 all_gather.51
  14.3 5.5 all_gather.52
  19.9 17.5 %gather_fusion = bf16[2048,1024]{1,0:T(8,128)(2,1)} fusion(bf16[6400,1024]{1,0:T(8,128)(2,1)} %param.27, s32[2048]{0:T(1024)S(1)} %broadcast_clamp_fusion), kind=kCustom, calls=%fused_computation | custom fusion | bytes 8396800 | tf_op jit(solution)/shard_map/jit(_take)/gather | solution.py:234
  42.1 44.9 %all_gather.53 = bf16[2,7,1024]{1,0,2:T(2,128)(2,1)S(1)} all-gather(bf16[2,7,32]{1,0,2:T(2,128)(2,1)S(1)} %copy.120), channel_id=1, replica_groups=mesh['seq'=8,'enc'=4] {'seq','enc'}, dimensions={2}, use_global_device_ids=true | all-gather | bytes 29568 | tf_op jit(solution)/shard_map/all_gather | solution.py:225
  87.0 47.8 %fusion.154 = (f32[1024]{0:T(1024)}, f32[1024]{0:T(1024)}, f32[1024]{0:T(1024)}, f32[1024]{0:T(1024)}, f32[1024]{0:T(1024)S(1)}, /*index=5*/f32[1024]{0:T(1024)S...) fusion(bf16[2,7,1024]{1,0,2:T(2,128)(2,1)S(1)} %all_gather.53), kind=kLoop, calls=%fused_computation.261 | loop fusion | flops 14336 | bytes 86016 | tf_op jit(solution)/shard_map/convert_element_type | solution.py:61
  137.1 43.1 %all-gather.14.cloned.1.call-done = bf16[3,1024,3072]{2,1,0:T(8,128)(2,1)} async-done(((bf16[3,32,3072]{2,1,0:T(8,128)(2,1)}), bf16[3,1024,3072]{2,1,0:T(8,128)(2,1)}) %all-gather.14.cloned.1.call-update) | async-done | bytes 18874384 | tf_op jit(solution)/shard_map/all_gather | solution.py:219
  180.2 12.7 slice_bitcast_fusion.14
  210.3 20.4 %all-gather.20.cloned.1.call-done = bf16[1024,2048]{1,0:T(8,128)(2,1)} async-done(((bf16[256,2048]{1,0:T(8,128)(2,1)}), bf16[1024,2048]{1,0:T(8,128)(2,1)}) %all-gather.20.cloned.1.call-update) | async-done | bytes 4194320 | tf_op jit(solution)/shard_map/all_gather | solution.py:68
  259.1 44.1 %all-gather.18.cloned.1.call-done = bf16[3,1024,1024]{2,1,0:T(8,128)(2,1)} async-done(((bf16[3,32,1024]{2,1,0:T(8,128)(2,1)}), bf16[3,1024,1024]{2,1,0:T(8,128)(2,1)}) %all-gather.18.cloned.1.call-update) | async-done | bytes 6291472 | tf_op jit(solution)/shard_map/all_gather | solution.py:220
  306.1 56.2 %all-gather.26.cloned.1.call-done = bf16[2,1024,512]{2,1,0:T(8,128)(2,1)} async-done(((bf16[2,32,512]{2,1,0:T(8,128)(2,1)}), bf16[2,1024,512]{2,1,0:T(8,128)(2,1)}) %all-gather.26.cloned.1.call-update) | async-done | bytes 2097168 | tf_op jit(solution)/shard_map/all_gather | solution.py:223
  366.0 113.3 %all-gather.22.cloned.1.call-done = bf16[2,1024,4096]{2,1,0:T(8,128)(2,1)} async-done(((bf16[2,32,4096]{2,1,0:T(8,128)(2,1)}), bf16[2,1024,4096]{2,1,0:T(8,128)(2,1)}) %all-gather.22.cloned.1.call-update) | async-done | bytes 16777232 | tf_op jit(solution)/shard_map/all_gather | solution.py:221
  479.3 7.8 fusion.29
  487.1 108.3 %all-gather.24.cloned.1.call-done = bf16[2,4096,1024]{2,1,0:T(8,128)(2,1)} async-done(((bf16[2,128,1024]{2,1,0:T(8,128)(2,1)}), bf16[2,4096,1024]{2,1,0:T(8,128)(2,1)}) %all-gather.24.cloned.1.call-update) | async-done | bytes 16777232 | tf_op jit(solution)/shard_map/all_gather | solution.py:222
  595.4 14.2 fusion.31
  609.7 44.3 %all-gather.28.cloned.1.call-done = bf16[2,512,1024]{2,1,0:T(8,128)(2,1)} async-done(((bf16[2,16,1024]{2,1,0:T(8,128)(2,1)}), bf16[2,512,1024]{2,1,0:T(8,128)(2,1)}) %all-gather.28.cloned.1.call-update) | async-done | bytes 2097168 | tf_op jit(solution)/shard_map/all_gather | solution.py:224
  667.8 21.3 %all-gather.16.cloned.1.call-done = bf16[1024,2048]{1,0:T(8,128)(2,1)} async-done(((bf16[256,2048]{1,0:T(8,128)(2,1)}), bf16[1024,2048]{1,0:T(8,128)(2,1)}) %all-gather.16.cloned.1.call-update) | async-done | bytes 4194320 | tf_op jit(solution)/shard_map/all_gather | solution.py:68
  757.1 6.3 fusion.33
  763.5 10.8 fusion.35
  782.7 16.4 all-gather.32.cloned.1.call-done
  799.1 56.3 %while.32 = (s32[]{:T(128)}, f32[2,512,6400]{2,1,0:T(8,128)}, f32[2,512]{1,0:T(2,128)S(1)}, f32[2,512]{1,0:T(2,128)S(1)}, f32[2,512]{1,0:T(2,128)S(1)}, /*index=...) while((s32[]{:T(128)}, f32[2,512,6400]{2,1,0:T(8,128)}, ...), condition=%wide.region_25.26_spmd.clone, body=%wide.region_21.25_spmd.clone.sunk | while | flops 6730546176 | bytes 66612372 | solution.py:289
  799.1 15.5 bitcast_dynamic-update-slice_fusion.2
  820.0 7.1 select_reduce_fusion.2
  827.2 15.5 bitcast_dynamic-update-slice_fusion.2
  848.2 7.1 select_reduce_fusion.2
  872.5 15.0 fusion.9
  887.6 14.9 convolution_convert_fusion
  903.1 31.1 %reduce-scatter.13.cloned.1.call-done = bf16[256,1024]{1,0:T(8,128)(2,1)} async-done(((bf16[1024,1024]{1,0:T(8,128)(2,1)}), bf16[256,1024]{1,0:T(8,128)(2,1)}) %reduce-scatter.13.cloned.1.call-update) | async-done | bytes 524304 | tf_op jit(solution)/shard_map/reduce_scatter | solution.py:317
  937.7 20.6 %fusion.32 = f32[256,1024]{1,0:T(8,128)S(1)} fusion(bf16[2,1024,4096]{2,1,0:T(8,128)(2,1)} %all-gather.22.cloned.1.call-done, bf16[2,4096,1024]{2,1,0:T(8,128)(2,1)} %all-gather.24.cloned.1.call-done, f32[256,4096]{1,0:T(8,128)} %copy-done.154, f32[256,1024]{1,0:T(8,128)S(1)} %get-tuple-element.275, f32[256]{0:T(256)S(1)} %negate_multiply_fusion.8), kind=kOutput, calls=%fused_computation.62 | convolution fusion | flops 4370989056 | bytes 23069696 | tf_op jit(solution)/shard_map/dot_general | solution.py:35
  966.2 9.2 fusion.71
  975.4 13.4 multiply_reduce_fusion.2
  988.9 7.8 multiply_convert_fusion.2
  1003.5 44.0 %reduce-scatter.15.cloned.1.call-done = bf16[256,2048]{0,1:T(8,128)(2,1)} async-done(((bf16[1024,2048]{0,1:T(8,128)(2,1)}), bf16[256,2048]{0,1:T(8,128)(2,1)}) %reduce-scatter.15.cloned.1.call-update) | async-done | bytes 1048592 | tf_op jit(solution)/shard_map/reduce_scatter | solution.py:144
  1052.5 20.8 %fusion.28 = f32[256,1024]{1,0:T(8,128)S(1)} fusion(bf16[2,1024,4096]{2,1,0:T(8,128)(2,1)} %all-gather.22.cloned.1.call-done, bf16[2,4096,1024]{2,1,0:T(8,128)(2,1)} %all-gather.24.cloned.1.call-done, f32[256,4096]{1,0:T(8,128)} %fusion.29, f32[256,1024]{1,0:T(8,128)S(1)} %get-tuple-element.271, f32[256]{0:T(256)S(1)} %negate_multiply_fusion.6), kind=kOutput, calls=%fused_computation.58 | convolution fusion | flops 4370989056 | bytes 23069696 | tf_op jit(solution)/shard_map/dot_general | solution.py:35
  1082.1 9.2 fusion.74
  1091.3 14.2 multiply_reduce_fusion.1
  1105.5 7.7 multiply_convert_fusion.1
  1121.1 6.2 fusion.129
  1136.1 15.9 multiply_reduce_fusion
  1154.1 7.8 multiply_convert_fusion
  1185.5 7.0 fusion.130
  1192.5 6.9 fusion.128
  1199.5 6.4 fusion.113
  1205.8 12.0 reduce-scatter.23.cloned.1.call-done
  1218.1 6.1 multiply_reduce_fusion.5
  1226.4 135.1 %reduce-scatter.17.cloned.1.call-done = f32[2,32,512]{2,1,0:T(8,128)} async-done(((f32[2,1024,512]{2,1,0:T(8,128)}), f32[2,32,512]{2,1,0:T(8,128)}) %reduce-scatter.17.cloned.1.call-update) | async-done | bytes 131088 | tf_op jit(solution)/shard_map/reduce_scatter | solution.py:355
  1363.0 137.5 %reduce-scatter.19.cloned.1.call-done = f32[2,16,1024]{2,1,0:T(8,128)} async-done(((f32[2,512,1024]{2,1,0:T(8,128)}), f32[2,16,1024]{2,1,0:T(8,128)}) %reduce-scatter.19.cloned.1.call-update) | async-done | bytes 131088 | tf_op jit(solution)/shard_map/reduce_scatter | solution.py:358
  1503.3 128.9 %reduce-scatter.25.cloned.1.call-done = f32[32,14]{1,0:T(8,128)} async-done(((f32[1024,14]{1,0:T(8,128)}), f32[32,14]{1,0:T(8,128)}) %reduce-scatter.25.cloned.1.call-update) | async-done | bytes 1808
  1634.4 37.1 %all-reduce = (f32[]{:T(128)}, f32[]{:T(128)}, f32[]{:T(128)}) all-reduce(f32[]{:T(128)} %dynamic-slice_reduce_fusion, f32[]{:T(128)S(6)} %convert_element_type.422, f32[]{:T(128)S(6)} %add.355), channel_id=1, replica_groups=mesh['seq'=8,'enc'=4] {'seq','enc'}, use_global_device_ids=true, to_apply=%region_29.30 | all-reduce | flops 3 | bytes 24 | tf_op jit(solution)/shard_map/psum | solution.py:368
  (571 shorter events, 262.3 us)
Async XLA Ops:
  8.0 126.9 %reduce-scatter.11.cloned.1.call-start = ((), (), s32[]{:S(2)}) async-start(), calls=%async_computation.8 | async-start | bytes 5242880 | tf_op jit(solution)/shard_map/reduce_scatter | solution.py:236
  41.3 93.5 %copy-start.51 = (bf16[2,256,1024]{2,1,0:T(8,128)(2,1)S(1)}, bf16[2,256,1024]{2,1,0:T(8,128)(2,1)}, u32[]{:S(2)}) copy-start(bf16[2,256,1024]{2,1,0:T(8,128)(2,1)} %param.28) | copy-start | bytes 3145732
  41.4 138.9 %all-gather.14.cloned.1.call-start = ((), (), s32[]{:S(2)}) async-start(), calls=%async_computation.9 | async-start | bytes 19464192 | tf_op jit(solution)/shard_map/all_gather | solution.py:219
  41.9 188.8 %all-gather.20.cloned.1.call-start = ((), (), s32[]{:S(2)}) async-start(), calls=%async_computation.12 | async-start | bytes 5242880 | tf_op jit(solution)/shard_map/all_gather | solution.py:68
  134.8 519.2 %copy-start.72 = (f32[1024]{0:T(1024)}, f32[1024]{0:T(1024)S(1)}, u32[]{:S(2)}) copy-start(f32[1024]{0:T(1024)S(1)} %get-tuple-element.213) | copy-start | bytes 12292
  134.8 519.2 %copy-start.88 = (f32[1024]{0:T(1024)}, f32[1024]{0:T(1024)S(1)}, u32[]{:S(2)}) copy-start(f32[1024]{0:T(1024)S(1)} %get-tuple-element.212) | copy-start | bytes 12292
  134.8 521.6 %copy-start.106 = (f32[1024]{0:T(1024)}, f32[1024]{0:T(1024)S(1)}, u32[]{:S(2)}) copy-start(f32[1024]{0:T(1024)S(1)} %get-tuple-element.211) | copy-start | bytes 12292
  134.8 616.3 %copy-start.77 = (f32[1024]{0:T(1024)}, f32[1024]{0:T(1024)S(1)}, u32[]{:S(2)}) copy-start(f32[1024]{0:T(1024)S(1)} %get-tuple-element.217) | copy-start | bytes 12292
  136.5 580.6 %copy-start.11 = (f32[2,256,1024]{2,1,0:T(8,128)}, f32[2,256,1024]{2,1,0:T(8,128)S(1)}, u32[]{:S(2)}) copy-start(f32[2,256,1024]{2,1,0:T(8,128)S(1)} %convert_add_fusion) | copy-start | bytes 6291460
  136.7 166.5 %copy-start.134 = (f32[256]{0:T(256)}, f32[256]{0:T(256)S(1)}, u32[]{:S(2)}) copy-start(f32[256]{0:T(256)S(1)} %get-tuple-element.329) | copy-start | bytes 3076
  136.7 580.4 %copy-start.136 = (f32[256]{0:T(256)}, f32[256]{0:T(256)S(1)}, u32[]{:S(2)}) copy-start(f32[256]{0:T(256)S(1)} %get-tuple-element.330) | copy-start | bytes 3076
  137.1 166.1 %copy-start.144 = (f32[256]{0:T(256)}, f32[256]{0:T(256)S(1)}, u32[]{:S(2)}) copy-start(f32[256]{0:T(256)S(1)} %add_rsqrt_fusion) | copy-start | bytes 3076
  197.9 105.2 %all-gather.18.cloned.1.call-start = ((), (), s32[]{:S(2)}) async-start(), calls=%async_computation.11 | async-start | bytes 6488064 | tf_op jit(solution)/shard_map/all_gather | solution.py:220
  198.7 163.6 %all-gather.26.cloned.1.call-start = ((), (), s32[]{:S(2)}) async-start(), calls=%async_computation.15 | async-start | bytes 2162688 | tf_op jit(solution)/shard_map/all_gather | solution.py:223
  199.4 279.9 %all-gather.22.cloned.1.call-start = ((), (), s32[]{:S(2)}) async-start(), calls=%async_computation.13 | async-start | bytes 17301504 | tf_op jit(solution)/shard_map/all_gather | solution.py:221
  200.0 395.4 %all-gather.24.cloned.1.call-start = ((), (), s32[]{:S(2)}) async-start(), calls=%async_computation.14 | async-start | bytes 17301504 | tf_op jit(solution)/shard_map/all_gather | solution.py:222
  200.6 453.4 %all-gather.28.cloned.1.call-start = ((), (), s32[]{:S(2)}) async-start(), calls=%async_computation.16 | async-start | bytes 2162688 | tf_op jit(solution)/shard_map/all_gather | solution.py:224
  201.3 487.8 %all-gather.16.cloned.1.call-start = ((), (), s32[]{:S(2)}) async-start(), calls=%async_computation.10 | async-start | bytes 5242880 | tf_op jit(solution)/shard_map/all_gather | solution.py:68
  202.7 514.5 %copy-start.146 = (f32[256]{0:T(256)}, f32[256]{0:T(256)S(1)}, u32[]{:S(2)}) copy-start(f32[256]{0:T(256)S(1)} %add_rsqrt_fusion.1) | copy-start | bytes 3076
  210.3 515.0 %all-gather.30.cloned.1.call-start = ((), (), s32[]{:S(2)}) async-start(), calls=%async_computation.17 | async-start | bytes 5242880 | tf_op jit(solution)/shard_map/all_gather | solution.py:68
  305.8 348.2 %copy-start.9 = (f32[256,1024]{1,0:T(8,128)}, f32[256,1024]{1,0:T(8,128)S(1)}, u32[]{:S(2)}) copy-start(f32[256,1024]{1,0:T(8,128)S(1)} %get-tuple-element.304) | copy-start | bytes 3145732
  305.8 348.2 %copy-start.94 = (f32[256]{0:T(256)}, f32[256]{0:T(256)S(1)}, u32[]{:S(2)}) copy-start(f32[256]{0:T(256)S(1)} %broadcast_multiply_fusion.3) | copy-start | bytes 3076
  306.1 56.2 %copy-start.118 = (f32[256]{0:T(256)}, f32[256]{0:T(256)S(1)}, u32[]{:S(2)}) copy-start(f32[256]{0:T(256)S(1)} %multiply_reduce_fusion.16) | copy-start | bytes 3076
  306.1 347.9 %copy-start.101 = (f32[256]{0:T(256)}, f32[256]{0:T(256)S(1)}, u32[]{:S(2)}) copy-start(f32[256]{0:T(256)S(1)} %fusion.201) | copy-start | bytes 3076
  366.0 288.0 %copy-start.47 = (bf16[256,512]{1,0:T(8,128)(2,1)}, bf16[256,512]{1,0:T(8,128)(2,1)S(1)}, u32[]{:S(2)}) copy-start(bf16[256,512]{1,0:T(8,128)(2,1)S(1)} %get-tuple-element.280) | copy-start | bytes 786436
  661.7 137.4 %all-gather.32.cloned.1.call-start = ((), (), s32[]{:S(2)}) async-start(), calls=%async_computation.18 | async-start | bytes 2621440 | tf_op jit(solution)/shard_map/all_gather | solution.py:275
  776.4 157.8 %reduce-scatter.13.cloned.1.call-start = ((), (), s32[]{:S(2)}) async-start(), calls=%async_computation.19 | async-start | bytes 2621440 | tf_op jit(solution)/shard_map/reduce_scatter | solution.py:317
  799.1 73.4 %copy-start.109 = (f32[1024]{0:T(1024)S(1)}, f32[1024]{0:T(1024)}, u32[]{:S(2)}) copy-start(f32[1024]{0:T(1024)} %get-tuple-element.332) | copy-start | bytes 12292
  902.6 144.9 %reduce-scatter.15.cloned.1.call-start = ((), (), s32[]{:S(2)}) async-start(), calls=%async_computation.20 | async-start | bytes 5242880 | tf_op jit(solution)/shard_map/reduce_scatter | solution.py:144
  1002.7 44.7 %copy-start.18 = (f32[256,1024]{1,0:T(8,128)S(1)}, f32[256,1024]{1,0:T(8,128)}, u32[]{:S(2)}) copy-start(f32[256,1024]{1,0:T(8,128)} %copy-done.17) | copy-start | bytes 3145732
  1002.7 44.7 %copy-start.107 = (f32[1024]{0:T(1024)S(1)}, f32[1024]{0:T(1024)}, u32[]{:S(2)}) copy-start(f32[1024]{0:T(1024)} %copy-done.106) | copy-start | bytes 12292
  1002.7 44.7 %copy-start.117 = (f32[256]{0:T(256)S(1)}, f32[256]{0:T(256)}, u32[]{:S(2)}) copy-start(f32[256]{0:T(256)} %copy-done.116) | copy-start | bytes 3076
  1002.7 196.7 %reduce-scatter.21.cloned.1.call-start = ((), (), s32[]{:S(2)}) async-start(), calls=%async_computation.23 | async-start | bytes 5242880 | tf_op jit(solution)/shard_map/reduce_scatter | solution.py:144
  1003.4 77.8 %copy-start.60 = (f32[16,256]{1,0:T(8,128)}, f32[16,256]{1,0:T(8,128)S(1)}, u32[]{:S(2)}) copy-start(f32[16,256]{1,0:T(8,128)S(1)} %log_add_fusion.1) | copy-start | bytes 49156
  1003.4 48.6 %copy-start.123 = (f32[256]{0:T(256)S(1)}, f32[256]{0:T(256)}, u32[]{:S(2)}) copy-start(f32[256]{0:T(256)} %copy-done.122) | copy-start | bytes 3076
  1119.5 98.4 %reduce-scatter.23.cloned.1.call-start = ((), (), s32[]{:S(2)}) async-start(), calls=%async_computation.24 | async-start | bytes 5242880 | tf_op jit(solution)/shard_map/reduce_scatter | solution.py:144
  1173.2 188.2 %reduce-scatter.17.cloned.1.call-start = ((), (), s32[]{:S(2)}) async-start(), calls=%async_computation.21 | async-start | bytes 4325376 | tf_op jit(solution)/shard_map/reduce_scatter | solution.py:355
  1178.3 322.2 %reduce-scatter.19.cloned.1.call-start = ((), (), s32[]{:S(2)}) async-start(), calls=%async_computation.22 | async-start | bytes 4325376 | tf_op jit(solution)/shard_map/reduce_scatter | solution.py:358
  1183.3 449.0 %reduce-scatter.25.cloned.1.call-start = ((), (), s32[]{:S(2)}) async-start(), calls=%async_computation.25 | async-start | bytes 540672
  1218.0 456.3 %copy-start.100 = (f32[2,7,32]{2,0,1:T(2,128)S(1)}, f32[2,7,32]{2,0,1:T(2,128)}, u32[]{:S(2)}) copy-start(f32[2,7,32]{2,0,1:T(2,128)} %param.35) | copy-start | bytes 5380
  1218.0 456.3 %copy-start.130 = (f32[2,7,32]{2,0,1:T(2,128)S(1)}, f32[2,7,32]{2,0,1:T(2,128)}, u32[]{:S(2)}) copy-start(f32[2,7,32]{2,0,1:T(2,128)} %param.41) | copy-start | bytes 5380
  1218.0 456.3 %copy-start.131 = (f32[2,7,32]{2,0,1:T(2,128)S(1)}, f32[2,7,32]{2,0,1:T(2,128)}, u32[]{:S(2)}) copy-start(f32[2,7,32]{2,0,1:T(2,128)} %param.40) | copy-start | bytes 5380
  1218.1 458.1 %copy-start.57 = (f32[2,32,512]{2,1,0:T(8,128)S(1)}, f32[2,32,512]{2,1,0:T(8,128)}, u32[]{:S(2)}) copy-start(f32[2,32,512]{2,1,0:T(8,128)} %param.33) | copy-start | bytes 393220
  1218.1 458.1 %copy-start.68 = (f32[2,32,512]{2,1,0:T(8,128)S(1)}, f32[2,32,512]{2,1,0:T(8,128)}, u32[]{:S(2)}) copy-start(f32[2,32,512]{2,1,0:T(8,128)} %param.37) | copy-start | bytes 393220
  1218.1 458.1 %copy-start.69 = (f32[2,32,512]{2,1,0:T(8,128)S(1)}, f32[2,32,512]{2,1,0:T(8,128)}, u32[]{:S(2)}) copy-start(f32[2,32,512]{2,1,0:T(8,128)} %param.36) | copy-start | bytes 393220
  1224.2 453.7 %copy-start.59 = (f32[2,16,1024]{2,1,0:T(8,128)S(1)}, f32[2,16,1024]{2,1,0:T(8,128)}, u32[]{:S(2)}) copy-start(f32[2,16,1024]{2,1,0:T(8,128)} %param.34) | copy-start | bytes 393220
  1224.2 453.7 %copy-start.70 = (f32[2,16,1024]{2,1,0:T(8,128)S(1)}, f32[2,16,1024]{2,1,0:T(8,128)}, u32[]{:S(2)}) copy-start(f32[2,16,1024]{2,1,0:T(8,128)} %param.39) | copy-start | bytes 393220
  1224.2 453.7 %copy-start.71 = (f32[2,16,1024]{2,1,0:T(8,128)S(1)}, f32[2,16,1024]{2,1,0:T(8,128)}, u32[]{:S(2)}) copy-start(f32[2,16,1024]{2,1,0:T(8,128)} %param.38) | copy-start | bytes 393220
  (145 other events, 1226.8 us)
Sparse Core Ops, SparseCore 0:
  41.5 48.7 reduce-scatter.10
  198.1 32.6 all-gather.19
  234.1 69.0 all-gather.17
  306.9 55.3 all-gather.25
  365.5 113.7 all-gather.21
  482.5 112.9 all-gather.23
  599.3 54.6 all-gather.27
  655.6 33.4 all-gather.15
  690.8 34.4 all-gather.29
  776.5 22.5 all-gather.31
  902.7 31.3 reduce-scatter.12
  1002.9 44.5 reduce-scatter.14
  1119.6 44.4 reduce-scatter.20
  1173.4 44.4 reduce-scatter.22
  1220.1 141.3 reduce-scatter.16
  1363.7 136.7 reduce-scatter.18
  1502.7 129.5 reduce-scatter.24
Sparse Core Ops, SparseCore 1:
  45.1 135.1 all-gather.13
where the time goes:
time: 1690 us
  waiting for transfers between devices  961 us (57%)
  matrix products  318 us (19%)
  other arithmetic  163 us (10%)
  blocking collectives  114 us (7%)
  local copies, waits for them, and re-layouts  106 us (6%)
  between operations  24.5 us (1%)
    reduce_scatter x1, waiting for transfers between devices, shards(): lax.psum_scatter(jnp.stack([up_enc, up_dec]), ('seq', 'enc'), scatter_dim...  137 us
    reduce_scatter x1, waiting for transfers between devices, shards(): lax.psum_scatter(jnp.stack([down_enc, down_dec]), ('seq', 'enc'), scatter...  135 us
    unnamed x19, waiting for transfers between devices  131 us
    all_gather x1, waiting for transfers between devices, shards(): lax.all_gather(feed_in, ('seq', 'enc'), axis=1, tiled=True)  113 us
    all_gather x1, waiting for transfers between devices, shards(): lax.all_gather(feed_out, ('seq', 'enc'), axis=1, tiled=True)  108 us
    dot_general x15, matrix products, dense_back(): lax.dot_general(left, right, (((1,), (1,)), ((), ())), preferred_element_...  108 us
    dot_general x18, matrix products, dense(): return jnp.dot(left, right, preferred_element_type=jnp.float32)  90.3 us
    all_gather x1, waiting for transfers between devices, shards(): lax.all_gather(adapter_down.astype(jnp.bfloat16), ('seq', 'enc'), axis=1,...  56.2 us
  transfers between devices with their start and end apart: 18, of which 16 were waited for; matrix products, arithmetic and copies ran while one was open for 15% of the time, Pallas kernels for 0%

commit v1 on v0

v1 whole, which is shorter than its diff:
```python
import jax
import jax.numpy as jnp
from jax import lax
from jax.experimental import pallas as pl
from jax.experimental.pallas import tpu as pltpu
from jax.sharding import PartitionSpec as P

HEAD_DIM = 64
STEP = 10

EPSILON = 1e-05
ADAPTER_SCALE = 4.0
CLIP_NORM = 0.25
RATE_ADAPTER = 0.05
RATE_NORMS = 0.5
BETA_FIRST = 0.9
BETA_SECOND = 0.999
ADAM_EPSILON = 1e-08
DECAY_ADAPTER = 0.01
MASKED_SCORE = -1000000000.0

LOW = jnp.bfloat16
F32 = jnp.float32
MIB = 1024 * 1024


def flip(value, axis, mask):
    count = lax.axis_size(axis)
    return lax.ppermute(value, axis, [(i, i ^ mask) for i in range(count)])


def bits(axis):
    count = lax.axis_size(axis)
    return [1 << i for i in range(count.bit_length() - 1)]


def unxor(blocks, me):
    blocks = list(blocks)
    mask = 1
    while mask < len(blocks):
        bit = (me & mask) != 0
        blocks = [jnp.where(bit, blocks[i ^ mask], blocks[i]) for i in range(len(blocks))]
        mask *= 2
    return blocks


def gather_enc(value):
    found = {0: value}
    for mask in bits("enc")[1:]:
        found.update({j | mask: flip(v, "enc", mask) for j, v in list(found.items())})
    found.update({j | 1: flip(v, "enc", 1) for j, v in list(found.items())})
    return [found[j] for j in range(len(found))]


def scatter_enc(blocks):
    held = dict(enumerate(blocks))
    for mask in bits("enc"):
        away = [j for j in held if j & mask]
        sent = [flip(held[j].astype(LOW), "enc", mask) for j in away]
        for j, part in zip(away, sent):
            held[j ^ mask] = held[j ^ mask].astype(F32) + part.astype(F32)
            del held[j]
    return held[0]


def swap_blocks(blocks):
    return [blocks[0]] + [flip(blocks[j], "enc", j) for j in range(1, len(blocks))]


def pair_split(shard, core):
    half = shard.shape[1] // 2
    first = core == 0
    low, high = shard[:, :half], shard[:, half:]
    keep = jnp.where(first, low, high)
    came = flip(jnp.where(first, high, low), "enc", 1)
    return jnp.concatenate([jnp.where(first, keep, came), jnp.where(first, came, keep)], 0)


def gather_first(value):
    stacked, offsets = value[None], [0]
    for mask in bits("seq")[1:]:
        stacked = jnp.concatenate([stacked, flip(stacked, "seq", mask)], 0)
        offsets = offsets + [o ^ mask for o in offsets]
    return stacked, offsets


def replicate(value, chips_last):
    stacked, offsets = gather_first(value)
    found = {(0, 0): stacked}
    near = [("seq", 1)]
    across = [("enc", mask) for mask in bits("enc")[1:]]
    for axis, mask in near + across if chips_last else across + near:
        fresh = {}
        for (s, e), v in found.items():
            fresh[(s ^ mask, e) if axis == "seq" else (s, e ^ mask)] = flip(v, axis, mask)
        found.update(fresh)
    return [(s, e, v) for (s, e), v in found.items()], offsets


def assemble(sources, pieces, places, outs):
    count = len(pieces)
    n_src, n_out = len(sources), len(outs)

    def kernel(*refs):
        table = refs[0]
        given = refs[1 : 1 + n_src]
        results = refs[1 + n_src : 1 + n_src + n_out]
        stage = refs[1 + n_src + n_out : 1 + n_src + n_out + count]
        sem_in, sem_out = refs[-2:]
        copies_in, copies_out = [], []
        for i, (src, block, row, column, rows, columns, out) in enumerate(pieces):
            copies_in.append(
                pltpu.make_async_copy(
                    given[src].at[block, pl.ds(row, rows), pl.ds(column, columns)],
                    stage[i],
                    sem_in.at[i],
                )
            )
            to_row = pl.multiple_of(table[2 * i], rows)
            to_column = pl.multiple_of(table[2 * i + 1], columns)
            copies_out.append(
                pltpu.make_async_copy(
                    stage[i],
                    results[out].at[pl.ds(to_row, rows), pl.ds(to_column, columns)],
                    sem_out.at[i],
                )
            )
        for copy in copies_in:
            copy.start()
        for i in range(count):
            copies_in[i].wait()
            copies_out[i].start()
        for copy in copies_out:
            copy.wait()

    size = sum(p[4] * p[5] * 2 for p in pieces)
    return pl.pallas_call(
        kernel,
        out_shape=[jax.ShapeDtypeStruct(shape, LOW) for shape in outs],
        in_specs=[pl.BlockSpec(memory_space=pltpu.SMEM)]
        + [pl.BlockSpec(memory_space=pl.ANY)] * n_src,
        out_specs=[pl.BlockSpec(memory_space=pl.ANY)] * n_out,
        scratch_shapes=[pltpu.VMEM((p[4], p[5]), LOW) for p in pieces]
        + [pltpu.SemaphoreType.DMA((count,)), pltpu.SemaphoreType.DMA((count,))],
        compiler_params=pltpu.CompilerParams(vmem_limit_bytes=size + 8 * MIB),
        cost_estimate=pl.CostEstimate(flops=0, bytes_accessed=2 * size, transcendentals=0),
    )(places, *sources)


def spread_matrix(shards, chips_last, layout, outs, seq, enc):
    n_enc = lax.axis_size("enc")
    core = enc & 1
    buffers, offsets = replicate(pair_split(shards, core), chips_last)
    sources, pieces, places = [], [], []
    for s_off, e_off, buffer in buffers:
        for mine, v in ((True, buffer), (False, flip(buffer, "enc", 1))):
            half = core if mine else 1 - core
            for n, o in enumerate(offsets):
                device = (seq ^ s_off ^ o) * n_enc + (enc ^ e_off)
                for row, column, rows, columns, out, to_row, to_column in layout(device >> 1, half):
                    pieces.append((len(sources), n, row, column, rows, columns, out))
                    places += [to_row, to_column]
            sources.append(v)
    return assemble(sources, pieces, jnp.stack([jnp.asarray(p, jnp.int32) for p in places]), outs)


def dense(left, right):
    return jnp.dot(left, right, preferred_element_type=F32)


def dense_back(left, right):
    return lax.dot_general(left, right, (((1,), (1,)), ((), ())), preferred_element_type=F32)


def inner_rows(left, right):
    return lax.dot_general(left, right, (((0,), (0,)), ((), ())), preferred_element_type=F32)


def layer_norm(values, gain, shift):
    middle = jnp.mean(values, -1, keepdims=True)
    centred = values - middle
    variance = jnp.mean(centred * centred, -1, keepdims=True)
    return centred * lax.rsqrt(variance + EPSILON) * gain + shift


def norm_forward(values, norms, index):
    return jax.vjp(layer_norm, values, norms[0, index], norms[1, index])


def adamw(grad, moment, second, weight, rate, decay):
    moment = BETA_FIRST * moment + (1.0 - BETA_FIRST) * grad
    second = BETA_SECOND * second + (1.0 - BETA_SECOND) * grad * grad
    corrected = moment / (1.0 - BETA_FIRST**STEP)
    scale_two = jnp.sqrt(second / (1.0 - BETA_SECOND**STEP))
    return (
        moment,
        second,
        weight - rate * (corrected / (scale_two + ADAM_EPSILON) + decay * weight),
    )


def masked_scores(query, key, spots, limit):
    raw = lax.dot_general(query, key, (((1,), (1,)), ((), ())), preferred_element_type=F32)
    return jnp.where(spots < limit, raw, MASKED_SCORE)


def attend_kernel(limit_ref, spot_ref, q_ref, k_ref, v_ref, context_ref, total_ref):
    scaled = q_ref[...] * jnp.asarray(0.125, LOW)
    key, value = k_ref[...], v_ref[...]
    side = lax.broadcasted_iota(jnp.int32, scaled.shape, 1) // HEAD_DIM
    context = jnp.zeros(scaled.shape, F32)
    total = jnp.zeros(scaled.shape, F32)
    for head in range(scaled.shape[1] // HEAD_DIM):
        own = side == head
        query = jnp.where(own, scaled, jnp.zeros((), LOW))
        scores = masked_scores(query, key, spot_ref[...], limit_ref[...])
        highest = jnp.max(scores, -1, keepdims=True)
        exponent = jnp.exp(scores - highest)
        summed = jnp.sum(exponent, -1, keepdims=True)
        mixed = jnp.dot(exponent.astype(LOW), value, preferred_element_type=F32) / summed
        context = jnp.where(own, mixed, context)
        total = jnp.where(own, highest + jnp.log(summed), total)
    context_ref[...] = context.astype(LOW)
    total_ref[...] = total


def attend(query, keys, key_at, value_at, limit, spots, rows):
    length = query.shape[0]
    width = keys.shape[1] // (2 if key_at == 0 else 3)
    pairs = width // 128
    steps = length // rows
    return pl.pallas_call(
        attend_kernel,
        grid=(pairs, steps),
        out_shape=[
            jax.ShapeDtypeStruct((length, width), LOW),
            jax.ShapeDtypeStruct((length, width), F32),
        ],
        in_specs=[
            pl.BlockSpec((rows, 1), lambda p, j: (j, 0)),
            pl.BlockSpec((1, length), lambda p, j: (0, 0)),
            pl.BlockSpec((rows, 128), lambda p, j: (j, p)),
            pl.BlockSpec((length, 128), lambda p, j: (0, key_at + p)),
            pl.BlockSpec((length, 128), lambda p, j: (0, value_at + p)),
        ],
        out_specs=[
            pl.BlockSpec((rows, 128), lambda p, j: (j, p)),
            pl.BlockSpec((rows, 128), lambda p, j: (j, p)),
        ],
        compiler_params=pltpu.CompilerParams(vmem_limit_bytes=48 * MIB),
        cost_estimate=pl.CostEstimate(
            flops=8 * length * length * width,
            bytes_accessed=8 * length * width,
            transcendentals=length * length * width // HEAD_DIM,
        ),
    )(limit, spots, query, keys, keys)


def attend_back_kernel(
    limit_ref, spot_ref, q_ref, k_ref, v_ref, grad_ref, total_ref, out_ref, dk_sum, dv_sum
):
    pair, step = pl.program_id(0), pl.program_id(1)
    pairs, steps = pl.num_programs(0), pl.num_programs(1)
    rows = q_ref.shape[0]

    @pl.when(step == 0)
    def _():
        dk_sum[...] = jnp.zeros_like(dk_sum)
        dv_sum[...] = jnp.zeros_like(dv_sum)

    scaled = q_ref[...] * jnp.asarray(0.125, LOW)
    key, value = k_ref[...], v_ref[...]
    grads, totals = grad_ref[...], total_ref[...]
    side = lax.broadcasted_iota(jnp.int32, scaled.shape, 1) // HEAD_DIM
    grad_query = jnp.zeros(scaled.shape, F32)
    nought = jnp.zeros((), LOW)
    for head in range(scaled.shape[1] // HEAD_DIM):
        own = side == head
        query = jnp.where(own, scaled, nought)
        grad = jnp.where(own, grads, nought)
        scores = masked_scores(query, key, spot_ref[...], limit_ref[...])
        soft = jnp.exp(scores - totals[:, head * HEAD_DIM : head * HEAD_DIM + 1])
        grad_soft = lax.dot_general(
            grad, value, (((1,), (1,)), ((), ())), preferred_element_type=F32
        )
        weighted = jnp.sum(soft * grad_soft, -1, keepdims=True)
        grad_scores = (soft * (grad_soft - weighted)).astype(LOW)
        grad_query = jnp.where(
            own, jnp.dot(grad_scores, key, preferred_element_type=F32), grad_query
        )
        dk_sum[...] += inner_rows(grad_scores, query)
        dv_sum[...] += inner_rows(soft.astype(LOW), grad)
    column = pl.multiple_of(pair * 128, 128)
    out_ref[pl.ds(pl.multiple_of(step * rows, rows), rows), pl.ds(column, 128)] = (
        grad_query * 0.125
    ).astype(LOW)

    @pl.when(step == steps - 1)
    def _():
        out_ref[:, pl.ds(pl.multiple_of((pairs + pair) * 128, 128), 128)] = dk_sum[...].astype(LOW)
        out_ref[:, pl.ds(pl.multiple_of((2 * pairs + pair) * 128, 128), 128)] = dv_sum[...].astype(
            LOW
        )


def attend_back(query, keys, key_at, value_at, limit, spots, rows, grads, totals):
    length, width = grads.shape
    pairs = width // 128
    steps = length // rows
    return pl.pallas_call(
        attend_back_kernel,
        grid=(pairs, steps),
        out_shape=jax.ShapeDtypeStruct((length, 3 * width), LOW),
        in_specs=[
            pl.BlockSpec((rows, 1), lambda p, j: (j, 0)),
            pl.BlockSpec((1, length), lambda p, j: (0, 0)),
            pl.BlockSpec((rows, 128), lambda p, j: (j, p)),
            pl.BlockSpec((length, 128), lambda p, j: (0, key_at + p)),
            pl.BlockSpec((length, 128), lambda p, j: (0, value_at + p)),
            pl.BlockSpec((rows, 128), lambda p, j: (j, p)),
            pl.BlockSpec((rows, 128), lambda p, j: (j, p)),
        ],
        out_specs=pl.BlockSpec((length, 3 * width), lambda p, j: (0, 0)),
        scratch_shapes=[pltpu.VMEM((length, 128), F32), pltpu.VMEM((length, 128), F32)],
        compiler_params=pltpu.CompilerParams(vmem_limit_bytes=56 * MIB),
        cost_estimate=pl.CostEstimate(
            flops=20 * length * length * width,
            bytes_accessed=16 * length * width,
            transcendentals=length * length * width // HEAD_DIM,
        ),
    )(limit, spots, query, keys, keys, grads, totals)


def gelu_both(values):
    below = 0.5 * (1.0 + lax.erf(values * 0.7071067811865476))
    bell = jnp.exp(values * values * -0.5) * 0.3989422804014327
    return values * below, below + values * bell


def branch_kernel(x_ref, in_ref, out_ref, down_ref, up_ref, y_ref, slope_ref, act_ref, bend_ref, total):
    step = pl.program_id(0)

    @pl.when(step == 0)
    def _():
        act, slope = gelu_both(jnp.dot(x_ref[...], down_ref[...], preferred_element_type=F32))
        act = act.astype(LOW)
        act_ref[...] = act
        bend_ref[...] = slope
        total[...] = ADAPTER_SCALE * jnp.dot(act, up_ref[...], preferred_element_type=F32)

    act, slope = gelu_both(jnp.dot(x_ref[...], in_ref[...], preferred_element_type=F32))
    slope_ref[...] = slope
    total[...] += jnp.dot(act.astype(LOW), out_ref[...], preferred_element_type=F32)

    @pl.when(step == pl.num_programs(0) - 1)
    def _():
        y_ref[...] = total[...]


def branch(rows_low, expand, reduce, down, up, layer, tile=512):
    rows, width = rows_low.shape
    hidden = expand.shape[1]
    small = down.shape[1]
    return pl.pallas_call(
        branch_kernel,
        grid=(hidden // tile,),
        out_shape=[
            jax.ShapeDtypeStruct((rows, width), F32),
            jax.ShapeDtypeStruct((rows, hidden), F32),
            jax.ShapeDtypeStruct((rows, small), LOW),
            jax.ShapeDtypeStruct((rows, small), F32),
        ],
        in_specs=[
            pl.BlockSpec((rows, width), lambda j: (0, 0)),
            pl.BlockSpec((width, tile), lambda j: (0, j)),
            pl.BlockSpec((tile, width), lambda j: (j, 0)),
            pl.BlockSpec((width, small), lambda j: (layer, 0)),
            pl.BlockSpec((small, width), lambda j: (layer, 0)),
        ],
        out_specs=[
            pl.BlockSpec((rows, width), lambda j: (0, 0)),
            pl.BlockSpec((rows, tile), lambda j: (0, j)),
            pl.BlockSpec((rows, small), lambda j: (0, 0)),
            pl.BlockSpec((rows, small), lambda j: (0, 0)),
        ],
        scratch_shapes=[pltpu.VMEM((rows, width), F32)],
        compiler_params=pltpu.CompilerParams(vmem_limit_bytes=48 * MIB),
        cost_estimate=pl.CostEstimate(
            flops=4 * rows * width * (hidden + small),
            bytes_accessed=4 * width * (hidden + small) + 4 * rows * hidden,
            transcendentals=2 * rows * hidden,
        ),
    )(rows_low, expand, reduce, down, up)


def branch_back_kernel(g_ref, ga_ref, in_ref, out_ref, down_ref, up_ref, slope_ref, bend_ref, dx_ref, dpre_ref, total):
    step = pl.program_id(0)

    @pl.when(step == 0)
    def _():
        grad = dense_back(ga_ref[...], up_ref[...])
        pre = (grad * bend_ref[...]).astype(LOW)
        dpre_ref[...] = pre
        total[...] = dense_back(pre, down_ref[...])

    grad = dense_back(g_ref[...], out_ref[...])
    total[...] += dense_back((grad * slope_ref[...]).astype(LOW), in_ref[...])

    @pl.when(step == pl.num_programs(0) - 1)
    def _():
        dx_ref[...] = total[...]


def branch_back(grad_out, kept, expand, reduce, down, up, layer, tile=512):
    rows_low, slope, act, bend = kept
    rows, width = rows_low.shape
    hidden = expand.shape[1]
    small = down.shape[1]
    grad_low = grad_out.astype(LOW)
    grad_adapter = (ADAPTER_SCALE * grad_out).astype(LOW)
    grad_rows, grad_pre = pl.pallas_call(
        branch_back_kernel,
        grid=(hidden // tile,),
        out_shape=[
            jax.ShapeDtypeStruct((rows, width), F32),
            jax.ShapeDtypeStruct((rows, small), LOW),
        ],
        in_specs=[
            pl.BlockSpec((rows, width), lambda j: (0, 0)),
            pl.BlockSpec((rows, width), lambda j: (0, 0)),
            pl.BlockSpec((width, tile), lambda j: (0, j)),
            pl.BlockSpec((tile, width), lambda j: (j, 0)),
            pl.BlockSpec((width, small), lambda j: (layer, 0)),
            pl.BlockSpec((small, width), lambda j: (layer, 0)),
            pl.BlockSpec((rows, tile), lambda j: (0, j)),
            pl.BlockSpec((rows, small), lambda j: (0, 0)),
        ],
        out_specs=[
            pl.BlockSpec((rows, width), lambda j: (0, 0)),
            pl.BlockSpec((rows, small), lambda j: (0, 0)),
        ],
        scratch_shapes=[pltpu.VMEM((rows, width), F32)],
        compiler_params=pltpu.CompilerParams(vmem_limit_bytes=48 * MIB),
        cost_estimate=pl.CostEstimate(
            flops=4 * rows * width * (hidden + small),
            bytes_accessed=4 * width * (hidden + small) + 4 * rows * hidden,
            transcendentals=0,
        ),
    )(grad_low, grad_adapter, expand, reduce, down, up, slope, bend)
    return grad_rows, inner_rows(rows_low, grad_pre), inner_rows(act, grad_adapter)


def head_kernel(o_ref, e_ref, g_ref, lse_ref, acc, peak, mass):
    step = pl.program_id(0)
    part = 256

    @pl.when(step == 0)
    def _():
        acc[...] = jnp.zeros_like(acc)
        peak[...] = jnp.full_like(peak, -1e30)
        mass[...] = jnp.zeros_like(mass)

    table = e_ref[...]
    for start in range(0, o_ref.shape[0], part):
        at = pl.ds(start, part)
        logits = dense_back(o_ref[at, :], table)
        before = peak[at, :1]
        highest = jnp.maximum(before, jnp.max(logits, -1, keepdims=True))
        exponent = jnp.exp(logits - highest)
        fade = jnp.exp(before - highest)
        mass[at, :] = mass[at, :] * fade + jnp.sum(exponent, -1, keepdims=True)
        acc[at, :] = acc[at, :] * fade + jnp.dot(
            exponent.astype(LOW), table, preferred_element_type=F32
        )
        peak[at, :] = jnp.broadcast_to(highest, (part, 128))

    @pl.when(step == pl.num_programs(0) - 1)
    def _():
        g_ref[...] = (acc[...] / mass[:, :1]).astype(LOW)
        lse_ref[...] = peak[...] + jnp.log(mass[...])


def head(rows_low, table):
    rows, width = rows_low.shape
    entries = table.shape[0]
    tile = next(t for t in (1280, 1024, 640, 512, 256, 128) if entries % t == 0)
    return pl.pallas_call(
        head_kernel,
        grid=(entries // tile,),
        out_shape=[
            jax.ShapeDtypeStruct((rows, width), LOW),
            jax.ShapeDtypeStruct((rows, 128), F32),
        ],
        in_specs=[
            pl.BlockSpec((rows, width), lambda j: (0, 0)),
            pl.BlockSpec((tile, width), lambda j: (j, 0)),
        ],
        out_specs=[
            pl.BlockSpec((rows, width), lambda j: (0, 0)),
            pl.BlockSpec((rows, 128), lambda j: (0, 0)),
        ],
        scratch_shapes=[
            pltpu.VMEM((rows, width), F32),
            pltpu.VMEM((rows, 128), F32),
            pltpu.VMEM((rows, 128), F32),
        ],
        compiler_params=pltpu.CompilerParams(vmem_limit_bytes=56 * MIB),
        cost_estimate=pl.CostEstimate(
            flops=4 * rows * width * entries,
            bytes_accessed=2 * width * entries,
            transcendentals=rows * entries,
        ),
    )(rows_low, table)


def reduce_shards(grad, seq, enc, order):
    n_seq, n_enc = lax.axis_size("seq"), lax.axis_size("enc")
    shard = grad.shape[0] // (n_seq * n_enc)
    seq_bits, enc_bits = len(bits("seq")), len(bits("enc"))
    held = grad.reshape((2,) * (seq_bits + enc_bits) + (shard, grad.shape[1]))
    left = [("seq", 1 << i) for i in reversed(range(seq_bits))]
    left += [("enc", 1 << i) for i in reversed(range(enc_bits))]
    for axis, mask in order:
        where = left.index((axis, mask))
        left.pop(where)
        bit = ((seq if axis == "seq" else enc) & mask) != 0
        low = lax.index_in_dim(held, 0, where, keepdims=False)
        high = lax.index_in_dim(held, 1, where, keepdims=False)
        keep = jnp.where(bit, high, low)
        send = jnp.where(bit, low, high)
        if axis == "enc" and mask == 1:
            held = keep + flip(send, axis, mask)
        else:
            held = keep + flip(send.astype(LOW), axis, mask).astype(F32)
    return held


def shards(
    source_ids,
    target_ids,
    labels,
    lengths,
    embedding,
    positions,
    attention_in,
    attention_out,
    feed_in,
    feed_out,
    adapter_down,
    adapter_up,
    norm_params,
    down_moment,
    down_second,
    up_moment,
    up_second,
    norm_moment,
    norm_second,
):
    n_seq, n_enc = lax.axis_size("seq"), lax.axis_size("enc")
    n_all = n_seq * n_enc
    seq, enc = lax.axis_index("seq"), lax.axis_index("enc")
    core = enc & 1
    own_rows = source_ids.shape[1]
    width = embedding.shape[1]
    entries = embedding.shape[0]
    length = own_rows * n_enc
    share = width // n_enc
    source_length, target_length = lengths[0, 0], lengths[0, 1]

    norms = norm_params.astype(LOW).reshape(1, 14, -1)
    for axis in ("enc", "seq"):
        for mask in bits(axis):
            norms = jnp.concatenate([norms, flip(norms, axis, mask)], 0)
    order = jnp.arange(n_all) ^ (seq * n_enc + enc)
    norms = jnp.take(norms, order, axis=0).transpose(1, 0, 2).reshape(2, 7, width).astype(F32)

    ids = jnp.concatenate([source_ids, target_ids, labels], 0)
    all_ids = jnp.stack(gather_enc(ids)) - enc * entries

    def lookup(which):
        local = all_ids[:, which]
        inside = (local >= 0) & (local < entries)
        found = jnp.take(embedding, jnp.clip(local, 0, entries - 1), axis=0)
        found = jnp.where(inside[:, :, None], found, jnp.zeros((), LOW))
        return scatter_enc([found[j] for j in range(n_enc)])

    source_rows = lookup(0) + positions[0].astype(F32)
    target_rows = lookup(1) + positions[1].astype(F32)
    label_rows = lookup(2)

    triple = attention_in.reshape(3, -1, 3, n_enc, share).transpose(3, 1, 0, 2, 4)
    triple = triple.reshape(n_enc, triple.shape[1], 9 * share)
    shard_rows = triple.shape[1]
    swapped = swap_blocks(
        [lax.dynamic_index_in_dim(triple, enc ^ j, 0, keepdims=False) for j in range(n_enc)]
    )
    strip = jnp.concatenate(unxor(swapped, enc), 0)
    strip_rows = n_enc * shard_rows
    stacked, offsets = gather_first(strip)
    strips = [(0, stacked), (1, flip(stacked, "seq", 1))]
    sources, pieces, places = [], [], []
    for s_off, buffer in strips:
        for n, o in enumerate(offsets):
            for k in range(3):
                pieces.append((len(sources), n, 0, k * 3 * share, strip_rows, 3 * share, k))
                places += [(seq ^ s_off ^ o) * strip_rows, 0]
        sources.append(buffer)
    attend_in = assemble(
        sources,
        pieces,
        jnp.stack([jnp.asarray(p, jnp.int32) for p in places]),
        [(width, 3 * share)] * 3,
    )

    half = width // 2
    packed = jnp.concatenate(
        [attention_out[k][:, h * half : (h + 1) * half] for h in range(2) for k in range(3)], 1
    )
    pair_rows = 2 * shard_rows

    def out_layout(pair, side):
        row = pair * pair_rows
        block = (row // share) ^ enc
        return [
            (0, k * half, pair_rows, half, k, block * share + row % share, side * half)
            for k in range(3)
        ]

    attend_out = spread_matrix(packed, True, out_layout, [(width, width)] * 3, seq, enc)

    hidden = feed_in.shape[2]

    def in_layout(pair, side):
        return [(0, 0, pair_rows, hidden // 2, 0, pair * pair_rows, side * (hidden // 2))]

    far_rows = 2 * feed_out.shape[1]

    def reduce_layout(pair, side):
        return [(0, 0, far_rows, half, 0, pair * far_rows, side * half)]

    expand = [
        spread_matrix(feed_in[k], True, in_layout, [(width, hidden)], seq, enc)[0] for k in range(2)
    ]
    reduce = [
        spread_matrix(feed_out[k], False, reduce_layout, [(hidden, width)], seq, enc)[0]
        for k in range(2)
    ]

    small = adapter_down.shape[2]
    up_rows = adapter_up.shape[1]
    down_shard = adapter_down.astype(LOW).transpose(1, 0, 2).reshape(shard_rows, 2 * small)
    up_shard = adapter_up.astype(LOW).reshape(2 * up_rows, width)
    both = unxor(gather_enc(jnp.concatenate([down_shard, up_shard], 0)), enc)
    downs = jnp.concatenate([v[:shard_rows] for v in both], 0)
    ups = [
        jnp.concatenate(
            [v[shard_rows + k * up_rows : shard_rows + (k + 1) * up_rows] for v in both], 0
        )
        for k in range(2)
    ]
    both = jnp.concatenate([downs] + ups, 0)
    both = jnp.where(core == 0, both[:, : width // 2], both[:, width // 2 :])
    stacked, offsets = gather_first(both)
    sources, pieces, places = [], [], []
    for s_off, buffer in [(0, stacked), (1, flip(stacked, "seq", 1))]:
        for side, v in ((core, buffer), (1 - core, flip(buffer, "enc", 1))):
            for n, o in enumerate(offsets):
                at = seq ^ s_off ^ o
                pieces.append((len(sources), n, 0, 0, strip_rows, small, 0))
                places += [side * width + at * strip_rows, 0]
                for k in range(2):
                    pieces.append(
                        (len(sources), n, strip_rows + k * n_enc * up_rows, 0, n_enc * up_rows, half, 1)
                    )
                    places += [k * small + at * n_enc * up_rows, side * half]
            sources.append(v)
    down_all, up_all = assemble(
        sources,
        pieces,
        jnp.stack([jnp.asarray(p, jnp.int32) for p in places]),
        [(2 * width, small), (2 * small, width)],
    )

    blocks = jnp.arange(n_enc) ^ enc
    spots = (blocks[:, None] * own_rows + jnp.arange(own_rows)[None, :]).reshape(length)
    spots = spots.astype(jnp.int32)
    source_limit = jnp.broadcast_to(source_length, (length, 1)).astype(jnp.int32)
    causal_limit = jnp.minimum(spots + 1, target_length)[:, None].astype(jnp.int32)
    spots = spots[None, :]
    in_strip = share // 128

    def gather_rows(rows_low):
        return jnp.concatenate(gather_enc(rows_low), 0)

    def finish_attention(context, k):
        parts = swap_blocks([context[j * own_rows : (j + 1) * own_rows] for j in range(n_enc)])
        return dense(jnp.concatenate(parts, 1), attend_out[k])

    def begin_attention_back(grad, k):
        spread = dense_back(grad.astype(LOW), attend_out[k]).astype(LOW)
        parts = swap_blocks([spread[:, j * share : (j + 1) * share] for j in range(n_enc)])
        return jnp.concatenate(parts, 0)

    def scatter_rows(partial):
        return scatter_enc([partial[j * own_rows : (j + 1) * own_rows] for j in range(n_enc)])

    encoder_in, pull_zero = norm_forward(source_rows, norms, 0)
    triple_encoder = dense(gather_rows(encoder_in.astype(LOW)), attend_in[0]).astype(LOW)
    enc_args = (triple_encoder, triple_encoder, in_strip, 2 * in_strip, source_limit, spots, own_rows)
    context, total_encoder = attend(*enc_args)
    after_self, pull_one = norm_forward(encoder_in + finish_attention(context, 0), norms, 1)
    after_self_low = after_self.astype(LOW)
    branched, *kept_enc = branch(after_self_low, expand[0], reduce[0], down_all, up_all, 0)
    encoded, pull_two = norm_forward(after_self + branched, norms, 2)
    encoded_all = gather_rows(encoded.astype(LOW))

    decoder_in, pull_three = norm_forward(target_rows, norms, 3)
    triple_decoder = dense(gather_rows(decoder_in.astype(LOW)), attend_in[1]).astype(LOW)
    dec_args = (triple_decoder, triple_decoder, in_strip, 2 * in_strip, causal_limit, spots, own_rows)
    context, total_decoder = attend(*dec_args)
    after_causal, pull_four = norm_forward(decoder_in + finish_attention(context, 1), norms, 4)
    query_cross = dense(gather_rows(after_causal.astype(LOW)), attend_in[2][:, :share]).astype(LOW)
    pairs_cross = dense(encoded_all, attend_in[2][:, share:]).astype(LOW)
    cross_args = (query_cross, pairs_cross, 0, in_strip, source_limit, spots, own_rows)
    context, total_cross = attend(*cross_args)
    after_cross, pull_five = norm_forward(after_causal + finish_attention(context, 2), norms, 5)
    after_cross_low = after_cross.astype(LOW)
    branched, *kept_dec = branch(after_cross_low, expand[1], reduce[1], down_all, up_all, 1)
    decoded, pull_six = norm_forward(after_cross + branched, norms, 6)

    decoded_low = decoded.astype(LOW)
    pulled, totals = head(gather_rows(decoded_low), embedding)
    totals = totals[:, :1]
    came = swap_blocks([totals[j * own_rows : (j + 1) * own_rows] for j in range(n_enc)])
    highest = came[0]
    for v in came[1:]:
        highest = jnp.maximum(highest, v)
    log_total = highest + jnp.log(sum(jnp.exp(v - highest) for v in came))
    row_spots = enc * own_rows + jnp.arange(own_rows)
    valid = (row_spots < target_length).astype(F32)[:, None]
    picked = jnp.sum(decoded_low.astype(F32) * label_rows, -1, keepdims=True)
    loss_own = jnp.sum((log_total - picked) * valid)
    all_totals = jnp.concatenate(gather_enc(log_total), 0)
    weight = jnp.exp(totals - all_totals)
    grad_decoded = (scatter_rows(pulled.astype(F32) * weight) - label_rows) * valid

    grad_res, gain_six, shift_six = pull_six(grad_decoded)
    grad_rows, down_dec, up_dec = branch_back(
        grad_res, [after_cross_low] + kept_dec, expand[1], reduce[1], down_all, up_all, 1
    )
    grad_res, gain_five, shift_five = pull_five(grad_res + grad_rows)
    grads = attend_back(*cross_args, begin_attention_back(grad_res, 2), total_cross)
    grad_encoded = scatter_rows(dense_back(grads[:, share:], attend_in[2][:, share:]))
    grad_causal = grad_res + scatter_rows(dense_back(grads[:, :share], attend_in[2][:, :share]))
    grad_res, gain_four, shift_four = pull_four(grad_causal)
    grads = attend_back(*dec_args, begin_attention_back(grad_res, 1), total_decoder)
    grad_decoder = grad_res + scatter_rows(dense_back(grads, attend_in[1]))
    grad_unused, gain_three, shift_three = pull_three(grad_decoder)
    grad_res, gain_two, shift_two = pull_two(grad_encoded)
    grad_rows, down_enc, up_enc = branch_back(
        grad_res, [after_self_low] + kept_enc, expand[0], reduce[0], down_all, up_all, 0
    )
    grad_res, gain_one, shift_one = pull_one(grad_res + grad_rows)
    grads = attend_back(*enc_args, begin_attention_back(grad_res, 0), total_encoder)
    grad_encoder = grad_res + scatter_rows(dense_back(grads, attend_in[0]))
    grad_unused, gain_zero, shift_zero = pull_zero(grad_encoder)

    near, across = [("seq", 1)], [("enc", mask) for mask in bits("enc")[1:]]
    slow = [("seq", mask) for mask in bits("seq")[1:]]
    pair = [("enc", 1)]
    grad_down = jnp.stack(
        [reduce_shards(g, seq, enc, pair + across + near + slow) for g in (down_enc, down_dec)]
    )
    grad_up = jnp.stack(
        [reduce_shards(g, seq, enc, pair + near + across + slow) for g in (up_enc, up_dec)]
    )
    count_own = jnp.clip(target_length - enc * own_rows, 0, own_rows).astype(F32)
    squares_own = jnp.sum(grad_down * grad_down) + jnp.sum(grad_up * grad_up)
    lanes = jnp.arange(width)
    scalars = jnp.where(
        lanes == 0, loss_own, jnp.where(lanes == 1, count_own, jnp.where(lanes == 2, squares_own, 0.0))
    )
    summed = jnp.stack(
        [gain_zero, gain_one, gain_two, gain_three, gain_four, gain_five, gain_six]
        + [shift_zero, shift_one, shift_two, shift_three, shift_four, shift_five, shift_six]
        + [scalars, jnp.zeros_like(scalars)]
    )
    for axis, mask in pair + across + near + slow:
        summed = summed + flip(summed, axis, mask)
    loss_sum, token_total = summed[14, 0], summed[14, 1]
    norm_grads = summed[:14]
    squares = summed[14, 2] + jnp.sum(norm_grads * norm_grads)
    per = width // n_all
    grad_norms = lax.dynamic_slice_in_dim(norm_grads, (seq * n_enc + enc) * per, per, 1)
    grad_norms = grad_norms.reshape(2, 7, per)

    grad_norm = jnp.sqrt(squares) / token_total
    factor = jnp.minimum(1.0, CLIP_NORM / grad_norm) / token_total
    moment_down, second_down, updated_down = adamw(
        grad_down * factor, down_moment, down_second, adapter_down, RATE_ADAPTER, DECAY_ADAPTER
    )
    moment_up, second_up, updated_up = adamw(
        grad_up * factor, up_moment, up_second, adapter_up, RATE_ADAPTER, DECAY_ADAPTER
    )
    moment_norms, second_norms, updated_norms = adamw(
        grad_norms * factor, norm_moment, norm_second, norm_params, RATE_NORMS, 0.0
    )
    return (
        loss_sum,
        token_total,
        grad_norm,
        moment_down,
        second_down,
        updated_down,
        moment_up,
        second_up,
        updated_up,
        moment_norms,
        second_norms,
        updated_norms,
    )


def solution(mesh):
    everywhere = P(None, ("seq", "enc"), None)
    columns = P(None, None, ("seq", "enc"))
    return jax.shard_map(
        shards,
        mesh=mesh,
        in_specs=(
            P("seq", "enc"),
            P("seq", "enc"),
            P("seq", "enc"),
            P("seq", None),
            P("enc", None),
            P(None, "enc", None),
            everywhere,
            everywhere,
            everywhere,
            everywhere,
            everywhere,
            everywhere,
            columns,
            everywhere,
            everywhere,
            everywhere,
            everywhere,
            columns,
            columns,
        ),
        out_specs=(
            P(),
            P(),
            P(),
            everywhere,
            everywhere,
            everywhere,
            everywhere,
            everywhere,
            everywhere,
            columns,
            columns,
            columns,
        ),
        check_vma=False,
    )
```

time: 1690 us -> 1020 us (0.60)
  waiting for transfers between devices: 961 us -> 441 us
  matrix products: 318 us -> 26.5 us
  Pallas kernels: 0 us -> 230 us
  starting transfers between devices: 1.74 us -> 120 us
  blocking collectives: 114 us -> 0 us
  other arithmetic: 163 us -> 76.5 us
    all_gather x10 -> x0, waiting for transfers between devices: 470 us -> none  [the longest x1 113 us: shards(): lax.all_gather(feed_in, ('seq', 'enc'), axis=1, tiled=True)]
    ppermute x0 -> x160, waiting for transfers between devices: none -> 441 us  [flip(): return lax.ppermute(value, axis, [(i, i ^ mask) for i in range(count)])]
    reduce_scatter x7 -> x0, waiting for transfers between devices: 360 us -> none  [the longest x1 137 us: shards(): lax.psum_scatter(jnp.stack([up_enc, up_dec]), ('seq', 'enc'), scatter_dim...]
    pallas_call x0 -> x18, Pallas kernels: none -> 230 us  [the longest x3 60.9 us: attend_back(): pl.pallas_call(attend_back_kernel, grid=(pairs, steps), out_shape=jax.Sha...]
    dot_general x36 -> x7, matrix products: 208 us -> 9.57 us  [dense(): return jnp.dot(left, right, preferred_element_type=F32)]
    unnamed x19 -> x0, waiting for transfers between devices: 131 us -> none
    ppermute x0 -> x160, starting transfers between devices: none -> 120 us  [flip(): return lax.ppermute(value, axis, [(i, i ^ mask) for i in range(count)])]
    dot_general x15 -> x7, matrix products: 108 us -> 15.1 us  [dense_back(): lax.dot_general(left, right, (((1,), (1,)), ((), ())), preferred_element_...]
  transfers between devices with their start and end apart: 18 -> 160, of which waited for: 16 -> 63; matrix products, arithmetic and copies ran while one was open for 15% -> 14% of each run, Pallas kernels for 0% -> 17%
where the time goes in v1:
time: 1020 us; the launch traced here: 1010 us
  waiting for transfers between devices  441 us (43%)
  Pallas kernels  230 us (23%)
  starting transfers between devices  120 us (12%)
  local copies, waits for them, and re-layouts  106 us (10%)
  other arithmetic  76.5 us (8%)
  matrix products  26.5 us (3%)
  between operations  11.3 us (1%)
    ppermute x160, waiting for transfers between devices, flip(): return lax.ppermute(value, axis, [(i, i ^ mask) for i in range(count)])  441 us
    ppermute x160, starting transfers between devices, flip(): return lax.ppermute(value, axis, [(i, i ^ mask) for i in range(count)])  120 us
    pallas_call x3, Pallas kernels, attend_back(): pl.pallas_call(attend_back_kernel, grid=(pairs, steps), out_shape=jax.Sha...  60.9 us
    pallas_call x1, Pallas kernels, head(): pl.pallas_call(head_kernel, grid=(entries // tile,), out_shape=[jax.Shape...  44.8 us
    unnamed x443, local copies, waits for them, and re-layouts  40.4 us
    gather x3, local copies, waits for them, and re-layouts, lookup(): found = jnp.take(embedding, jnp.clip(local, 0, entries - 1), axis=0)  37.3 us
    pallas_call x7, Pallas kernels, assemble(): pl.pallas_call(kernel, out_shape=[jax.ShapeDtypeStruct(shape, LOW) for sh...  36.9 us
    pallas_call x3, Pallas kernels, attend(): pl.pallas_call(attend_kernel, grid=(pairs, steps), out_shape=[jax.ShapeDt...  32.3 us
  transfers between devices with their start and end apart: 160, of which 63 were waited for; matrix products, arithmetic and copies ran while one was open for 14% of the time, Pallas kernels for 17%

profile of v1, /device:TPU:0, one launch (start us, length us, event | category | flops | bytes accessed | tf_op | source)
XLA Modules:
  0.0 1010.8 jit_solution(17153849546256603659)
XLA Ops:
  28.3 12.5 %gather_fusion.1 = bf16[1024,1024]{1,0:T(8,128)(2,1)} fusion(bf16[6400,1024]{1,0:T(8,128)(2,1)} %e_ref.1, s32[1024]{0:T(1024)S(1)} %broadcast_clamp_fusion.2), kind=kCustom, calls=%fused_computation.clone | custom fusion | bytes 4198400 | tf_op jit(solution)/shard_map/jit(_take)/gather | solution.py:583
  40.7 11.8 %gather_fusion.2 = bf16[1024,1024]{1,0:T(8,128)(2,1)S(1)} fusion(bf16[6400,1024]{1,0:T(8,128)(2,1)} %e_ref.1, s32[1024]{0:T(1024)} %broadcast_clamp_fusion.1), kind=kCustom, calls=%fused_computation.1.clone | custom fusion | bytes 4198400 | tf_op jit(solution)/shard_map/jit(_take)/gather | solution.py:583
  99.9 5.5 collective-permute-done.56
  111.1 4.1 collective-permute-done.68
  125.1 14.0 %collective-permute-done.28 = bf16[2,64,1536]{2,1,0:T(8,128)(2,1)S(1)} collective-permute-done((bf16[2,64,1536]{2,1,0:T(8,128)(2,1)S(1)}, bf16[2,64,1536]{2,1,0:T(8,128)(2,1)S(1)}, u32[]{:S(2)}, u32[]{:S(2)}) %collective-permute-start.28) | collective-permute-done | bytes 393248 | tf_op jit(solution)/shard_map/ppermute | solution.py:29
  144.2 33.7 %collective-permute-done.81 = bf16[2,64,2048]{2,1,0:T(8,128)(2,1)S(1)} collective-permute-done((bf16[2,64,2048]{2,1,0:T(8,128)(2,1)S(1)}, bf16[2,64,2048]{2,1,0:T(8,128)(2,1)S(1)}, u32[]{:S(2)}, u32[]{:S(2)}) %collective-permute-start.81) | collective-permute-done | bytes 524320 | tf_op jit(solution)/shard_map/ppermute | solution.py:29
  178.9 21.5 %collective-permute-done.57 = bf16[2,256,512]{2,1,0:T(8,128)(2,1)S(1)} collective-permute-done((bf16[2,256,512]{2,1,0:T(8,128)(2,1)S(1)}, bf16[2,256,512]{2,1,0:T(8,128)(2,1)S(1)}, u32[]{:S(2)}, u32[]{:S(2)}) %collective-permute-start.57) | collective-permute-done | bytes 524320 | tf_op jit(solution)/shard_map/ppermute | solution.py:29
  201.1 7.2 collective-permute-start.32
  209.8 18.7 %collective-permute-done.91 = bf16[2,256,512]{2,1,0:T(8,128)(2,1)S(1)} collective-permute-done((bf16[2,256,512]{2,1,0:T(8,128)(2,1)S(1)}, bf16[2,256,512]{2,1,0:T(8,128)(2,1)S(1)}, u32[]{:S(2)}, u32[]{:S(2)}) %collective-permute-start.91) | collective-permute-done | bytes 524320 | tf_op jit(solution)/shard_map/ppermute | solution.py:29
  228.5 23.9 %collective-permute-done.47 = bf16[2,64,2048]{2,1,0:T(8,128)(2,1)S(1)} collective-permute-done((bf16[2,64,2048]{2,1,0:T(8,128)(2,1)S(1)}, bf16[2,64,2048]{2,1,0:T(8,128)(2,1)S(1)}, u32[]{:S(2)}, u32[]{:S(2)}) %collective-permute-start.47) | collective-permute-done | bytes 524320 | tf_op jit(solution)/shard_map/ppermute | solution.py:29
  252.4 23.9 %collective-permute-done.69 = bf16[2,256,512]{2,1,0:T(8,128)(2,1)S(1)} collective-permute-done((bf16[2,256,512]{2,1,0:T(8,128)(2,1)S(1)}, bf16[2,256,512]{2,1,0:T(8,128)(2,1)S(1)}, u32[]{:S(2)}, u32[]{:S(2)}) %collective-permute-start.69) | collective-permute-done | bytes 524320 | tf_op jit(solution)/shard_map/ppermute | solution.py:29
  280.5 29.9 %collective-permute-done.40 = bf16[256,1024]{1,0:T(8,128)(2,1)S(1)} collective-permute-done((bf16[256,1024]{1,0:T(8,128)(2,1)S(1)}, bf16[256,1024]{1,0:T(8,128)(2,1)S(1)}, u32[]{:S(2)}, u32[]{:S(2)}) %collective-permute-start.40) | collective-permute-done | bytes 524320 | tf_op jit(solution)/shard_map/ppermute | solution.py:29
  315.4 21.2 %collective-permute-done.49.refs_3_ = bf16[4,64,2048]{2,1,0:T(8,128)(2,1)} collective-permute-done((bf16[4,64,2048]{2,1,0:T(8,128)(2,1)S(1)}, bf16[4,64,2048]{2,1,0:T(8,128)(2,1)}, u32[]{:S(2)}, u32[]{:S(2)}) %collective-permute-start.49) | collective-permute-done | bytes 1048608 | tf_op jit(solution)/shard_map/ppermute | solution.py:29
  339.7 15.2 %collective-permute-done.71.refs_3_ = bf16[4,256,512]{2,1,0:T(8,128)(2,1)S(1)} collective-permute-done((bf16[4,256,512]{2,1,0:T(8,128)(2,1)S(1)}, bf16[4,256,512]{2,1,0:T(8,128)(2,1)S(1)}, u32[]{:S(2)}, u32[]{:S(2)}) %collective-permute-start.71) | collective-permute-done | bytes 1048608 | tf_op jit(solution)/shard_map/ppermute | solution.py:29
  364.7 12.2 %collective-permute-done.63.refs_7_ = bf16[4,256,512]{2,1,0:T(8,128)(2,1)} collective-permute-done((bf16[4,256,512]{2,1,0:T(8,128)(2,1)}, bf16[4,256,512]{2,1,0:T(8,128)(2,1)}, u32[]{:S(2)}, u32[]{:S(2)}) %collective-permute-start.63) | collective-permute-done | bytes 1048608 | tf_op jit(solution)/shard_map/ppermute | solution.py:29
  377.0 13.0 %gather_fusion.3 = bf16[1024,1024]{1,0:T(8,128)(2,1)} fusion(bf16[6400,1024]{1,0:T(8,128)(2,1)} %e_ref.1, s32[1024]{0:T(1024)S(1)} %broadcast_clamp_fusion), kind=kCustom, calls=%fused_computation.2.clone | custom fusion | bytes 4198400 | tf_op jit(solution)/shard_map/jit(_take)/gather | solution.py:583
  400.8 5.1 shard_map.276
  409.9 8.9 shard_map.280
  420.1 3.9 shard_map.279.out_ref
  437.0 8.1 shard_map.274
  448.3 10.8 %shard_map.277 = (bf16[1024,256]{1,0:T(8,128)(2,1)S(1)}, f32[1024,256]{1,0:T(8,128)S(1)}) custom-call(s32[1024,1]{1,0:T(8,128)S(1)} %broadcast_in_dim.138.limit_ref, s32[1,1024]{1,0:T(1,128)S(1)} %bitcast.414, bf16[1024,768]{1,0:T(8,128)(2,1)S(1)} %fusion.32.q_ref.k_ref.v_ref, bf16[1024,768]{1,0:T(8,128)(2,1)S(1)} %fusion.32.q_ref.k_ref.v_ref, ...), custom_call_target="tpu_custom_call" | custom-call | flops 2147483648 | bytes 2097152 | tf_op jit(solution)/shard_map/pallas_call | solution.py:232
  464.5 10.6 %shard_map.275 = (bf16[1024,256]{1,0:T(8,128)(2,1)S(1)}, f32[1024,256]{1,0:T(8,128)S(1)}) custom-call(s32[1024,1]{1,0:T(8,128)S(1)} %bitcast.413, s32[1,1024]{1,0:T(1,128)S(1)} %bitcast.415, bf16[1024,768]{1,0:T(8,128)(2,1)S(1)} %fusion.35.q_ref.k_ref.v_ref, bf16[1024,768]{1,0:T(8,128)(2,1)S(1)} %fusion.35.q_ref.k_ref.v_ref, ...), custom_call_target="tpu_custom_call" | custom-call | flops 2147483648 | bytes 2097152 | tf_op jit(solution)/shard_map/pallas_call | solution.py:232
  479.7 14.1 %shard_map.281 = (f32[256,1024]{1,0:T(8,128)S(1)}, f32[256,4096]{1,0:T(8,128)}, bf16[256,512]{1,0:T(8,128)(2,1)S(1)}, f32[256,512]{1,0:T(8,128)S(1)}) custom-call(bf16[256,1024]{1,0:T(8,128)(2,1)S(1)} %fusion.71.x_ref, bf16[1024,4096]{1,0:T(8,128)(2,1)} %copy-done.1, bf16[4096,1024]{1,0:T(8,128)(2,1)} %copy-done, ...), custom_call_target="tpu_custom_call" | custom-call | flops 4831838208 | bytes 23068672 | tf_op jit(solution)/shard_map/pallas_call | solution.py:364
  495.1 9.7 collective-permute-done.24
  509.6 21.4 %collective-permute-done.93.refs_3_ = bf16[4,256,512]{2,1,0:T(8,128)(2,1)S(1)} collective-permute-done((bf16[4,256,512]{2,1,0:T(8,128)(2,1)S(1)}, bf16[4,256,512]{2,1,0:T(8,128)(2,1)S(1)}, u32[]{:S(2)}, u32[]{:S(2)}) %collective-permute-start.93) | collective-permute-done | bytes 1048608 | tf_op jit(solution)/shard_map/ppermute | solution.py:29
  535.8 17.7 %collective-permute-done.87.refs_7_ = bf16[4,64,2048]{2,1,0:T(8,128)(2,1)} collective-permute-done((bf16[4,64,2048]{2,1,0:T(8,128)(2,1)S(1)}, bf16[4,64,2048]{2,1,0:T(8,128)(2,1)}, u32[]{:S(2)}, u32[]{:S(2)}) %collective-permute-start.87) | collective-permute-done | bytes 1048608 | tf_op jit(solution)/shard_map/ppermute | solution.py:29
  553.5 11.1 %collective-permute-done.74 = bf16[256,1024]{1,0:T(8,128)(2,1)S(1)} collective-permute-done((bf16[256,1024]{1,0:T(8,128)(2,1)S(1)}, bf16[256,1024]{1,0:T(8,128)(2,1)S(1)}, u32[]{:S(2)}, u32[]{:S(2)}) %collective-permute-start.74) | collective-permute-done | bytes 524320 | tf_op jit(solution)/shard_map/ppermute | solution.py:29
  566.2 8.4 collective-permute-done.37
  578.2 10.9 %shard_map.282 = (bf16[1024,256]{1,0:T(8,128)(2,1)S(1)}, f32[1024,256]{1,0:T(8,128)S(1)}) custom-call(s32[1024,1]{1,0:T(8,128)S(1)} %broadcast_in_dim.138.limit_ref, s32[1,1024]{1,0:T(1,128)S(1)} %bitcast.416, bf16[1024,256]{1,0:T(8,128)(2,1)S(1)} %fusion.41.q_ref, bf16[1024,512]{1,0:T(8,128)(2,1)S(1)} %fusion.38.k_ref.v_ref, ...), custom_call_target="tpu_custom_call" | custom-call | flops 2147483648 | bytes 2097152 | tf_op jit(solution)/shard_map/pallas_call | solution.py:232
  608.3 14.1 %shard_map.285 = (f32[256,1024]{1,0:T(8,128)S(1)}, f32[256,4096]{1,0:T(8,128)}, bf16[256,512]{1,0:T(8,128)(2,1)S(1)}, f32[256,512]{1,0:T(8,128)S(1)}) custom-call(bf16[256,1024]{1,0:T(8,128)(2,1)S(1)} %fusion.73.x_ref, bf16[1024,4096]{1,0:T(8,128)(2,1)} %copy-done.2, bf16[4096,1024]{1,0:T(8,128)(2,1)} %copy-done.3, ...), custom_call_target="tpu_custom_call" | custom-call | flops 4831838208 | bytes 23068672 | tf_op jit(solution)/shard_map/pallas_call | solution.py:364
  627.8 11.9 %collective-permute-done.100 = bf16[256,1024]{1,0:T(8,128)(2,1)S(1)} collective-permute-done((bf16[256,1024]{1,0:T(8,128)(2,1)S(1)}, bf16[256,1024]{1,0:T(8,128)(2,1)S(1)}, u32[]{:S(2)}, u32[]{:S(2)}) %collective-permute-start.100) | collective-permute-done | bytes 524320 | tf_op jit(solution)/shard_map/ppermute | solution.py:29
  643.2 44.8 %shard_map.286 = (bf16[1024,1024]{1,0:T(8,128)(2,1)}, f32[1024,128]{1,0:T(8,128)}) custom-call(bf16[1024,1024]{1,0:T(8,128)(2,1)} %pad_maximum_fusion.1.o_ref, bf16[6400,1024]{1,0:T(8,128)(2,1)} %e_ref.1), custom_call_target="tpu_custom_call" | custom-call | flops 26843545600 | bytes 13107200 | tf_op jit(solution)/shard_map/pallas_call | solution.py:487
  702.6 4.1 collective-permute-done.106
  725.6 11.5 %collective-permute-done.110 = bf16[256,1024]{1,0:T(8,128)(2,1)} collective-permute-done((bf16[256,1024]{1,0:T(8,128)(2,1)}, bf16[256,1024]{1,0:T(8,128)(2,1)}, u32[]{:S(2)}, u32[]{:S(2)}) %collective-permute-start.110) | collective-permute-done | bytes 524320 | tf_op jit(solution)/shard_map/ppermute | solution.py:29
  741.2 13.3 %shard_map.287 = (f32[256,1024]{1,0:T(8,128)S(1)}, bf16[256,512]{1,0:T(8,128)(2,1)S(1)}) custom-call(bf16[256,1024]{1,0:T(8,128)(2,1)S(1)} %get-tuple-element.189.g_ref, bf16[256,1024]{1,0:T(8,128)(2,1)S(1)} %get-tuple-element.188.ga_ref, bf16[1024,4096]{1,0:T(8,128)(2,1)} %copy-done.2, bf16[4096,1024]{1,0:T(8,128)(2,1)} %copy-done.3, ...), custom_call_target="tpu_custom_call" | custom-call | flops 4831838208 | bytes 23068672 | tf_op jit(solution)/shard_map/pallas_call | solution.py:421
  767.1 20.2 %shard_map.288 = bf16[1024,768]{1,0:T(8,128)(2,1)} custom-call(s32[1024,1]{1,0:T(8,128)} %copy-done.30, s32[1,1024]{1,0:T(1,128)} %bitcast.417, bf16[1024,256]{1,0:T(8,128)(2,1)} %copy-done.54, bf16[1024,512]{1,0:T(8,128)(2,1)} %copy-done.52, bf16[1024,512]{1,0:T(8,128)(2,1)} %copy-done.52, bf16[1024,256]{1,0:T(8,128)(2,1)} %pad_maximum_fusion.14.grad_ref, ...), custom_call_target="tpu_custom_call" | custom-call | flops 5368709120 | bytes 4194304 | tf_op jit(solution)/shard_map/pallas_call | solution.py:310
  802.0 7.1 collective-permute-done.119
  809.2 11.2 %collective-permute-done.128 = bf16[256,1024]{1,0:T(8,128)(2,1)S(1)} collective-permute-done((bf16[256,1024]{1,0:T(8,128)(2,1)S(1)}, bf16[256,1024]{1,0:T(8,128)(2,1)S(1)}, u32[]{:S(2)}, u32[]{:S(2)}) %collective-permute-start.128) | collective-permute-done | bytes 524320 | tf_op jit(solution)/shard_map/ppermute | solution.py:29
  824.2 13.2 %shard_map.289 = (f32[256,1024]{1,0:T(8,128)S(1)}, bf16[256,512]{1,0:T(8,128)(2,1)S(1)}) custom-call(bf16[256,1024]{1,0:T(8,128)(2,1)S(1)} %get-tuple-element.187.g_ref, bf16[256,1024]{1,0:T(8,128)(2,1)S(1)} %get-tuple-element.186.ga_ref, bf16[1024,4096]{1,0:T(8,128)(2,1)} %copy-done.1, bf16[4096,1024]{1,0:T(8,128)(2,1)} %copy-done, ...), custom_call_target="tpu_custom_call" | custom-call | flops 4831838208 | bytes 23068672 | tf_op jit(solution)/shard_map/pallas_call | solution.py:421
  856.6 20.2 %shard_map.291 = bf16[1024,768]{1,0:T(8,128)(2,1)} custom-call(s32[1024,1]{1,0:T(8,128)} %bitcast.412, s32[1,1024]{1,0:T(1,128)} %bitcast.418, bf16[1024,768]{1,0:T(8,128)(2,1)} %copy-done.49, bf16[1024,768]{1,0:T(8,128)(2,1)} %copy-done.49, bf16[1024,768]{1,0:T(8,128)(2,1)} %copy-done.49, bf16[1024,256]{1,0:T(8,128)(2,1)} %pad_maximum_fusion.16.grad_ref, ...), custom_call_target="tpu_custom_call" | custom-call | flops 5368709120 | bytes 4194304 | tf_op jit(solution)/shard_map/pallas_call | solution.py:310
  876.8 5.2 fusion.199
  886.5 20.5 %shard_map.290 = bf16[1024,768]{1,0:T(8,128)(2,1)} custom-call(s32[1024,1]{1,0:T(8,128)} %copy-done.30, s32[1,1024]{1,0:T(1,128)} %bitcast.419, bf16[1024,768]{1,0:T(8,128)(2,1)} %copy-done.48, bf16[1024,768]{1,0:T(8,128)(2,1)} %copy-done.48, bf16[1024,768]{1,0:T(8,128)(2,1)} %copy-done.48, bf16[1024,256]{1,0:T(8,128)(2,1)} %pad_maximum_fusion.15.grad_ref, ...), custom_call_target="tpu_custom_call" | custom-call | flops 5368709120 | bytes 4194304 | tf_op jit(solution)/shard_map/pallas_call | solution.py:310
  911.6 4.3 collective-permute-done.153
  916.2 3.9 collective-permute-done.143
  940.5 6.4 collective-permute-done.134
  947.4 10.8 %collective-permute-done.125 = bf16[256,1024]{1,0:T(8,128)(2,1)S(1)} collective-permute-done((bf16[256,1024]{1,0:T(8,128)(2,1)S(1)}, bf16[256,1024]{1,0:T(8,128)(2,1)S(1)}, u32[]{:S(2)}, u32[]{:S(2)}) %collective-permute-start.125) | collective-permute-done | bytes 524320 | tf_op jit(solution)/shard_map/ppermute | solution.py:29
  959.5 4.3 collective-permute-done.136
  991.4 4.1 collective-permute-done.158
  (997 shorter events, 359.2 us)
Async XLA Ops:
  3.3 71.4 %collective-permute-start.65 = (bf16[64,1024]{1,0:T(8,128)(2,1)}, bf16[64,1024]{1,0:T(8,128)(2,1)}, u32[]{:S(2)}, u32[]{:S(2)}) collective-permute-start(bf16[64,1024]{1,0:T(8,128)(2,1)} %pad_maximum_fusion.18), channel_id=1, source_target_pairs={{0,2},{1,3},{2,0},{3,1},{4,6},{5,7},{6,4},{7,5},{8,10},{9,11},{10,... | collective-permute-start | bytes 393224 | tf_op jit(solution)/shard_map/ppermute | solution.py:29
  6.2 76.3 %collective-permute-start.67 = (bf16[64,1024]{1,0:T(8,128)(2,1)}, bf16[64,1024]{1,0:T(8,128)(2,1)}, u32[]{:S(2)}, u32[]{:S(2)}) collective-permute-start(bf16[64,1024]{1,0:T(8,128)(2,1)} %pad_maximum_fusion.18), channel_id=1, source_target_pairs={{0,1},{1,0},{2,3},{3,2},{4,5},{5,4},{6,7},{7,6},{8,9},{9,8},{10,11... | collective-permute-start | bytes 393224 | tf_op jit(solution)/shard_map/ppermute | solution.py:29
  20.8 49.4 %collective-permute-start.79 = (bf16[32,2048]{1,0:T(8,128)(2,1)}, bf16[32,2048]{1,0:T(8,128)(2,1)}, u32[]{:S(2)}, u32[]{:S(2)}) collective-permute-start(bf16[32,2048]{1,0:T(8,128)(2,1)} %broadcast_select_fusion.24), channel_id=1, source_target_pairs={{0,1},{1,0},{2,3},{3,2},{4,5},{5,4},{6,7},{7,6},{8,9},{9,8},{10,11... | collective-permute-start | bytes 393224 | tf_op jit(solution)/shard_map/ppermute | solution.py:29
  22.5 48.7 %collective-permute-start.89 = (bf16[128,512]{1,0:T(8,128)(2,1)}, bf16[128,512]{1,0:T(8,128)(2,1)}, u32[]{:S(2)}, u32[]{:S(2)}) collective-permute-start(bf16[128,512]{1,0:T(8,128)(2,1)} %broadcast_select_fusion.16), channel_id=1, source_target_pairs={{0,1},{1,0},{2,3},{3,2},{4,5},{5,4},{6,7},{7,6},{8,9},{9,8},{10,11... | collective-permute-start | bytes 393224 | tf_op jit(solution)/shard_map/ppermute | solution.py:29
  22.7 34.8 %collective-permute-start.11 = (bf16[4,14,32]{2,1,0:T(8,128)(2,1)}, bf16[4,14,32]{2,1,0:T(8,128)(2,1)}, u32[]{:S(2)}, u32[]{:S(2)}) collective-permute-start(bf16[4,14,32]{2,1,0:T(8,128)(2,1)} %pad_maximum_fusion.24), channel_id=1, source_target_pairs={{0,4},{4,0},{8,12},{12,8},{16,20},{20,16},{24,28},{28,24},{1,5},{5... | collective-permute-start | bytes 10760 | tf_op jit(solution)/shard_map/ppermute | solution.py:29
  74.8 42.1 %collective-permute-start.4 = (bf16[256,1024]{1,0:T(8,128)(2,1)S(1)}, bf16[256,1024]{1,0:T(8,128)(2,1)S(1)}, u32[]{:S(2)}, u32[]{:S(2)}) collective-permute-start(bf16[256,1024]{1,0:T(8,128)(2,1)S(1)} %copy-done.120), channel_id=1, source_target_pairs={{0,1},{1,0},{2,3},{3,2},{4,5},{5,4},{6,7},{7,6},{8,9},{9,8},{10,11... | collective-permute-start | bytes 1572872 | tf_op jit(solution)/shard_map/ppermute | solution.py:29
  77.4 42.7 %collective-permute-start.7 = (bf16[256,1024]{1,0:T(8,128)(2,1)S(1)}, bf16[256,1024]{1,0:T(8,128)(2,1)S(1)}, u32[]{:S(2)}, u32[]{:S(2)}) collective-permute-start(bf16[256,1024]{1,0:T(8,128)(2,1)S(1)} %copy-done.122), channel_id=1, source_target_pairs={{0,1},{1,0},{2,3},{3,2},{4,5},{5,4},{6,7},{7,6},{8,9},{9,8},{10,11... | collective-permute-start | bytes 1572872 | tf_op jit(solution)/shard_map/ppermute | solution.py:29
  120.2 57.8 %collective-permute-start.81 = (bf16[2,64,2048]{2,1,0:T(8,128)(2,1)S(1)}, bf16[2,64,2048]{2,1,0:T(8,128)(2,1)S(1)}, u32[]{:S(2)}, u32[]{:S(2)}) collective-permute-start(bf16[2,64,2048]{2,1,0:T(8,128)(2,1)S(1)} %pad_maximum_fusion.12), channel_id=1, source_target_pairs={{0,16},{4,20},{8,24},{12,28},{16,0},{20,4},{24,8},{28,12},{1,17},{... | collective-permute-start | bytes 1572872 | tf_op jit(solution)/shard_map/ppermute | solution.py:29
  120.7 79.7 %collective-permute-start.57 = (bf16[2,256,512]{2,1,0:T(8,128)(2,1)S(1)}, bf16[2,256,512]{2,1,0:T(8,128)(2,1)S(1)}, u32[]{:S(2)}, u32[]{:S(2)}) collective-permute-start(bf16[2,256,512]{2,1,0:T(8,128)(2,1)S(1)} %pad_maximum_fusion.10), channel_id=1, source_target_pairs={{0,16},{4,20},{8,24},{12,28},{16,0},{20,4},{24,8},{28,12},{1,17},{... | collective-permute-start | bytes 1572872 | tf_op jit(solution)/shard_map/ppermute | solution.py:29
  123.6 77.5 %collective-permute-start.5 = (bf16[256,1024]{1,0:T(8,128)(2,1)S(1)}, bf16[256,1024]{1,0:T(8,128)(2,1)S(1)}, u32[]{:S(2)}, u32[]{:S(2)}) collective-permute-start(bf16[256,1024]{1,0:T(8,128)(2,1)S(1)} %fusion.65), channel_id=1, source_target_pairs={{0,2},{1,3},{2,0},{3,1},{4,6},{5,7},{6,4},{7,5},{8,10},{9,11},{10,... | collective-permute-start | bytes 1572872 | tf_op jit(solution)/shard_map/ppermute | solution.py:29
  139.1 62.0 %collective-permute-start.8 = (bf16[256,1024]{1,0:T(8,128)(2,1)S(1)}, bf16[256,1024]{1,0:T(8,128)(2,1)S(1)}, u32[]{:S(2)}, u32[]{:S(2)}) collective-permute-start(bf16[256,1024]{1,0:T(8,128)(2,1)S(1)} %fusion.63), channel_id=1, source_target_pairs={{0,2},{1,3},{2,0},{3,1},{4,6},{5,7},{6,4},{7,5},{8,10},{9,11},{10,... | collective-permute-start | bytes 1572872 | tf_op jit(solution)/shard_map/ppermute | solution.py:29
  141.8 86.7 %collective-permute-start.91 = (bf16[2,256,512]{2,1,0:T(8,128)(2,1)S(1)}, bf16[2,256,512]{2,1,0:T(8,128)(2,1)S(1)}, u32[]{:S(2)}, u32[]{:S(2)}) collective-permute-start(bf16[2,256,512]{2,1,0:T(8,128)(2,1)S(1)} %pad_maximum_fusion.13), channel_id=1, source_target_pairs={{0,16},{4,20},{8,24},{12,28},{16,0},{20,4},{24,8},{28,12},{1,17},{... | collective-permute-start | bytes 1572872 | tf_op jit(solution)/shard_map/ppermute | solution.py:29
  178.8 73.6 %collective-permute-start.47 = (bf16[2,64,2048]{2,1,0:T(8,128)(2,1)S(1)}, bf16[2,64,2048]{2,1,0:T(8,128)(2,1)S(1)}, u32[]{:S(2)}, u32[]{:S(2)}) collective-permute-start(bf16[2,64,2048]{2,1,0:T(8,128)(2,1)S(1)} %pad_maximum_fusion.9), channel_id=1, source_target_pairs={{0,16},{4,20},{8,24},{12,28},{16,0},{20,4},{24,8},{28,12},{1,17},{... | collective-permute-start | bytes 1572872 | tf_op jit(solution)/shard_map/ppermute | solution.py:29
  200.4 77.6 %collective-permute-start.30 = (bf16[4,64,1536]{2,1,0:T(8,128)(2,1)S(1)}, bf16[4,64,1536]{2,1,0:T(8,128)(2,1)}, u32[]{:S(2)}, u32[]{:S(2)}) collective-permute-start(bf16[4,64,1536]{2,1,0:T(8,128)(2,1)S(1)} %pad_maximum_fusion.8.refs_1_), channel_id=1, source_target_pairs={{0,4},{4,0},{8,12},{12,8},{16,20},{20,16},{24,28},{28,24},{1,5},{5... | collective-permute-start | bytes 2359304 | tf_op jit(solution)/shard_map/ppermute | solution.py:29
  201.0 75.2 %collective-permute-start.69 = (bf16[2,256,512]{2,1,0:T(8,128)(2,1)S(1)}, bf16[2,256,512]{2,1,0:T(8,128)(2,1)S(1)}, u32[]{:S(2)}, u32[]{:S(2)}) collective-permute-start(bf16[2,256,512]{2,1,0:T(8,128)(2,1)S(1)} %pad_maximum_fusion.11), channel_id=1, source_target_pairs={{0,16},{4,20},{8,24},{12,28},{16,0},{20,4},{24,8},{28,12},{1,17},{... | collective-permute-start | bytes 1572872 | tf_op jit(solution)/shard_map/ppermute | solution.py:29
  201.1 77.4 %collective-permute-start.32 = (bf16[4,64,1536]{2,1,0:T(8,128)(2,1)S(1)}, bf16[4,64,1536]{2,1,0:T(8,128)(2,1)}, u32[]{:S(2)}, u32[]{:S(2)}) collective-permute-start(bf16[4,64,1536]{2,1,0:T(8,128)(2,1)S(1)} %pad_maximum_fusion.8.refs_1_), channel_id=1, source_target_pairs={{0,2},{1,3},{2,0},{3,1},{4,6},{5,7},{6,4},{7,5},{8,10},{9,11},{10,... | collective-permute-start | bytes 2359304 | tf_op jit(solution)/shard_map/ppermute | solution.py:29
  228.5 50.5 %collective-permute-start.29 = (bf16[4,64,1536]{2,1,0:T(8,128)(2,1)S(1)}, bf16[4,64,1536]{2,1,0:T(8,128)(2,1)S(1)}, u32[]{:S(2)}, u32[]{:S(2)}) collective-permute-start(bf16[4,64,1536]{2,1,0:T(8,128)(2,1)S(1)} %pad_maximum_fusion.8.refs_1_), channel_id=1, source_target_pairs={{0,1},{1,0},{2,3},{3,2},{4,5},{5,4},{6,7},{7,6},{8,9},{9,8},{10,11... | collective-permute-start | bytes 2359304 | tf_op jit(solution)/shard_map/ppermute | solution.py:29
  252.4 58.1 %collective-permute-start.21 = (bf16[2,128,2304]{2,1,0:T(8,128)(2,1)S(1)}, bf16[2,128,2304]{2,1,0:T(8,128)(2,1)S(1)}, u32[]{:S(2)}, u32[]{:S(2)}) collective-permute-start(bf16[2,128,2304]{2,1,0:T(8,128)(2,1)S(1)} %pad_maximum_fusion.2), channel_id=1, source_target_pairs={{0,16},{4,20},{8,24},{12,28},{16,0},{20,4},{24,8},{28,12},{1,17},{... | collective-permute-start | bytes 3538952 | tf_op jit(solution)/shard_map/ppermute | solution.py:29
  276.2 35.8 %collective-permute-start.59 = (bf16[4,256,512]{2,1,0:T(8,128)(2,1)S(1)}, bf16[4,256,512]{2,1,0:T(8,128)(2,1)}, u32[]{:S(2)}, u32[]{:S(2)}) collective-permute-start(bf16[4,256,512]{2,1,0:T(8,128)(2,1)S(1)} %pad_maximum_fusion.4.refs_1_), channel_id=1, source_target_pairs={{0,2},{1,3},{2,0},{3,1},{4,6},{5,7},{6,4},{7,5},{8,10},{9,11},{10,... | collective-permute-start | bytes 3145736 | tf_op jit(solution)/shard_map/ppermute | solution.py:29
  278.0 34.2 %collective-permute-start.61 = (bf16[4,256,512]{2,1,0:T(8,128)(2,1)S(1)}, bf16[4,256,512]{2,1,0:T(8,128)(2,1)}, u32[]{:S(2)}, u32[]{:S(2)}) collective-permute-start(bf16[4,256,512]{2,1,0:T(8,128)(2,1)S(1)} %pad_maximum_fusion.4.refs_1_), channel_id=1, source_target_pairs={{0,4},{4,0},{8,12},{12,8},{16,20},{20,16},{24,28},{28,24},{1,5},{5... | collective-permute-start | bytes 3145736 | tf_op jit(solution)/shard_map/ppermute | solution.py:29
  278.6 35.6 %collective-permute-start.58 = (bf16[4,256,512]{2,1,0:T(8,128)(2,1)S(1)}, bf16[4,256,512]{2,1,0:T(8,128)(2,1)S(1)}, u32[]{:S(2)}, u32[]{:S(2)}) collective-permute-start(bf16[4,256,512]{2,1,0:T(8,128)(2,1)S(1)} %pad_maximum_fusion.4.refs_1_), channel_id=1, source_target_pairs={{0,1},{1,0},{2,3},{3,2},{4,5},{5,4},{6,7},{7,6},{8,9},{9,8},{10,11... | collective-permute-start | bytes 3145736 | tf_op jit(solution)/shard_map/ppermute | solution.py:29
  279.9 30.6 %collective-permute-start.40 = (bf16[256,1024]{1,0:T(8,128)(2,1)S(1)}, bf16[256,1024]{1,0:T(8,128)(2,1)S(1)}, u32[]{:S(2)}, u32[]{:S(2)}) collective-permute-start(bf16[256,1024]{1,0:T(8,128)(2,1)S(1)} %fusion.75), channel_id=1, source_target_pairs={{0,2},{1,3},{2,0},{3,1},{4,6},{5,7},{6,4},{7,5},{8,10},{9,11},{10,... | collective-permute-start | bytes 1572872 | tf_op jit(solution)/shard_map/ppermute | solution.py:29
  312.2 42.7 %collective-permute-start.71 = (bf16[4,256,512]{2,1,0:T(8,128)(2,1)S(1)}, bf16[4,256,512]{2,1,0:T(8,128)(2,1)S(1)}, u32[]{:S(2)}, u32[]{:S(2)}) collective-permute-start(bf16[4,256,512]{2,1,0:T(8,128)(2,1)S(1)} %pad_maximum_fusion.5.refs_1_), channel_id=1, source_target_pairs={{0,4},{4,0},{8,12},{12,8},{16,20},{20,16},{24,28},{28,24},{1,5},{5... | collective-permute-start | bytes 3145736 | tf_op jit(solution)/shard_map/ppermute | solution.py:29
  315.2 40.8 %collective-permute-start.70 = (bf16[4,256,512]{2,1,0:T(8,128)(2,1)S(1)}, bf16[4,256,512]{2,1,0:T(8,128)(2,1)}, u32[]{:S(2)}, u32[]{:S(2)}) collective-permute-start(bf16[4,256,512]{2,1,0:T(8,128)(2,1)S(1)} %pad_maximum_fusion.5.refs_1_), channel_id=1, source_target_pairs={{0,1},{1,0},{2,3},{3,2},{4,5},{5,4},{6,7},{7,6},{8,9},{9,8},{10,11... | collective-permute-start | bytes 3145736 | tf_op jit(solution)/shard_map/ppermute | solution.py:29
  359.3 31.3 %collective-permute-start.53 = (bf16[4,64,2048]{2,1,0:T(8,128)(2,1)}, bf16[4,64,2048]{2,1,0:T(8,128)(2,1)}, u32[]{:S(2)}, u32[]{:S(2)}) collective-permute-start(bf16[4,64,2048]{2,1,0:T(8,128)(2,1)} %collective-permute-done.49.refs_3_), channel_id=1, source_target_pairs={{0,2},{1,3},{2,0},{3,1},{4,6},{5,7},{6,4},{7,5},{8,10},{9,11},{10,... | collective-permute-start | bytes 3145736 | tf_op jit(solution)/shard_map/ppermute | solution.py:29
  360.9 31.7 %collective-permute-start.50 = (bf16[4,64,2048]{2,1,0:T(8,128)(2,1)}, bf16[4,64,2048]{2,1,0:T(8,128)(2,1)}, u32[]{:S(2)}, u32[]{:S(2)}) collective-permute-start(bf16[4,64,2048]{2,1,0:T(8,128)(2,1)} %collective-permute-done.49.refs_3_), channel_id=1, source_target_pairs={{0,1},{1,0},{2,3},{3,2},{4,5},{5,4},{6,7},{7,6},{8,9},{9,8},{10,11... | collective-permute-start | bytes 3145736 | tf_op jit(solution)/shard_map/ppermute | solution.py:29
  376.9 58.1 %collective-permute-start.22 = (bf16[4,128,2304]{2,1,0:T(8,128)(2,1)}, bf16[4,128,2304]{2,1,0:T(8,128)(2,1)}, u32[]{:S(2)}, u32[]{:S(2)}) collective-permute-start(bf16[4,128,2304]{2,1,0:T(8,128)(2,1)} %pad_maximum_fusion.refs_1_), channel_id=1, source_target_pairs={{0,4},{4,0},{8,12},{12,8},{16,20},{20,16},{24,28},{28,24},{1,5},{5... | collective-permute-start | bytes 7077896 | tf_op jit(solution)/shard_map/ppermute | solution.py:29
  393.4 34.0 %collective-permute-start.54 = (bf16[4,64,2048]{2,1,0:T(8,128)(2,1)}, bf16[4,64,2048]{2,1,0:T(8,128)(2,1)S(1)}, u32[]{:S(2)}, u32[]{:S(2)}) collective-permute-start(bf16[4,64,2048]{2,1,0:T(8,128)(2,1)} %collective-permute-done.53.refs_7_), channel_id=1, source_target_pairs={{0,1},{1,0},{2,3},{3,2},{4,5},{5,4},{6,7},{7,6},{8,9},{9,8},{10,11... | collective-permute-start | bytes 3145736 | tf_op jit(solution)/shard_map/ppermute | solution.py:29
  395.7 49.5 %collective-permute-start.39 = (bf16[256,1024]{1,0:T(8,128)(2,1)S(1)}, bf16[256,1024]{1,0:T(8,128)(2,1)S(1)}, u32[]{:S(2)}, u32[]{:S(2)}) collective-permute-start(bf16[256,1024]{1,0:T(8,128)(2,1)S(1)} %copy-done.114), channel_id=1, source_target_pairs={{0,1},{1,0},{2,3},{3,2},{4,5},{5,4},{6,7},{7,6},{8,9},{9,8},{10,11... | collective-permute-start | bytes 1572872 | tf_op jit(solution)/shard_map/ppermute | solution.py:29
  396.1 49.2 %collective-permute-start.15 = (bf16[256,1024]{1,0:T(8,128)(2,1)S(1)}, bf16[256,1024]{1,0:T(8,128)(2,1)}, u32[]{:S(2)}, u32[]{:S(2)}) collective-permute-start(bf16[256,1024]{1,0:T(8,128)(2,1)S(1)} %fusion.74), channel_id=1, source_target_pairs={{0,2},{1,3},{2,0},{3,1},{4,6},{5,7},{6,4},{7,5},{8,10},{9,11},{10,... | collective-permute-start | bytes 1572872 | tf_op jit(solution)/shard_map/ppermute | solution.py:29
  398.5 47.2 %collective-permute-start.41 = (bf16[256,1024]{1,0:T(8,128)(2,1)S(1)}, bf16[256,1024]{1,0:T(8,128)(2,1)S(1)}, u32[]{:S(2)}, u32[]{:S(2)}) collective-permute-start(bf16[256,1024]{1,0:T(8,128)(2,1)S(1)} %copy-done.207), channel_id=1, source_target_pairs={{0,1},{1,0},{2,3},{3,2},{4,5},{5,4},{6,7},{7,6},{8,9},{9,8},{10,11... | collective-permute-start | bytes 1572872 | tf_op jit(solution)/shard_map/ppermute | solution.py:29
  427.4 66.9 %collective-permute-start.112 = (bf16[256,1024]{1,0:T(8,128)(2,1)}, bf16[256,1024]{1,0:T(8,128)(2,1)S(1)}, u32[]{:S(2)}, u32[]{:S(2)}) collective-permute-start(bf16[256,1024]{1,0:T(8,128)(2,1)} %get-tuple-element.181), channel_id=1, source_target_pairs={{0,1},{1,0},{2,3},{3,2},{4,5},{5,4},{6,7},{7,6},{8,9},{9,8},{10,11... | collective-permute-start | bytes 1572872 | tf_op jit(solution)/shard_map/ppermute | solution.py:29
  435.0 72.5 %collective-permute-start.83 = (bf16[4,64,2048]{2,1,0:T(8,128)(2,1)S(1)}, bf16[4,64,2048]{2,1,0:T(8,128)(2,1)S(1)}, u32[]{:S(2)}, u32[]{:S(2)}) collective-permute-start(bf16[4,64,2048]{2,1,0:T(8,128)(2,1)S(1)} %pad_maximum_fusion.6.refs_1_), channel_id=1, source_target_pairs={{0,4},{4,0},{8,12},{12,8},{16,20},{20,16},{24,28},{28,24},{1,5},{5... | collective-permute-start | bytes 3145736 | tf_op jit(solution)/shard_map/ppermute | solution.py:29
  476.1 32.5 %collective-permute-start.85 = (bf16[4,64,2048]{2,1,0:T(8,128)(2,1)S(1)}, bf16[4,64,2048]{2,1,0:T(8,128)(2,1)S(1)}, u32[]{:S(2)}, u32[]{:S(2)}) collective-permute-start(bf16[4,64,2048]{2,1,0:T(8,128)(2,1)S(1)} %pad_maximum_fusion.6.refs_1_), channel_id=1, source_target_pairs={{0,2},{1,3},{2,0},{3,1},{4,6},{5,7},{6,4},{7,5},{8,10},{9,11},{10,... | collective-permute-start | bytes 3145736 | tf_op jit(solution)/shard_map/ppermute | solution.py:29
  508.6 45.0 %collective-permute-start.87 = (bf16[4,64,2048]{2,1,0:T(8,128)(2,1)S(1)}, bf16[4,64,2048]{2,1,0:T(8,128)(2,1)}, u32[]{:S(2)}, u32[]{:S(2)}) collective-permute-start(bf16[4,64,2048]{2,1,0:T(8,128)(2,1)S(1)} %collective-permute-done.83.refs_3_), channel_id=1, source_target_pairs={{0,2},{1,3},{2,0},{3,1},{4,6},{5,7},{6,4},{7,5},{8,10},{9,11},{10,... | collective-permute-start | bytes 3145736 | tf_op jit(solution)/shard_map/ppermute | solution.py:29
  509.2 55.4 %collective-permute-start.84 = (bf16[4,64,2048]{2,1,0:T(8,128)(2,1)S(1)}, bf16[4,64,2048]{2,1,0:T(8,128)(2,1)S(1)}, u32[]{:S(2)}, u32[]{:S(2)}) collective-permute-start(bf16[4,64,2048]{2,1,0:T(8,128)(2,1)S(1)} %collective-permute-done.83.refs_3_), channel_id=1, source_target_pairs={{0,1},{1,0},{2,3},{3,2},{4,5},{5,4},{6,7},{7,6},{8,9},{9,8},{10,11... | collective-permute-start | bytes 3145736 | tf_op jit(solution)/shard_map/ppermute | solution.py:29
  531.0 43.6 %collective-permute-start.97 = (bf16[4,256,512]{2,1,0:T(8,128)(2,1)S(1)}, bf16[4,256,512]{2,1,0:T(8,128)(2,1)}, u32[]{:S(2)}, u32[]{:S(2)}) collective-permute-start(bf16[4,256,512]{2,1,0:T(8,128)(2,1)S(1)} %collective-permute-done.93.refs_3_), channel_id=1, source_target_pairs={{0,4},{4,0},{8,12},{12,8},{16,20},{20,16},{24,28},{28,24},{1,5},{5... | collective-permute-start | bytes 3145736 | tf_op jit(solution)/shard_map/ppermute | solution.py:29
  532.6 32.1 %collective-permute-start.74 = (bf16[256,1024]{1,0:T(8,128)(2,1)S(1)}, bf16[256,1024]{1,0:T(8,128)(2,1)S(1)}, u32[]{:S(2)}, u32[]{:S(2)}) collective-permute-start(bf16[256,1024]{1,0:T(8,128)(2,1)S(1)} %add_convert_fusion.1), channel_id=1, source_target_pairs={{0,2},{1,3},{2,0},{3,1},{4,6},{5,7},{6,4},{7,5},{8,10},{9,11},{10,... | collective-permute-start | bytes 1572872 | tf_op jit(solution)/shard_map/ppermute | solution.py:29
  534.5 40.0 %collective-permute-start.37 = (bf16[256,1024]{1,0:T(8,128)(2,1)S(1)}, bf16[256,1024]{1,0:T(8,128)(2,1)S(1)}, u32[]{:S(2)}, u32[]{:S(2)}) collective-permute-start(bf16[256,1024]{1,0:T(8,128)(2,1)S(1)} %fusion.69), channel_id=1, source_target_pairs={{0,2},{1,3},{2,0},{3,1},{4,6},{5,7},{6,4},{7,5},{8,10},{9,11},{10,... | collective-permute-start | bytes 1572872 | tf_op jit(solution)/shard_map/ppermute | solution.py:29
  761.7 34.6 %collective-permute-start.150 = (f32[2,2,2,2,16,1024]{5,4,0,1,3,2:T(8,128)}, f32[2,2,2,2,16,1024]{5,4,0,1,3,2:T(8,128)}, u32[]{:S(2)}, u32[]{:S(2)}) collective-permute-start(f32[2,2,2,2,16,1024]{5,4,0,1,3,2:T(8,128)} %select_bitcast_fusion), channel_id=1, source_target_pairs={{0,1},{1,0},{2,3},{3,2},{4,5},{5,4},{6,7},{7,6},{8,9},{9,8},{10,11... | collective-permute-start | bytes 3145736 | tf_op jit(solution)/shard_map/ppermute | solution.py:29
  799.1 47.1 %collective-permute-start.151 = (bf16[2,2,2,16,1024]{4,3,0,1,2:T(8,128)(2,1)}, bf16[2,2,2,16,1024]{4,3,0,1,2:T(8,128)(2,1)}, u32[]{:S(2)}, u32[]{:S(2)}) collective-permute-start(bf16[2,2,2,16,1024]{4,3,0,1,2:T(8,128)(2,1)} %fusion.107), channel_id=1, source_target_pairs={{0,4},{4,0},{8,12},{12,8},{16,20},{20,16},{24,28},{28,24},{1,5},{5... | collective-permute-start | bytes 786440 | tf_op jit(solution)/shard_map/ppermute | solution.py:29
  800.3 49.3 %collective-permute-start.141 = (bf16[2,2,2,32,512]{4,3,0,1,2:T(8,128)(2,1)}, bf16[2,2,2,32,512]{4,3,0,1,2:T(8,128)(2,1)}, u32[]{:S(2)}, u32[]{:S(2)}) collective-permute-start(bf16[2,2,2,32,512]{4,3,0,1,2:T(8,128)(2,1)} %fusion.105), channel_id=1, source_target_pairs={{0,2},{1,3},{2,0},{3,1},{4,6},{5,7},{6,4},{7,5},{8,10},{9,11},{10,... | collective-permute-start | bytes 786440 | tf_op jit(solution)/shard_map/ppermute | solution.py:29
  824.2 108.8 %collective-permute-start.145 = (f32[2,2,2,2,16,1024]{5,4,0,1,3,2:T(8,128)}, f32[2,2,2,2,16,1024]{5,4,0,1,3,2:T(8,128)}, u32[]{:S(2)}, u32[]{:S(2)}) collective-permute-start(f32[2,2,2,2,16,1024]{5,4,0,1,3,2:T(8,128)} %select_bitcast_fusion.1), channel_id=1, source_target_pairs={{0,1},{1,0},{2,3},{3,2},{4,5},{5,4},{6,7},{7,6},{8,9},{9,8},{10,11... | collective-permute-start | bytes 3145736 | tf_op jit(solution)/shard_map/ppermute | solution.py:29
  839.4 96.6 %collective-permute-start.135 = (f32[2,2,2,2,32,512]{5,4,0,1,2,3:T(8,128)}, f32[2,2,2,2,32,512]{5,4,0,1,2,3:T(8,128)}, u32[]{:S(2)}, u32[]{:S(2)}) collective-permute-start(f32[2,2,2,2,32,512]{5,4,0,1,2,3:T(8,128)} %select_bitcast_fusion.3), channel_id=1, source_target_pairs={{0,1},{1,0},{2,3},{3,2},{4,5},{5,4},{6,7},{7,6},{8,9},{9,8},{10,11... | collective-permute-start | bytes 3145736 | tf_op jit(solution)/shard_map/ppermute | solution.py:29
  851.5 31.6 %collective-permute-start.120 = (bf16[256,256]{1,0:T(8,128)(2,1)S(1)}, bf16[256,256]{1,0:T(8,128)(2,1)}, u32[]{:S(2)}, u32[]{:S(2)}) collective-permute-start(bf16[256,256]{1,0:T(8,128)(2,1)S(1)} %get-tuple-element.206), channel_id=1, source_target_pairs={{0,1},{1,0},{2,3},{3,2},{4,5},{5,4},{6,7},{7,6},{8,9},{9,8},{10,11... | collective-permute-start | bytes 393224 | tf_op jit(solution)/shard_map/ppermute | solution.py:29
  852.0 32.5 %collective-permute-start.121 = (bf16[256,256]{1,0:T(8,128)(2,1)S(1)}, bf16[256,256]{1,0:T(8,128)(2,1)}, u32[]{:S(2)}, u32[]{:S(2)}) collective-permute-start(bf16[256,256]{1,0:T(8,128)(2,1)S(1)} %get-tuple-element.205), channel_id=1, source_target_pairs={{0,2},{1,3},{2,0},{3,1},{4,6},{5,7},{6,4},{7,5},{8,10},{9,11},{10,... | collective-permute-start | bytes 393224 | tf_op jit(solution)/shard_map/ppermute | solution.py:29
  855.3 29.3 %collective-permute-start.122 = (bf16[256,256]{1,0:T(8,128)(2,1)}, bf16[256,256]{1,0:T(8,128)(2,1)}, u32[]{:S(2)}, u32[]{:S(2)}) collective-permute-start(bf16[256,256]{1,0:T(8,128)(2,1)} %get-tuple-element.204), channel_id=1, source_target_pairs={{0,3},{1,2},{2,1},{3,0},{4,7},{5,6},{6,5},{7,4},{8,11},{9,10},{10,... | collective-permute-start | bytes 393224 | tf_op jit(solution)/shard_map/ppermute | solution.py:29
  884.5 45.7 %collective-permute-start.133 = (bf16[256,1024]{1,0:T(8,128)(2,1)}, bf16[256,1024]{1,0:T(8,128)(2,1)}, u32[]{:S(2)}, u32[]{:S(2)}) collective-permute-start(bf16[256,1024]{1,0:T(8,128)(2,1)} %get-tuple-element.171), channel_id=1, source_target_pairs={{0,1},{1,0},{2,3},{3,2},{4,5},{5,4},{6,7},{7,6},{8,9},{9,8},{10,11... | collective-permute-start | bytes 1572872 | tf_op jit(solution)/shard_map/ppermute | solution.py:29
  (320 other events, 5962.5 us)

commit v2 on v1

v2 whole, which is shorter than its diff:
```python
import jax
import jax.numpy as jnp
from jax import lax
from jax.experimental import pallas as pl
from jax.experimental.pallas import tpu as pltpu
from jax.sharding import PartitionSpec as P

HEAD_DIM = 64
STEP = 10

EPSILON = 1e-05
ADAPTER_SCALE = 4.0
CLIP_NORM = 0.25
RATE_ADAPTER = 0.05
RATE_NORMS = 0.5
BETA_FIRST = 0.9
BETA_SECOND = 0.999
ADAM_EPSILON = 1e-08
DECAY_ADAPTER = 0.01
MASKED_SCORE = -1000000000.0

LOW = jnp.bfloat16
F32 = jnp.float32
MIB = 1024 * 1024


def flip(value, axis, mask):
    count = lax.axis_size(axis)
    return lax.ppermute(value, axis, [(i, i ^ mask) for i in range(count)])


def bits(axis):
    count = lax.axis_size(axis)
    return [1 << i for i in range(count.bit_length() - 1)]


def unxor(blocks, me):
    blocks = list(blocks)
    mask = 1
    while mask < len(blocks):
        bit = (me & mask) != 0
        blocks = [jnp.where(bit, blocks[i ^ mask], blocks[i]) for i in range(len(blocks))]
        mask *= 2
    return blocks


def gather_enc(value):
    found = {0: value}
    for mask in bits("enc")[1:]:
        found.update({j | mask: flip(v, "enc", mask) for j, v in list(found.items())})
    found.update({j | 1: flip(v, "enc", 1) for j, v in list(found.items())})
    return [found[j] for j in range(len(found))]


def scatter_steps(blocks):
    held = dict(enumerate(blocks))
    middle = []
    for mask in bits("enc"):
        away = [j for j in held if j & mask]
        parts = [held[j].astype(LOW) for j in away]
        if mask > 1:
            middle += parts
        sent = [flip(part, "enc", mask) for part in parts]
        for j, part in zip(away, sent):
            held[j ^ mask] = held[j ^ mask].astype(F32) + part.astype(F32)
            del held[j]
    return held[0], middle


def scatter_enc(blocks):
    return scatter_steps(blocks)[0]


def merge_enc(blocks, totals):
    held = {j: (b, t) for j, (b, t) in enumerate(zip(blocks, totals))}
    for mask in bits("enc"):
        away = [j for j in held if j & mask]
        sent = [(flip(held[j][0].astype(LOW), "enc", mask), flip(held[j][1], "enc", mask)) for j in away]
        for j, (mean, total) in zip(away, sent):
            own_mean, own_total = held[j ^ mask]
            highest = jnp.maximum(own_total, total)
            first, second = jnp.exp(own_total - highest), jnp.exp(total - highest)
            both = first + second
            mean = (own_mean.astype(F32) * first + mean.astype(F32) * second) / both
            held[j ^ mask] = (mean, highest + jnp.log(both))
            del held[j]
    return held[0]


def swap_blocks(blocks):
    return [blocks[0]] + [flip(blocks[j], "enc", j) for j in range(1, len(blocks))]


def pair_split(shard, core):
    half = shard.shape[1] // 2
    first = core == 0
    low, high = shard[:, :half], shard[:, half:]
    keep = jnp.where(first, low, high)
    came = flip(jnp.where(first, high, low), "enc", 1)
    return jnp.concatenate([jnp.where(first, keep, came), jnp.where(first, came, keep)], 0)


def gate(arrays):
    def kernel(*refs):
        pass

    return pl.pallas_call(
        kernel,
        out_shape=[jax.ShapeDtypeStruct(v.shape, v.dtype) for v in arrays],
        in_specs=[pl.BlockSpec(memory_space=pl.ANY)] * len(arrays),
        out_specs=[pl.BlockSpec(memory_space=pl.ANY)] * len(arrays),
        input_output_aliases={i: i for i in range(len(arrays))},
        cost_estimate=pl.CostEstimate(flops=0, bytes_accessed=0, transcendentals=0),
    )(*arrays)


def flip_both(value, seq_mask, enc_mask):
    n_enc = lax.axis_size("enc")
    perm = []
    for i in range(lax.axis_size("seq") * n_enc):
        s, e = divmod(i, n_enc)
        perm.append((i, (s ^ seq_mask) * n_enc + (e ^ enc_mask)))
    return lax.ppermute(value, ("seq", "enc"), perm)


def tree_sum(values):
    values = list(values)
    while len(values) > 1:
        values = [values[i] + values[i + 1] for i in range(0, len(values), 2)]
    return values[0]


def plane_offsets():
    near = lax.axis_size("seq") // 4
    return [(s, e) for e in range(0, lax.axis_size("enc"), 2) for s in range(near)]


def line_offsets():
    return [k * (lax.axis_size("seq") // 4) for k in range(4)]


def mixed_flip(value, for_even, for_odd):
    n_enc = lax.axis_size("enc")
    perm = []
    for i in range(lax.axis_size("seq") * n_enc):
        s, e = divmod(i, n_enc)
        axis, mask = for_odd if e & 1 else for_even
        perm.append((i, (s ^ mask) * n_enc + e if axis == "seq" else s * n_enc + (e ^ mask)))
    return lax.ppermute(value, ("seq", "enc"), perm)


def near_bits():
    return [("seq", mask) for mask in bits("seq") if mask < lax.axis_size("seq") // 4]


def across_bits():
    return [("enc", mask) for mask in bits("enc")[1:]]


def moved(offset, step):
    return (offset[0] ^ step[1], offset[1]) if step[0] == "seq" else (offset[0], offset[1] ^ step[1])


def slow_flips(value):
    return [flip(value, "seq", o) for o in line_offsets()[1:]]


def plane_steps():
    return list(zip(near_bits() + across_bits(), across_bits() + near_bits()))


def plane_start(stacked):
    return [mixed_flip(stacked, *step) for step in plane_steps()]


def plane_finish(stacked, singles, core):
    found = [((0, 0), (0, 0), stacked)]
    for step, single in zip(plane_steps(), singles):
        fresh = [(moved((0, 0), step[0]), moved((0, 0), step[1]), single)]
        fresh += [
            (moved(o, step[0]), moved(p, step[1]), mixed_flip(v, *step)) for o, p, v in found[1:]
        ]
        found += fresh
    own = [tuple(jnp.where(core == 0, i, k) for i, k in zip(o, p)) for o, p, _ in found]
    other = [tuple(jnp.where(core == 0, k, i) for i, k in zip(o, p)) for o, p, _ in found]
    return own, other, [v for _, _, v in found]


def near_flips(stacked):
    found = [(0, stacked)]
    for _, mask in near_bits():
        found += [(o ^ mask, flip(v, "seq", mask)) for o, v in found]
    return [o for o, _ in found], [v for _, v in found]


def assemble(sources, pieces, places, outs):
    count = len(pieces)
    n_src, n_out = len(sources), len(outs)

    def kernel(*refs):
        table = refs[0]
        given = refs[1 : 1 + n_src]
        results = refs[1 + n_src : 1 + n_src + n_out]
        stage = refs[1 + n_src + n_out : 1 + n_src + n_out + count]
        sem_in, sem_out = refs[-2:]
        copies_in, copies_out = [], []
        for i, (src, block, row, column, rows, columns, out) in enumerate(pieces):
            copies_in.append(
                pltpu.make_async_copy(
                    given[src].at[block, pl.ds(row, rows), pl.ds(column, columns)],
                    stage[i],
                    sem_in.at[i],
                )
            )
            to_row = pl.multiple_of(table[2 * i], rows)
            to_column = pl.multiple_of(table[2 * i + 1], columns)
            copies_out.append(
                pltpu.make_async_copy(
                    stage[i],
                    results[out].at[pl.ds(to_row, rows), pl.ds(to_column, columns)],
                    sem_out.at[i],
                )
            )
        for copy in copies_in:
            copy.start()
        for i in range(count):
            copies_in[i].wait()
            copies_out[i].start()
        for copy in copies_out:
            copy.wait()

    size = sum(p[4] * p[5] * 2 for p in pieces)
    return pl.pallas_call(
        kernel,
        out_shape=[jax.ShapeDtypeStruct(shape, LOW) for shape in outs],
        in_specs=[pl.BlockSpec(memory_space=pltpu.SMEM)]
        + [pl.BlockSpec(memory_space=pl.ANY)] * n_src,
        out_specs=[pl.BlockSpec(memory_space=pl.ANY)] * n_out,
        scratch_shapes=[pltpu.VMEM((p[4], p[5]), LOW) for p in pieces]
        + [pltpu.SemaphoreType.DMA((count,)), pltpu.SemaphoreType.DMA((count,))],
        compiler_params=pltpu.CompilerParams(vmem_limit_bytes=size + 8 * MIB),
        cost_estimate=pl.CostEstimate(flops=0, bytes_accessed=2 * size, transcendentals=0),
    )(places, *sources)


def place_table(places):
    return jnp.stack([jnp.asarray(p, jnp.int32) for p in places])


def assemble_matrix(own, other, mine, partners, layout, outs, seq, enc):
    n_enc = lax.axis_size("enc")
    core = enc & 1
    sources, pieces, places = [], [], []
    for offsets, half, buffers in ((own, core, mine), (other, 1 - core, partners)):
        for (s_off, e_off), v in zip(offsets, buffers):
            for n, o in enumerate(line_offsets()):
                device = (seq ^ s_off ^ o) * n_enc + (enc ^ e_off)
                for row, column, rows, columns, out, to_row, to_column in layout(device >> 1, half):
                    pieces.append((len(sources), n, row, column, rows, columns, out))
                    places += [to_row, to_column]
            sources.append(v)
    return assemble(sources, pieces, place_table(places), outs)


def assemble_strips(offsets, buffers, count, seq):
    rows, width = buffers[0].shape[1], buffers[0].shape[2] // count
    pieces, places = [], []
    for i, s_off in enumerate(offsets):
        for n, o in enumerate(line_offsets()):
            for k in range(count):
                pieces.append((i, n, 0, k * width, rows, width, k))
                places += [(seq ^ s_off ^ o) * rows, 0]
    total = rows * lax.axis_size("seq")
    return assemble(buffers, pieces, place_table(places), [(total, width)] * count)


def dense(left, right):
    return jnp.dot(left, right, preferred_element_type=F32)


def dense_back(left, right):
    return lax.dot_general(left, right, (((1,), (1,)), ((), ())), preferred_element_type=F32)


def inner_rows(left, right):
    return lax.dot_general(left, right, (((0,), (0,)), ((), ())), preferred_element_type=F32)


def layer_norm(values, gain, shift):
    middle = jnp.mean(values, -1, keepdims=True)
    centred = values - middle
    variance = jnp.mean(centred * centred, -1, keepdims=True)
    return centred * lax.rsqrt(variance + EPSILON) * gain + shift


def norm_forward(values, norms, index):
    return jax.vjp(layer_norm, values, norms[0, index], norms[1, index])


def norm_start(values, norms, index):
    middle = jnp.mean(values, -1, keepdims=True)
    centred = values - middle
    hat = centred * lax.rsqrt(jnp.mean(centred * centred, -1, keepdims=True) + EPSILON)
    return hat * norms[0, index] + norms[1, index], hat


def adamw(grad, moment, second, weight, rate, decay):
    moment = BETA_FIRST * moment + (1.0 - BETA_FIRST) * grad
    second = BETA_SECOND * second + (1.0 - BETA_SECOND) * grad * grad
    corrected = moment / (1.0 - BETA_FIRST**STEP)
    scale_two = jnp.sqrt(second / (1.0 - BETA_SECOND**STEP))
    return (
        moment,
        second,
        weight - rate * (corrected / (scale_two + ADAM_EPSILON) + decay * weight),
    )


def scores_of(left, right):
    return lax.dot_general(left, right, (((1,), (1,)), ((), ())), preferred_element_type=F32)


def head_parts(values):
    side = lax.broadcasted_iota(jnp.int32, values.shape, 1) // HEAD_DIM
    count = values.shape[1] // HEAD_DIM
    return [jnp.where(side == h, values, jnp.zeros((), values.dtype)) for h in range(count)]


def head_join(parts):
    side = lax.broadcasted_iota(jnp.int32, (parts[0].shape[0], 128), 1) // HEAD_DIM
    joined = jnp.broadcast_to(parts[0], side.shape)
    for h in range(1, len(parts)):
        joined = jnp.where(side == h, parts[h], joined)
    return joined


def attend_kernel(limit_ref, spot_ref, q_ref, k_ref, v_ref, *rest):
    context_ref, total_ref = rest[-2:]
    queries = head_parts(q_ref[...] * jnp.asarray(0.125, LOW))
    key, value = k_ref[...], v_ref[...]
    allowed = spot_ref[...] < limit_ref[...]
    raw = [scores_of(query, key) for query in queries]
    contexts, totals = [], []
    for scores in raw:
        scores = jnp.where(allowed, scores, MASKED_SCORE)
        highest = jnp.max(scores, -1, keepdims=True)
        exponent = jnp.exp(scores - highest)
        summed = jnp.sum(exponent, -1, keepdims=True)
        contexts.append(jnp.dot(exponent.astype(LOW), value, preferred_element_type=F32) / summed)
        totals.append(highest + jnp.log(summed))
    context_ref[...] = head_join(contexts).astype(LOW)
    total_ref[...] = head_join(totals)


def attend_specs(rows, length, key_at, value_at, count):
    block = pl.BlockSpec((rows, 128), lambda p, j: (j, p))
    return [
        pl.BlockSpec((rows, 1), lambda p, j: (j, 0)),
        pl.BlockSpec((1, length), lambda p, j: (0, 0)),
        block,
        pl.BlockSpec((length, 128), lambda p, j: (0, key_at + p)),
        pl.BlockSpec((length, 128), lambda p, j: (0, value_at + p)),
    ] + [block] * count


def query_rows(length):
    return 512 if length <= 1024 else 256


def attend(query, keys, key_at, value_at, limit, spots, after=()):
    length = query.shape[0]
    width = keys.shape[1] // (2 if key_at == 0 else 3)
    pairs = width // 128
    rows = query_rows(length)
    block = pl.BlockSpec((rows, 128), lambda p, j: (j, p))
    return pl.pallas_call(
        attend_kernel,
        grid=(pairs, length // rows),
        out_shape=[
            jax.ShapeDtypeStruct((length, width), LOW),
            jax.ShapeDtypeStruct((length, width), F32),
        ],
        in_specs=attend_specs(rows, length, key_at, value_at, 0)
        + [pl.BlockSpec(memory_space=pl.ANY)] * len(after),
        out_specs=[block, block],
        compiler_params=pltpu.CompilerParams(vmem_limit_bytes=56 * MIB),
        cost_estimate=pl.CostEstimate(
            flops=8 * length * length * width,
            bytes_accessed=8 * length * width,
            transcendentals=length * length * width // HEAD_DIM,
        ),
    )(limit, spots, query, keys, keys, *after)


def attend_back_kernel(limit_ref, spot_ref, q_ref, k_ref, v_ref, grad_ref, total_ref, *rest):
    out_ref, dk_sum, dv_sum = rest[-3:]
    pair, step = pl.program_id(0), pl.program_id(1)
    pairs, steps = pl.num_programs(0), pl.num_programs(1)
    rows = q_ref.shape[0]

    @pl.when(step == 0)
    def _():
        dk_sum[...] = jnp.zeros_like(dk_sum)
        dv_sum[...] = jnp.zeros_like(dv_sum)

    queries = head_parts(q_ref[...] * jnp.asarray(0.125, LOW))
    grads = head_parts(grad_ref[...])
    key, value, totals = k_ref[...], v_ref[...], total_ref[...]
    allowed = spot_ref[...] < limit_ref[...]
    raw = [scores_of(query, key) for query in queries]
    grad_softs = [scores_of(grad, value) for grad in grads]
    grad_scores, soft_lows = [], []
    for h, (scores, grad_soft) in enumerate(zip(raw, grad_softs)):
        scores = jnp.where(allowed, scores, MASKED_SCORE)
        soft = jnp.exp(scores - totals[:, h * HEAD_DIM : h * HEAD_DIM + 1])
        weighted = jnp.sum(soft * grad_soft, -1, keepdims=True)
        grad_scores.append((soft * (grad_soft - weighted)).astype(LOW))
        soft_lows.append(soft.astype(LOW))
    dk_sum[...] += inner_rows(jnp.concatenate(grad_scores, 0), jnp.concatenate(queries, 0))
    dv_sum[...] += inner_rows(jnp.concatenate(soft_lows, 0), jnp.concatenate(grads, 0))
    grad_query = head_join([jnp.dot(g, key, preferred_element_type=F32) for g in grad_scores])
    column = pl.multiple_of(pair * 128, 128)
    out_ref[pl.ds(pl.multiple_of(step * rows, rows), rows), pl.ds(column, 128)] = (
        grad_query * 0.125
    ).astype(LOW)

    @pl.when(step == steps - 1)
    def _():
        out_ref[:, pl.ds(pl.multiple_of((pairs + pair) * 128, 128), 128)] = dk_sum[...].astype(LOW)
        out_ref[:, pl.ds(pl.multiple_of((2 * pairs + pair) * 128, 128), 128)] = dv_sum[...].astype(
            LOW
        )


def attend_back(query, keys, key_at, value_at, limit, spots, grads, totals, after=()):
    length, width = grads.shape
    pairs = width // 128
    rows = query_rows(length)
    return pl.pallas_call(
        attend_back_kernel,
        grid=(pairs, length // rows),
        out_shape=jax.ShapeDtypeStruct((length, 3 * width), LOW),
        in_specs=attend_specs(rows, length, key_at, value_at, 2)
        + [pl.BlockSpec(memory_space=pl.ANY)] * len(after),
        out_specs=pl.BlockSpec((length, 3 * width), lambda p, j: (0, 0)),
        scratch_shapes=[pltpu.VMEM((length, 128), F32), pltpu.VMEM((length, 128), F32)],
        compiler_params=pltpu.CompilerParams(vmem_limit_bytes=60 * MIB),
        cost_estimate=pl.CostEstimate(
            flops=20 * length * length * width,
            bytes_accessed=16 * length * width,
            transcendentals=length * length * width // HEAD_DIM,
        ),
    )(limit, spots, query, keys, keys, grads, totals, *after)


def gelu_both(values):
    below = 0.5 * (1.0 + lax.erf(values * 0.7071067811865476))
    bell = jnp.exp(values * values * -0.5) * 0.3989422804014327
    return values * below, below + values * bell


def pack_feed(expand, reduce, down, up):
    rows, width = expand.shape[0], reduce.shape[1]
    parts = [expand[:, q * width : (q + 1) * width] for q in range(4)]
    return jnp.concatenate(
        parts + [reduce, jnp.concatenate([down[: rows // 2], down[rows // 2 :]], 1), up], 0
    )


def gather_feed(expand, reduce, down, up):
    everyone = ("seq", "enc")
    if expand.shape[0] % 32 == 0:
        return lax.all_gather(pack_feed(expand, reduce, down, up), everyone)
    whole = [lax.all_gather(v, everyone, axis=0, tiled=True) for v in (expand, reduce, down, up)]
    return pack_feed(*whole)[None]


def feed_specs(packed, tile):
    count, depth, width = packed.shape
    rows = depth // 9
    per = width // tile
    if 4 * rows <= tile:
        reduce = pl.BlockSpec((tile // (4 * rows), 4 * rows, width), lambda j: (j, 1, 0))
    else:
        first = 4 * rows // tile
        reduce = pl.BlockSpec((1, tile, width), lambda j: (0, first + j, 0))
    return [
        pl.BlockSpec((count, rows, tile), lambda j: (0, j // per, j % per)),
        reduce,
        pl.BlockSpec((count, rows, width), lambda j: (0, 8, 0)),
    ]


def flat(block):
    return block.reshape(block.shape[0] * block.shape[1], block.shape[2])


def adapter_parts(block):
    count, rows, width = block.shape
    half = rows // 2
    down = jnp.stack([block[:, :half, : width // 2], block[:, :half, width // 2 :]], 1)
    return down.reshape(count * rows, width // 2), flat(block[:, half:])


def branch_kernel(
    x_ref, in_ref, out_ref, small_ref, y_ref, slope_ref, act_ref, bend_ref, total
):
    step = pl.program_id(0)

    @pl.when(step == 0)
    def _():
        down, up = adapter_parts(small_ref[...])
        act, slope = gelu_both(jnp.dot(x_ref[...], down, preferred_element_type=F32))
        act = act.astype(LOW)
        act_ref[...] = act
        bend_ref[...] = slope
        total[...] = ADAPTER_SCALE * jnp.dot(act, up, preferred_element_type=F32)

    part = 256
    x = x_ref[...]
    expand, reduce = flat(in_ref[...]), flat(out_ref[...])
    tile = expand.shape[1]
    pre = jnp.dot(x, expand[:, :part], preferred_element_type=F32)
    for start in range(0, tile, part):
        now = pre
        if start + part < tile:
            pre = jnp.dot(x, expand[:, start + part : start + 2 * part], preferred_element_type=F32)
        act, slope = gelu_both(now)
        slope_ref[:, start : start + part] = slope
        total[...] += jnp.dot(
            act.astype(LOW), reduce[start : start + part], preferred_element_type=F32
        )

    @pl.when(step == pl.num_programs(0) - 1)
    def _():
        y_ref[...] = total[...]


def branch(rows_low, packed, tile=1024):
    rows, width = rows_low.shape
    hidden, small = 4 * width, width // 2
    return pl.pallas_call(
        branch_kernel,
        grid=(hidden // tile,),
        out_shape=[
            jax.ShapeDtypeStruct((rows, width), F32),
            jax.ShapeDtypeStruct((rows, hidden), F32),
            jax.ShapeDtypeStruct((rows, small), LOW),
            jax.ShapeDtypeStruct((rows, small), F32),
        ],
        in_specs=[pl.BlockSpec((rows, width), lambda j: (0, 0))] + feed_specs(packed, tile),
        out_specs=[
            pl.BlockSpec((rows, width), lambda j: (0, 0)),
            pl.BlockSpec((rows, tile), lambda j: (0, j)),
            pl.BlockSpec((rows, small), lambda j: (0, 0)),
            pl.BlockSpec((rows, small), lambda j: (0, 0)),
        ],
        scratch_shapes=[pltpu.VMEM((rows, width), F32)],
        compiler_params=pltpu.CompilerParams(vmem_limit_bytes=56 * MIB),
        cost_estimate=pl.CostEstimate(
            flops=4 * rows * width * (hidden + small),
            bytes_accessed=4 * width * (hidden + small) + 4 * rows * hidden,
            transcendentals=2 * rows * hidden,
        ),
    )(rows_low, packed, packed, packed)


def branch_back_kernel(
    g_ref, ga_ref, in_ref, out_ref, small_ref, slope_ref, bend_ref, dx_ref, dpre_ref, total
):
    step = pl.program_id(0)

    @pl.when(step == 0)
    def _():
        down, up = adapter_parts(small_ref[...])
        grad = dense_back(ga_ref[...], up)
        pre = (grad * bend_ref[...]).astype(LOW)
        dpre_ref[...] = pre
        total[...] = dense_back(pre, down)

    part = 256
    g = g_ref[...]
    expand, reduce = flat(in_ref[...]), flat(out_ref[...])
    tile = expand.shape[1]
    grad = dense_back(g, reduce[:part])
    for start in range(0, tile, part):
        now = grad
        if start + part < tile:
            grad = dense_back(g, reduce[start + part : start + 2 * part])
        pre = (now * slope_ref[:, start : start + part]).astype(LOW)
        total[...] += dense_back(pre, expand[:, start : start + part])

    @pl.when(step == pl.num_programs(0) - 1)
    def _():
        dx_ref[...] = total[...]


def branch_back(grad_out, kept, packed, tile=1024):
    rows_low, slope, act, bend = kept
    rows, width = rows_low.shape
    hidden, small = 4 * width, width // 2
    grad_low = grad_out.astype(LOW)
    grad_adapter = (ADAPTER_SCALE * grad_out).astype(LOW)
    whole = pl.BlockSpec((rows, width), lambda j: (0, 0))
    narrow = pl.BlockSpec((rows, small), lambda j: (0, 0))
    grad_rows, grad_pre = pl.pallas_call(
        branch_back_kernel,
        grid=(hidden // tile,),
        out_shape=[
            jax.ShapeDtypeStruct((rows, width), F32),
            jax.ShapeDtypeStruct((rows, small), LOW),
        ],
        in_specs=[whole, whole]
        + feed_specs(packed, tile)
        + [pl.BlockSpec((rows, tile), lambda j: (0, j)), narrow],
        out_specs=[whole, narrow],
        scratch_shapes=[pltpu.VMEM((rows, width), F32)],
        compiler_params=pltpu.CompilerParams(vmem_limit_bytes=56 * MIB),
        cost_estimate=pl.CostEstimate(
            flops=4 * rows * width * (hidden + small),
            bytes_accessed=4 * width * (hidden + small) + 4 * rows * hidden,
            transcendentals=0,
        ),
    )(grad_low, grad_adapter, packed, packed, packed, slope, bend)
    return grad_rows, inner_rows(rows_low, grad_pre), inner_rows(act, grad_adapter)


def head_kernel(o_ref, e_ref, g_ref, lse_ref, acc, peak, mass):
    step = pl.program_id(0)
    part = 512

    @pl.when(step == 0)
    def _():
        acc[...] = jnp.zeros_like(acc)
        peak[...] = jnp.full_like(peak, -1e30)
        mass[...] = jnp.zeros_like(mass)

    table = e_ref[...]
    starts = list(range(0, o_ref.shape[0], part))
    spans = [pl.ds(start, part) for start in starts]
    before = [peak[at, :1] for at in spans]
    held = [mass[at, :] for at in spans]
    coming = scores_of(o_ref[spans[0], :], table)
    highest, summed = [], []
    for h, at in enumerate(spans):
        logits = coming
        if h + 1 < len(spans):
            coming = scores_of(o_ref[spans[h + 1], :], table)
        highest.append(jnp.maximum(before[h], jnp.max(logits, -1, keepdims=True)))
        exponent = jnp.exp(logits - highest[h])
        fade = jnp.exp(before[h] - highest[h])
        summed.append(held[h] * fade + jnp.sum(exponent, -1, keepdims=True))
        acc[at, :] = acc[at, :] * fade + jnp.dot(
            exponent.astype(LOW), table, preferred_element_type=F32
        )
    for h, at in enumerate(spans):
        mass[at, :] = summed[h]
        peak[at, :] = jnp.broadcast_to(highest[h], (part, 128))

    @pl.when(step == pl.num_programs(0) - 1)
    def _():
        g_ref[...] = (acc[...] / mass[:, :1]).astype(LOW)
        lse_ref[...] = peak[...] + jnp.log(mass[...])


def head(rows_low, table):
    rows, width = rows_low.shape
    entries = table.shape[0]
    tile = next(t for t in (1280, 1024, 640, 512, 256, 128) if entries % t == 0)
    return pl.pallas_call(
        head_kernel,
        grid=(entries // tile,),
        out_shape=[
            jax.ShapeDtypeStruct((rows, width), LOW),
            jax.ShapeDtypeStruct((rows, 128), F32),
        ],
        in_specs=[
            pl.BlockSpec((rows, width), lambda j: (0, 0)),
            pl.BlockSpec((tile, width), lambda j: (j, 0)),
        ],
        out_specs=[
            pl.BlockSpec((rows, width), lambda j: (0, 0)),
            pl.BlockSpec((rows, 128), lambda j: (0, 0)),
        ],
        scratch_shapes=[
            pltpu.VMEM((rows, width), F32),
            pltpu.VMEM((rows, 128), F32),
            pltpu.VMEM((rows, 128), F32),
        ],
        compiler_params=pltpu.CompilerParams(vmem_limit_bytes=56 * MIB),
        cost_estimate=pl.CostEstimate(
            flops=4 * rows * width * entries,
            bytes_accessed=2 * width * entries,
            transcendentals=rows * entries,
        ),
    )(rows_low, table)


def reduce_adapters(grad_down, grad_up, seq, enc):
    n_seq, n_enc = lax.axis_size("seq"), lax.axis_size("enc")
    near = n_seq // 4
    width, small = grad_down.shape
    rows = width // (n_seq * n_enc)
    folded = grad_down.reshape(-1, 2, rows // 2, small).transpose(0, 2, 1, 3)
    folded = folded.reshape(-1, rows // 2, 2 * small)
    both = jnp.concatenate([folded, grad_up.reshape(-1, rows // 2, width)], 1)
    both = both.reshape(4, near, n_enc // 2, 2, rows, width)
    first = (enc & 1) == 0
    low, high = both[:, :, :, 0], both[:, :, :, 1]
    held = jnp.where(first, low, high) + flip(jnp.where(first, high, low), "enc", 1)

    def block(s_off, e_off):
        start = (0, (seq & (near - 1)) ^ s_off, (enc >> 1) ^ (e_off >> 1), 0, 0)
        return lax.dynamic_slice(held, start, (4, 1, 1, rows, width))[:, 0, 0]

    parts = [block(0, 0)] + [
        flip_both(block(s, e).astype(LOW), s, e).astype(F32) for s, e in plane_offsets()[1:]
    ]
    held = tree_sum(parts)
    slow = seq // near
    parts = [lax.dynamic_index_in_dim(held, slow ^ k, 0, keepdims=False) for k in range(4)]
    held = tree_sum(
        parts[:1]
        + [flip(p.astype(LOW), "seq", o).astype(F32) for p, o in zip(parts[1:], line_offsets()[1:])]
    )
    down = held[: rows // 2].reshape(rows // 2, 2, small).transpose(1, 0, 2)
    return down.reshape(rows, small), held[rows // 2 :]


def sum_everywhere(values):
    values = values + flip(values, "enc", 1)
    values = tree_sum([values] + [flip_both(values, s, e) for s, e in plane_offsets()[1:]])
    return tree_sum([values] + [flip(values, "seq", o) for o in line_offsets()[1:]])


def shards(
    source_ids,
    target_ids,
    labels,
    lengths,
    embedding,
    positions,
    attention_in,
    attention_out,
    feed_in,
    feed_out,
    adapter_down,
    adapter_up,
    norm_params,
    down_moment,
    down_second,
    up_moment,
    up_second,
    norm_moment,
    norm_second,
):
    n_seq, n_enc = lax.axis_size("seq"), lax.axis_size("enc")
    n_all = n_seq * n_enc
    seq, enc = lax.axis_index("seq"), lax.axis_index("enc")
    core = enc & 1
    own_rows = source_ids.shape[1]
    width = embedding.shape[1]
    entries = embedding.shape[0]
    length = own_rows * n_enc
    share = width // n_enc
    source_length, target_length = lengths[0, 0], lengths[0, 1]

    blocks = jnp.arange(n_enc) ^ enc
    spots = (blocks[:, None] * own_rows + jnp.arange(own_rows)[None, :]).reshape(length)
    spots = spots.astype(jnp.int32)
    source_limit = jnp.broadcast_to(source_length, (length, 1)).astype(jnp.int32)
    causal_limit = jnp.minimum(spots + 1, target_length)[:, None].astype(jnp.int32)
    spots = spots[None, :]
    in_strip = share // 128

    def gather_rows(rows_low):
        return jnp.concatenate(gather_enc(rows_low), 0)

    def lookup(ids):
        inside = (ids >= 0) & (ids < entries)
        found = jnp.take(embedding, jnp.clip(ids, 0, entries - 1), axis=0)
        return jnp.where(inside[:, :, None], found, jnp.zeros((), LOW))

    def rows_of(found):
        return scatter_enc([found[j] for j in range(n_enc)])

    def finish_attention(context, k):
        parts = swap_blocks([context[j * own_rows : (j + 1) * own_rows] for j in range(n_enc)])
        return dense(jnp.concatenate(parts, 1), attend_out[k])

    def begin_attention_back(grad, k):
        spread = dense_back(grad.astype(LOW), attend_out[k]).astype(LOW)
        parts = swap_blocks([spread[:, j * share : (j + 1) * share] for j in range(n_enc)])
        return jnp.concatenate(parts, 0)

    def scatter_rows(partial):
        return scatter_enc([partial[j * own_rows : (j + 1) * own_rows] for j in range(n_enc)])

    def start_grads(grads, k, grad_res, hat, hats):
        partial = dense_back(grads, attend_in[k])
        gain = jnp.sum(partial * hats.astype(F32), 0) + jnp.sum(grad_res * hat, 0)
        return gain, jnp.sum(partial, 0) + jnp.sum(grad_res, 0)

    down_low, up_low = adapter_down.astype(LOW), adapter_up.astype(LOW)
    feeds = [gather_feed(feed_in[k], feed_out[k], down_low[k], up_low[k]) for k in range(2)]

    gains = norm_params.astype(LOW).astype(F32)
    ids = jnp.concatenate([source_ids, target_ids, labels], 0).astype(F32)
    small_own = jnp.concatenate([ids.reshape(1, -1), gains.reshape(1, -1)], 1)
    small_all = unxor([v[0] for v in jnp.split(lax.all_gather(small_own, "enc"), n_enc)], enc)
    small_all = jnp.concatenate(small_all, 0)
    all_ids = small_all[:, : 3 * own_rows].astype(jnp.int32).reshape(n_enc, 3, own_rows)
    all_ids = all_ids - enc * entries
    gains = small_all[:, 3 * own_rows :].astype(LOW)[None]

    triple = attention_in.reshape(3, -1, 3, n_enc, share).transpose(3, 1, 0, 2, 4)
    shard_rows = triple.shape[1]
    strip_rows, pair_rows = n_enc * shard_rows, 2 * shard_rows
    triple = triple.reshape(n_enc, shard_rows, 9 * share)
    strip = lax.all_to_all(triple, "enc", 0, 0, tiled=True).reshape(strip_rows, 9 * share)
    strip, late = strip[:, : 6 * share], strip[:, 6 * share :]
    half = width // 2
    packed = jnp.concatenate(
        [attention_out[k][:, h * half : (h + 1) * half] for h in range(2) for k in range(3)], 1
    )
    pair_out = pair_split(packed, core)

    ids = [all_ids[:, k] for k in range(3)]

    slow = slow_flips(strip)
    for mask in bits("seq"):
        gains = jnp.concatenate([gains, flip(gains, "seq", mask)], 0)
    found = [lookup(ids[0]), lookup(ids[1])]
    pair_out, *slow = gate([pair_out] + slow)
    order_seq, order_enc = jnp.arange(n_seq) ^ seq, jnp.arange(n_enc) ^ enc
    gains = jnp.take(jnp.take(gains, order_seq, axis=0), order_enc, axis=1)
    gains = gains.reshape(n_all, 14, width // n_all).transpose(1, 0, 2)
    norms = gains.reshape(2, 7, width).astype(F32)

    strip_offsets, strips = near_flips(jnp.stack([strip] + slow))
    source_rows, target_rows = rows_of(found[0]), rows_of(found[1])
    slow = slow_flips(pair_out)
    found = lookup(ids[2])
    late, *slow = gate([late] + slow)

    in_enc, in_dec = assemble_strips(strip_offsets, strips, 2, seq)
    encoder_in, encoder_hat = norm_start(source_rows + positions[0].astype(F32), norms, 0)
    decoder_in, decoder_hat = norm_start(target_rows + positions[1].astype(F32), norms, 3)
    encoder_all = gather_rows(encoder_in.astype(LOW))
    decoder_all = gather_rows(decoder_in.astype(LOW))
    stacked = jnp.stack([pair_out] + slow)
    singles = plane_start(stacked)

    own, other, mine = plane_finish(stacked, singles, core)
    partners = [flip(v, "enc", 1) for v in mine]
    slow = slow_flips(late)
    triple_encoder = dense(encoder_all, in_enc).astype(LOW)
    enc_args = (triple_encoder, triple_encoder, in_strip, 2 * in_strip, source_limit, spots)
    context_enc, total_encoder = attend(*enc_args)
    triple_decoder = dense(decoder_all, in_dec).astype(LOW)
    dec_args = (triple_decoder, triple_decoder, in_strip, 2 * in_strip, causal_limit, spots)
    context_dec, total_decoder = attend(*dec_args)

    def out_layout(pair, side):
        row = pair * pair_rows
        block = (row // share) ^ enc
        return [
            (0, k * half, pair_rows, half, k, block * share + row % share, side * half)
            for k in range(3)
        ]

    attend_out = assemble_matrix(
        own, other, mine, partners, out_layout, [(width, width)] * 3, seq, enc
    )
    late_offsets, strips = near_flips(jnp.stack([late] + slow))
    after_self, pull_one = norm_forward(encoder_in + finish_attention(context_enc, 0), norms, 1)
    after_causal, pull_four = norm_forward(decoder_in + finish_attention(context_dec, 1), norms, 4)
    label_rows = rows_of(found)

    in_cross = assemble_strips(late_offsets, strips, 1, seq)[0]
    attend_in = [in_enc, in_dec, in_cross]
    causal_all = gather_rows(after_causal.astype(LOW))
    after_self_low = after_self.astype(LOW)
    branched, *kept_enc = branch(after_self_low, feeds[0])
    encoded, pull_two = norm_forward(after_self + branched, norms, 2)
    encoded_low = encoded.astype(LOW)
    query_cross = dense(causal_all, in_cross[:, :share]).astype(LOW)

    encoded_all = gather_rows(encoded_low)
    pairs_cross = dense(encoded_all, in_cross[:, share:]).astype(LOW)
    cross_args = (query_cross, pairs_cross, 0, in_strip, source_limit, spots)
    context, total_cross = attend(*cross_args)
    after_cross, pull_five = norm_forward(after_causal + finish_attention(context, 2), norms, 5)
    after_cross_low = after_cross.astype(LOW)
    branched, *kept_dec = branch(after_cross_low, feeds[1])
    decoded, pull_six = norm_forward(after_cross + branched, norms, 6)
    decoded_low = decoded.astype(LOW)

    decoded_all, encoder_hat, decoder_hat = gate(
        [gather_rows(decoded_low), encoder_hat, decoder_hat]
    )
    pulled, totals = head(decoded_all, embedding)
    encoder_hats = gather_rows(encoder_hat.astype(LOW))
    decoder_hats = gather_rows(decoder_hat.astype(LOW))
    parts = [slice(j * own_rows, (j + 1) * own_rows) for j in range(n_enc)]
    pulled, log_total = merge_enc([pulled[p] for p in parts], [totals[p, :1] for p in parts])
    row_spots = enc * own_rows + jnp.arange(own_rows)
    valid = (row_spots < target_length).astype(F32)[:, None]
    picked = jnp.sum(decoded_low.astype(F32) * label_rows, -1, keepdims=True)
    loss_own = jnp.sum((log_total - picked) * valid)
    grad_decoded = (pulled - label_rows) * valid

    grad_res, gain_six, shift_six = pull_six(grad_decoded)
    grad_rows, down_dec, up_dec = branch_back(
        grad_res, [after_cross_low] + kept_dec, feeds[1]
    )
    grad_res, gain_five, shift_five = pull_five(grad_res + grad_rows)
    grads = attend_back(*cross_args, begin_attention_back(grad_res, 2), total_cross)
    grad_encoded = scatter_rows(dense_back(grads[:, share:], attend_in[2][:, share:]))
    grad_causal = grad_res + scatter_rows(dense_back(grads[:, :share], attend_in[2][:, :share]))
    grad_res, gain_four, shift_four = pull_four(grad_causal)
    grads = attend_back(*dec_args, begin_attention_back(grad_res, 1), total_decoder)
    gain_three, shift_three = start_grads(grads, 1, grad_res, decoder_hat, decoder_hats)
    grad_res, gain_two, shift_two = pull_two(grad_encoded)
    grad_rows, down_enc, up_enc = branch_back(
        grad_res, [after_self_low] + kept_enc, feeds[0]
    )
    grad_res, gain_one, shift_one = pull_one(grad_res + grad_rows)
    owned_dec = reduce_adapters(down_dec, up_dec, seq, enc)
    owned_enc = reduce_adapters(down_enc, up_enc, seq, enc)
    grads = attend_back(*enc_args, begin_attention_back(grad_res, 0), total_encoder, after=owned_dec)
    gain_zero, shift_zero = start_grads(grads, 0, grad_res, encoder_hat, encoder_hats)

    grad_down = jnp.stack([owned_enc[0], owned_dec[0]])
    grad_up = jnp.stack([owned_enc[1], owned_dec[1]])
    count_own = jnp.clip(target_length - enc * own_rows, 0, own_rows).astype(F32)
    squares_own = jnp.sum(grad_down * grad_down) + jnp.sum(grad_up * grad_up)
    lanes = jnp.arange(width)
    scalars = jnp.where(
        lanes == 0, loss_own, jnp.where(lanes == 1, count_own, jnp.where(lanes == 2, squares_own, 0.0))
    )
    summed = jnp.stack(
        [gain_zero, gain_one, gain_two, gain_three, gain_four, gain_five, gain_six]
        + [shift_zero, shift_one, shift_two, shift_three, shift_four, shift_five, shift_six]
        + [scalars, jnp.zeros_like(scalars)]
    )
    summed = sum_everywhere(summed)
    loss_sum, token_total = summed[14, 0], summed[14, 1]
    norm_grads = summed[:14]
    squares = summed[14, 2] + jnp.sum(norm_grads * norm_grads)
    per = width // n_all
    grad_norms = lax.dynamic_slice_in_dim(norm_grads, (seq * n_enc + enc) * per, per, 1)
    grad_norms = grad_norms.reshape(2, 7, per)

    grad_norm = jnp.sqrt(squares) / token_total
    factor = jnp.minimum(1.0, CLIP_NORM / grad_norm) / token_total
    moment_down, second_down, updated_down = adamw(
        grad_down * factor, down_moment, down_second, adapter_down, RATE_ADAPTER, DECAY_ADAPTER
    )
    moment_up, second_up, updated_up = adamw(
        grad_up * factor, up_moment, up_second, adapter_up, RATE_ADAPTER, DECAY_ADAPTER
    )
    moment_norms, second_norms, updated_norms = adamw(
        grad_norms * factor, norm_moment, norm_second, norm_params, RATE_NORMS, 0.0
    )
    return (
        loss_sum,
        token_total,
        grad_norm,
        moment_down,
        second_down,
        updated_down,
        moment_up,
        second_up,
        updated_up,
        moment_norms,
        second_norms,
        updated_norms,
    )


def solution(mesh):
    everywhere = P(None, ("seq", "enc"), None)
    columns = P(None, None, ("seq", "enc"))
    return jax.shard_map(
        shards,
        mesh=mesh,
        in_specs=(
            P("seq", "enc"),
            P("seq", "enc"),
            P("seq", "enc"),
            P("seq", None),
            P("enc", None),
            P(None, "enc", None),
            everywhere,
            everywhere,
            everywhere,
            everywhere,
            everywhere,
            everywhere,
            columns,
            everywhere,
            everywhere,
            everywhere,
            everywhere,
            columns,
            columns,
        ),
        out_specs=(
            P(),
            P(),
            P(),
            everywhere,
            everywhere,
            everywhere,
            everywhere,
            everywhere,
            everywhere,
            columns,
            columns,
            columns,
        ),
        check_vma=False,
    )
```

time: 1020 us -> 707 us (0.69)
  waiting for transfers between devices: 441 us -> 146 us
  Pallas kernels: 230 us -> 182 us
  between operations: 11.3 us -> 23.6 us
  matrix products: 26.5 us -> 38.1 us
    ppermute x160 -> x91, waiting for transfers between devices: 441 us -> 131 us  [flip(): return lax.ppermute(value, axis, [(i, i ^ mask) for i in range(count)])]
    ppermute x160 -> x91, starting transfers between devices: 120 us -> 96.9 us  [flip(): return lax.ppermute(value, axis, [(i, i ^ mask) for i in range(count)])]
    unnamed x443 -> x294, local copies, waits for them, and re-layouts: 40.4 us -> 17.9 us
    pallas_call x7 -> x3, Pallas kernels: 36.9 us -> 15 us  [assemble(): pl.pallas_call(kernel, out_shape=[jax.ShapeDtypeStruct(shape, LOW) for sh...]
    ppermute x0 -> x12, starting transfers between devices: none -> 17.3 us  [the longest x9 11.3 us: flip_both(): return lax.ppermute(value, ('seq', 'enc'), perm)]
    ppermute x0 -> x12, waiting for transfers between devices: none -> 14.2 us  [the longest x3 10.9 us: mixed_flip(): return lax.ppermute(value, ('seq', 'enc'), perm)]
    pallas_call x6 -> x9, Pallas kernels: 93.2 us -> 80.7 us  [the longest x3 51.7 us: attend_back(): pl.pallas_call(attend_back_kernel, grid=(pairs, length // rows), out_shap...]
    pallas_call x1, Pallas kernels: 44.8 us -> 34.1 us  [head(): pl.pallas_call(head_kernel, grid=(entries // tile,), out_shape=[jax.Shape...]
  transfers between devices with their start and end apart: 160 -> 106, of which waited for: 63 -> 32; matrix products, arithmetic and copies ran while one was open for 14% -> 26% of each run, Pallas kernels for 17% -> 17%
where the time goes in v2:
time: 707 us; the launch traced here: 699 us
  Pallas kernels  182 us (26%)
  waiting for transfers between devices  146 us (21%)
  starting transfers between devices  119 us (17%)
  local copies, waits for them, and re-layouts  101 us (14%)
  other arithmetic  83.8 us (12%)
  matrix products  38.1 us (5%)
  between operations  23.6 us (3%)
    ppermute x91, waiting for transfers between devices, flip(): return lax.ppermute(value, axis, [(i, i ^ mask) for i in range(count)])  131 us
    ppermute x91, starting transfers between devices, flip(): return lax.ppermute(value, axis, [(i, i ^ mask) for i in range(count)])  96.9 us
    pallas_call x3, Pallas kernels, attend_back(): pl.pallas_call(attend_back_kernel, grid=(pairs, length // rows), out_shap...  51.7 us
    gather x3, local copies, waits for them, and re-layouts, lookup(): found = jnp.take(embedding, jnp.clip(ids, 0, entries - 1), axis=0)  37.7 us
    pallas_call x1, Pallas kernels, head(): pl.pallas_call(head_kernel, grid=(entries // tile,), out_shape=[jax.Shape...  34.1 us
    pallas_call x3, Pallas kernels, attend(): pl.pallas_call(attend_kernel, grid=(pairs, length // rows), out_shape=[ja...  28.9 us
    pallas_call x2, Pallas kernels, branch(): pl.pallas_call(branch_kernel, grid=(hidden // tile,), out_shape=[jax.Shap...  26.7 us
    pallas_call x2, Pallas kernels, branch_back(): pl.pallas_call(branch_back_kernel, grid=(hidden // tile,), out_shape=[jax...  25.4 us
  transfers between devices with their start and end apart: 106, of which 32 were waited for; matrix products, arithmetic and copies ran while one was open for 26% of the time, Pallas kernels for 17%

profile of v2, /device:TPU:0, one launch (start us, length us, event | category | flops | bytes accessed | tf_op | source)
XLA Modules:
  0.0 699.2 jit_solution(5331383349367147927)
XLA Ops:
  11.4 6.2 all-gather.3
  18.3 12.8 %gather_fusion.3 = bf16[1024,1024]{1,0:T(8,128)(2,1)} fusion(bf16[6400,1024]{1,0:T(8,128)(2,1)} %e_ref.1, s32[1024]{0:T(1024)S(1)} %get-tuple-element.348), kind=kCustom, calls=%fused_computation.1.clone | custom fusion | bytes 4198400 | tf_op jit(solution)/shard_map/jit(_take)/gather | solution.py:781
  35.5 12.4 %gather_fusion.2 = bf16[1024,1024]{1,0:T(8,128)(2,1)} fusion(bf16[6400,1024]{1,0:T(8,128)(2,1)} %e_ref.1, s32[1024]{0:T(1024)S(1)} %broadcast_clamp_fusion.2), kind=kCustom, calls=%fused_computation.clone | custom fusion | bytes 4198400 | tf_op jit(solution)/shard_map/jit(_take)/gather | solution.py:781
  62.0 4.4 all-to-all-start
  81.8 2.8 collective-permute-start.11
  89.3 28.0 %collective-permute-done.10.refs_1_ = bf16[128,1536]{1,0:T(8,128)(2,1)S(1)} collective-permute-done((bf16[128,1536]{1,0:T(8,128)(2,1)S(1)}, bf16[128,1536]{1,0:T(8,128)(2,1)S(1)}, u32[]{:S(2)}, u32[]{:S(2)}) %collective-permute-start.10) | collective-permute-done | bytes 393248 | tf_op jit(solution)/shard_map/ppermute | solution.py:29
  119.1 3.9 collective-permute-done.11.refs_2_
  125.5 10.0 %collective-permute-done.12.refs_3_ = bf16[128,1536]{1,0:T(8,128)(2,1)S(1)} collective-permute-done((bf16[128,1536]{1,0:T(8,128)(2,1)S(1)}, bf16[128,1536]{1,0:T(8,128)(2,1)S(1)}, u32[]{:S(2)}, u32[]{:S(2)}) %collective-permute-start.12) | collective-permute-done | bytes 393248 | tf_op jit(solution)/shard_map/ppermute | solution.py:29
  136.2 25.2 %collective-permute-start.23 = (bf16[64,1536]{1,0:T(8,128)(2,1)}, bf16[64,1536]{1,0:T(8,128)(2,1)S(1)}, u32[]{:S(2)}, u32[]{:S(2)}) collective-permute-start(bf16[64,1536]{1,0:T(8,128)(2,1)} %get-tuple-element.55), channel_id=1, source_target_pairs={{0,8},{4,12},{8,0},{12,4},{16,24},{20,28},{24,16},{28,20},{1,9},{5... | collective-permute-start | bytes 589832 | tf_op jit(solution)/shard_map/ppermute | solution.py:29
  171.3 3.9 fusion.60
  185.2 5.2 collective-permute-done.18
  194.5 10.4 %collective-permute-done.13.refs_2_ = bf16[4,128,1536]{2,1,0:T(8,128)(2,1)} collective-permute-done((bf16[4,128,1536]{2,1,0:T(8,128)(2,1)S(1)}, bf16[4,128,1536]{2,1,0:T(8,128)(2,1)}, u32[]{:S(2)}, u32[]{:S(2)}) %collective-permute-start.13) | collective-permute-done | bytes 1572896 | tf_op jit(solution)/shard_map/ppermute | solution.py:29
  206.7 5.1 shard_map.275
  215.0 9.6 %collective-permute-done.26.refs_2_ = bf16[4,64,1536]{2,1,0:T(8,128)(2,1)S(1)} collective-permute-done((bf16[4,64,1536]{2,1,0:T(8,128)(2,1)S(1)}, bf16[4,64,1536]{2,1,0:T(8,128)(2,1)S(1)}, u32[]{:S(2)}, u32[]{:S(2)}) %collective-permute-start.26) | collective-permute-done | bytes 786464 | tf_op jit(solution)/shard_map/ppermute | solution.py:149
  227.2 4.5 fusion.34.q_ref.k_ref.v_ref
  231.7 9.9 %shard_map.276 = (bf16[1024,256]{1,0:T(8,128)(2,1)}, f32[1024,256]{1,0:T(8,128)}) custom-call(s32[1024,1]{1,0:T(8,128)} %bitcast.378, s32[1,1024]{1,0:T(1,128)} %bitcast.443, bf16[1024,768]{1,0:T(8,128)(2,1)} %fusion.34.q_ref.k_ref.v_ref, bf16[1024,768]{1,0:T(8,128)(2,1)} %fusion.34.q_ref.k_ref.v_ref, bf16[1024,768]{1,0:T(8,128)(2,1)} %fusion.34.q_ref.k_ref.v_ref), custom_call_target="tpu_custom_call" | custom-call | flops 2147483648 | bytes 2097152 | tf_op jit(solution)/shard_map/pallas_call | solution.py:376
  245.4 4.5 fusion.37.q_ref.k_ref.v_ref
  251.4 9.5 %shard_map.280 = (bf16[1024,256]{1,0:T(8,128)(2,1)}, f32[1024,256]{1,0:T(8,128)}) custom-call(s32[1024,1]{1,0:T(8,128)} %broadcast_in_dim.132.limit_ref, s32[1,1024]{1,0:T(1,128)} %bitcast.444, bf16[1024,768]{1,0:T(8,128)(2,1)} %fusion.37.q_ref.k_ref.v_ref, bf16[1024,768]{1,0:T(8,128)(2,1)} %fusion.37.q_ref.k_ref.v_ref, ...), custom_call_target="tpu_custom_call" | custom-call | flops 2147483648 | bytes 2097152 | tf_op jit(solution)/shard_map/pallas_call | solution.py:376
  266.2 5.1 shard_map.278
  282.4 4.4 collective-permute-done.42
  289.1 13.3 %shard_map.281 = (f32[256,1024]{1,0:T(8,128)}, f32[256,4096]{1,0:T(8,128)}, bf16[256,512]{1,0:T(8,128)(2,1)}, f32[256,512]{1,0:T(8,128)}) custom-call(bf16[256,1024]{1,0:T(8,128)(2,1)} %fusion.65.x_ref, bf16[32,288,1024]{2,1,0:T(8,128)(2,1)} %bitcast.344, bf16[32,288,1024]{2,1,0:T(8,128)(2,1)} %bitcast.345, bf16[32,288,1024]{2,1,0:T(8,128)(2,1)} %bitcast.346), custom_call_target="tpu_custom_call" | custom-call | flops 4831838208 | bytes 23068672 | tf_op jit(solution)/shard_map/pallas_call | solution.py:542
  307.3 12.4 %gather_fusion.4 = bf16[1024,1024]{1,0:T(8,128)(2,1)} fusion(bf16[6400,1024]{1,0:T(8,128)(2,1)} %e_ref.1, s32[1024]{0:T(1024)S(1)} %copy-done.116), kind=kCustom, calls=%fused_computation.2.clone | custom fusion | bytes 4198400 | tf_op jit(solution)/shard_map/jit(_take)/gather | solution.py:781
  322.5 3.1 collective-permute-done.44
  327.0 4.8 shard_map.279
  331.9 2.7 fusion.43.q_ref
  334.7 3.6 fusion.40.k_ref.v_ref
  338.2 9.5 %shard_map.282 = (bf16[1024,256]{1,0:T(8,128)(2,1)}, f32[1024,256]{1,0:T(8,128)}) custom-call(s32[1024,1]{1,0:T(8,128)} %broadcast_in_dim.132.limit_ref, s32[1,1024]{1,0:T(1,128)} %bitcast.445, bf16[1024,256]{1,0:T(8,128)(2,1)} %fusion.43.q_ref, bf16[1024,512]{1,0:T(8,128)(2,1)} %fusion.40.k_ref.v_ref, bf16[1024,512]{1,0:T(8,128)(2,1)} %fusion.40.k_ref.v_ref), custom_call_target="tpu_custom_call" | custom-call | flops 2147483648 | bytes 2097152 | tf_op jit(solution)/shard_map/pallas_call | solution.py:376
  353.2 2.8 collective-permute-done.47
  359.3 13.4 %shard_map.283 = (f32[256,1024]{1,0:T(8,128)}, f32[256,4096]{1,0:T(8,128)}, bf16[256,512]{1,0:T(8,128)(2,1)}, f32[256,512]{1,0:T(8,128)}) custom-call(bf16[256,1024]{1,0:T(8,128)(2,1)} %fusion.67.x_ref, bf16[32,288,1024]{2,1,0:T(8,128)(2,1)} %bitcast.350, bf16[32,288,1024]{2,1,0:T(8,128)(2,1)} %bitcast.351, bf16[32,288,1024]{2,1,0:T(8,128)(2,1)} %bitcast.352), custom_call_target="tpu_custom_call" | custom-call | flops 4831838208 | bytes 23068672 | tf_op jit(solution)/shard_map/pallas_call | solution.py:542
  379.6 12.3 %collective-permute-done.50 = bf16[256,1024]{1,0:T(8,128)(2,1)S(1)} collective-permute-done((bf16[256,1024]{1,0:T(8,128)(2,1)S(1)}, bf16[256,1024]{1,0:T(8,128)(2,1)S(1)}, u32[]{:S(2)}, u32[]{:S(2)}) %collective-permute-start.50) | collective-permute-done | bytes 524320 | tf_op jit(solution)/shard_map/ppermute | solution.py:29
  395.3 34.1 %shard_map.285 = (bf16[1024,1024]{1,0:T(8,128)(2,1)}, f32[1024,128]{1,0:T(8,128)}) custom-call(bf16[1024,1024]{1,0:T(8,128)(2,1)} %get-tuple-element.67.o_ref, bf16[6400,1024]{1,0:T(8,128)(2,1)} %e_ref.1), custom_call_target="tpu_custom_call" | custom-call | flops 26843545600 | bytes 13107200 | tf_op jit(solution)/shard_map/pallas_call | solution.py:670
  442.5 12.5 %collective-permute-done.55 = f32[256,1]{1,0:T(8,128)S(1)} collective-permute-done((f32[256,1]{1,0:T(8,128)}, f32[256,1]{1,0:T(8,128)S(1)}, u32[]{:S(2)}, u32[]{:S(2)}) %collective-permute-start.55) | collective-permute-done | bytes 1056 | tf_op jit(solution)/shard_map/ppermute | solution.py:29
  456.4 2.9 multiply_reduce_fusion.3
  461.0 12.9 %shard_map.286 = (f32[256,1024]{1,0:T(8,128)}, bf16[256,512]{1,0:T(8,128)(2,1)}) custom-call(bf16[256,1024]{1,0:T(8,128)(2,1)} %get-tuple-element.232.g_ref, bf16[256,1024]{1,0:T(8,128)(2,1)} %get-tuple-element.231.ga_ref, bf16[32,288,1024]{2,1,0:T(8,128)(2,1)} %bitcast.353, bf16[32,288,1024]{2,1,0:T(8,128)(2,1)} %bitcast.354, ...), custom_call_target="tpu_custom_call" | custom-call | flops 4831838208 | bytes 23068672 | tf_op jit(solution)/shard_map/pallas_call | solution.py:606
  482.8 3.0 copy.185
  485.8 4.1 concatenate.120
  489.9 4.8 fusion.1
  495.5 17.3 %shard_map.287 = bf16[1024,768]{1,0:T(8,128)(2,1)} custom-call(s32[1024,1]{1,0:T(8,128)} %broadcast_in_dim.132.limit_ref, s32[1,1024]{1,0:T(1,128)} %bitcast.446, bf16[1024,256]{1,0:T(8,128)(2,1)} %fusion.43.q_ref, bf16[1024,512]{1,0:T(8,128)(2,1)} %fusion.40.k_ref.v_ref, bf16[1024,512]{1,0:T(8,128)(2,1)} %fusion.40.k_ref.v_ref, ...), custom_call_target="tpu_custom_call" | custom-call | flops 5368709120 | bytes 4194304 | tf_op jit(solution)/shard_map/pallas_call | solution.py:439
  526.7 7.5 %collective-permute-done.66 = bf16[256,1024]{1,0:T(8,128)(2,1)S(1)} collective-permute-done((bf16[256,1024]{1,0:T(8,128)(2,1)S(1)}, bf16[256,1024]{1,0:T(8,128)(2,1)S(1)}, u32[]{:S(2)}, u32[]{:S(2)}) %collective-permute-start.66) | collective-permute-done | bytes 524320 | tf_op jit(solution)/shard_map/ppermute | solution.py:29
  536.3 12.5 %shard_map.288 = (f32[256,1024]{1,0:T(8,128)}, bf16[256,512]{1,0:T(8,128)(2,1)}) custom-call(bf16[256,1024]{1,0:T(8,128)(2,1)} %get-tuple-element.230.g_ref, bf16[256,1024]{1,0:T(8,128)(2,1)} %get-tuple-element.229.ga_ref, bf16[32,288,1024]{2,1,0:T(8,128)(2,1)} %bitcast.347, bf16[32,288,1024]{2,1,0:T(8,128)(2,1)} %bitcast.348, ...), custom_call_target="tpu_custom_call" | custom-call | flops 4831838208 | bytes 23068672 | tf_op jit(solution)/shard_map/pallas_call | solution.py:606
  550.3 3.0 copy.184
  553.2 4.3 concatenate.126
  581.2 6.0 collective-permute-done.68
  592.1 17.2 %shard_map.290 = bf16[1024,768]{1,0:T(8,128)(2,1)} custom-call(s32[1024,1]{1,0:T(8,128)} %bitcast.379, s32[1,1024]{1,0:T(1,128)} %bitcast.447, bf16[1024,768]{1,0:T(8,128)(2,1)} %fusion.34.q_ref.k_ref.v_ref, bf16[1024,768]{1,0:T(8,128)(2,1)} %fusion.34.q_ref.k_ref.v_ref, bf16[1024,768]{1,0:T(8,128)(2,1)} %fusion.34.q_ref.k_ref.v_ref, ...), custom_call_target="tpu_custom_call" | custom-call | flops 5368709120 | bytes 4194304 | tf_op jit(solution)/shard_map/pallas_call | solution.py:439
  617.4 3.6 fusion.154
  625.7 2.9 bitcast_add_fusion
  633.6 17.2 %shard_map.289 = bf16[1024,768]{1,0:T(8,128)(2,1)} custom-call(s32[1024,1]{1,0:T(8,128)} %broadcast_in_dim.132.limit_ref, s32[1,1024]{1,0:T(1,128)} %bitcast.448, bf16[1024,768]{1,0:T(8,128)(2,1)} %fusion.37.q_ref.k_ref.v_ref, bf16[1024,768]{1,0:T(8,128)(2,1)} %fusion.37.q_ref.k_ref.v_ref, bf16[1024,768]{1,0:T(8,128)(2,1)} %fusion.37.q_ref.k_ref.v_ref, ...), custom_call_target="tpu_custom_call" | custom-call | flops 5368709120 | bytes 4194304 | tf_op jit(solution)/shard_map/pallas_call | solution.py:439
  656.6 3.8 fusion.155
  (688 shorter events, 250.3 us)
Async XLA Ops:
  7.2 281.9 %all-gather.7.cloned.1.call-start = ((), (), s32[]{:S(2)}) async-start(), calls=%async_computation.1 | async-start | bytes 19464192 | tf_op jit(solution)/shard_map/all_gather | solution.py:473
  10.5 348.8 %all-gather.9.cloned.1.call-start = ((), (), s32[]{:S(2)}) async-start(), calls=%async_computation.2 | async-start | bytes 19464192 | tf_op jit(solution)/shard_map/all_gather | solution.py:473
  35.2 46.6 %collective-permute-start.15 = (bf16[256,1024]{1,0:T(8,128)(2,1)}, bf16[256,1024]{1,0:T(8,128)(2,1)}, u32[]{:S(2)}, u32[]{:S(2)}) collective-permute-start(bf16[256,1024]{1,0:T(8,128)(2,1)} %get-tuple-element.228), channel_id=1, source_target_pairs={{0,1},{1,0},{2,3},{3,2},{4,5},{5,4},{6,7},{7,6},{8,9},{9,8},{10,11... | collective-permute-start | bytes 1572872 | tf_op jit(solution)/shard_map/ppermute | solution.py:29
  52.1 34.6 %collective-permute-start.1 = (bf16[256,1024]{1,0:T(8,128)(2,1)}, bf16[256,1024]{1,0:T(8,128)(2,1)}, u32[]{:S(2)}, u32[]{:S(2)}) collective-permute-start(bf16[256,1024]{1,0:T(8,128)(2,1)} %get-tuple-element.226), channel_id=1, source_target_pairs={{0,1},{1,0},{2,3},{3,2},{4,5},{5,4},{6,7},{7,6},{8,9},{9,8},{10,11... | collective-permute-start | bytes 1572872 | tf_op jit(solution)/shard_map/ppermute | solution.py:29
  52.3 110.9 %collective-permute-start.14 = (bf16[256,1024]{1,0:T(8,128)(2,1)}, bf16[256,1024]{1,0:T(8,128)(2,1)S(1)}, u32[]{:S(2)}, u32[]{:S(2)}) collective-permute-start(bf16[256,1024]{1,0:T(8,128)(2,1)} %get-tuple-element.227), channel_id=1, source_target_pairs={{0,1},{1,0},{2,3},{3,2},{4,5},{5,4},{6,7},{7,6},{8,9},{9,8},{10,11... | collective-permute-start | bytes 1572872 | tf_op jit(solution)/shard_map/ppermute | solution.py:29
  52.6 110.7 %collective-permute-start = (bf16[256,1024]{1,0:T(8,128)(2,1)}, bf16[256,1024]{1,0:T(8,128)(2,1)}, u32[]{:S(2)}, u32[]{:S(2)}) collective-permute-start(bf16[256,1024]{1,0:T(8,128)(2,1)} %get-tuple-element.225), channel_id=1, source_target_pairs={{0,1},{1,0},{2,3},{3,2},{4,5},{5,4},{6,7},{7,6},{8,9},{9,8},{10,11... | collective-permute-start | bytes 1572872 | tf_op jit(solution)/shard_map/ppermute | solution.py:29
  80.5 36.8 %collective-permute-start.10 = (bf16[128,1536]{1,0:T(8,128)(2,1)S(1)}, bf16[128,1536]{1,0:T(8,128)(2,1)S(1)}, u32[]{:S(2)}, u32[]{:S(2)}) collective-permute-start(bf16[128,1536]{1,0:T(8,128)(2,1)S(1)} %get-tuple-element.240), channel_id=1, source_target_pairs={{0,8},{4,12},{8,0},{12,4},{16,24},{20,28},{24,16},{28,20},{1,9},{5... | collective-permute-start | bytes 1179656 | tf_op jit(solution)/shard_map/ppermute | solution.py:29
  81.8 41.2 %collective-permute-start.11 = (bf16[128,1536]{1,0:T(8,128)(2,1)S(1)}, bf16[128,1536]{1,0:T(8,128)(2,1)S(1)}, u32[]{:S(2)}, u32[]{:S(2)}) collective-permute-start(bf16[128,1536]{1,0:T(8,128)(2,1)S(1)} %get-tuple-element.240), channel_id=1, source_target_pairs={{0,16},{4,20},{8,24},{12,28},{16,0},{20,4},{24,8},{28,12},{1,17},{... | collective-permute-start | bytes 1179656 | tf_op jit(solution)/shard_map/ppermute | solution.py:29
  88.9 46.5 %collective-permute-start.12 = (bf16[128,1536]{1,0:T(8,128)(2,1)S(1)}, bf16[128,1536]{1,0:T(8,128)(2,1)S(1)}, u32[]{:S(2)}, u32[]{:S(2)}) collective-permute-start(bf16[128,1536]{1,0:T(8,128)(2,1)S(1)} %get-tuple-element.240), channel_id=1, source_target_pairs={{0,24},{4,28},{8,16},{12,20},{16,8},{20,12},{24,0},{28,4},{1,25},{... | collective-permute-start | bytes 1179656 | tf_op jit(solution)/shard_map/ppermute | solution.py:29
  117.3 48.2 %collective-permute-start.16 = (bf16[256,1024]{1,0:T(8,128)(2,1)}, bf16[256,1024]{1,0:T(8,128)(2,1)}, u32[]{:S(2)}, u32[]{:S(2)}) collective-permute-start(bf16[256,1024]{1,0:T(8,128)(2,1)} %fusion.55), channel_id=1, source_target_pairs={{0,2},{1,3},{2,0},{3,1},{4,6},{5,7},{6,4},{7,5},{8,10},{9,11},{10,... | collective-permute-start | bytes 1572872 | tf_op jit(solution)/shard_map/ppermute | solution.py:29
  123.0 43.7 %collective-permute-start.2 = (bf16[256,1024]{1,0:T(8,128)(2,1)}, bf16[256,1024]{1,0:T(8,128)(2,1)}, u32[]{:S(2)}, u32[]{:S(2)}) collective-permute-start(bf16[256,1024]{1,0:T(8,128)(2,1)} %fusion.57), channel_id=1, source_target_pairs={{0,2},{1,3},{2,0},{3,1},{4,6},{5,7},{6,4},{7,5},{8,10},{9,11},{10,... | collective-permute-start | bytes 1572872 | tf_op jit(solution)/shard_map/ppermute | solution.py:29
  136.2 42.0 %collective-permute-start.23 = (bf16[64,1536]{1,0:T(8,128)(2,1)}, bf16[64,1536]{1,0:T(8,128)(2,1)S(1)}, u32[]{:S(2)}, u32[]{:S(2)}) collective-permute-start(bf16[64,1536]{1,0:T(8,128)(2,1)} %get-tuple-element.55), channel_id=1, source_target_pairs={{0,8},{4,12},{8,0},{12,4},{16,24},{20,28},{24,16},{28,20},{1,9},{5... | collective-permute-start | bytes 589832 | tf_op jit(solution)/shard_map/ppermute | solution.py:29
  165.5 39.4 %collective-permute-start.13 = (bf16[4,128,1536]{2,1,0:T(8,128)(2,1)S(1)}, bf16[4,128,1536]{2,1,0:T(8,128)(2,1)}, u32[]{:S(2)}, u32[]{:S(2)}) collective-permute-start(bf16[4,128,1536]{2,1,0:T(8,128)(2,1)S(1)} %pad_maximum_fusion.3.refs_1_), channel_id=1, source_target_pairs={{0,4},{4,0},{8,12},{12,8},{16,20},{20,16},{24,28},{28,24},{1,5},{5... | collective-permute-start | bytes 4718600 | tf_op jit(solution)/shard_map/ppermute | solution.py:29
  181.9 42.7 %collective-permute-start.26 = (bf16[4,64,1536]{2,1,0:T(8,128)(2,1)S(1)}, bf16[4,64,1536]{2,1,0:T(8,128)(2,1)S(1)}, u32[]{:S(2)}, u32[]{:S(2)}) collective-permute-start(bf16[4,64,1536]{2,1,0:T(8,128)(2,1)S(1)} %pad_maximum_fusion.4.refs_1_), channel_id=1, source_target_pairs={{0,4},{1,3},{2,6},{3,1},{4,0},{5,7},{6,2},{7,5},{8,12},{9,11},{10,... | collective-permute-start | bytes 2359304 | tf_op jit(solution)/shard_map/ppermute | solution.py:149
  183.7 29.3 %collective-permute-start.7 = (bf16[256,1024]{1,0:T(8,128)(2,1)}, bf16[256,1024]{1,0:T(8,128)(2,1)}, u32[]{:S(2)}, u32[]{:S(2)}) collective-permute-start(bf16[256,1024]{1,0:T(8,128)(2,1)} %get-tuple-element.235), channel_id=1, source_target_pairs={{0,2},{1,3},{2,0},{3,1},{4,6},{5,7},{6,4},{7,5},{8,10},{9,11},{10,... | collective-permute-start | bytes 1572872 | tf_op jit(solution)/shard_map/ppermute | solution.py:29
  185.2 29.8 %collective-permute-start.17 = (bf16[256,1024]{1,0:T(8,128)(2,1)}, bf16[256,1024]{1,0:T(8,128)(2,1)}, u32[]{:S(2)}, u32[]{:S(2)}) collective-permute-start(bf16[256,1024]{1,0:T(8,128)(2,1)} %get-tuple-element.203), channel_id=1, source_target_pairs={{0,1},{1,0},{2,3},{3,2},{4,5},{5,4},{6,7},{7,6},{8,9},{9,8},{10,11... | collective-permute-start | bytes 1572872 | tf_op jit(solution)/shard_map/ppermute | solution.py:29
  190.4 34.3 %collective-permute-start.19 = (bf16[256,1024]{1,0:T(8,128)(2,1)}, bf16[256,1024]{1,0:T(8,128)(2,1)}, u32[]{:S(2)}, u32[]{:S(2)}) collective-permute-start(bf16[256,1024]{1,0:T(8,128)(2,1)} %collective-permute-done.18), channel_id=1, source_target_pairs={{0,1},{1,0},{2,3},{3,2},{4,5},{5,4},{6,7},{7,6},{8,9},{9,8},{10,11... | collective-permute-start | bytes 1572872 | tf_op jit(solution)/shard_map/ppermute | solution.py:29
  204.9 38.7 %collective-permute-start.27 = (bf16[4,64,1536]{2,1,0:T(8,128)(2,1)S(1)}, bf16[4,64,1536]{2,1,0:T(8,128)(2,1)S(1)}, u32[]{:S(2)}, u32[]{:S(2)}) collective-permute-start(bf16[4,64,1536]{2,1,0:T(8,128)(2,1)S(1)} %pad_maximum_fusion.4.refs_1_), channel_id=1, source_target_pairs={{0,2},{1,5},{2,0},{3,7},{4,6},{5,1},{6,4},{7,3},{8,10},{9,13},{10,... | collective-permute-start | bytes 2359304 | tf_op jit(solution)/shard_map/ppermute | solution.py:149
  213.0 47.8 %collective-permute-start.29 = (bf16[4,64,1536]{2,1,0:T(8,128)(2,1)S(1)}, bf16[4,64,1536]{2,1,0:T(8,128)(2,1)S(1)}, u32[]{:S(2)}, u32[]{:S(2)}) collective-permute-start(bf16[4,64,1536]{2,1,0:T(8,128)(2,1)S(1)} %pad_maximum_fusion.4.refs_1_), channel_id=1, source_target_pairs={{0,1},{1,0},{2,3},{3,2},{4,5},{5,4},{6,7},{7,6},{8,9},{9,8},{10,11... | collective-permute-start | bytes 2359304 | tf_op jit(solution)/shard_map/ppermute | solution.py:29
  215.0 26.6 %collective-permute-start.6 = (bf16[256,1024]{1,0:T(8,128)(2,1)S(1)}, bf16[256,1024]{1,0:T(8,128)(2,1)}, u32[]{:S(2)}, u32[]{:S(2)}) collective-permute-start(bf16[256,1024]{1,0:T(8,128)(2,1)S(1)} %copy-done.57), channel_id=1, source_target_pairs={{0,1},{1,0},{2,3},{3,2},{4,5},{5,4},{6,7},{7,6},{8,9},{9,8},{10,11... | collective-permute-start | bytes 1572872 | tf_op jit(solution)/shard_map/ppermute | solution.py:29
  224.7 19.4 %collective-permute-start.8 = (bf16[256,1024]{1,0:T(8,128)(2,1)}, bf16[256,1024]{1,0:T(8,128)(2,1)}, u32[]{:S(2)}, u32[]{:S(2)}) collective-permute-start(bf16[256,1024]{1,0:T(8,128)(2,1)} %collective-permute-done.7), channel_id=1, source_target_pairs={{0,1},{1,0},{2,3},{3,2},{4,5},{5,4},{6,7},{7,6},{8,9},{9,8},{10,11... | collective-permute-start | bytes 1572872 | tf_op jit(solution)/shard_map/ppermute | solution.py:29
  224.7 20.7 %collective-permute-start.28 = (bf16[4,64,1536]{2,1,0:T(8,128)(2,1)S(1)}, bf16[4,64,1536]{2,1,0:T(8,128)(2,1)S(1)}, u32[]{:S(2)}, u32[]{:S(2)}) collective-permute-start(bf16[4,64,1536]{2,1,0:T(8,128)(2,1)S(1)} %collective-permute-done.26.refs_2_), channel_id=1, source_target_pairs={{0,2},{1,5},{2,0},{3,7},{4,6},{5,1},{6,4},{7,3},{8,10},{9,13},{10,... | collective-permute-start | bytes 2359304 | tf_op jit(solution)/shard_map/ppermute | solution.py:149
  241.6 19.8 %collective-permute-start.30 = (bf16[4,64,1536]{2,1,0:T(8,128)(2,1)S(1)}, bf16[4,64,1536]{2,1,0:T(8,128)(2,1)S(1)}, u32[]{:S(2)}, u32[]{:S(2)}) collective-permute-start(bf16[4,64,1536]{2,1,0:T(8,128)(2,1)S(1)} %collective-permute-done.26.refs_2_), channel_id=1, source_target_pairs={{0,1},{1,0},{2,3},{3,2},{4,5},{5,4},{6,7},{7,6},{8,9},{9,8},{10,11... | collective-permute-start | bytes 2359304 | tf_op jit(solution)/shard_map/ppermute | solution.py:29
  243.6 20.3 %collective-permute-start.31 = (bf16[4,64,1536]{2,1,0:T(8,128)(2,1)S(1)}, bf16[4,64,1536]{2,1,0:T(8,128)(2,1)S(1)}, u32[]{:S(2)}, u32[]{:S(2)}) collective-permute-start(bf16[4,64,1536]{2,1,0:T(8,128)(2,1)S(1)} %collective-permute-done.27.refs_3_), channel_id=1, source_target_pairs={{0,1},{1,0},{2,3},{3,2},{4,5},{5,4},{6,7},{7,6},{8,9},{9,8},{10,11... | collective-permute-start | bytes 2359304 | tf_op jit(solution)/shard_map/ppermute | solution.py:29
  244.1 28.6 %collective-permute-start.20 = (bf16[256,256]{1,0:T(8,128)(2,1)}, bf16[256,256]{1,0:T(8,128)(2,1)}, u32[]{:S(2)}, u32[]{:S(2)}) collective-permute-start(bf16[256,256]{1,0:T(8,128)(2,1)} %get-tuple-element.272), channel_id=1, source_target_pairs={{0,1},{1,0},{2,3},{3,2},{4,5},{5,4},{6,7},{7,6},{8,9},{9,8},{10,11... | collective-permute-start | bytes 393224 | tf_op jit(solution)/shard_map/ppermute | solution.py:29
  263.9 42.0 %collective-permute-start.36 = (bf16[128,768]{1,0:T(8,128)(2,1)S(1)}, bf16[128,768]{1,0:T(8,128)(2,1)S(1)}, u32[]{:S(2)}, u32[]{:S(2)}) collective-permute-start(bf16[128,768]{1,0:T(8,128)(2,1)S(1)} %copy-done.46), channel_id=1, source_target_pairs={{0,8},{4,12},{8,0},{12,4},{16,24},{20,28},{24,16},{28,20},{1,9},{5... | collective-permute-start | bytes 589832 | tf_op jit(solution)/shard_map/ppermute | solution.py:29
  264.6 41.4 %collective-permute-start.37 = (bf16[128,768]{1,0:T(8,128)(2,1)S(1)}, bf16[128,768]{1,0:T(8,128)(2,1)S(1)}, u32[]{:S(2)}, u32[]{:S(2)}) collective-permute-start(bf16[128,768]{1,0:T(8,128)(2,1)S(1)} %copy-done.46), channel_id=1, source_target_pairs={{0,16},{4,20},{8,24},{12,28},{16,0},{20,4},{24,8},{28,12},{1,17},{... | collective-permute-start | bytes 589832 | tf_op jit(solution)/shard_map/ppermute | solution.py:29
  279.3 26.7 %collective-permute-start.38 = (bf16[128,768]{1,0:T(8,128)(2,1)S(1)}, bf16[128,768]{1,0:T(8,128)(2,1)S(1)}, u32[]{:S(2)}, u32[]{:S(2)}) collective-permute-start(bf16[128,768]{1,0:T(8,128)(2,1)S(1)} %copy-done.46), channel_id=1, source_target_pairs={{0,24},{4,28},{8,16},{12,20},{16,8},{20,12},{24,0},{28,4},{1,25},{... | collective-permute-start | bytes 589832 | tf_op jit(solution)/shard_map/ppermute | solution.py:29
  281.9 38.2 %collective-permute-start.34 = (bf16[256,1024]{1,0:T(8,128)(2,1)}, bf16[256,1024]{1,0:T(8,128)(2,1)}, u32[]{:S(2)}, u32[]{:S(2)}) collective-permute-start(bf16[256,1024]{1,0:T(8,128)(2,1)} %fusion.63), channel_id=1, source_target_pairs={{0,2},{1,3},{2,0},{3,1},{4,6},{5,7},{6,4},{7,5},{8,10},{9,11},{10,... | collective-permute-start | bytes 1572872 | tf_op jit(solution)/shard_map/ppermute | solution.py:29
  305.4 20.2 %collective-permute-start.44 = (bf16[256,1024]{1,0:T(8,128)(2,1)}, bf16[256,1024]{1,0:T(8,128)(2,1)}, u32[]{:S(2)}, u32[]{:S(2)}) collective-permute-start(bf16[256,1024]{1,0:T(8,128)(2,1)} %add_convert_fusion.1), channel_id=1, source_target_pairs={{0,2},{1,3},{2,0},{3,1},{4,6},{5,7},{6,4},{7,5},{8,10},{9,11},{10,... | collective-permute-start | bytes 1572872 | tf_op jit(solution)/shard_map/ppermute | solution.py:29
  306.1 20.4 %collective-permute-start.39 = (bf16[4,128,768]{2,1,0:T(8,128)(2,1)S(1)}, bf16[4,128,768]{2,1,0:T(8,128)(2,1)S(1)}, u32[]{:S(2)}, u32[]{:S(2)}) collective-permute-start(bf16[4,128,768]{2,1,0:T(8,128)(2,1)S(1)} %pad_maximum_fusion.5.refs_1_), channel_id=1, source_target_pairs={{0,4},{4,0},{8,12},{12,8},{16,20},{20,16},{24,28},{28,24},{1,5},{5... | collective-permute-start | bytes 2359304 | tf_op jit(solution)/shard_map/ppermute | solution.py:29
  326.5 24.5 %collective-permute-start.59 = (bf16[256,1024]{1,0:T(8,128)(2,1)S(1)}, bf16[256,1024]{1,0:T(8,128)(2,1)S(1)}, u32[]{:S(2)}, u32[]{:S(2)}) collective-permute-start(bf16[256,1024]{1,0:T(8,128)(2,1)S(1)} %get-tuple-element.224), channel_id=1, source_target_pairs={{0,1},{1,0},{2,3},{3,2},{4,5},{5,4},{6,7},{7,6},{8,9},{9,8},{10,11... | collective-permute-start | bytes 1572872 | tf_op jit(solution)/shard_map/ppermute | solution.py:29
  331.8 42.8 %collective-permute-start.58 = (bf16[256,1024]{1,0:T(8,128)(2,1)}, bf16[256,1024]{1,0:T(8,128)(2,1)S(1)}, u32[]{:S(2)}, u32[]{:S(2)}) collective-permute-start(bf16[256,1024]{1,0:T(8,128)(2,1)} %get-tuple-element.223), channel_id=1, source_target_pairs={{0,1},{1,0},{2,3},{3,2},{4,5},{5,4},{6,7},{7,6},{8,9},{9,8},{10,11... | collective-permute-start | bytes 1572872 | tf_op jit(solution)/shard_map/ppermute | solution.py:29
  352.0 22.6 %collective-permute-start.60 = (bf16[256,1024]{1,0:T(8,128)(2,1)}, bf16[256,1024]{1,0:T(8,128)(2,1)}, u32[]{:S(2)}, u32[]{:S(2)}) collective-permute-start(bf16[256,1024]{1,0:T(8,128)(2,1)} %fusion.53), channel_id=1, source_target_pairs={{0,2},{1,3},{2,0},{3,1},{4,6},{5,7},{6,4},{7,5},{8,10},{9,11},{10,... | collective-permute-start | bytes 1572872 | tf_op jit(solution)/shard_map/ppermute | solution.py:29
  432.6 23.8 %collective-permute-start.53 = (bf16[256,1024]{1,0:T(8,128)(2,1)}, bf16[256,1024]{1,0:T(8,128)(2,1)}, u32[]{:S(2)}, u32[]{:S(2)}) collective-permute-start(bf16[256,1024]{1,0:T(8,128)(2,1)} %get-tuple-element.221), channel_id=1, source_target_pairs={{0,1},{1,0},{2,3},{3,2},{4,5},{5,4},{6,7},{7,6},{8,9},{9,8},{10,11... | collective-permute-start | bytes 1572872 | tf_op jit(solution)/shard_map/ppermute | solution.py:29
  523.5 50.7 %collective-permute-start.70 = (f32[4,2,2,32,1024]{4,3,0,2,1:T(8,128)}, f32[4,2,2,32,1024]{4,3,0,2,1:T(8,128)}, u32[]{:S(2)}, u32[]{:S(2)}) collective-permute-start(f32[4,2,2,32,1024]{4,3,0,2,1:T(8,128)} %select_bitcast_fusion.1), channel_id=1, source_target_pairs={{0,1},{1,0},{2,3},{3,2},{4,5},{5,4},{6,7},{7,6},{8,9},{9,8},{10,11... | collective-permute-start | bytes 6291464 | tf_op jit(solution)/shard_map/ppermute | solution.py:29
  523.9 35.3 %collective-permute-start.80 = (bf16[256,1024]{1,0:T(8,128)(2,1)}, bf16[256,1024]{1,0:T(8,128)(2,1)}, u32[]{:S(2)}, u32[]{:S(2)}) collective-permute-start(bf16[256,1024]{1,0:T(8,128)(2,1)} %get-tuple-element.214), channel_id=1, source_target_pairs={{0,1},{1,0},{2,3},{3,2},{4,5},{5,4},{6,7},{7,6},{8,9},{9,8},{10,11... | collective-permute-start | bytes 1572872 | tf_op jit(solution)/shard_map/ppermute | solution.py:29
  525.0 34.2 %collective-permute-start.82 = (bf16[256,1024]{1,0:T(8,128)(2,1)}, bf16[256,1024]{1,0:T(8,128)(2,1)}, u32[]{:S(2)}, u32[]{:S(2)}) collective-permute-start(bf16[256,1024]{1,0:T(8,128)(2,1)} %fusion.46), channel_id=1, source_target_pairs={{0,2},{1,3},{2,0},{3,1},{4,6},{5,7},{6,4},{7,5},{8,10},{9,11},{10,... | collective-permute-start | bytes 1572872 | tf_op jit(solution)/shard_map/ppermute | solution.py:29
  566.1 21.1 %collective-permute-start.87 = (bf16[256,1024]{1,0:T(8,128)(2,1)S(1)}, bf16[256,1024]{1,0:T(8,128)(2,1)}, u32[]{:S(2)}, u32[]{:S(2)}) collective-permute-start(bf16[256,1024]{1,0:T(8,128)(2,1)S(1)} %get-tuple-element.233), channel_id=1, source_target_pairs={{0,2},{1,3},{2,0},{3,1},{4,6},{5,7},{6,4},{7,5},{8,10},{9,11},{10,... | collective-permute-start | bytes 1572872 | tf_op jit(solution)/shard_map/ppermute | solution.py:29
  580.1 45.5 %collective-permute-start.89 = (f32[4,2,2,32,1024]{4,3,0,2,1:T(8,128)}, f32[4,2,2,32,1024]{4,3,0,2,1:T(8,128)}, u32[]{:S(2)}, u32[]{:S(2)}) collective-permute-start(f32[4,2,2,32,1024]{4,3,0,2,1:T(8,128)} %select_bitcast_fusion), channel_id=1, source_target_pairs={{0,1},{1,0},{2,3},{3,2},{4,5},{5,4},{6,7},{7,6},{8,9},{9,8},{10,11... | collective-permute-start | bytes 6291464 | tf_op jit(solution)/shard_map/ppermute | solution.py:29
  587.2 27.0 %collective-permute-start.86 = (bf16[256,1024]{1,0:T(8,128)(2,1)S(1)}, bf16[256,1024]{1,0:T(8,128)(2,1)S(1)}, u32[]{:S(2)}, u32[]{:S(2)}) collective-permute-start(bf16[256,1024]{1,0:T(8,128)(2,1)S(1)} %get-tuple-element.233), channel_id=1, source_target_pairs={{0,1},{1,0},{2,3},{3,2},{4,5},{5,4},{6,7},{7,6},{8,9},{9,8},{10,11... | collective-permute-start | bytes 1572872 | tf_op jit(solution)/shard_map/ppermute | solution.py:29
  587.2 29.5 %collective-permute-start.88 = (bf16[256,1024]{1,0:T(8,128)(2,1)}, bf16[256,1024]{1,0:T(8,128)(2,1)}, u32[]{:S(2)}, u32[]{:S(2)}) collective-permute-start(bf16[256,1024]{1,0:T(8,128)(2,1)} %collective-permute-done.87), channel_id=1, source_target_pairs={{0,1},{1,0},{2,3},{3,2},{4,5},{5,4},{6,7},{7,6},{8,9},{9,8},{10,11... | collective-permute-start | bytes 1572872 | tf_op jit(solution)/shard_map/ppermute | solution.py:29
  589.1 21.0 %collective-permute-start.72 = (bf16[4,32,1024]{2,1,0:T(8,128)(2,1)S(1)}, bf16[4,32,1024]{2,1,0:T(8,128)(2,1)S(1)}, u32[]{:S(2)}, u32[]{:S(2)}) collective-permute-start(bf16[4,32,1024]{2,1,0:T(8,128)(2,1)S(1)} %get-tuple-element.218), channel_id=1, source_target_pairs={{0,2},{1,3},{2,0},{3,1},{4,6},{5,7},{6,4},{7,5},{8,10},{9,11},{10,... | collective-permute-start | bytes 786440 | tf_op jit(solution)/shard_map/ppermute | solution.py:123
  590.7 20.7 %collective-permute-start.73 = (bf16[4,32,1024]{2,1,0:T(8,128)(2,1)S(1)}, bf16[4,32,1024]{2,1,0:T(8,128)(2,1)S(1)}, u32[]{:S(2)}, u32[]{:S(2)}) collective-permute-start(bf16[4,32,1024]{2,1,0:T(8,128)(2,1)S(1)} %get-tuple-element.217), channel_id=1, source_target_pairs={{0,6},{1,7},{2,4},{3,5},{4,2},{5,3},{6,0},{7,1},{8,14},{9,15},{10,... | collective-permute-start | bytes 786440 | tf_op jit(solution)/shard_map/ppermute | solution.py:123
  623.8 32.8 %collective-permute-start.77 = (bf16[256,1024]{1,0:T(8,128)(2,1)S(1)}, bf16[256,1024]{1,0:T(8,128)(2,1)}, u32[]{:S(2)}, u32[]{:S(2)}) collective-permute-start(bf16[256,1024]{1,0:T(8,128)(2,1)S(1)} %get-tuple-element.234), channel_id=1, source_target_pairs={{0,1},{1,0},{2,3},{3,2},{4,5},{5,4},{6,7},{7,6},{8,9},{9,8},{10,11... | collective-permute-start | bytes 1572872 | tf_op jit(solution)/shard_map/ppermute | solution.py:29
  623.8 32.8 %collective-permute-start.79 = (bf16[256,1024]{1,0:T(8,128)(2,1)}, bf16[256,1024]{1,0:T(8,128)(2,1)}, u32[]{:S(2)}, u32[]{:S(2)}) collective-permute-start(bf16[256,1024]{1,0:T(8,128)(2,1)} %collective-permute-done.78), channel_id=1, source_target_pairs={{0,1},{1,0},{2,3},{3,2},{4,5},{5,4},{6,7},{7,6},{8,9},{9,8},{10,11... | collective-permute-start | bytes 1572872 | tf_op jit(solution)/shard_map/ppermute | solution.py:29
  630.0 20.8 %collective-permute-start.90 = (bf16[4,32,1024]{2,1,0:T(8,128)(2,1)S(1)}, bf16[4,32,1024]{2,1,0:T(8,128)(2,1)S(1)}, u32[]{:S(2)}, u32[]{:S(2)}) collective-permute-start(bf16[4,32,1024]{2,1,0:T(8,128)(2,1)S(1)} %get-tuple-element.211), channel_id=1, source_target_pairs={{0,4},{1,5},{2,6},{3,7},{4,0},{5,1},{6,2},{7,3},{8,12},{9,13},{10,... | collective-permute-start | bytes 786440 | tf_op jit(solution)/shard_map/ppermute | solution.py:123
  630.6 20.2 %collective-permute-start.91 = (bf16[4,32,1024]{2,1,0:T(8,128)(2,1)S(1)}, bf16[4,32,1024]{2,1,0:T(8,128)(2,1)S(1)}, u32[]{:S(2)}, u32[]{:S(2)}) collective-permute-start(bf16[4,32,1024]{2,1,0:T(8,128)(2,1)S(1)} %get-tuple-element.213), channel_id=1, source_target_pairs={{0,2},{1,3},{2,0},{3,1},{4,6},{5,7},{6,4},{7,5},{8,10},{9,11},{10,... | collective-permute-start | bytes 786440 | tf_op jit(solution)/shard_map/ppermute | solution.py:123
  (196 other events, 2130.2 us)
Sparse Core Ops, SparseCore 0:
  10.9 168.6 all-gather.6
  182.6 160.5 all-gather.8

commit v3 on v2

--- a/solution.py
+++ b/solution.py
@@ -44,31 +44,44 @@
     return blocks
 
 
-def gather_enc(value):
+def gather_across(value):
     found = {0: value}
     for mask in bits("enc")[1:]:
         found.update({j | mask: flip(v, "enc", mask) for j, v in list(found.items())})
-    found.update({j | 1: flip(v, "enc", 1) for j, v in list(found.items())})
-    return [found[j] for j in range(len(found))]
-
-
-def scatter_steps(blocks):
+    return [found[j] for j in sorted(found)]
+
+
+def gather_pair(blocks):
+    return [v for block in blocks for v in (block, flip(block, "enc", 1))]
+
+
+def gather_enc(value):
+    return gather_pair(gather_across(value))
+
+
+def scatter_two(blocks):
     held = dict(enumerate(blocks))
-    middle = []
     for mask in bits("enc"):
         away = [j for j in held if j & mask]
-        parts = [held[j].astype(LOW) for j in away]
-        if mask > 1:
-            middle += parts
-        sent = [flip(part, "enc", mask) for part in parts]
+        sent = [flip(held[j].astype(LOW), "enc", mask) for j in away]
         for j, part in zip(away, sent):
+            if len(held) == 2:
+                return held[j ^ mask], part
             held[j ^ mask] = held[j ^ mask].astype(F32) + part.astype(F32)
             del held[j]
-    return held[0], middle
 
 
 def scatter_enc(blocks):
-    return scatter_steps(blocks)[0]
+    own, came = scatter_two(blocks)
+    return own.astype(F32) + came.astype(F32)
+
+
+def merge_means(first, second):
+    (mean, total), (other, other_total) = first, second
+    highest = jnp.maximum(total, other_total)
+    own, far = jnp.exp(total - highest), jnp.exp(other_total - highest)
+    both = own + far
+    return (mean.astype(F32) * own + other.astype(F32) * far) / both, highest + jnp.log(both)
 
 
 def merge_enc(blocks, totals):
@@ -76,15 +89,11 @@
     for mask in bits("enc"):
         away = [j for j in held if j & mask]
         sent = [(flip(held[j][0].astype(LOW), "enc", mask), flip(held[j][1], "enc", mask)) for j in away]
-        for j, (mean, total) in zip(away, sent):
-            own_mean, own_total = held[j ^ mask]
-            highest = jnp.maximum(own_total, total)
-            first, second = jnp.exp(own_total - highest), jnp.exp(total - highest)
-            both = first + second
-            mean = (own_mean.astype(F32) * first + mean.astype(F32) * second) / both
-            held[j ^ mask] = (mean, highest + jnp.log(both))
+        for j, came in zip(away, sent):
+            if len(held) == 2:
+                return held[j ^ mask], came
+            held[j ^ mask] = merge_means(held[j ^ mask], came)
             del held[j]
-    return held[0]
 
 
 def swap_blocks(blocks):
@@ -293,10 +302,6 @@
     return centred * lax.rsqrt(variance + EPSILON) * gain + shift
 
 
-def norm_forward(values, norms, index):
-    return jax.vjp(layer_norm, values, norms[0, index], norms[1, index])
-
-
 def norm_start(values, norms, index):
     middle = jnp.mean(values, -1, keepdims=True)
     centred = values - middle
@@ -314,6 +319,84 @@
         second,
         weight - rate * (corrected / (scale_two + ADAM_EPSILON) + decay * weight),
     )
+
+
+def payload_kernel(n_line, loss_ref, count_ref, *refs):
+    zero, three, four, enc, dec = refs[n_line : n_line + 5]
+    out_ref, down_ref, up_ref = refs[-3:]
+    total = tree_sum([r[...].astype(F32) for r in refs[:n_line]])
+    squares = jnp.sum(jnp.sum(total * total, 1, keepdims=True), 0, keepdims=True)
+    rows, small = down_ref.shape[1:]
+    half = rows // 2
+    for k in range(2):
+        top, middle, end = k * rows, k * rows + half, (k + 1) * rows
+        down_ref[k, :half, :] = total[top:middle, :small]
+        down_ref[k, half:, :] = total[top:middle, small:]
+        up_ref[k] = total[middle:end]
+    rows = [zero, (enc, 0), (enc, 2), three, four, (dec, 0), (dec, 2)]
+    for at in range(2):
+        for i, row in enumerate(rows):
+            ref, first = row if isinstance(row, tuple) else (row, 0)
+            out_ref[7 * at + i : 7 * at + i + 1, :] = ref[first + at : first + at + 1, :]
+    lane = lax.broadcasted_iota(jnp.int32, (1, out_ref.shape[1]), 1)
+    scalars = jnp.where(lane == 2, squares, 0.0)
+    scalars = jnp.where(lane == 1, count_ref[...], scalars)
+    out_ref[14:15, :] = jnp.where(lane == 0, loss_ref[...], scalars)
+    out_ref[15:16, :] = jnp.zeros((1, out_ref.shape[1]), F32)
+
+
+def payload(loss, count, line, sums, small):
+    depth, width = line[0].shape
+    rows = depth // 2
+    given = [loss.reshape(1, 1), count.reshape(1, 1)] + line + sums
+    vmem = pl.BlockSpec(memory_space=pltpu.VMEM)
+    return pl.pallas_call(
+        lambda *refs: payload_kernel(len(line), *refs),
+        out_shape=[
+            jax.ShapeDtypeStruct((16, width), F32),
+            jax.ShapeDtypeStruct((2, rows, small), F32),
+            jax.ShapeDtypeStruct((2, rows // 2, width), F32),
+        ],
+        in_specs=[vmem] * len(given),
+        out_specs=[vmem] * 3,
+        cost_estimate=pl.CostEstimate(flops=MIB, bytes_accessed=MIB, transcendentals=0),
+    )(*given)
+
+
+def step_kernel(summed_ref, *refs):
+    grads, states, outs = refs[:2], refs[2:8], refs[8:]
+    norm_grads = summed_ref[0:14, :]
+    loss, count = summed_ref[14:15, 0:1], summed_ref[14:15, 1:2]
+    squares = summed_ref[14:15, 2:3] + jnp.sum(
+        jnp.sum(norm_grads * norm_grads, 1, keepdims=True), 0, keepdims=True
+    )
+    norm = jnp.sqrt(squares) / count
+    factor = jnp.minimum(1.0, CLIP_NORM / norm) / count
+    for ref, value in zip(outs, (loss, count, norm, factor)):
+        ref[...] = value
+    for i in range(2):
+        moment, second, weight = states[3 * i : 3 * i + 3]
+        for k in range(2):
+            new = adamw(
+                grads[i][k] * factor, moment[k], second[k], weight[k], RATE_ADAPTER, DECAY_ADAPTER
+            )
+            for j in range(3):
+                outs[4 + 3 * i + j][k] = new[j]
+
+
+def optimizer_step(summed, grads, states):
+    vmem = pl.BlockSpec(memory_space=pltpu.VMEM)
+    given = [summed] + grads + states
+    outs = [jax.ShapeDtypeStruct((1, 1), F32)] * 4
+    outs += [jax.ShapeDtypeStruct(states[i - i % 3].shape, F32) for i in range(6)]
+    results = pl.pallas_call(
+        step_kernel,
+        out_shape=outs,
+        in_specs=[vmem] * len(given),
+        out_specs=[vmem] * len(outs),
+        cost_estimate=pl.CostEstimate(flops=MIB, bytes_accessed=2 * MIB, transcendentals=0),
+    )(*given)
+    return [r.reshape(()) for r in results[:4]] + list(results[4:])
 
 
 def scores_of(left, right):
@@ -392,8 +475,7 @@
     )(limit, spots, query, keys, keys, *after)
 
 
-def attend_back_kernel(limit_ref, spot_ref, q_ref, k_ref, v_ref, grad_ref, total_ref, *rest):
-    out_ref, dk_sum, dv_sum = rest[-3:]
+def attend_back_step(limit_ref, spot_ref, q_ref, k_ref, v_ref, grad_ref, total_ref, out_ref, dk_sum, dv_sum):
     pair, step = pl.program_id(0), pl.program_id(1)
     pairs, steps = pl.num_programs(0), pl.num_programs(1)
     rows = q_ref.shape[0]
@@ -432,25 +514,84 @@
         )
 
 
-def attend_back(query, keys, key_at, value_at, limit, spots, grads, totals, after=()):
+def attend_back_kernel(*refs):
+    attend_back_step(*refs[:7], *refs[-3:])
+
+
+def attend_sums_kernel(*refs):
+    hat_ref, weight_ref, own_hat_ref, own_grad_ref = refs[7:11]
+    sums_ref, out_ref, dk_sum, dv_sum, hats, weights, sem = refs[-7:]
+    pair, step = pl.program_id(0), pl.program_id(1)
+    copies = [
+        pltpu.make_async_copy(hat_ref, hats, sem.at[0]),
+        pltpu.make_async_copy(weight_ref, weights, sem.at[1]),
+    ]
+
+    @pl.when((pair == 0) & (step == 0))
+    def _():
+        for copy in copies:
+            copy.start()
+
+    attend_back_step(*refs[:7], out_ref, dk_sum, dv_sum)
+
+    @pl.when((pair == pl.num_programs(0) - 1) & (step == pl.num_programs(1) - 1))
+    def _():
+        for copy in copies:
+            copy.wait()
+        weight = weights[...]
+        length = out_ref.shape[0]
+        coming = scores_of(out_ref[:PART, :], weight)
+        own = own_grad_ref[...]
+        gain = jnp.sum(own * own_hat_ref[...], 0, keepdims=True)
+        shift = jnp.sum(own, 0, keepdims=True)
+        for start in range(0, length, PART):
+            now = coming
+            if start + PART < length:
+                coming = scores_of(out_ref[start + PART : start + 2 * PART, :], weight)
+            gain += jnp.sum(now * hats[start : start + PART, :].astype(F32), 0, keepdims=True)
+            shift += jnp.sum(now, 0, keepdims=True)
+        sums_ref[0:1, :] = gain
+        sums_ref[1:2, :] = shift
+
+
+def attend_back(
+    query, keys, key_at, value_at, limit, spots, grads, totals, sum_with=None, after=()
+):
     length, width = grads.shape
     pairs = width // 128
     rows = query_rows(length)
+    hbm = pl.BlockSpec(memory_space=pl.ANY)
+    scratch = [pltpu.VMEM((length, 128), F32), pltpu.VMEM((length, 128), F32)]
+    extra = () if sum_with is None else tuple(sum_with)
+    if sum_with is None:
+        kernel = attend_back_kernel
+        out = jax.ShapeDtypeStruct((length, 3 * width), LOW)
+    else:
+        kernel = attend_sums_kernel
+        out = jax.ShapeDtypeStruct((2, extra[0].shape[1]), F32)
+        scratch = (
+            [pltpu.VMEM((length, 3 * width), LOW)]
+            + scratch
+            + [pltpu.VMEM(v.shape, LOW) for v in extra[:2]]
+            + [pltpu.SemaphoreType.DMA((2,))]
+        )
     return pl.pallas_call(
-        attend_back_kernel,
+        kernel,
         grid=(pairs, length // rows),
-        out_shape=jax.ShapeDtypeStruct((length, 3 * width), LOW),
+        out_shape=out,
         in_specs=attend_specs(rows, length, key_at, value_at, 2)
-        + [pl.BlockSpec(memory_space=pl.ANY)] * len(after),
-        out_specs=pl.BlockSpec((length, 3 * width), lambda p, j: (0, 0)),
-        scratch_shapes=[pltpu.VMEM((length, 128), F32), pltpu.VMEM((length, 128), F32)],
+        + [hbm] * len(extra[:2])
+        + [pl.BlockSpec(v.shape, lambda p, j: (0, 0)) for v in extra[2:]]
+        + [hbm] * len(after),
+        out_specs=pl.BlockSpec(out.shape, lambda p, j: (0, 0)),
+        scratch_shapes=scratch,
         compiler_params=pltpu.CompilerParams(vmem_limit_bytes=60 * MIB),
         cost_estimate=pl.CostEstimate(
             flops=20 * length * length * width,
             bytes_accessed=16 * length * width,
             transcendentals=length * length * width // HEAD_DIM,
         ),
-    )(limit, spots, query, keys, keys, grads, totals, *after)
+    )(limit, spots, query, keys, keys, grads, totals, *extra, *after)
 
 
 def gelu_both(values):
@@ -475,22 +616,6 @@
     return pack_feed(*whole)[None]
 
 
-def feed_specs(packed, tile):
-    count, depth, width = packed.shape
-    rows = depth // 9
-    per = width // tile
-    if 4 * rows <= tile:
-        reduce = pl.BlockSpec((tile // (4 * rows), 4 * rows, width), lambda j: (j, 1, 0))
-    else:
-        first = 4 * rows // tile
-        reduce = pl.BlockSpec((1, tile, width), lambda j: (0, first + j, 0))
-    return [
-        pl.BlockSpec((count, rows, tile), lambda j: (0, j // per, j % per)),
-        reduce,
-        pl.BlockSpec((count, rows, width), lambda j: (0, 8, 0)),
-    ]
-
-
 def flat(block):
     return block.reshape(block.shape[0] * block.shape[1], block.shape[2])
 
@@ -502,132 +627,339 @@
     return down.reshape(count * rows, width // 2), flat(block[:, half:])
 
 
-def branch_kernel(
-    x_ref, in_ref, out_ref, small_ref, y_ref, slope_ref, act_ref, bend_ref, total
-):
-    step = pl.program_id(0)
-
-    @pl.when(step == 0)
-    def _():
-        down, up = adapter_parts(small_ref[...])
-        act, slope = gelu_both(jnp.dot(x_ref[...], down, preferred_element_type=F32))
-        act = act.astype(LOW)
-        act_ref[...] = act
-        bend_ref[...] = slope
-        total[...] = ADAPTER_SCALE * jnp.dot(act, up, preferred_element_type=F32)
-
-    part = 256
-    x = x_ref[...]
-    expand, reduce = flat(in_ref[...]), flat(out_ref[...])
-    tile = expand.shape[1]
-    pre = jnp.dot(x, expand[:, :part], preferred_element_type=F32)
-    for start in range(0, tile, part):
-        now = pre
-        if start + part < tile:
-            pre = jnp.dot(x, expand[:, start + part : start + 2 * part], preferred_element_type=F32)
-        act, slope = gelu_both(now)
-        slope_ref[:, start : start + part] = slope
+def feed_scratch(packed):
+    count, depth, width = packed.shape
+    rows = depth // 9
+    spread = max(count // 4, 1)
+    return (
+        [pltpu.VMEM((count, rows, width), LOW) for _ in range(4)]
+        + [pltpu.VMEM((spread, width // spread, width), LOW) for _ in range(4)]
+        + [pltpu.VMEM((count, rows, width), LOW), pltpu.VMEM((width, width), LOW)]
+        + [pltpu.SemaphoreType.DMA((10,))]
+    )
+
+
+def feed_copies(packed_ref, out_ref, scratch):
+    *rooms, sem = scratch
+    count, depth, width = packed_ref.shape
+    rows = depth // 9
+    places = [packed_ref.at[:, pl.ds(q * rows, rows), :] for q in range(4)]
+    for q in range(4):
+        if count >= 4:
+            spread = count // 4
+            places.append(packed_ref.at[pl.ds(q * spread, spread), pl.ds(4 * rows, 4 * rows), :])
+        else:
+            places.append(packed_ref.at[:, pl.ds(4 * rows + q * width, width), :])
+    places += [packed_ref.at[:, pl.ds(8 * rows, rows), :], out_ref]
+    copies = [
+        pltpu.make_async_copy(place, room, sem.at[i])
+        for i, (place, room) in enumerate(zip(places, rooms))
+    ]
+    return copies[:4], copies[4:8], copies[8], copies[9]
+
+
+def norm_stats(values):
+    middle = jnp.mean(values, -1, keepdims=True)
+    centred = values - middle
+    scale = lax.rsqrt(jnp.mean(centred * centred, -1, keepdims=True) + EPSILON)
+    return centred * scale, scale
+
+
+def norm_back(grad, values, gain):
+    hat, scale = norm_stats(values)
+    scaled = grad * gain
+    inner = scaled - jnp.mean(scaled, -1, keepdims=True)
+    inner = inner - hat * jnp.mean(scaled * hat, -1, keepdims=True)
+    return (
+        inner * scale,
+        jnp.sum(grad * hat, 0, keepdims=True),
+        jnp.sum(grad, 0, keepdims=True),
+    )
+
+
+PART = 256
+
+
+def branch_kernel(first, n_parts, *refs):
+    parts, refs = refs[:n_parts], refs[n_parts:]
+    res_ref, norm_ref, packed_ref, proj_ref = refs[:4]
+    va_ref, x_ref, slope_ref, act_ref, bend_ref, vb_ref, low_ref = refs[4:11]
+    total, slopes, slope_sem = refs[11:14]
+    scratch = refs[14:]
+    expands, reduces, small, proj = feed_copies(packed_ref, proj_ref, scratch)
+    width = res_ref.shape[1]
+    for copy in [proj] + [c for pair in zip(expands, reduces) for c in pair] + [small]:
+        copy.start()
+    proj.wait()
+    context = jnp.concatenate([p[...] for p in parts], 1)
+    va = res_ref[...] + jnp.dot(context, scratch[9][...], preferred_element_type=F32)
+    va_ref[...] = va
+    hat, _ = norm_stats(va)
+    after = hat * norm_ref[first : first + 1, :] + norm_ref[7 + first : 8 + first, :]
+    x = after.astype(LOW)
+    x_ref[...] = x
+    total[...] = after
+    sends = []
+    for q in range(4):
+        expands[q].wait()
+        expand = flat(scratch[q][...])
+        pre = jnp.dot(x, expand[:, :PART], preferred_element_type=F32)
+        acts = []
+        for start in range(0, width, PART):
+            now = pre
+            if start + PART < width:
+                pre = jnp.dot(
+                    x, expand[:, start + PART : start + 2 * PART], preferred_element_type=F32
+                )
+            act, slope = gelu_both(now)
+            slopes[q, :, start : start + PART] = slope
+            acts.append(act.astype(LOW))
+        sends.append(
+            pltpu.make_async_copy(
+                slopes.at[q], slope_ref.at[:, pl.ds(q * width, width)], slope_sem.at[q]
+            )
+        )
+        sends[q].start()
+        reduces[q].wait()
         total[...] += jnp.dot(
-            act.astype(LOW), reduce[start : start + part], preferred_element_type=F32
+            jnp.concatenate(acts, 1), flat(scratch[4 + q][...]), preferred_element_type=F32
         )
-
-    @pl.when(step == pl.num_programs(0) - 1)
-    def _():
-        y_ref[...] = total[...]
-
-
-def branch(rows_low, packed, tile=1024):
-    rows, width = rows_low.shape
+    small.wait()
+    down, up = adapter_parts(scratch[8][...])
+    act, slope = gelu_both(jnp.dot(x, down, preferred_element_type=F32))
+    act = act.astype(LOW)
+    act_ref[...] = act
+    bend_ref[...] = slope
+    vb = total[...] + ADAPTER_SCALE * jnp.dot(act, up, preferred_element_type=F32)
+    vb_ref[...] = vb
+    hat, _ = norm_stats(vb)
+    low_ref[...] = (
+        hat * norm_ref[first + 1 : first + 2, :] + norm_ref[8 + first : 9 + first, :]
+    ).astype(LOW)
+    for send in sends:
+        send.wait()
+
+
+def branch(parts, residual, norms, first, packed, proj):
+    rows, width = residual.shape
     hidden, small = 4 * width, width // 2
-    return pl.pallas_call(
-        branch_kernel,
-        grid=(hidden // tile,),
+    vmem = pl.BlockSpec(memory_space=pltpu.VMEM)
+    hbm = pl.BlockSpec(memory_space=pl.ANY)
+    va, x, slope, act, bend, vb, low = pl.pallas_call(
+        lambda *refs: branch_kernel(first, len(parts), *refs),
         out_shape=[
             jax.ShapeDtypeStruct((rows, width), F32),
+            jax.ShapeDtypeStruct((rows, width), LOW),
             jax.ShapeDtypeStruct((rows, hidden), F32),
             jax.ShapeDtypeStruct((rows, small), LOW),
             jax.ShapeDtypeStruct((rows, small), F32),
+            jax.ShapeDtypeStruct((rows, width), F32),
+            jax.ShapeDtypeStruct((rows, width), LOW),
         ],
-        in_specs=[pl.BlockSpec((rows, width), lambda j: (0, 0))] + feed_specs(packed, tile),
-        out_specs=[
-            pl.BlockSpec((rows, width), lambda j: (0, 0)),
-            pl.BlockSpec((rows, tile), lambda j: (0, j)),
-            pl.BlockSpec((rows, small), lambda j: (0, 0)),
-            pl.BlockSpec((rows, small), lambda j: (0, 0)),
-        ],
-        scratch_shapes=[pltpu.VMEM((rows, width), F32)],
+        in_specs=[vmem] * (len(parts) + 2) + [hbm, hbm],
+        out_specs=[vmem, vmem, hbm, vmem, vmem, vmem, vmem],
+        scratch_shapes=[
+            pltpu.VMEM((rows, width), F32),
+            pltpu.VMEM((4, rows, width), F32),
+            pltpu.SemaphoreType.DMA((4,)),
+        ]
+        + feed_scratch(packed),
         compiler_params=pltpu.CompilerParams(vmem_limit_bytes=56 * MIB),
         cost_estimate=pl.CostEstimate(
-            flops=4 * rows * width * (hidden + small),
+            flops=4 * rows * width * (hidden + small) + 2 * rows * width * width,
             bytes_accessed=4 * width * (hidden + small) + 4 * rows * hidden,
             transcendentals=2 * rows * hidden,
         ),
-    )(rows_low, packed, packed, packed)
-
-
-def branch_back_kernel(
-    g_ref, ga_ref, in_ref, out_ref, small_ref, slope_ref, bend_ref, dx_ref, dpre_ref, total
-):
-    step = pl.program_id(0)
-
-    @pl.when(step == 0)
-    def _():
-        down, up = adapter_parts(small_ref[...])
-        grad = dense_back(ga_ref[...], up)
-        pre = (grad * bend_ref[...]).astype(LOW)
-        dpre_ref[...] = pre
-        total[...] = dense_back(pre, down)
-
-    part = 256
-    g = g_ref[...]
-    expand, reduce = flat(in_ref[...]), flat(out_ref[...])
-    tile = expand.shape[1]
-    grad = dense_back(g, reduce[:part])
-    for start in range(0, tile, part):
-        now = grad
-        if start + part < tile:
-            grad = dense_back(g, reduce[start + part : start + 2 * part])
-        pre = (now * slope_ref[:, start : start + part]).astype(LOW)
-        total[...] += dense_back(pre, expand[:, start : start + part])
-
-    @pl.when(step == pl.num_programs(0) - 1)
-    def _():
-        dx_ref[...] = total[...]
-
-
-def branch_back(grad_out, kept, packed, tile=1024):
-    rows_low, slope, act, bend = kept
-    rows, width = rows_low.shape
+    )(*parts, residual, norms, packed, proj)
+    return low, (va, x, slope, act, bend, vb)
+
+
+def branch_back_kernel(first, n_parts, *refs):
+    n_given, refs = (refs[0], refs[1:])
+    given, refs = refs[:n_given], refs[n_given:]
+    vb_ref, va_ref, norm_ref, bend_ref, slope_ref, packed_ref, proj_ref = refs[:7]
+    dva_ref, sums_ref, dpre_ref, ga_ref = refs[7:11]
+    spread_refs, refs = refs[11 : 11 + n_parts], refs[11 + n_parts :]
+    total, slopes, slope_sem = refs[:3]
+    scratch = refs[3:]
+    expands, reduces, small, proj = feed_copies(packed_ref, proj_ref, scratch)
+    width = va_ref.shape[1]
+    gets = [
+        pltpu.make_async_copy(
+            slope_ref.at[:, pl.ds(q * width, width)], slopes.at[q], slope_sem.at[q]
+        )
+        for q in range(4)
+    ]
+    for copy in [small] + [c for three in zip(reduces, gets, expands) for c in three] + [proj]:
+        copy.start()
+    if n_given == 2:
+        grad = given[0][...].astype(F32) + given[1][...].astype(F32)
+    else:
+        mean, total_own, other, total_other, label, valid = [r[...] for r in given]
+        grad = merge_means((mean, total_own), (other, total_other))[0]
+        grad = (grad - label.astype(F32)) * valid
+    grad_out, gain, shift = norm_back(grad, vb_ref[...], norm_ref[first + 1 : first + 2, :])
+    sums_ref[2:3, :] = gain
+    sums_ref[3:4, :] = shift
+    g = grad_out.astype(LOW)
+    ga = (ADAPTER_SCALE * grad_out).astype(LOW)
+    ga_ref[...] = ga
+    small.wait()
+    down, up = adapter_parts(scratch[8][...])
+    pre = (dense_back(ga, up) * bend_ref[...]).astype(LOW)
+    dpre_ref[...] = pre
+    total[...] = grad_out + dense_back(pre, down)
+    for q in range(4):
+        reduces[q].wait()
+        reduce = flat(scratch[4 + q][...])
+        gets[q].wait()
+        grad = dense_back(g, reduce[:PART])
+        pres = []
+        for start in range(0, width, PART):
+            now = grad
+            if start + PART < width:
+                grad = dense_back(g, reduce[start + PART : start + 2 * PART])
+            pres.append((now * slopes[q, :, start : start + PART]).astype(LOW))
+        expands[q].wait()
+        total[...] += dense_back(jnp.concatenate(pres, 1), flat(scratch[q][...]))
+    dva, gain, shift = norm_back(total[...], va_ref[...], norm_ref[first : first + 1, :])
+    sums_ref[0:1, :] = gain
+    sums_ref[1:2, :] = shift
+    dva_ref[...] = dva
+    proj.wait()
+    spread = dense_back(dva.astype(LOW), scratch[9][...]).astype(LOW)
+    share = width // n_parts
+    for j in range(n_parts):
+        spread_refs[j][...] = spread[:, j * share : (j + 1) * share]
+
+
+def branch_back(given, kept, norms, first, packed, proj, n_parts):
+    va, x, slope, act, bend, vb = kept
+    rows, width = va.shape
     hidden, small = 4 * width, width // 2
-    grad_low = grad_out.astype(LOW)
-    grad_adapter = (ADAPTER_SCALE * grad_out).astype(LOW)
-    whole = pl.BlockSpec((rows, width), lambda j: (0, 0))
-    narrow = pl.BlockSpec((rows, small), lambda j: (0, 0))
-    grad_rows, grad_pre = pl.pallas_call(
-        branch_back_kernel,
-        grid=(hidden // tile,),
+    vmem = pl.BlockSpec(memory_space=pltpu.VMEM)
+    hbm = pl.BlockSpec(memory_space=pl.ANY)
+    dva, sums, dpre, ga, *spread = pl.pallas_call(
+        lambda *refs: branch_back_kernel(first, n_parts, len(given), *refs),
         out_shape=[
             jax.ShapeDtypeStruct((rows, width), F32),
+            jax.ShapeDtypeStruct((4, width), F32),
             jax.ShapeDtypeStruct((rows, small), LOW),
-        ],
-        in_specs=[whole, whole]
-        + feed_specs(packed, tile)
-        + [pl.BlockSpec((rows, tile), lambda j: (0, j)), narrow],
-        out_specs=[whole, narrow],
-        scratch_shapes=[pltpu.VMEM((rows, width), F32)],
+            jax.ShapeDtypeStruct((rows, width), LOW),
+        ]
+        + [jax.ShapeDtypeStruct((rows, width // n_parts), LOW)] * n_parts,
+        in_specs=[vmem] * (4 + len(given)) + [hbm] * 3,
+        out_specs=[vmem] * (4 + n_parts),
+        scratch_shapes=[
+            pltpu.VMEM((rows, width), F32),
+            pltpu.VMEM((4, rows, width), F32),
+            pltpu.SemaphoreType.DMA((4,)),
+        ]
+        + feed_scratch(packed),
         compiler_params=pltpu.CompilerParams(vmem_limit_bytes=56 * MIB),
         cost_estimate=pl.CostEstimate(
-            flops=4 * rows * width * (hidden + small),
+            flops=4 * rows * width * (hidden + small) + 2 * rows * width * width,
             bytes_accessed=4 * width * (hidden + small) + 4 * rows * hidden,
             transcendentals=0,
         ),
-    )(grad_low, grad_adapter, packed, packed, packed, slope, bend)
-    return grad_rows, inner_rows(rows_low, grad_pre), inner_rows(act, grad_adapter)
-
-
-def head_kernel(o_ref, e_ref, g_ref, lse_ref, acc, peak, mass):
+    )(*given, vb, va, norms, bend, slope, packed, proj)
+    return dva, spread, sums, (x, dpre, act, ga)
+
+
+def middle_back_kernel(first, n_parts, *refs):
+    res_ref, own_ref, far_ref, va_ref, norm_ref, proj_ref = refs[:6]
+    dva_ref, sums_ref = refs[6:8]
+    grad = res_ref[...] + own_ref[...].astype(F32) + far_ref[...].astype(F32)
+    dva, gain, shift = norm_back(grad, va_ref[...], norm_ref[first : first + 1, :])
+    dva_ref[...] = dva
+    sums_ref[0:1, :] = gain
+    sums_ref[1:2, :] = shift
+    spread = dense_back(dva.astype(LOW), proj_ref[...]).astype(LOW)
+    share = spread.shape[1] // n_parts
+    for j in range(n_parts):
+        refs[8 + j][...] = spread[:, j * share : (j + 1) * share]
+
+
+def middle_back(residual, own, far, va, norms, first, proj, n_parts):
+    rows, width = va.shape
+    vmem = pl.BlockSpec(memory_space=pltpu.VMEM)
+    dva, sums, *spread = pl.pallas_call(
+        lambda *refs: middle_back_kernel(first, n_parts, *refs),
+        out_shape=[
+            jax.ShapeDtypeStruct((rows, width), F32),
+            jax.ShapeDtypeStruct((2, width), F32),
+        ]
+        + [jax.ShapeDtypeStruct((rows, width // n_parts), LOW)] * n_parts,
+        in_specs=[vmem] * 6,
+        out_specs=[vmem] * (2 + n_parts),
+        compiler_params=pltpu.CompilerParams(vmem_limit_bytes=32 * MIB),
+        cost_estimate=pl.CostEstimate(
+            flops=2 * rows * width * width, bytes_accessed=8 * MIB, transcendentals=0
+        ),
+    )(residual, own, far, va, norms, proj)
+    return dva, spread, sums
+
+
+def adapter_grad_kernel(core_ref, *refs):
+    keep_ref, send_ref, down, up = refs[-4:]
+    core = core_ref[0]
+    pairs, depth, width = keep_ref.shape
+    rows = depth // 2
+    half, small = rows // 2, width // 2
+    for k in range(2):
+        x_ref, dpre_ref, act_ref, ga_ref = refs[4 * k : 4 * k + 4]
+        down[...] = inner_rows(x_ref[...], dpre_ref[...])
+        up[...] = inner_rows(act_ref[...], ga_ref[...])
+        top, middle, end = k * rows, k * rows + half, (k + 1) * rows
+        for ref, side in ((keep_ref, core), (send_ref, 1 - core)):
+            for pair in range(pairs):
+                device = 2 * pair + side
+                at = pl.multiple_of(device * rows, rows)
+                ref[pair, top:middle, :small] = down[pl.ds(at, half), :].astype(ref.dtype)
+                ref[pair, top:middle, small:] = down[pl.ds(at + half, half), :].astype(ref.dtype)
+                ref[pair, middle:end, :] = up[
+                    pl.ds(pl.multiple_of(device * half, half), half), :
+                ].astype(ref.dtype)
+
+
+def adapter_grads(given, core):
+    width, small = given[0][0].shape[1], given[0][1].shape[1]
+    n_all = lax.axis_size("seq") * lax.axis_size("enc")
+    rows = width // n_all
+    if rows % 16:
+        layers = []
+        for x, dpre, act, ga in given:
+            down, up = inner_rows(x, dpre), inner_rows(act, ga)
+            folded = down.reshape(n_all, 2, rows // 2, small).transpose(0, 2, 1, 3)
+            layers += [folded.reshape(n_all, rows // 2, width), up.reshape(n_all, rows // 2, width)]
+        both = jnp.concatenate(layers, 1).reshape(n_all // 2, 2, 2 * rows, width)
+        first = core == 0
+        keep, send = jnp.where(first, both[:, 0], both[:, 1]), jnp.where(first, both[:, 1], both[:, 0])
+        return keep, send.astype(LOW)
+    shape = (n_all // 2, 2 * rows, width)
+    vmem = pl.BlockSpec(memory_space=pltpu.VMEM)
+    return pl.pallas_call(
+        adapter_grad_kernel,
+        out_shape=[jax.ShapeDtypeStruct(shape, F32), jax.ShapeDtypeStruct(shape, LOW)],
+        in_specs=[pl.BlockSpec(memory_space=pltpu.SMEM)] + [vmem] * 8,
+        out_specs=[vmem] * 2,
+        scratch_shapes=[pltpu.VMEM((width, small), F32), pltpu.VMEM((small, width), F32)],
+        compiler_params=pltpu.CompilerParams(vmem_limit_bytes=40 * MIB),
+        cost_estimate=pl.CostEstimate(
+            flops=8 * given[0][0].shape[0] * width * small,
+            bytes_accessed=16 * MIB,
+            transcendentals=0,
+        ),
+    )(core.reshape(1).astype(jnp.int32), *given[0], *given[1])
+
+
+def head_kernel(n_blocks, *refs):
+    o_refs, e_ref = refs[:n_blocks], refs[n_blocks]
+    g_refs, lse_refs = refs[n_blocks + 1 : 2 * n_blocks + 1], refs[2 * n_blocks + 1 : -3]
+    acc, peak, mass = refs[-3:]
     step = pl.program_id(0)
-    part = 512
+    rows = o_refs[0].shape[0]
+    part = 2 * rows
 
     @pl.when(step == 0)
     def _():
@@ -636,16 +968,20 @@
         mass[...] = jnp.zeros_like(mass)
 
     table = e_ref[...]
-    starts = list(range(0, o_ref.shape[0], part))
-    spans = [pl.ds(start, part) for start in starts]
+    spans = [pl.ds(start, part) for start in range(0, n_blocks * rows, part)]
+
+    def logits_of(h):
+        both = jnp.concatenate([o_refs[2 * h][...], o_refs[2 * h + 1][...]], 0)
+        return scores_of(both, table)
+
     before = [peak[at, :1] for at in spans]
     held = [mass[at, :] for at in spans]
-    coming = scores_of(o_ref[spans[0], :], table)
+    coming = logits_of(0)
     highest, summed = [], []
     for h, at in enumerate(spans):
         logits = coming
         if h + 1 < len(spans):
-            coming = scores_of(o_ref[spans[h + 1], :], table)
+            coming = logits_of(h + 1)
         highest.append(jnp.maximum(before[h], jnp.max(logits, -1, keepdims=True)))
         exponent = jnp.exp(logits - highest[h])
         fade = jnp.exp(before[h] - highest[h])
@@ -659,72 +995,60 @@
 
     @pl.when(step == pl.num_programs(0) - 1)
     def _():
-        g_ref[...] = (acc[...] / mass[:, :1]).astype(LOW)
-        lse_ref[...] = peak[...] + jnp.log(mass[...])
-
-
-def head(rows_low, table):
-    rows, width = rows_low.shape
+        for j in range(n_blocks):
+            at = pl.ds(j * rows, rows)
+            g_refs[j][...] = (acc[at, :] / mass[at, :1]).astype(LOW)
+            lse_refs[j][...] = peak[at, :1] + jnp.log(mass[at, :1])
+
+
+def head(blocks, table):
+    rows, width = blocks[0].shape
+    count = len(blocks)
     entries = table.shape[0]
     tile = next(t for t in (1280, 1024, 640, 512, 256, 128) if entries % t == 0)
-    return pl.pallas_call(
-        head_kernel,
+    block = pl.BlockSpec((rows, width), lambda j: (0, 0))
+    results = pl.pallas_call(
+        lambda *refs: head_kernel(count, *refs),
         grid=(entries // tile,),
-        out_shape=[
-            jax.ShapeDtypeStruct((rows, width), LOW),
-            jax.ShapeDtypeStruct((rows, 128), F32),
+        out_shape=[jax.ShapeDtypeStruct((rows, width), LOW)] * count
+        + [jax.ShapeDtypeStruct((rows, 1), F32)] * count,
+        in_specs=[block] * count + [pl.BlockSpec((tile, width), lambda j: (j, 0))],
+        out_specs=[block] * count + [pl.BlockSpec((rows, 1), lambda j: (0, 0))] * count,
+        scratch_shapes=[
+            pltpu.VMEM((count * rows, width), F32),
+            pltpu.VMEM((count * rows, 128), F32),
+            pltpu.VMEM((count * rows, 128), F32),
         ],
-        in_specs=[
-            pl.BlockSpec((rows, width), lambda j: (0, 0)),
-            pl.BlockSpec((tile, width), lambda j: (j, 0)),
-        ],
-        out_specs=[
-            pl.BlockSpec((rows, width), lambda j: (0, 0)),
-            pl.BlockSpec((rows, 128), lambda j: (0, 0)),
-        ],
-        scratch_shapes=[
-            pltpu.VMEM((rows, width), F32),
-            pltpu.VMEM((rows, 128), F32),
-            pltpu.VMEM((rows, 128), F32),
-        ],
-        compiler_params=pltpu.CompilerParams(vmem_limit_bytes=56 * MIB),
+        compiler_params=pltpu.CompilerParams(vmem_limit_bytes=60 * MIB),
         cost_estimate=pl.CostEstimate(
-            flops=4 * rows * width * entries,
+            flops=4 * count * rows * width * entries,
             bytes_accessed=2 * width * entries,
-            transcendentals=rows * entries,
+            transcendentals=count * rows * entries,
         ),
-    )(rows_low, table)
-
-
-def reduce_adapters(grad_down, grad_up, seq, enc):
+    )(*blocks, table)
+    return list(results[:count]), list(results[count:])
+
+
+def adapters_plane(held, seq, enc):
     n_seq, n_enc = lax.axis_size("seq"), lax.axis_size("enc")
     near = n_seq // 4
-    width, small = grad_down.shape
-    rows = width // (n_seq * n_enc)
-    folded = grad_down.reshape(-1, 2, rows // 2, small).transpose(0, 2, 1, 3)
-    folded = folded.reshape(-1, rows // 2, 2 * small)
-    both = jnp.concatenate([folded, grad_up.reshape(-1, rows // 2, width)], 1)
-    both = both.reshape(4, near, n_enc // 2, 2, rows, width)
-    first = (enc & 1) == 0
-    low, high = both[:, :, :, 0], both[:, :, :, 1]
-    held = jnp.where(first, low, high) + flip(jnp.where(first, high, low), "enc", 1)
+    rows, width = held.shape[1:]
+    held = held.reshape(4, near, n_enc // 2, rows, width)
 
     def block(s_off, e_off):
         start = (0, (seq & (near - 1)) ^ s_off, (enc >> 1) ^ (e_off >> 1), 0, 0)
         return lax.dynamic_slice(held, start, (4, 1, 1, rows, width))[:, 0, 0]
 
-    parts = [block(0, 0)] + [
-        flip_both(block(s, e).astype(LOW), s, e).astype(F32) for s, e in plane_offsets()[1:]
+    return [block(0, 0)] + [flip_both(block(s, e).astype(LOW), s, e) for s, e in plane_offsets()[1:]]
+
+
+def adapters_line(parts, seq):
+    held = tree_sum([p.astype(F32) for p in parts])
+    slow = seq // (lax.axis_size("seq") // 4)
+    parts = [lax.dynamic_index_in_dim(held, slow ^ k, 0, keepdims=False) for k in range(4)]
+    return parts[:1] + [
+        flip(p.astype(LOW), "seq", o) for p, o in zip(parts[1:], line_offsets()[1:])
     ]
-    held = tree_sum(parts)
-    slow = seq // near
-    parts = [lax.dynamic_index_in_dim(held, slow ^ k, 0, keepdims=False) for k in range(4)]
-    held = tree_sum(
-        parts[:1]
-        + [flip(p.astype(LOW), "seq", o).astype(F32) for p, o in zip(parts[1:], line_offsets()[1:])]
-    )
-    down = held[: rows // 2].reshape(rows // 2, 2, small).transpose(1, 0, 2)
-    return down.reshape(rows, small), held[rows // 2 :]
 
 
 def sum_everywhere(values):
@@ -784,22 +1108,14 @@
     def rows_of(found):
         return scatter_enc([found[j] for j in range(n_enc)])
 
-    def finish_attention(context, k):
-        parts = swap_blocks([context[j * own_rows : (j + 1) * own_rows] for j in range(n_enc)])
-        return dense(jnp.concatenate(parts, 1), attend_out[k])
-
-    def begin_attention_back(grad, k):
-        spread = dense_back(grad.astype(LOW), attend_out[k]).astype(LOW)
-        parts = swap_blocks([spread[:, j * share : (j + 1) * share] for j in range(n_enc)])
-        return jnp.concatenate(parts, 0)
-
-    def scatter_rows(partial):
-        return scatter_enc([partial[j * own_rows : (j + 1) * own_rows] for j in range(n_enc)])
-
-    def start_grads(grads, k, grad_res, hat, hats):
-        partial = dense_back(grads, attend_in[k])
-        gain = jnp.sum(partial * hats.astype(F32), 0) + jnp.sum(grad_res * hat, 0)
-        return gain, jnp.sum(partial, 0) + jnp.sum(grad_res, 0)
+    def own_parts(context):
+        return swap_blocks([context[j * own_rows : (j + 1) * own_rows] for j in range(n_enc)])
+
+    def all_heads(spread):
+        return jnp.concatenate(swap_blocks(spread), 0)
+
+    def row_blocks(partial):
+        return [partial[j * own_rows : (j + 1) * own_rows] for j in range(n_enc)]
 
     down_low, up_low = adapter_down.astype(LOW), adapter_up.astype(LOW)
     feeds = [gather_feed(feed_in[k], feed_out[k], down_low[k], up_low[k]) for k in range(2)]
@@ -830,7 +1146,7 @@
     slow = slow_flips(strip)
     for mask in bits("seq"):
         gains = jnp.concatenate([gains, flip(gains, "seq", mask)], 0)
-    found = [lookup(ids[0]), lookup(ids[1])]
+    found = [lookup(ids[0]), lookup(ids[1]), lookup(ids[2])]
     pair_out, *slow = gate([pair_out] + slow)
     order_seq, order_enc = jnp.arange(n_seq) ^ seq, jnp.arange(n_enc) ^ enc
     gains = jnp.take(jnp.take(gains, order_seq, axis=0), order_enc, axis=1)
@@ -840,7 +1156,6 @@
     strip_offsets, strips = near_flips(jnp.stack([strip] + slow))
     source_rows, target_rows = rows_of(found[0]), rows_of(found[1])
     slow = slow_flips(pair_out)
-    found = lookup(ids[2])
     late, *slow = gate([late] + slow)
 
     in_enc, in_dec = assemble_strips(strip_offsets, strips, 2, seq)
@@ -851,12 +1166,13 @@
     stacked = jnp.stack([pair_out] + slow)
     singles = plane_start(stacked)
 
+    triple_encoder = dense(encoder_all, in_enc).astype(LOW)
+    enc_args = (triple_encoder, triple_encoder, in_strip, 2 * in_strip, source_limit, spots)
+    context_enc, total_encoder = attend(*enc_args)
+    context_enc, *singles = gate([context_enc] + singles)
     own, other, mine = plane_finish(stacked, singles, core)
     partners = [flip(v, "enc", 1) for v in mine]
     slow = slow_flips(late)
-    triple_encoder = dense(encoder_all, in_enc).astype(LOW)
-    enc_args = (triple_encoder, triple_encoder, in_strip, 2 * in_strip, source_limit, spots)
-    context_enc, total_encoder = attend(*enc_args)
     triple_decoder = dense(decoder_all, in_dec).astype(LOW)
     dec_args = (triple_decoder, triple_decoder, in_strip, 2 * in_strip, causal_limit, spots)
     context_dec, total_decoder = attend(*dec_args)
@@ -873,110 +1189,117 @@
         own, other, mine, partners, out_layout, [(width, width)] * 3, seq, enc
     )
     late_offsets, strips = near_flips(jnp.stack([late] + slow))
-    after_self, pull_one = norm_forward(encoder_in + finish_attention(context_enc, 0), norms, 1)
-    after_causal, pull_four = norm_forward(decoder_in + finish_attention(context_dec, 1), norms, 4)
-    label_rows = rows_of(found)
-
+    attended = dense(jnp.concatenate(own_parts(context_dec), 1), attend_out[1])
+    causal_in = decoder_in + attended
+    after_causal = norm_start(causal_in, norms, 4)[0]
     in_cross = assemble_strips(late_offsets, strips, 1, seq)[0]
     attend_in = [in_enc, in_dec, in_cross]
     causal_all = gather_rows(after_causal.astype(LOW))
-    after_self_low = after_self.astype(LOW)
-    branched, *kept_enc = branch(after_self_low, feeds[0])
-    encoded, pull_two = norm_forward(after_self + branched, norms, 2)
-    encoded_low = encoded.astype(LOW)
+    norm_rows = norms.reshape(14, width)
+    encoded_low, kept_enc = branch(
+        own_parts(context_enc), encoder_in, norm_rows, 1, feeds[0], attend_out[0]
+    )
     query_cross = dense(causal_all, in_cross[:, :share]).astype(LOW)
 
-    encoded_all = gather_rows(encoded_low)
+    encoded_all, found[2] = gate([gather_rows(encoded_low), found[2]])
+    label_rows, label_came = scatter_two([found[2][j] for j in range(n_enc)])
     pairs_cross = dense(encoded_all, in_cross[:, share:]).astype(LOW)
     cross_args = (query_cross, pairs_cross, 0, in_strip, source_limit, spots)
     context, total_cross = attend(*cross_args)
-    after_cross, pull_five = norm_forward(after_causal + finish_attention(context, 2), norms, 5)
-    after_cross_low = after_cross.astype(LOW)
-    branched, *kept_dec = branch(after_cross_low, feeds[1])
-    decoded, pull_six = norm_forward(after_cross + branched, norms, 6)
-    decoded_low = decoded.astype(LOW)
-
-    decoded_all, encoder_hat, decoder_hat = gate(
-        [gather_rows(decoded_low), encoder_hat, decoder_hat]
+    decoded_low, kept_dec = branch(
+        own_parts(context), after_causal, norm_rows, 5, feeds[1], attend_out[2]
+    )
+
+    decoded_low, label_came = gate([decoded_low, label_came])
+
+    *decoded_all, encoder_low, decoder_low = gate(
+        gather_enc(decoded_low) + [encoder_hat.astype(LOW), decoder_hat.astype(LOW)]
     )
     pulled, totals = head(decoded_all, embedding)
-    encoder_hats = gather_rows(encoder_hat.astype(LOW))
-    decoder_hats = gather_rows(decoder_hat.astype(LOW))
-    parts = [slice(j * own_rows, (j + 1) * own_rows) for j in range(n_enc)]
-    pulled, log_total = merge_enc([pulled[p] for p in parts], [totals[p, :1] for p in parts])
+    hats = gather_across(encoder_low) + gather_across(decoder_low)
+    results = gate(pulled + totals + hats)
+    pulled, totals, hats = results[:n_enc], results[n_enc : 2 * n_enc], results[2 * n_enc :]
+    label_rows = (label_rows.astype(F32) + label_came.astype(F32)).astype(LOW)
     row_spots = enc * own_rows + jnp.arange(own_rows)
     valid = (row_spots < target_length).astype(F32)[:, None]
-    picked = jnp.sum(decoded_low.astype(F32) * label_rows, -1, keepdims=True)
+    picked = jnp.sum(decoded_low.astype(F32) * label_rows.astype(F32), -1, keepdims=True)
+    own_mean, far_mean = merge_enc(pulled, totals)
+    half_hats = len(hats) // 2
+    hats = gather_pair(hats[:half_hats]) + gather_pair(hats[half_hats:])
+    far, *hats = gate([far_mean[0]] + hats)
+    encoder_hats, decoder_hats = jnp.concatenate(hats[:n_enc], 0), jnp.concatenate(hats[n_enc:], 0)
+    highest = jnp.maximum(own_mean[1], far_mean[1])
+    log_total = highest + jnp.log(
+        jnp.exp(own_mean[1] - highest) + jnp.exp(far_mean[1] - highest)
+    )
     loss_own = jnp.sum((log_total - picked) * valid)
-    grad_decoded = (pulled - label_rows) * valid
-
-    grad_res, gain_six, shift_six = pull_six(grad_decoded)
-    grad_rows, down_dec, up_dec = branch_back(
-        grad_res, [after_cross_low] + kept_dec, feeds[1]
-    )
-    grad_res, gain_five, shift_five = pull_five(grad_res + grad_rows)
-    grads = attend_back(*cross_args, begin_attention_back(grad_res, 2), total_cross)
-    grad_encoded = scatter_rows(dense_back(grads[:, share:], attend_in[2][:, share:]))
-    grad_causal = grad_res + scatter_rows(dense_back(grads[:, :share], attend_in[2][:, :share]))
-    grad_res, gain_four, shift_four = pull_four(grad_causal)
-    grads = attend_back(*dec_args, begin_attention_back(grad_res, 1), total_decoder)
-    gain_three, shift_three = start_grads(grads, 1, grad_res, decoder_hat, decoder_hats)
-    grad_res, gain_two, shift_two = pull_two(grad_encoded)
-    grad_rows, down_enc, up_enc = branch_back(
-        grad_res, [after_self_low] + kept_enc, feeds[0]
-    )
-    grad_res, gain_one, shift_one = pull_one(grad_res + grad_rows)
-    owned_dec = reduce_adapters(down_dec, up_dec, seq, enc)
-    owned_enc = reduce_adapters(down_enc, up_enc, seq, enc)
-    grads = attend_back(*enc_args, begin_attention_back(grad_res, 0), total_encoder, after=owned_dec)
-    gain_zero, shift_zero = start_grads(grads, 0, grad_res, encoder_hat, encoder_hats)
-
-    grad_down = jnp.stack([owned_enc[0], owned_dec[0]])
-    grad_up = jnp.stack([owned_enc[1], owned_dec[1]])
+
+    grad_res, spread, sums_dec, given_dec = branch_back(
+        [own_mean[0], own_mean[1], far, far_mean[1], label_rows, valid],
+        kept_dec,
+        norm_rows,
+        5,
+        feeds[1],
+        attend_out[2],
+        n_enc,
+    )
+    grads = attend_back(*cross_args, all_heads(spread), total_cross)
+    own_encoded, far_encoded = scatter_two(
+        row_blocks(dense_back(grads[:, share:], attend_in[2][:, share:]))
+    )
+    own_causal, far_causal = scatter_two(
+        row_blocks(dense_back(grads[:, :share], attend_in[2][:, :share]))
+    )
+    grad_enc, spread, sums_enc, given_enc = branch_back(
+        [own_encoded, far_encoded], kept_enc, norm_rows, 1, feeds[0], attend_out[0], n_enc
+    )
+    spread = swap_blocks(spread)
+    x, dpre, act, ga = given_enc
+    spread[1], dpre, far_causal = gate([spread[1], dpre, far_causal])
+    keep, send = adapter_grads([(x, dpre, act, ga), given_dec], core)
+    held = keep + flip(send, "enc", 1).astype(F32)
+    grad_dec, spread_dec, sums_four = middle_back(
+        grad_res, own_causal, far_causal, causal_in, norm_rows, 4, attend_out[1], n_enc
+    )
+    sums_zero = attend_back(
+        *enc_args,
+        jnp.concatenate(spread, 0),
+        total_encoder,
+        sum_with=(encoder_hats, in_enc, encoder_hat, grad_enc),
+        after=[held, grad_dec],
+    )
+    parts = adapters_plane(held, seq, enc)
+    sums_zero, *parts[1:] = gate([sums_zero] + parts[1:])
+    parts = adapters_line(parts, seq)
+    sums_three = attend_back(
+        *dec_args,
+        all_heads(spread_dec),
+        total_decoder,
+        sum_with=(decoder_hats, in_dec, decoder_hat, grad_dec),
+        after=[sums_zero],
+    )
+    sums_three, *parts[1:] = gate([sums_three] + parts[1:])
+
     count_own = jnp.clip(target_length - enc * own_rows, 0, own_rows).astype(F32)
-    squares_own = jnp.sum(grad_down * grad_down) + jnp.sum(grad_up * grad_up)
-    lanes = jnp.arange(width)
-    scalars = jnp.where(
-        lanes == 0, loss_own, jnp.where(lanes == 1, count_own, jnp.where(lanes == 2, squares_own, 0.0))
-    )
-    summed = jnp.stack(
-        [gain_zero, gain_one, gain_two, gain_three, gain_four, gain_five, gain_six]
-        + [shift_zero, shift_one, shift_two, shift_three, shift_four, shift_five, shift_six]
-        + [scalars, jnp.zeros_like(scalars)]
+    summed, grad_down, grad_up = payload(
+        loss_own,
+        count_own,
+        parts,
+        [sums_zero, sums_three, sums_four, sums_enc, sums_dec],
+        adapter_down.shape[2],
     )
     summed = sum_everywhere(summed)
-    loss_sum, token_total = summed[14, 0], summed[14, 1]
-    norm_grads = summed[:14]
-    squares = summed[14, 2] + jnp.sum(norm_grads * norm_grads)
     per = width // n_all
-    grad_norms = lax.dynamic_slice_in_dim(norm_grads, (seq * n_enc + enc) * per, per, 1)
-    grad_norms = grad_norms.reshape(2, 7, per)
-
-    grad_norm = jnp.sqrt(squares) / token_total
-    factor = jnp.minimum(1.0, CLIP_NORM / grad_norm) / token_total
-    moment_down, second_down, updated_down = adamw(
-        grad_down * factor, down_moment, down_second, adapter_down, RATE_ADAPTER, DECAY_ADAPTER
-    )
-    moment_up, second_up, updated_up = adamw(
-        grad_up * factor, up_moment, up_second, adapter_up, RATE_ADAPTER, DECAY_ADAPTER
-    )
-    moment_norms, second_norms, updated_norms = adamw(
-        grad_norms * factor, norm_moment, norm_second, norm_params, RATE_NORMS, 0.0
-    )
-    return (
-        loss_sum,
-        token_total,
-        grad_norm,
-        moment_down,
-        second_down,
-        updated_down,
-        moment_up,
-        second_up,
-        updated_up,
-        moment_norms,
-        second_norms,
-        updated_norms,
-    )
+    own = lax.dynamic_slice_in_dim(summed, (seq * n_enc + enc) * per, per, 1)[:14]
+    loss_sum, token_total, grad_norm, factor, *adapters = optimizer_step(
+        summed,
+        [grad_down, grad_up],
+        [down_moment, down_second, adapter_down, up_moment, up_second, adapter_up],
+    )
+    new_norms = adamw(
+        own.reshape(2, 7, per) * factor, norm_moment, norm_second, norm_params, RATE_NORMS, 0.0
+    )
+    return (loss_sum, token_total, grad_norm, *adapters, *new_norms)
 
 
 def solution(mesh):

time: 707 us -> 672 us (0.950)
  starting transfers between devices: 119 us -> 97.5 us
  Pallas kernels: 182 us -> 202 us
  matrix products: 38.1 us -> 20.1 us
  other arithmetic: 83.8 us -> 68.9 us
  waiting for transfers between devices: 146 us -> 157 us
  local copies, waits for them, and re-layouts: 101 us -> 91.2 us
  between operations: 23.6 us -> 16.5 us
    pallas_call x8 -> x12, Pallas kernels: 138 us -> 159 us  [the longest x3 56.1 us: attend_back(): pl.pallas_call(kernel, grid=(pairs, length // rows), out_shape=out, in_sp...]
    reduce_sum x23 -> x1, other arithmetic: 20 us -> 2.56 us  [shards(): jnp.sum(decoded_low.astype(F32) * label_rows.astype(F32), -1, keepdims=True)]
    unnamed x294 -> x224, local copies, waits for them, and re-layouts: 17.9 us -> 30.9 us
    ppermute x91 -> x87, starting transfers between devices: 96.9 us -> 84 us  [flip(): return lax.ppermute(value, axis, [(i, i ^ mask) for i in range(count)])]
    dot_general x7 -> x2, matrix products: 13.9 us -> 4.29 us  [dense_back(): lax.dot_general(left, right, (((1,), (1,)), ((), ())), preferred_element_...]
    concatenate x2 -> x0, local copies, waits for them, and re-layouts: 8.41 us -> none  [reduce_adapters(): both = jnp.concatenate([folded, grad_up.reshape(-1, rows // 2, width)], 1)]
    ppermute x91 -> x87, waiting for transfers between devices: 131 us -> 136 us  [flip(): return lax.ppermute(value, axis, [(i, i ^ mask) for i in range(count)])]
    dot_general x7 -> x5, matrix products: 18.8 us -> 15.9 us  [dense(): return jnp.dot(left, right, preferred_element_type=F32)]
  transfers between devices with their start and end apart: 106 -> 99, of which waited for: 32 -> 34; matrix products, arithmetic and copies ran while one was open for 26% -> 21% of each run, Pallas kernels for 17% -> 24%
where the time goes in v3:
time: 672 us; the launch traced here: 660 us
  Pallas kernels  202 us (30%)
  waiting for transfers between devices  157 us (23%)
  starting transfers between devices  97.5 us (15%)
  local copies, waits for them, and re-layouts  91.2 us (14%)
  other arithmetic  68.9 us (10%)
  matrix products  20.1 us (3%)
  between operations  16.5 us (2%)
    ppermute x87, waiting for transfers between devices, flip(): return lax.ppermute(value, axis, [(i, i ^ mask) for i in range(count)])  136 us
    ppermute x87, starting transfers between devices, flip(): return lax.ppermute(value, axis, [(i, i ^ mask) for i in range(count)])  84 us
    pallas_call x3, Pallas kernels, attend_back(): pl.pallas_call(kernel, grid=(pairs, length // rows), out_shape=out, in_sp...  56.1 us
    gather x3, local copies, waits for them, and re-layouts, lookup(): found = jnp.take(embedding, jnp.clip(ids, 0, entries - 1), axis=0)  37.5 us
    pallas_call x1, Pallas kernels, head(): pl.pallas_call(lambda *refs: head_kernel(count, *refs), grid=(entries //...  34.3 us
    unnamed x224, local copies, waits for them, and re-layouts  30.9 us
    pallas_call x2, Pallas kernels, branch_back(): pl.pallas_call(lambda *refs: branch_back_kernel(first, n_parts, len(given...  30.6 us
    pallas_call x3, Pallas kernels, attend(): pl.pallas_call(attend_kernel, grid=(pairs, length // rows), out_shape=[ja...  28.4 us
  transfers between devices with their start and end apart: 99, of which 34 were waited for; matrix products, arithmetic and copies ran while one was open for 21% of the time, Pallas kernels for 24%

profile of v3, /device:TPU:0, one launch (start us, length us, event | category | flops | bytes accessed | tf_op | source)
XLA Modules:
  0.0 660.2 jit_solution(15452632658149822491)
XLA Ops:
  11.4 6.2 all-gather.3
  21.9 3.5 all-to-all-start
  26.6 12.5 %gather_fusion.2 = bf16[1024,1024]{1,0:T(8,128)(2,1)} fusion(bf16[6400,1024]{1,0:T(8,128)(2,1)} %refs_4_.2, s32[1024]{0:T(1024)S(1)} %broadcast_clamp_fusion.2), kind=kCustom, calls=%fused_computation.clone | custom fusion | bytes 4198400 | tf_op jit(solution)/shard_map/jit(_take)/gather | solution.py:1105
  44.4 12.5 %gather_fusion.3 = bf16[1024,1024]{1,0:T(8,128)(2,1)} fusion(bf16[6400,1024]{1,0:T(8,128)(2,1)} %refs_4_.2, s32[1024]{0:T(1024)S(1)} %get-tuple-element.424), kind=kCustom, calls=%fused_computation.1.clone | custom fusion | bytes 4198400 | tf_op jit(solution)/shard_map/jit(_take)/gather | solution.py:1105
  76.6 3.1 collective-permute-start.11
  83.4 22.3 %collective-permute-done.10.refs_1_ = bf16[128,1536]{1,0:T(8,128)(2,1)S(1)} collective-permute-done((bf16[128,1536]{1,0:T(8,128)(2,1)S(1)}, bf16[128,1536]{1,0:T(8,128)(2,1)S(1)}, u32[]{:S(2)}, u32[]{:S(2)}) %collective-permute-start.10) | collective-permute-done | bytes 393248 | tf_op jit(solution)/shard_map/ppermute | solution.py:29
  107.7 15.1 %collective-permute-done.11.refs_2_ = bf16[128,1536]{1,0:T(8,128)(2,1)S(1)} collective-permute-done((bf16[128,1536]{1,0:T(8,128)(2,1)S(1)}, bf16[128,1536]{1,0:T(8,128)(2,1)S(1)}, u32[]{:S(2)}, u32[]{:S(2)}) %collective-permute-start.11) | collective-permute-done | bytes 393248 | tf_op jit(solution)/shard_map/ppermute | solution.py:29
  122.8 3.0 collective-permute-start.22
  130.6 7.7 %collective-permute-done.22 = bf16[256,1024]{1,0:T(8,128)(2,1)} collective-permute-done((bf16[256,1024]{1,0:T(8,128)(2,1)}, bf16[256,1024]{1,0:T(8,128)(2,1)}, u32[]{:S(2)}, u32[]{:S(2)}) %collective-permute-start.22) | collective-permute-done | bytes 524320 | tf_op jit(solution)/shard_map/ppermute | solution.py:29
  142.9 3.3 fusion.99
  148.8 18.6 %collective-permute-start.17 = (bf16[64,1536]{1,0:T(8,128)(2,1)S(1)}, bf16[64,1536]{1,0:T(8,128)(2,1)S(1)}, u32[]{:S(2)}, u32[]{:S(2)}) collective-permute-start(bf16[64,1536]{1,0:T(8,128)(2,1)S(1)} %copy-done.50), channel_id=1, source_target_pairs={{0,8},{4,12},{8,0},{12,4},{16,24},{20,28},{24,16},{28,20},{1,9},{5... | collective-permute-start | bytes 589832 | tf_op jit(solution)/shard_map/ppermute | solution.py:29
  175.2 3.6 collective-permute-done.18.refs_2_
  186.4 5.3 shard_map.275
  192.9 5.1 fusion.24.q_ref.k_ref.v_ref.refs_2_.refs_3_.refs_4_
  199.4 9.4 %shard_map.278 = (bf16[1024,256]{1,0:T(8,128)(2,1)}, f32[1024,256]{1,0:T(8,128)}) custom-call(s32[1024,1]{1,0:T(8,128)} %broadcast_in_dim.79.limit_ref.refs_0_, s32[1,1024]{1,0:T(1,128)} %bitcast.311, bf16[1024,768]{1,0:T(8,128)(2,1)} %fusion.24.q_ref.k_ref.v_ref.refs_2_.refs_3_.refs_4_, bf16[1024,768]{1,0:T(8,128)(2,1)} %fusion.24.q_ref.k_ref.v_ref.refs_2_.refs_3_.refs_4_, ...), custom_call_target="tpu_custom_call" | custom-call | flops 2147483648 | bytes 2097152 | tf_op jit(solution)/shard_map/pallas_call | solution.py:459
  211.0 10.9 %collective-permute-done.7 = bf16[256,1024]{1,0:T(8,128)(2,1)} collective-permute-done((bf16[256,1024]{1,0:T(8,128)(2,1)}, bf16[256,1024]{1,0:T(8,128)(2,1)}, u32[]{:S(2)}, u32[]{:S(2)}) %collective-permute-start.7) | collective-permute-done | bytes 524320 | tf_op jit(solution)/shard_map/ppermute | solution.py:29
  225.1 14.4 %collective-permute-done.28.refs_4_ = bf16[4,64,1536]{2,1,0:T(8,128)(2,1)S(1)} collective-permute-done((bf16[4,64,1536]{2,1,0:T(8,128)(2,1)}, bf16[4,64,1536]{2,1,0:T(8,128)(2,1)S(1)}, u32[]{:S(2)}, u32[]{:S(2)}) %collective-permute-start.28) | collective-permute-done | bytes 786464 | tf_op jit(solution)/shard_map/ppermute | solution.py:158
  239.6 4.7 fusion.27.q_ref.k_ref.v_ref.refs_2_.refs_3_.refs_4_
  244.3 9.5 %shard_map.276 = (bf16[1024,256]{1,0:T(8,128)(2,1)}, f32[1024,256]{1,0:T(8,128)}) custom-call(s32[1024,1]{1,0:T(8,128)} %bitcast.288, s32[1,1024]{1,0:T(1,128)} %bitcast.312, bf16[1024,768]{1,0:T(8,128)(2,1)} %fusion.27.q_ref.k_ref.v_ref.refs_2_.refs_3_.refs_4_, bf16[1024,768]{1,0:T(8,128)(2,1)} %fusion.27.q_ref.k_ref.v_ref.refs_2_.refs_3_.refs_4_, ...), custom_call_target="tpu_custom_call" | custom-call | flops 2147483648 | bytes 2097152 | tf_op jit(solution)/shard_map/pallas_call | solution.py:459
  259.4 2.9 collective-permute-start.37
  262.3 5.3 shard_map.280
  280.9 3.1 collective-permute-done.42.refs_3_
  284.7 14.1 %shard_map.282 = (f32[256,1024]{1,0:T(8,128)}, bf16[256,1024]{1,0:T(8,128)(2,1)}, f32[256,4096]{1,0:T(8,128)}, bf16[256,512]{1,0:T(8,128)(2,1)}, f32[256,512]{1,...) custom-call(bf16[256,256]{1,0:T(8,128)(2,1)} %get-tuple-element.367.refs_0_, bf16[256,256]{1,0:T(8,128)(2,1)} %copy-done.80, ...), custom_call_target="tpu_custom_call" | custom-call | flops 5368709120 | bytes 23068672 | tf_op jit(solution)/shard_map/pallas_call | solution.py:748
  301.5 5.9 collective-permute-done.34
  307.4 12.4 %gather_fusion.4 = bf16[1024,1024]{1,0:T(8,128)(2,1)} fusion(bf16[6400,1024]{1,0:T(8,128)(2,1)} %refs_4_.2, s32[1024]{0:T(1024)S(1)} %copy-done.92), kind=kCustom, calls=%fused_computation.2.clone | custom fusion | bytes 4198400 | tf_op jit(solution)/shard_map/jit(_take)/gather | solution.py:1105
  320.3 2.9 collective-permute-done.44
  323.3 3.2 select_select_fusion.refs_1_
  328.8 4.8 shard_map.281
  333.6 3.0 fusion.30.q_ref.refs_2_
  336.6 3.3 pad_maximum_fusion.refs_0_
  344.6 9.4 %shard_map.284 = (bf16[1024,256]{1,0:T(8,128)(2,1)}, f32[1024,256]{1,0:T(8,128)}) custom-call(s32[1024,1]{1,0:T(8,128)} %broadcast_in_dim.79.limit_ref.refs_0_, s32[1,1024]{1,0:T(1,128)} %bitcast.313, bf16[1024,256]{1,0:T(8,128)(2,1)} %fusion.30.q_ref.refs_2_, bf16[1024,512]{1,0:T(8,128)(2,1)} %convolution_convert_fusion.k_ref.v_ref.refs_3_.refs_4_, ...), custom_call_target="tpu_custom_call" | custom-call | flops 2147483648 | bytes 2097152 | tf_op jit(solution)/shard_map/pallas_call | solution.py:459
  364.8 13.9 %shard_map.285 = (f32[256,1024]{1,0:T(8,128)}, bf16[256,1024]{1,0:T(8,128)(2,1)}, f32[256,4096]{1,0:T(8,128)}, bf16[256,512]{1,0:T(8,128)(2,1)}, f32[256,512]{1,...) custom-call(bf16[256,256]{1,0:T(8,128)(2,1)} %get-tuple-element.363.refs_0_, bf16[256,256]{1,0:T(8,128)(2,1)} %copy-done.83, ...), custom_call_target="tpu_custom_call" | custom-call | flops 5368709120 | bytes 23068672 | tf_op jit(solution)/shard_map/pallas_call | solution.py:748
  381.2 13.1 %collective-permute-done.52.refs_2_ = bf16[256,1024]{1,0:T(8,128)(2,1)S(1)} collective-permute-done((bf16[256,1024]{1,0:T(8,128)(2,1)}, bf16[256,1024]{1,0:T(8,128)(2,1)S(1)}, u32[]{:S(2)}, u32[]{:S(2)}) %collective-permute-start.52) | collective-permute-done | bytes 524320 | tf_op jit(solution)/shard_map/ppermute | solution.py:29
  400.6 34.3 %shard_map.288 = (bf16[256,1024]{1,0:T(8,128)(2,1)}, bf16[256,1024]{1,0:T(8,128)(2,1)}, bf16[256,1024]{1,0:T(8,128)(2,1)}, bf16[256,1024]{1,0:T(8,128)(2,1)}, f3...) custom-call(bf16[256,1024]{1,0:T(8,128)(2,1)} %get-tuple-element.160.refs_0_, ...), custom_call_target="tpu_custom_call" | custom-call | flops 26843545600 | bytes 13107200 | tf_op jit(solution)/shard_map/pallas_call | solution.py:1010
  447.7 2.9 fusion.69
  453.0 6.9 %collective-permute-done.62.refs_0_ = bf16[256,1024]{1,0:T(8,128)(2,1)} collective-permute-done((bf16[256,1024]{1,0:T(8,128)(2,1)}, bf16[256,1024]{1,0:T(8,128)(2,1)}, u32[]{:S(2)}, u32[]{:S(2)}) %collective-permute-start.62) | collective-permute-done | bytes 524320 | tf_op jit(solution)/shard_map/ppermute | solution.py:29
  459.9 15.5 %shard_map.291 = (f32[256,1024]{1,0:T(8,128)}, f32[4,1024]{1,0:T(4,128)}, bf16[256,512]{1,0:T(8,128)(2,1)}, bf16[256,1024]{1,0:T(8,128)(2,1)}, bf16[256,256]{1,0...) custom-call(f32[256,1024]{1,0:T(8,128)} %add_divide_fusion.refs_0_, ...), custom_call_target="tpu_custom_call" | custom-call | flops 5368709120 | bytes 23068672 | tf_op jit(solution)/shard_map/pallas_call | solution.py:842
  477.3 4.1 collective-permute-done.69
  485.7 17.5 %shard_map.292 = bf16[1024,768]{1,0:T(8,128)(2,1)} custom-call(s32[1024,1]{1,0:T(8,128)} %broadcast_in_dim.79.limit_ref.refs_0_, s32[1,1024]{1,0:T(1,128)} %bitcast.314, bf16[1024,256]{1,0:T(8,128)(2,1)} %fusion.30.q_ref.refs_2_, bf16[1024,512]{1,0:T(8,128)(2,1)} %convolution_convert_fusion.k_ref.v_ref.refs_3_.refs_4_, ...), custom_call_target="tpu_custom_call" | custom-call | flops 5368709120 | bytes 4194304 | tf_op jit(solution)/shard_map/pallas_call | solution.py:578
  512.6 12.3 %collective-permute-done.72.refs_1_ = bf16[256,1024]{1,0:T(8,128)(2,1)S(1)} collective-permute-done((bf16[256,1024]{1,0:T(8,128)(2,1)S(1)}, bf16[256,1024]{1,0:T(8,128)(2,1)S(1)}, u32[]{:S(2)}, u32[]{:S(2)}) %collective-permute-start.72) | collective-permute-done | bytes 524320 | tf_op jit(solution)/shard_map/ppermute | solution.py:29
  525.8 15.1 %shard_map.293 = (f32[256,1024]{1,0:T(8,128)}, f32[4,1024]{1,0:T(4,128)}, bf16[256,512]{1,0:T(8,128)(2,1)}, bf16[256,1024]{1,0:T(8,128)(2,1)}, bf16[256,256]{1,0...) custom-call(f32[256,1024]{1,0:T(8,128)} %get-tuple-element.338.refs_0_, ...), custom_call_target="tpu_custom_call" | custom-call | flops 5368709120 | bytes 23068672 | tf_op jit(solution)/shard_map/pallas_call | solution.py:842
  549.1 2.9 shard_map.295
  554.9 2.9 pad_maximum_fusion.1.refs_7_
  560.0 3.0 pad_maximum_fusion.2.refs_7_
  574.8 19.2 %shard_map.297.refs_0_ = f32[2,1024]{1,0:T(2,128)} custom-call(s32[1024,1]{1,0:T(8,128)} %broadcast_in_dim.79.limit_ref.refs_0_, s32[1,1024]{1,0:T(1,128)} %bitcast.315, bf16[1024,768]{1,0:T(8,128)(2,1)} %fusion.24.q_ref.k_ref.v_ref.refs_2_.refs_3_.refs_4_, bf16[1024,768]{1,0:T(8,128)(2,1)} %fusion.24.q_ref.k_ref.v_ref.refs_2_.refs_3_.refs_4_, ...), custom_call_target="tpu_custom_call" | custom-call | flops 5368709120 | bytes 4194304 | tf_op jit(solution)/shard_map/pallas_call | solution.py:578
  594.0 2.8 collective-permute-done.82.refs_3_
  604.2 19.4 %shard_map.299.refs_0_ = f32[2,1024]{1,0:T(2,128)} custom-call(s32[1024,1]{1,0:T(8,128)} %bitcast.289, s32[1,1024]{1,0:T(1,128)} %bitcast.316, bf16[1024,768]{1,0:T(8,128)(2,1)} %fusion.27.q_ref.k_ref.v_ref.refs_2_.refs_3_.refs_4_, bf16[1024,768]{1,0:T(8,128)(2,1)} %fusion.27.q_ref.k_ref.v_ref.refs_2_.refs_3_.refs_4_, ...), custom_call_target="tpu_custom_call" | custom-call | flops 5368709120 | bytes 4194304 | tf_op jit(solution)/shard_map/pallas_call | solution.py:578
  642.3 3.0 collective-permute-done.94
  (533 shorter events, 213.3 us)
Async XLA Ops:
  7.2 276.8 %all-gather.7.cloned.1.call-start = ((), (), s32[]{:S(2)}) async-start(), calls=%async_computation.1 | async-start | bytes 19464192 | tf_op jit(solution)/shard_map/all_gather | solution.py:614
  10.5 349.8 %all-gather.9.cloned.1.call-start = ((), (), s32[]{:S(2)}) async-start(), calls=%async_computation.2 | async-start | bytes 19464192 | tf_op jit(solution)/shard_map/all_gather | solution.py:614
  17.7 43.6 %collective-permute-start.3 = (bf16[1,4,448]{2,1,0:T(4,128)(2,1)S(1)}, bf16[1,4,448]{2,1,0:T(4,128)(2,1)S(1)}, u32[]{:S(2)}, u32[]{:S(2)}) collective-permute-start(bf16[1,4,448]{2,1,0:T(4,128)(2,1)S(1)} %fusion.82), channel_id=1, source_target_pairs={{0,4},{4,0},{8,12},{12,8},{16,20},{20,16},{24,28},{28,24},{1,5},{5... | collective-permute-start | bytes 10760 | tf_op jit(solution)/shard_map/ppermute | solution.py:29
  21.9 52.6 %all-to-all-start = ((bf16[4,32,2304]{2,1,0:T(8,128)(2,1)}), bf16[4,32,2304]{2,1,0:T(8,128)(2,1)S(1)}, u32[]{:S(2)}, u32[]{:S(2)}) async-start(bf16[4,32,2304]{2,1,0:T(8,128)(2,1)} %reshape.477), calls=%async_computation | async-start | bytes 1179648 | tf_op jit(solution)/shard_map/all_to_all | solution.py:1136
  26.1 57.1 %collective-permute-start.9 = (bf16[32,1536]{1,0:T(8,128)(2,1)}, bf16[32,1536]{1,0:T(8,128)(2,1)}, u32[]{:S(2)}, u32[]{:S(2)}) collective-permute-start(bf16[32,1536]{1,0:T(8,128)(2,1)} %broadcast_select_fusion.2), channel_id=1, source_target_pairs={{0,1},{1,0},{2,3},{3,2},{4,5},{5,4},{6,7},{7,6},{8,9},{9,8},{10,11... | collective-permute-start | bytes 294920 | tf_op jit(solution)/shard_map/ppermute | solution.py:29
  43.2 33.4 %collective-permute-start.1 = (bf16[256,1024]{1,0:T(8,128)(2,1)}, bf16[256,1024]{1,0:T(8,128)(2,1)S(1)}, u32[]{:S(2)}, u32[]{:S(2)}) collective-permute-start(bf16[256,1024]{1,0:T(8,128)(2,1)} %get-tuple-element.348), channel_id=1, source_target_pairs={{0,1},{1,0},{2,3},{3,2},{4,5},{5,4},{6,7},{7,6},{8,9},{9,8},{10,11... | collective-permute-start | bytes 1572872 | tf_op jit(solution)/shard_map/ppermute | solution.py:29
  43.3 86.5 %collective-permute-start = (bf16[256,1024]{1,0:T(8,128)(2,1)}, bf16[256,1024]{1,0:T(8,128)(2,1)}, u32[]{:S(2)}, u32[]{:S(2)}) collective-permute-start(bf16[256,1024]{1,0:T(8,128)(2,1)} %get-tuple-element.347), channel_id=1, source_target_pairs={{0,1},{1,0},{2,3},{3,2},{4,5},{5,4},{6,7},{7,6},{8,9},{9,8},{10,11... | collective-permute-start | bytes 1572872 | tf_op jit(solution)/shard_map/ppermute | solution.py:29
  61.1 19.6 %collective-permute-start.21 = (bf16[256,1024]{1,0:T(8,128)(2,1)}, bf16[256,1024]{1,0:T(8,128)(2,1)}, u32[]{:S(2)}, u32[]{:S(2)}) collective-permute-start(bf16[256,1024]{1,0:T(8,128)(2,1)} %get-tuple-element.346), channel_id=1, source_target_pairs={{0,1},{1,0},{2,3},{3,2},{4,5},{5,4},{6,7},{7,6},{8,9},{9,8},{10,11... | collective-permute-start | bytes 1572872 | tf_op jit(solution)/shard_map/ppermute | solution.py:29
  75.4 30.3 %collective-permute-start.10 = (bf16[128,1536]{1,0:T(8,128)(2,1)S(1)}, bf16[128,1536]{1,0:T(8,128)(2,1)S(1)}, u32[]{:S(2)}, u32[]{:S(2)}) collective-permute-start(bf16[128,1536]{1,0:T(8,128)(2,1)S(1)} %get-tuple-element.355), channel_id=1, source_target_pairs={{0,8},{4,12},{8,0},{12,4},{16,24},{20,28},{24,16},{28,20},{1,9},{5... | collective-permute-start | bytes 1179656 | tf_op jit(solution)/shard_map/ppermute | solution.py:29
  76.6 46.2 %collective-permute-start.11 = (bf16[128,1536]{1,0:T(8,128)(2,1)S(1)}, bf16[128,1536]{1,0:T(8,128)(2,1)S(1)}, u32[]{:S(2)}, u32[]{:S(2)}) collective-permute-start(bf16[128,1536]{1,0:T(8,128)(2,1)S(1)} %get-tuple-element.355), channel_id=1, source_target_pairs={{0,16},{4,20},{8,24},{12,28},{16,0},{20,4},{24,8},{28,12},{1,17},{... | collective-permute-start | bytes 1179656 | tf_op jit(solution)/shard_map/ppermute | solution.py:29
  80.8 49.1 %collective-permute-start.20 = (bf16[256,1024]{1,0:T(8,128)(2,1)}, bf16[256,1024]{1,0:T(8,128)(2,1)S(1)}, u32[]{:S(2)}, u32[]{:S(2)}) collective-permute-start(bf16[256,1024]{1,0:T(8,128)(2,1)} %get-tuple-element.345), channel_id=1, source_target_pairs={{0,1},{1,0},{2,3},{3,2},{4,5},{5,4},{6,7},{7,6},{8,9},{9,8},{10,11... | collective-permute-start | bytes 1572872 | tf_op jit(solution)/shard_map/ppermute | solution.py:29
  83.3 44.2 %collective-permute-start.12 = (bf16[128,1536]{1,0:T(8,128)(2,1)S(1)}, bf16[128,1536]{1,0:T(8,128)(2,1)S(1)}, u32[]{:S(2)}, u32[]{:S(2)}) collective-permute-start(bf16[128,1536]{1,0:T(8,128)(2,1)S(1)} %get-tuple-element.355), channel_id=1, source_target_pairs={{0,24},{4,28},{8,16},{12,20},{16,8},{20,12},{24,0},{28,4},{1,25},{... | collective-permute-start | bytes 1179656 | tf_op jit(solution)/shard_map/ppermute | solution.py:29
  105.6 25.0 %collective-permute-start.2 = (bf16[256,1024]{1,0:T(8,128)(2,1)}, bf16[256,1024]{1,0:T(8,128)(2,1)}, u32[]{:S(2)}, u32[]{:S(2)}) collective-permute-start(bf16[256,1024]{1,0:T(8,128)(2,1)} %fusion.42), channel_id=1, source_target_pairs={{0,2},{1,3},{2,0},{3,1},{4,6},{5,7},{6,4},{7,5},{8,10},{9,11},{10,... | collective-permute-start | bytes 1572872 | tf_op jit(solution)/shard_map/ppermute | solution.py:29
  129.8 55.6 %collective-permute-start.13 = (bf16[4,128,1536]{2,1,0:T(8,128)(2,1)S(1)}, bf16[4,128,1536]{2,1,0:T(8,128)(2,1)}, u32[]{:S(2)}, u32[]{:S(2)}) collective-permute-start(bf16[4,128,1536]{2,1,0:T(8,128)(2,1)S(1)} %pad_maximum_fusion.3.refs_1_), channel_id=1, source_target_pairs={{0,4},{4,0},{8,12},{12,8},{16,20},{20,16},{24,28},{28,24},{1,5},{5... | collective-permute-start | bytes 4718600 | tf_op jit(solution)/shard_map/ppermute | solution.py:29
  148.6 23.1 %collective-permute-start.24 = (bf16[256,1024]{1,0:T(8,128)(2,1)}, bf16[256,1024]{1,0:T(8,128)(2,1)}, u32[]{:S(2)}, u32[]{:S(2)}) collective-permute-start(bf16[256,1024]{1,0:T(8,128)(2,1)} %get-tuple-element.330), channel_id=1, source_target_pairs={{0,2},{1,3},{2,0},{3,1},{4,6},{5,7},{6,4},{7,5},{8,10},{9,11},{10,... | collective-permute-start | bytes 1572872 | tf_op jit(solution)/shard_map/ppermute | solution.py:29
  148.8 22.8 %collective-permute-start.17 = (bf16[64,1536]{1,0:T(8,128)(2,1)S(1)}, bf16[64,1536]{1,0:T(8,128)(2,1)S(1)}, u32[]{:S(2)}, u32[]{:S(2)}) collective-permute-start(bf16[64,1536]{1,0:T(8,128)(2,1)S(1)} %copy-done.50), channel_id=1, source_target_pairs={{0,8},{4,12},{8,0},{12,4},{16,24},{20,28},{24,16},{28,20},{1,9},{5... | collective-permute-start | bytes 589832 | tf_op jit(solution)/shard_map/ppermute | solution.py:29
  171.6 21.3 %collective-permute-start.23 = (bf16[256,1024]{1,0:T(8,128)(2,1)}, bf16[256,1024]{1,0:T(8,128)(2,1)}, u32[]{:S(2)}, u32[]{:S(2)}) collective-permute-start(bf16[256,1024]{1,0:T(8,128)(2,1)} %get-tuple-element.330), channel_id=1, source_target_pairs={{0,1},{1,0},{2,3},{3,2},{4,5},{5,4},{6,7},{7,6},{8,9},{9,8},{10,11... | collective-permute-start | bytes 1572872 | tf_op jit(solution)/shard_map/ppermute | solution.py:29
  171.6 21.3 %collective-permute-start.25 = (bf16[256,1024]{1,0:T(8,128)(2,1)}, bf16[256,1024]{1,0:T(8,128)(2,1)}, u32[]{:S(2)}, u32[]{:S(2)}) collective-permute-start(bf16[256,1024]{1,0:T(8,128)(2,1)} %collective-permute-done.24), channel_id=1, source_target_pairs={{0,1},{1,0},{2,3},{3,2},{4,5},{5,4},{6,7},{7,6},{8,9},{9,8},{10,11... | collective-permute-start | bytes 1572872 | tf_op jit(solution)/shard_map/ppermute | solution.py:29
  181.4 27.5 %collective-permute-start.26 = (bf16[4,64,1536]{2,1,0:T(8,128)(2,1)S(1)}, bf16[4,64,1536]{2,1,0:T(8,128)(2,1)S(1)}, u32[]{:S(2)}, u32[]{:S(2)}) collective-permute-start(bf16[4,64,1536]{2,1,0:T(8,128)(2,1)S(1)} %pad_maximum_fusion.4.refs_1_), channel_id=1, source_target_pairs={{0,4},{1,3},{2,6},{3,1},{4,0},{5,7},{6,2},{7,5},{8,12},{9,11},{10,... | collective-permute-start | bytes 2359304 | tf_op jit(solution)/shard_map/ppermute | solution.py:158
  182.2 26.7 %collective-permute-start.27 = (bf16[4,64,1536]{2,1,0:T(8,128)(2,1)S(1)}, bf16[4,64,1536]{2,1,0:T(8,128)(2,1)S(1)}, u32[]{:S(2)}, u32[]{:S(2)}) collective-permute-start(bf16[4,64,1536]{2,1,0:T(8,128)(2,1)S(1)} %pad_maximum_fusion.4.refs_1_), channel_id=1, source_target_pairs={{0,2},{1,5},{2,0},{3,7},{4,6},{5,1},{6,4},{7,3},{8,10},{9,13},{10,... | collective-permute-start | bytes 2359304 | tf_op jit(solution)/shard_map/ppermute | solution.py:158
  185.4 36.6 %collective-permute-start.7 = (bf16[256,1024]{1,0:T(8,128)(2,1)}, bf16[256,1024]{1,0:T(8,128)(2,1)}, u32[]{:S(2)}, u32[]{:S(2)}) collective-permute-start(bf16[256,1024]{1,0:T(8,128)(2,1)} %fusion.45), channel_id=1, source_target_pairs={{0,2},{1,3},{2,0},{3,1},{4,6},{5,7},{6,4},{7,5},{8,10},{9,11},{10,... | collective-permute-start | bytes 1572872 | tf_op jit(solution)/shard_map/ppermute | solution.py:29
  210.0 29.5 %collective-permute-start.28 = (bf16[4,64,1536]{2,1,0:T(8,128)(2,1)}, bf16[4,64,1536]{2,1,0:T(8,128)(2,1)S(1)}, u32[]{:S(2)}, u32[]{:S(2)}) collective-permute-start(bf16[4,64,1536]{2,1,0:T(8,128)(2,1)} %get-tuple-element.147.refs_2_), channel_id=1, source_target_pairs={{0,2},{1,5},{2,0},{3,7},{4,6},{5,1},{6,4},{7,3},{8,10},{9,13},{10,... | collective-permute-start | bytes 2359304 | tf_op jit(solution)/shard_map/ppermute | solution.py:158
  222.0 17.6 %collective-permute-start.8 = (bf16[256,1024]{1,0:T(8,128)(2,1)}, bf16[256,1024]{1,0:T(8,128)(2,1)S(1)}, u32[]{:S(2)}, u32[]{:S(2)}) collective-permute-start(bf16[256,1024]{1,0:T(8,128)(2,1)} %collective-permute-done.7), channel_id=1, source_target_pairs={{0,1},{1,0},{2,3},{3,2},{4,5},{5,4},{6,7},{7,6},{8,9},{9,8},{10,11... | collective-permute-start | bytes 1572872 | tf_op jit(solution)/shard_map/ppermute | solution.py:29
  224.1 33.1 %collective-permute-start.29 = (bf16[4,64,1536]{2,1,0:T(8,128)(2,1)S(1)}, bf16[4,64,1536]{2,1,0:T(8,128)(2,1)S(1)}, u32[]{:S(2)}, u32[]{:S(2)}) collective-permute-start(bf16[4,64,1536]{2,1,0:T(8,128)(2,1)S(1)} %pad_maximum_fusion.4.refs_1_), channel_id=1, source_target_pairs={{0,1},{1,0},{2,3},{3,2},{4,5},{5,4},{6,7},{7,6},{8,9},{9,8},{10,11... | collective-permute-start | bytes 2359304 | tf_op jit(solution)/shard_map/ppermute | solution.py:29
  224.6 32.9 %collective-permute-start.30 = (bf16[4,64,1536]{2,1,0:T(8,128)(2,1)}, bf16[4,64,1536]{2,1,0:T(8,128)(2,1)S(1)}, u32[]{:S(2)}, u32[]{:S(2)}) collective-permute-start(bf16[4,64,1536]{2,1,0:T(8,128)(2,1)} %get-tuple-element.147.refs_2_), channel_id=1, source_target_pairs={{0,1},{1,0},{2,3},{3,2},{4,5},{5,4},{6,7},{7,6},{8,9},{9,8},{10,11... | collective-permute-start | bytes 2359304 | tf_op jit(solution)/shard_map/ppermute | solution.py:29
  224.6 33.6 %collective-permute-start.31 = (bf16[4,64,1536]{2,1,0:T(8,128)(2,1)}, bf16[4,64,1536]{2,1,0:T(8,128)(2,1)S(1)}, u32[]{:S(2)}, u32[]{:S(2)}) collective-permute-start(bf16[4,64,1536]{2,1,0:T(8,128)(2,1)} %get-tuple-element.148.refs_3_), channel_id=1, source_target_pairs={{0,1},{1,0},{2,3},{3,2},{4,5},{5,4},{6,7},{7,6},{8,9},{9,8},{10,11... | collective-permute-start | bytes 2359304 | tf_op jit(solution)/shard_map/ppermute | solution.py:29
  239.6 19.8 %collective-permute-start.32 = (bf16[4,64,1536]{2,1,0:T(8,128)(2,1)S(1)}, bf16[4,64,1536]{2,1,0:T(8,128)(2,1)S(1)}, u32[]{:S(2)}, u32[]{:S(2)}) collective-permute-start(bf16[4,64,1536]{2,1,0:T(8,128)(2,1)S(1)} %collective-permute-done.28.refs_4_), channel_id=1, source_target_pairs={{0,1},{1,0},{2,3},{3,2},{4,5},{5,4},{6,7},{7,6},{8,9},{9,8},{10,11... | collective-permute-start | bytes 2359304 | tf_op jit(solution)/shard_map/ppermute | solution.py:29
  258.2 41.2 %collective-permute-start.38 = (bf16[128,768]{1,0:T(8,128)(2,1)S(1)}, bf16[128,768]{1,0:T(8,128)(2,1)S(1)}, u32[]{:S(2)}, u32[]{:S(2)}) collective-permute-start(bf16[128,768]{1,0:T(8,128)(2,1)S(1)} %copy-done.49), channel_id=1, source_target_pairs={{0,24},{4,28},{8,16},{12,20},{16,8},{20,12},{24,0},{28,4},{1,25},{... | collective-permute-start | bytes 589832 | tf_op jit(solution)/shard_map/ppermute | solution.py:29
  259.4 40.4 %collective-permute-start.37 = (bf16[128,768]{1,0:T(8,128)(2,1)S(1)}, bf16[128,768]{1,0:T(8,128)(2,1)S(1)}, u32[]{:S(2)}, u32[]{:S(2)}) collective-permute-start(bf16[128,768]{1,0:T(8,128)(2,1)S(1)} %copy-done.49), channel_id=1, source_target_pairs={{0,16},{4,20},{8,24},{12,28},{16,0},{20,4},{24,8},{28,12},{1,17},{... | collective-permute-start | bytes 589832 | tf_op jit(solution)/shard_map/ppermute | solution.py:29
  275.6 24.2 %collective-permute-start.36 = (bf16[128,768]{1,0:T(8,128)(2,1)S(1)}, bf16[128,768]{1,0:T(8,128)(2,1)S(1)}, u32[]{:S(2)}, u32[]{:S(2)}) collective-permute-start(bf16[128,768]{1,0:T(8,128)(2,1)S(1)} %copy-done.49), channel_id=1, source_target_pairs={{0,8},{4,12},{8,0},{12,4},{16,24},{20,28},{24,16},{28,20},{1,9},{5... | collective-permute-start | bytes 589832 | tf_op jit(solution)/shard_map/ppermute | solution.py:29
  279.2 28.2 %collective-permute-start.34 = (bf16[256,1024]{1,0:T(8,128)(2,1)}, bf16[256,1024]{1,0:T(8,128)(2,1)}, u32[]{:S(2)}, u32[]{:S(2)}) collective-permute-start(bf16[256,1024]{1,0:T(8,128)(2,1)} %get-tuple-element.328), channel_id=1, source_target_pairs={{0,2},{1,3},{2,0},{3,1},{4,6},{5,7},{6,4},{7,5},{8,10},{9,11},{10,... | collective-permute-start | bytes 1572872 | tf_op jit(solution)/shard_map/ppermute | solution.py:29
  298.8 24.5 %collective-permute-start.44 = (bf16[256,1024]{1,0:T(8,128)(2,1)}, bf16[256,1024]{1,0:T(8,128)(2,1)}, u32[]{:S(2)}, u32[]{:S(2)}) collective-permute-start(bf16[256,1024]{1,0:T(8,128)(2,1)} %get-tuple-element.153), channel_id=1, source_target_pairs={{0,2},{1,3},{2,0},{3,1},{4,6},{5,7},{6,4},{7,5},{8,10},{9,11},{10,... | collective-permute-start | bytes 1572872 | tf_op jit(solution)/shard_map/ppermute | solution.py:29
  299.9 26.7 %collective-permute-start.39 = (bf16[4,128,768]{2,1,0:T(8,128)(2,1)S(1)}, bf16[4,128,768]{2,1,0:T(8,128)(2,1)S(1)}, u32[]{:S(2)}, u32[]{:S(2)}) collective-permute-start(bf16[4,128,768]{2,1,0:T(8,128)(2,1)S(1)} %pad_maximum_fusion.5.refs_1_), channel_id=1, source_target_pairs={{0,4},{4,0},{8,12},{12,8},{16,20},{20,16},{24,28},{28,24},{1,5},{5... | collective-permute-start | bytes 2359304 | tf_op jit(solution)/shard_map/ppermute | solution.py:29
  301.4 32.2 %collective-permute-start.33 = (bf16[256,1024]{1,0:T(8,128)(2,1)}, bf16[256,1024]{1,0:T(8,128)(2,1)}, u32[]{:S(2)}, u32[]{:S(2)}) collective-permute-start(bf16[256,1024]{1,0:T(8,128)(2,1)} %get-tuple-element.328), channel_id=1, source_target_pairs={{0,1},{1,0},{2,3},{3,2},{4,5},{5,4},{6,7},{7,6},{8,9},{9,8},{10,11... | collective-permute-start | bytes 1572872 | tf_op jit(solution)/shard_map/ppermute | solution.py:29
  307.4 26.2 %collective-permute-start.35 = (bf16[256,1024]{1,0:T(8,128)(2,1)}, bf16[256,1024]{1,0:T(8,128)(2,1)}, u32[]{:S(2)}, u32[]{:S(2)}) collective-permute-start(bf16[256,1024]{1,0:T(8,128)(2,1)} %collective-permute-done.34), channel_id=1, source_target_pairs={{0,1},{1,0},{2,3},{3,2},{4,5},{5,4},{6,7},{7,6},{8,9},{9,8},{10,11... | collective-permute-start | bytes 1572872 | tf_op jit(solution)/shard_map/ppermute | solution.py:29
  319.8 16.8 %collective-permute-start.43 = (bf16[256,1024]{1,0:T(8,128)(2,1)}, bf16[256,1024]{1,0:T(8,128)(2,1)}, u32[]{:S(2)}, u32[]{:S(2)}) collective-permute-start(bf16[256,1024]{1,0:T(8,128)(2,1)} %get-tuple-element.153), channel_id=1, source_target_pairs={{0,1},{1,0},{2,3},{3,2},{4,5},{5,4},{6,7},{7,6},{8,9},{9,8},{10,11... | collective-permute-start | bytes 1572872 | tf_op jit(solution)/shard_map/ppermute | solution.py:29
  359.8 18.9 %collective-permute-start.50 = (bf16[256,1024]{1,0:T(8,128)(2,1)}, bf16[256,1024]{1,0:T(8,128)(2,1)S(1)}, u32[]{:S(2)}, u32[]{:S(2)}) collective-permute-start(bf16[256,1024]{1,0:T(8,128)(2,1)} %fusion.39), channel_id=1, source_target_pairs={{0,2},{1,3},{2,0},{3,1},{4,6},{5,7},{6,4},{7,5},{8,10},{9,11},{10,... | collective-permute-start | bytes 1572872 | tf_op jit(solution)/shard_map/ppermute | solution.py:29
  380.8 16.1 %collective-permute-start.51 = (bf16[256,1024]{1,0:T(8,128)(2,1)}, bf16[256,1024]{1,0:T(8,128)(2,1)S(1)}, u32[]{:S(2)}, u32[]{:S(2)}) collective-permute-start(bf16[256,1024]{1,0:T(8,128)(2,1)} %get-tuple-element.159.refs_0_), channel_id=1, source_target_pairs={{0,1},{1,0},{2,3},{3,2},{4,5},{5,4},{6,7},{7,6},{8,9},{9,8},{10,11... | collective-permute-start | bytes 1572872 | tf_op jit(solution)/shard_map/ppermute | solution.py:29
  398.6 36.3 %collective-permute-start.54 = (bf16[256,1024]{1,0:T(8,128)(2,1)}, bf16[256,1024]{1,0:T(8,128)(2,1)S(1)}, u32[]{:S(2)}, u32[]{:S(2)}) collective-permute-start(bf16[256,1024]{1,0:T(8,128)(2,1)} %get-tuple-element.172.refs_8_), channel_id=1, source_target_pairs={{0,2},{1,3},{2,0},{3,1},{4,6},{5,7},{6,4},{7,5},{8,10},{9,11},{10,... | collective-permute-start | bytes 1572872 | tf_op jit(solution)/shard_map/ppermute | solution.py:29
  399.5 35.4 %collective-permute-start.55 = (bf16[256,1024]{1,0:T(8,128)(2,1)}, bf16[256,1024]{1,0:T(8,128)(2,1)}, u32[]{:S(2)}, u32[]{:S(2)}) collective-permute-start(bf16[256,1024]{1,0:T(8,128)(2,1)} %get-tuple-element.173.refs_10_), channel_id=1, source_target_pairs={{0,2},{1,3},{2,0},{3,1},{4,6},{5,7},{6,4},{7,5},{8,10},{9,11},{10,... | collective-permute-start | bytes 1572872 | tf_op jit(solution)/shard_map/ppermute | solution.py:29
  436.7 16.3 %collective-permute-start.63 = (bf16[256,1024]{1,0:T(8,128)(2,1)}, bf16[256,1024]{1,0:T(8,128)(2,1)}, u32[]{:S(2)}, u32[]{:S(2)}) collective-permute-start(bf16[256,1024]{1,0:T(8,128)(2,1)} %get-tuple-element.184.refs_1_), channel_id=1, source_target_pairs={{0,1},{1,0},{2,3},{3,2},{4,5},{5,4},{6,7},{7,6},{8,9},{9,8},{10,11... | collective-permute-start | bytes 1572872 | tf_op jit(solution)/shard_map/ppermute | solution.py:29
  511.4 29.5 %collective-permute-start.75 = (bf16[256,1024]{1,0:T(8,128)(2,1)S(1)}, bf16[256,1024]{1,0:T(8,128)(2,1)S(1)}, u32[]{:S(2)}, u32[]{:S(2)}) collective-permute-start(bf16[256,1024]{1,0:T(8,128)(2,1)S(1)} %get-tuple-element.336), channel_id=1, source_target_pairs={{0,2},{1,3},{2,0},{3,1},{4,6},{5,7},{6,4},{7,5},{8,10},{9,11},{10,... | collective-permute-start | bytes 1572872 | tf_op jit(solution)/shard_map/ppermute | solution.py:29
  570.4 23.6 %collective-permute-start.80 = (bf16[4,64,1024]{2,1,0:T(8,128)(2,1)S(1)}, bf16[4,64,1024]{2,1,0:T(8,128)(2,1)S(1)}, u32[]{:S(2)}, u32[]{:S(2)}) collective-permute-start(bf16[4,64,1024]{2,1,0:T(8,128)(2,1)S(1)} %get-tuple-element.334), channel_id=1, source_target_pairs={{0,4},{1,5},{2,6},{3,7},{4,0},{5,1},{6,2},{7,3},{8,12},{9,13},{10,... | collective-permute-start | bytes 1572872 | tf_op jit(solution)/shard_map/ppermute | solution.py:132
  571.9 22.1 %collective-permute-start.81 = (bf16[4,64,1024]{2,1,0:T(8,128)(2,1)S(1)}, bf16[4,64,1024]{2,1,0:T(8,128)(2,1)S(1)}, u32[]{:S(2)}, u32[]{:S(2)}) collective-permute-start(bf16[4,64,1024]{2,1,0:T(8,128)(2,1)S(1)} %get-tuple-element.333), channel_id=1, source_target_pairs={{0,2},{1,3},{2,0},{3,1},{4,6},{5,7},{6,4},{7,5},{8,10},{9,11},{10,... | collective-permute-start | bytes 1572872 | tf_op jit(solution)/shard_map/ppermute | solution.py:132
  572.9 23.9 %collective-permute-start.82 = (bf16[4,64,1024]{2,1,0:T(8,128)(2,1)S(1)}, bf16[4,64,1024]{2,1,0:T(8,128)(2,1)S(1)}, u32[]{:S(2)}, u32[]{:S(2)}) collective-permute-start(bf16[4,64,1024]{2,1,0:T(8,128)(2,1)S(1)} %get-tuple-element.332), channel_id=1, source_target_pairs={{0,6},{1,7},{2,4},{3,5},{4,2},{5,3},{6,0},{7,1},{8,14},{9,15},{10,... | collective-permute-start | bytes 1572872 | tf_op jit(solution)/shard_map/ppermute | solution.py:132
  599.8 24.6 %collective-permute-start.86 = (bf16[64,1024]{1,0:T(8,128)(2,1)S(1)}, bf16[64,1024]{1,0:T(8,128)(2,1)S(1)}, u32[]{:S(2)}, u32[]{:S(2)}) collective-permute-start(bf16[64,1024]{1,0:T(8,128)(2,1)S(1)} %get-tuple-element.351), channel_id=1, source_target_pairs={{0,8},{4,12},{8,0},{12,4},{16,24},{20,28},{24,16},{28,20},{1,9},{5... | collective-permute-start | bytes 393224 | tf_op jit(solution)/shard_map/ppermute | solution.py:29
  601.7 22.7 %collective-permute-start.87 = (bf16[64,1024]{1,0:T(8,128)(2,1)S(1)}, bf16[64,1024]{1,0:T(8,128)(2,1)S(1)}, u32[]{:S(2)}, u32[]{:S(2)}) collective-permute-start(bf16[64,1024]{1,0:T(8,128)(2,1)S(1)} %get-tuple-element.350), channel_id=1, source_target_pairs={{0,16},{4,20},{8,24},{12,28},{16,0},{20,4},{24,8},{28,12},{1,17},{... | collective-permute-start | bytes 393224 | tf_op jit(solution)/shard_map/ppermute | solution.py:29
  603.9 20.5 %collective-permute-start.88 = (bf16[64,1024]{1,0:T(8,128)(2,1)S(1)}, bf16[64,1024]{1,0:T(8,128)(2,1)S(1)}, u32[]{:S(2)}, u32[]{:S(2)}) collective-permute-start(bf16[64,1024]{1,0:T(8,128)(2,1)S(1)} %get-tuple-element.349), channel_id=1, source_target_pairs={{0,24},{4,28},{8,16},{12,20},{16,8},{20,12},{24,0},{28,4},{1,25},{... | collective-permute-start | bytes 393224 | tf_op jit(solution)/shard_map/ppermute | solution.py:29
  (154 other events, 1218.0 us)
Sparse Core Ops, SparseCore 0:
  10.9 160.9 all-gather.6
  174.8 164.3 all-gather.8

commit v4 on v3

--- a/solution.py
+++ b/solution.py
@@ -84,14 +84,17 @@
     return (mean.astype(F32) * own + other.astype(F32) * far) / both, highest + jnp.log(both)
 
 
-def merge_enc(blocks, totals):
+def merge_enc(blocks, totals, beside):
     held = {j: (b, t) for j, (b, t) in enumerate(zip(blocks, totals))}
     for mask in bits("enc"):
         away = [j for j in held if j & mask]
-        sent = [(flip(held[j][0].astype(LOW), "enc", mask), flip(held[j][1], "enc", mask)) for j in away]
+        means = [held[j][0].astype(LOW) for j in away]
+        if len(held) == 2:
+            means[0], *beside = gate([means[0]] + beside)
+        sent = [(flip(m, "enc", mask), flip(held[j][1], "enc", mask)) for j, m in zip(away, means)]
         for j, came in zip(away, sent):
             if len(held) == 2:
-                return held[j ^ mask], came
+                return held[j ^ mask], came, beside
             held[j ^ mask] = merge_means(held[j ^ mask], came)
             del held[j]
 
@@ -113,14 +116,16 @@
     def kernel(*refs):
         pass
 
-    return pl.pallas_call(
+    results = pl.pallas_call(
         kernel,
         out_shape=[jax.ShapeDtypeStruct(v.shape, v.dtype) for v in arrays],
         in_specs=[pl.BlockSpec(memory_space=pl.ANY)] * len(arrays),
         out_specs=[pl.BlockSpec(memory_space=pl.ANY)] * len(arrays),
         input_output_aliases={i: i for i in range(len(arrays))},
+        compiler_params=pltpu.CompilerParams(vmem_limit_bytes=60 * MIB),
         cost_estimate=pl.CostEstimate(flops=0, bytes_accessed=0, transcendentals=0),
     )(*arrays)
+    return list(results)
 
 
 def flip_both(value, seq_mask, enc_mask):
@@ -172,6 +177,12 @@
 
 def slow_flips(value):
     return [flip(value, "seq", o) for o in line_offsets()[1:]]
+
+
+def slow_flips_both(first, second):
+    if first.shape[1] != second.shape[1]:
+        return slow_flips(first), slow_flips(second)
+    return slow_flips(jnp.concatenate([first, second], 0)), None
 
 
 def plane_steps():
@@ -518,14 +529,15 @@
     attend_back_step(*refs[:7], *refs[-3:])
 
 
-def attend_sums_kernel(*refs):
-    hat_ref, weight_ref, own_hat_ref, own_grad_ref = refs[7:11]
+def attend_sums_kernel(n_blocks, *refs):
+    *hat_refs, weight_ref, own_hat_ref, own_grad_ref = refs[7 : 10 + n_blocks]
     sums_ref, out_ref, dk_sum, dv_sum, hats, weights, sem = refs[-7:]
+    rows = hat_refs[0].shape[0]
     pair, step = pl.program_id(0), pl.program_id(1)
     copies = [
-        pltpu.make_async_copy(hat_ref, hats, sem.at[0]),
-        pltpu.make_async_copy(weight_ref, weights, sem.at[1]),
-    ]
+        pltpu.make_async_copy(ref, hats.at[pl.ds(j * rows, rows), :], sem.at[j])
+        for j, ref in enumerate(hat_refs)
+    ] + [pltpu.make_async_copy(weight_ref, weights, sem.at[n_blocks])]
 
     @pl.when((pair == 0) & (step == 0))
     def _():
@@ -562,26 +574,30 @@
     rows = query_rows(length)
     hbm = pl.BlockSpec(memory_space=pl.ANY)
     scratch = [pltpu.VMEM((length, 128), F32), pltpu.VMEM((length, 128), F32)]
-    extra = () if sum_with is None else tuple(sum_with)
+    extra = () if sum_with is None else tuple(sum_with[0]) + tuple(sum_with[1:])
+    n_blocks = len(extra) - 3
     if sum_with is None:
         kernel = attend_back_kernel
         out = jax.ShapeDtypeStruct((length, 3 * width), LOW)
     else:
-        kernel = attend_sums_kernel
+
+        def kernel(*refs):
+            attend_sums_kernel(n_blocks, *refs)
+
         out = jax.ShapeDtypeStruct((2, extra[0].shape[1]), F32)
         scratch = (
             [pltpu.VMEM((length, 3 * width), LOW)]
             + scratch
-            + [pltpu.VMEM(v.shape, LOW) for v in extra[:2]]
-            + [pltpu.SemaphoreType.DMA((2,))]
+            + [pltpu.VMEM((length, extra[0].shape[1]), LOW), pltpu.VMEM(extra[n_blocks].shape, LOW)]
+            + [pltpu.SemaphoreType.DMA((n_blocks + 1,))]
         )
     return pl.pallas_call(
         kernel,
         grid=(pairs, length // rows),
         out_shape=out,
         in_specs=attend_specs(rows, length, key_at, value_at, 2)
-        + [hbm] * len(extra[:2])
-        + [pl.BlockSpec(v.shape, lambda p, j: (0, 0)) for v in extra[2:]]
+        + [hbm] * len(extra[:-2])
+        + [pl.BlockSpec(v.shape, lambda p, j: (0, 0)) for v in extra[-2:]]
         + [hbm] * len(after),
         out_specs=pl.BlockSpec(out.shape, lambda p, j: (0, 0)),
         scratch_shapes=scratch,
@@ -894,32 +910,47 @@
         out_specs=[vmem] * (2 + n_parts),
         compiler_params=pltpu.CompilerParams(vmem_limit_bytes=32 * MIB),
         cost_estimate=pl.CostEstimate(
-            flops=2 * rows * width * width, bytes_accessed=8 * MIB, transcendentals=0
+            flops=0, bytes_accessed=0, transcendentals=0
         ),
     )(residual, own, far, va, norms, proj)
     return dva, spread, sums
 
 
 def adapter_grad_kernel(core_ref, *refs):
-    keep_ref, send_ref, down, up = refs[-4:]
+    given, refs = refs[:8], refs[8:]
+    keep_ref, send_ref = refs[:2]
+    rooms, (down, up, keep, send, sem, sem_out) = refs[2:10], refs[10:]
+    copies = [pltpu.make_async_copy(g, r, sem.at[i]) for i, (g, r) in enumerate(zip(given, rooms))]
+    for copy in copies:
+        copy.start()
     core = core_ref[0]
-    pairs, depth, width = keep_ref.shape
+    pairs, depth, width = keep.shape
     rows = depth // 2
     half, small = rows // 2, width // 2
     for k in range(2):
-        x_ref, dpre_ref, act_ref, ga_ref = refs[4 * k : 4 * k + 4]
-        down[...] = inner_rows(x_ref[...], dpre_ref[...])
-        up[...] = inner_rows(act_ref[...], ga_ref[...])
+        for copy in copies[4 * k : 4 * k + 4]:
+            copy.wait()
+        x, dpre, act, ga = rooms[4 * k : 4 * k + 4]
+        down[...] = inner_rows(x[...], dpre[...])
+        up[...] = inner_rows(act[...], ga[...])
         top, middle, end = k * rows, k * rows + half, (k + 1) * rows
-        for ref, side in ((keep_ref, core), (send_ref, 1 - core)):
+        for ref, side in ((send, 1 - core), (keep, core)):
             for pair in range(pairs):
                 device = 2 * pair + side
                 at = pl.multiple_of(device * rows, rows)
-                ref[pair, top:middle, :small] = down[pl.ds(at, half), :].astype(ref.dtype)
-                ref[pair, top:middle, small:] = down[pl.ds(at + half, half), :].astype(ref.dtype)
+                ref[pair, top:middle, :small] = down[pl.ds(at, half), :].astype(LOW)
+                ref[pair, top:middle, small:] = down[pl.ds(at + half, half), :].astype(LOW)
                 ref[pair, middle:end, :] = up[
                     pl.ds(pl.multiple_of(device * half, half), half), :
-                ].astype(ref.dtype)
+                ].astype(LOW)
+    outs = [
+        pltpu.make_async_copy(send, send_ref, sem_out.at[0]),
+        pltpu.make_async_copy(keep, keep_ref, sem_out.at[1]),
+    ]
+    for copy in outs:
+        copy.start()
+    for copy in outs:
+        copy.wait()
 
 
 def adapter_grads(given, core):
@@ -935,22 +966,22 @@
         both = jnp.concatenate(layers, 1).reshape(n_all // 2, 2, 2 * rows, width)
         first = core == 0
         keep, send = jnp.where(first, both[:, 0], both[:, 1]), jnp.where(first, both[:, 1], both[:, 0])
-        return keep, send.astype(LOW)
+        return keep.astype(LOW), send.astype(LOW)
     shape = (n_all // 2, 2 * rows, width)
-    vmem = pl.BlockSpec(memory_space=pltpu.VMEM)
+    hbm = pl.BlockSpec(memory_space=pl.ANY)
+    loads = list(given[0]) + list(given[1])
     return pl.pallas_call(
         adapter_grad_kernel,
-        out_shape=[jax.ShapeDtypeStruct(shape, F32), jax.ShapeDtypeStruct(shape, LOW)],
-        in_specs=[pl.BlockSpec(memory_space=pltpu.SMEM)] + [vmem] * 8,
-        out_specs=[vmem] * 2,
-        scratch_shapes=[pltpu.VMEM((width, small), F32), pltpu.VMEM((small, width), F32)],
-        compiler_params=pltpu.CompilerParams(vmem_limit_bytes=40 * MIB),
-        cost_estimate=pl.CostEstimate(
-            flops=8 * given[0][0].shape[0] * width * small,
-            bytes_accessed=16 * MIB,
-            transcendentals=0,
-        ),
-    )(core.reshape(1).astype(jnp.int32), *given[0], *given[1])
+        out_shape=[jax.ShapeDtypeStruct(shape, LOW)] * 2,
+        in_specs=[pl.BlockSpec(memory_space=pltpu.SMEM)] + [hbm] * 8,
+        out_specs=[hbm] * 2,
+        scratch_shapes=[pltpu.VMEM(v.shape, LOW) for v in loads]
+        + [pltpu.VMEM((width, small), F32), pltpu.VMEM((small, width), F32)]
+        + [pltpu.VMEM(shape, LOW), pltpu.VMEM(shape, LOW)]
+        + [pltpu.SemaphoreType.DMA((8,)), pltpu.SemaphoreType.DMA((2,))],
+        compiler_params=pltpu.CompilerParams(vmem_limit_bytes=60 * MIB),
+        cost_estimate=pl.CostEstimate(flops=0, bytes_accessed=0, transcendentals=0),
+    )(core.reshape(1).astype(jnp.int32), *loads)
 
 
 def head_kernel(n_blocks, *refs):
@@ -1029,15 +1060,16 @@
     return list(results[:count]), list(results[count:])
 
 
-def adapters_plane(held, seq, enc):
+def adapters_plane(keep, came, seq, enc):
     n_seq, n_enc = lax.axis_size("seq"), lax.axis_size("enc")
     near = n_seq // 4
-    rows, width = held.shape[1:]
-    held = held.reshape(4, near, n_enc // 2, rows, width)
+    rows, width = keep.shape[1:]
 
     def block(s_off, e_off):
         start = (0, (seq & (near - 1)) ^ s_off, (enc >> 1) ^ (e_off >> 1), 0, 0)
-        return lax.dynamic_slice(held, start, (4, 1, 1, rows, width))[:, 0, 0]
+        parts = [v.reshape(4, near, n_enc // 2, rows, width) for v in (keep, came)]
+        parts = [lax.dynamic_slice(v, start, (4, 1, 1, rows, width))[:, 0, 0] for v in parts]
+        return parts[0].astype(F32) + parts[1].astype(F32)
 
     return [block(0, 0)] + [flip_both(block(s, e).astype(LOW), s, e) for s, e in plane_offsets()[1:]]
 
@@ -1142,12 +1174,16 @@
     pair_out = pair_split(packed, core)
 
     ids = [all_ids[:, k] for k in range(3)]
-
-    slow = slow_flips(strip)
+    strip, pair_out, *ids = gate([strip, pair_out] + ids)
+
+    slow, slow_out = slow_flips_both(strip, pair_out)
     for mask in bits("seq"):
         gains = jnp.concatenate([gains, flip(gains, "seq", mask)], 0)
-    found = [lookup(ids[0]), lookup(ids[1]), lookup(ids[2])]
-    pair_out, *slow = gate([pair_out] + slow)
+    arrived = gate([lookup(v) for v in ids] + slow + (slow_out or []))
+    found, slow, slow_out = arrived[:3], arrived[3:6], arrived[6:]
+    if not slow_out:
+        slow_out = [v[strip_rows:] for v in slow]
+        slow = [v[:strip_rows] for v in slow]
     order_seq, order_enc = jnp.arange(n_seq) ^ seq, jnp.arange(n_enc) ^ enc
     gains = jnp.take(jnp.take(gains, order_seq, axis=0), order_enc, axis=1)
     gains = gains.reshape(n_all, 14, width // n_all).transpose(1, 0, 2)
@@ -1155,27 +1191,28 @@
 
     strip_offsets, strips = near_flips(jnp.stack([strip] + slow))
     source_rows, target_rows = rows_of(found[0]), rows_of(found[1])
-    slow = slow_flips(pair_out)
-    late, *slow = gate([late] + slow)
 
     in_enc, in_dec = assemble_strips(strip_offsets, strips, 2, seq)
     encoder_in, encoder_hat = norm_start(source_rows + positions[0].astype(F32), norms, 0)
     decoder_in, decoder_hat = norm_start(target_rows + positions[1].astype(F32), norms, 3)
-    encoder_all = gather_rows(encoder_in.astype(LOW))
-    decoder_all = gather_rows(decoder_in.astype(LOW))
-    stacked = jnp.stack([pair_out] + slow)
+    across = gather_across(encoder_in.astype(LOW))
+    decoder_low, *across[1:] = gate([decoder_in.astype(LOW)] + across[1:])
+    encoder_all = jnp.concatenate(gather_pair(across), 0)
+    decoder_all = gather_rows(decoder_low)
+    stacked = jnp.stack([pair_out] + slow_out)
     singles = plane_start(stacked)
 
     triple_encoder = dense(encoder_all, in_enc).astype(LOW)
     enc_args = (triple_encoder, triple_encoder, in_strip, 2 * in_strip, source_limit, spots)
     context_enc, total_encoder = attend(*enc_args)
-    context_enc, *singles = gate([context_enc] + singles)
+    slow = slow_flips(late)
+    context_enc, *arrived = gate([context_enc] + slow + singles)
+    slow, singles = arrived[:3], arrived[3:]
     own, other, mine = plane_finish(stacked, singles, core)
     partners = [flip(v, "enc", 1) for v in mine]
-    slow = slow_flips(late)
     triple_decoder = dense(decoder_all, in_dec).astype(LOW)
     dec_args = (triple_decoder, triple_decoder, in_strip, 2 * in_strip, causal_limit, spots)
-    context_dec, total_decoder = attend(*dec_args)
+    context_dec, total_decoder = attend(*dec_args, after=[context_enc])
 
     def out_layout(pair, side):
         row = pair * pair_rows
@@ -1201,11 +1238,12 @@
     )
     query_cross = dense(causal_all, in_cross[:, :share]).astype(LOW)
 
-    encoded_all, found[2] = gate([gather_rows(encoded_low), found[2]])
-    label_rows, label_came = scatter_two([found[2][j] for j in range(n_enc)])
+    encoded_all = gather_rows(encoded_low)
     pairs_cross = dense(encoded_all, in_cross[:, share:]).astype(LOW)
     cross_args = (query_cross, pairs_cross, 0, in_strip, source_limit, spots)
     context, total_cross = attend(*cross_args)
+    context, found_label = gate([context, found[2]])
+    label_rows, label_came = scatter_two([found_label[j] for j in range(n_enc)])
     decoded_low, kept_dec = branch(
         own_parts(context), after_causal, norm_rows, 5, feeds[1], attend_out[2]
     )
@@ -1217,17 +1255,19 @@
     )
     pulled, totals = head(decoded_all, embedding)
     hats = gather_across(encoder_low) + gather_across(decoder_low)
-    results = gate(pulled + totals + hats)
+    *results, decoded_low, label_came = gate(
+        pulled + totals + hats + [decoded_all[0], label_came]
+    )
     pulled, totals, hats = results[:n_enc], results[n_enc : 2 * n_enc], results[2 * n_enc :]
     label_rows = (label_rows.astype(F32) + label_came.astype(F32)).astype(LOW)
     row_spots = enc * own_rows + jnp.arange(own_rows)
     valid = (row_spots < target_length).astype(F32)[:, None]
     picked = jnp.sum(decoded_low.astype(F32) * label_rows.astype(F32), -1, keepdims=True)
-    own_mean, far_mean = merge_enc(pulled, totals)
+    own_mean, far_mean, hats = merge_enc(pulled, totals, hats)
     half_hats = len(hats) // 2
     hats = gather_pair(hats[:half_hats]) + gather_pair(hats[half_hats:])
     far, *hats = gate([far_mean[0]] + hats)
-    encoder_hats, decoder_hats = jnp.concatenate(hats[:n_enc], 0), jnp.concatenate(hats[n_enc:], 0)
+    encoder_hats, decoder_hats = hats[:n_enc], hats[n_enc:]
     highest = jnp.maximum(own_mean[1], far_mean[1])
     log_total = highest + jnp.log(
         jnp.exp(own_mean[1] - highest) + jnp.exp(far_mean[1] - highest)
@@ -1255,9 +1295,9 @@
     )
     spread = swap_blocks(spread)
     x, dpre, act, ga = given_enc
-    spread[1], dpre, far_causal = gate([spread[1], dpre, far_causal])
+    dpre, far_causal = gate([dpre, far_causal])
     keep, send = adapter_grads([(x, dpre, act, ga), given_dec], core)
-    held = keep + flip(send, "enc", 1).astype(F32)
+    came = flip(send, "enc", 1)
     grad_dec, spread_dec, sums_four = middle_back(
         grad_res, own_causal, far_causal, causal_in, norm_rows, 4, attend_out[1], n_enc
     )
@@ -1266,9 +1306,9 @@
         jnp.concatenate(spread, 0),
         total_encoder,
         sum_with=(encoder_hats, in_enc, encoder_hat, grad_enc),
-        after=[held, grad_dec],
-    )
-    parts = adapters_plane(held, seq, enc)
+        after=[grad_dec],
+    )
+    parts = adapters_plane(keep, came, seq, enc)
     sums_zero, *parts[1:] = gate([sums_zero] + parts[1:])
     parts = adapters_line(parts, seq)
     sums_three = attend_back(

time: 672 us -> 658 us (0.979)
  waiting for transfers between devices: 157 us -> 184 us
  other arithmetic: 68.9 us -> 44.2 us
  starting transfers between devices: 97.5 us -> 84.7 us
    all_gather x2, waiting for transfers between devices: 0.01 us -> 18.6 us  [gather_feed(): return lax.all_gather(pack_feed(expand, reduce, down, up), everyone)]
    ppermute x87 -> x84, waiting for transfers between devices: 136 us -> 151 us  [flip(): return lax.ppermute(value, axis, [(i, i ^ mask) for i in range(count)])]
    ppermute x87 -> x84, starting transfers between devices: 84 us -> 71.5 us  [flip(): return lax.ppermute(value, axis, [(i, i ^ mask) for i in range(count)])]
    concatenate x3 -> x0, other arithmetic: 9.28 us -> none  [the longest x1 3.33 us: gather_rows(): return jnp.concatenate(gather_enc(rows_low), 0)]
    ppermute x3, waiting for transfers between devices: 14.4 us -> 6.71 us  [mixed_flip(): return lax.ppermute(value, ('seq', 'enc'), perm)]
    unnamed x224 -> x213, local copies, waits for them, and re-layouts: 30.9 us -> 24.8 us
  transfers between devices with their start and end apart: 99 -> 96, of which waited for: 34 -> 29; matrix products, arithmetic and copies ran while one was open for 21% -> 18% of each run, Pallas kernels for 24% -> 25%
where the time goes in v4:
time: 658 us; the launch traced here: 648 us
  Pallas kernels  204 us (31%)
  waiting for transfers between devices  184 us (28%)
  local copies, waits for them, and re-layouts  86.3 us (13%)
  starting transfers between devices  84.7 us (13%)
  other arithmetic  44.2 us (7%)
  matrix products  21 us (3%)
  between operations  17.4 us (3%)
    ppermute x84, waiting for transfers between devices, flip(): return lax.ppermute(value, axis, [(i, i ^ mask) for i in range(count)])  151 us
    ppermute x84, starting transfers between devices, flip(): return lax.ppermute(value, axis, [(i, i ^ mask) for i in range(count)])  71.5 us
    pallas_call x3, Pallas kernels, attend_back(): pl.pallas_call(kernel, grid=(pairs, length // rows), out_shape=out, in_sp...  56 us
    gather x3, local copies, waits for them, and re-layouts, lookup(): found = jnp.take(embedding, jnp.clip(ids, 0, entries - 1), axis=0)  36.4 us
    pallas_call x1, Pallas kernels, head(): pl.pallas_call(lambda *refs: head_kernel(count, *refs), grid=(entries //...  34.2 us
    pallas_call x2, Pallas kernels, branch_back(): pl.pallas_call(lambda *refs: branch_back_kernel(first, n_parts, len(given...  30.5 us
    pallas_call x3, Pallas kernels, attend(): pl.pallas_call(attend_kernel, grid=(pairs, length // rows), out_shape=[ja...  29.1 us
    pallas_call x2, Pallas kernels, branch(): pl.pallas_call(lambda *refs: branch_kernel(first, len(parts), *refs), out...  28 us
  transfers between devices with their start and end apart: 96, of which 29 were waited for; matrix products, arithmetic and copies ran while one was open for 18% of the time, Pallas kernels for 25%

profile of v4, /device:TPU:0, one launch (start us, length us, event | category | flops | bytes accessed | tf_op | source)
XLA Modules:
  0.0 647.8 jit_solution(3082773900846385165)
XLA Ops:
  11.4 6.2 all-gather.3
  21.9 3.5 all-to-all-start
  32.5 2.6 collective-permute-start.9
  46.4 2.7 collective-permute-start.2
  50.8 11.4 %gather_fusion.2 = bf16[1024,1024]{1,0:T(8,128)(2,1)S(1)} fusion(bf16[6400,1024]{1,0:T(8,128)(2,1)} %refs_4_.2, s32[1024]{0:T(1024)S(1)} %broadcast_clamp_fusion.2), kind=kCustom, calls=%fused_computation.clone | custom fusion | bytes 4198400 | tf_op jit(solution)/shard_map/jit(_take)/gather | solution.py:1137
  62.2 12.5 %gather_fusion.3 = bf16[1024,1024]{1,0:T(8,128)(2,1)} fusion(bf16[6400,1024]{1,0:T(8,128)(2,1)} %refs_4_.2, s32[1024]{0:T(1024)S(1)} %broadcast_clamp_fusion.1), kind=kCustom, calls=%fused_computation.1.clone | custom fusion | bytes 4198400 | tf_op jit(solution)/shard_map/jit(_take)/gather | solution.py:1137
  74.8 12.5 %gather_fusion.4 = bf16[1024,1024]{1,0:T(8,128)(2,1)} fusion(bf16[6400,1024]{1,0:T(8,128)(2,1)} %refs_4_.2, s32[1024]{0:T(1024)S(1)} %broadcast_clamp_fusion), kind=kCustom, calls=%fused_computation.2.clone | custom fusion | bytes 4198400 | tf_op jit(solution)/shard_map/jit(_take)/gather | solution.py:1137
  94.0 2.7 collective-permute-done.1.refs_3_
  96.7 15.3 %collective-permute-done.3.refs_5_ = bf16[192,1536]{1,0:T(8,128)(2,1)} collective-permute-done((bf16[192,1536]{1,0:T(8,128)(2,1)}, bf16[192,1536]{1,0:T(8,128)(2,1)}, u32[]{:S(2)}, u32[]{:S(2)}) %collective-permute-start.3) | collective-permute-done | bytes 589856 | tf_op jit(solution)/shard_map/ppermute | solution.py:29
  122.2 20.1 %collective-permute-done.12 = bf16[256,1024]{1,0:T(8,128)(2,1)S(1)} collective-permute-done((bf16[256,1024]{1,0:T(8,128)(2,1)S(1)}, bf16[256,1024]{1,0:T(8,128)(2,1)S(1)}, u32[]{:S(2)}, u32[]{:S(2)}) %collective-permute-start.12) | collective-permute-done | bytes 524320 | tf_op jit(solution)/shard_map/ppermute | solution.py:29
  142.3 22.1 %collective-permute-done.6 = bf16[256,1024]{1,0:T(8,128)(2,1)S(1)} collective-permute-done((bf16[256,1024]{1,0:T(8,128)(2,1)S(1)}, bf16[256,1024]{1,0:T(8,128)(2,1)S(1)}, u32[]{:S(2)}, u32[]{:S(2)}) %collective-permute-start.6) | collective-permute-done | bytes 524320 | tf_op jit(solution)/shard_map/ppermute | solution.py:29
  171.7 13.2 %collective-permute-done.13.refs_1_ = bf16[256,1024]{1,0:T(8,128)(2,1)S(1)} collective-permute-done((bf16[256,1024]{1,0:T(8,128)(2,1)}, bf16[256,1024]{1,0:T(8,128)(2,1)S(1)}, u32[]{:S(2)}, u32[]{:S(2)}) %collective-permute-start.13) | collective-permute-done | bytes 524320 | tf_op jit(solution)/shard_map/ppermute | solution.py:29
  190.6 9.0 %collective-permute-start.20 = (bf16[128,768]{1,0:T(8,128)(2,1)S(1)}, bf16[128,768]{1,0:T(8,128)(2,1)S(1)}, u32[]{:S(2)}, u32[]{:S(2)}) collective-permute-start(bf16[128,768]{1,0:T(8,128)(2,1)S(1)} %get-tuple-element.371), channel_id=1, source_target_pairs={{0,8},{4,12},{8,0},{12,4},{16,24},{20,28},{24,16},{28,20},{1,9},{5... | collective-permute-start | bytes 589832 | tf_op jit(solution)/shard_map/ppermute | solution.py:29
  199.5 5.1 shard_map.277
  208.3 4.2 fusion.32.q_ref.k_ref.v_ref.refs_2_.refs_3_.refs_4_
  216.2 9.5 %shard_map.278 = (bf16[1024,256]{1,0:T(8,128)(2,1)}, f32[1024,256]{1,0:T(8,128)}) custom-call(s32[1024,1]{1,0:T(8,128)} %broadcast_in_dim.79.limit_ref.refs_0_, s32[1,1024]{1,0:T(1,128)} %bitcast.287, bf16[1024,768]{1,0:T(8,128)(2,1)} %fusion.32.q_ref.k_ref.v_ref.refs_2_.refs_3_.refs_4_, bf16[1024,768]{1,0:T(8,128)(2,1)} %fusion.32.q_ref.k_ref.v_ref.refs_2_.refs_3_.refs_4_, ...), custom_call_target="tpu_custom_call" | custom-call | flops 2147483648 | bytes 2097152 | tf_op jit(solution)/shard_map/pallas_call | solution.py:470
  232.5 6.7 %collective-permute-done.28.refs_4_ = bf16[4,64,1536]{2,1,0:T(8,128)(2,1)S(1)} collective-permute-done((bf16[4,64,1536]{2,1,0:T(8,128)(2,1)}, bf16[4,64,1536]{2,1,0:T(8,128)(2,1)S(1)}, u32[]{:S(2)}, u32[]{:S(2)}) %collective-permute-start.28) | collective-permute-done | bytes 786464 | tf_op jit(solution)/shard_map/ppermute | solution.py:163
  239.2 5.0 fusion.35.q_ref.k_ref.v_ref.refs_2_.refs_3_.refs_4_
  244.2 9.7 %shard_map.280 = (bf16[1024,256]{1,0:T(8,128)(2,1)}, f32[1024,256]{1,0:T(8,128)}) custom-call(s32[1024,1]{1,0:T(8,128)} %bitcast.269, s32[1,1024]{1,0:T(1,128)} %bitcast.288, bf16[1024,768]{1,0:T(8,128)(2,1)} %fusion.35.q_ref.k_ref.v_ref.refs_2_.refs_3_.refs_4_, bf16[1024,768]{1,0:T(8,128)(2,1)} %fusion.35.q_ref.k_ref.v_ref.refs_2_.refs_3_.refs_4_, ...), custom_call_target="tpu_custom_call" | custom-call | flops 2147483648 | bytes 2097152 | tf_op jit(solution)/shard_map/pallas_call | solution.py:470
  258.5 5.1 shard_map.281
  264.5 3.5 collective-permute-done.26
  274.5 14.0 %shard_map.283 = (f32[256,1024]{1,0:T(8,128)}, bf16[256,1024]{1,0:T(8,128)(2,1)}, f32[256,4096]{1,0:T(8,128)}, bf16[256,512]{1,0:T(8,128)(2,1)}, f32[256,512]{1,...) custom-call(bf16[256,256]{1,0:T(8,128)(2,1)} %get-tuple-element.383.refs_0_, bf16[256,256]{1,0:T(8,128)(2,1)} %copy-done.68, ...), custom_call_target="tpu_custom_call" | custom-call | flops 5368709120 | bytes 23068672 | tf_op jit(solution)/shard_map/pallas_call | solution.py:764
  289.7 24.8 %collective-permute-done.41 = bf16[256,1024]{1,0:T(8,128)(2,1)} collective-permute-done((bf16[256,1024]{1,0:T(8,128)(2,1)}, bf16[256,1024]{1,0:T(8,128)(2,1)}, u32[]{:S(2)}, u32[]{:S(2)}) %collective-permute-start.41) | collective-permute-done | bytes 524320 | tf_op jit(solution)/shard_map/ppermute | solution.py:29
  314.7 3.8 shard_map.282
  318.5 3.1 fusion.41.q_ref.refs_2_
  321.6 3.6 fusion.38.k_ref.v_ref.refs_3_.refs_4_
  325.2 9.8 %shard_map.284 = (bf16[1024,256]{1,0:T(8,128)(2,1)}, f32[1024,256]{1,0:T(8,128)}) custom-call(s32[1024,1]{1,0:T(8,128)} %broadcast_in_dim.79.limit_ref.refs_0_, s32[1,1024]{1,0:T(1,128)} %bitcast.289, bf16[1024,256]{1,0:T(8,128)(2,1)} %fusion.41.q_ref.refs_2_, bf16[1024,512]{1,0:T(8,128)(2,1)} %fusion.38.k_ref.v_ref.refs_3_.refs_4_, ...), custom_call_target="tpu_custom_call" | custom-call | flops 2147483648 | bytes 2097152 | tf_op jit(solution)/shard_map/pallas_call | solution.py:470
  343.1 18.6 %all-gather.9.cloned.1.call-done = bf16[9216,1024]{1,0:T(8,128)(2,1)} async-done(((bf16[288,1024]{1,0:T(8,128)(2,1)}), bf16[9216,1024]{1,0:T(8,128)(2,1)}) %all-gather.9.cloned.1.call-update) | async-done | bytes 18874384 | tf_op jit(solution)/shard_map/all_gather | solution.py:630
  362.4 14.0 %shard_map.286 = (f32[256,1024]{1,0:T(8,128)}, bf16[256,1024]{1,0:T(8,128)(2,1)}, f32[256,4096]{1,0:T(8,128)}, bf16[256,512]{1,0:T(8,128)(2,1)}, f32[256,512]{1,...) custom-call(bf16[256,256]{1,0:T(8,128)(2,1)} %get-tuple-element.379.refs_0_, bf16[256,256]{1,0:T(8,128)(2,1)} %copy-done.71, ...), custom_call_target="tpu_custom_call" | custom-call | flops 5368709120 | bytes 23068672 | tf_op jit(solution)/shard_map/pallas_call | solution.py:764
  378.8 12.7 %collective-permute-done.49.refs_2_ = bf16[256,1024]{1,0:T(8,128)(2,1)S(1)} collective-permute-done((bf16[256,1024]{1,0:T(8,128)(2,1)}, bf16[256,1024]{1,0:T(8,128)(2,1)S(1)}, u32[]{:S(2)}, u32[]{:S(2)}) %collective-permute-start.49) | collective-permute-done | bytes 524320 | tf_op jit(solution)/shard_map/ppermute | solution.py:29
  396.3 34.2 %shard_map.289 = (bf16[256,1024]{1,0:T(8,128)(2,1)}, bf16[256,1024]{1,0:T(8,128)(2,1)}, bf16[256,1024]{1,0:T(8,128)(2,1)}, bf16[256,1024]{1,0:T(8,128)(2,1)}, f3...) custom-call(bf16[256,1024]{1,0:T(8,128)(2,1)} %get-tuple-element.182.refs_0_.refs_12_, ...), custom_call_target="tpu_custom_call" | custom-call | flops 26843545600 | bytes 13107200 | tf_op jit(solution)/shard_map/pallas_call | solution.py:1041
  444.7 2.9 fusion.80
  447.6 2.5 add_divide_fusion.refs_0_
  450.1 4.7 collective-permute-done.59.refs_0_
  454.8 15.4 %shard_map.293 = (f32[256,1024]{1,0:T(8,128)}, f32[4,1024]{1,0:T(4,128)}, bf16[256,512]{1,0:T(8,128)(2,1)}, bf16[256,1024]{1,0:T(8,128)(2,1)}, bf16[256,256]{1,0...) custom-call(f32[256,1024]{1,0:T(8,128)} %add_divide_fusion.refs_0_, ...), custom_call_target="tpu_custom_call" | custom-call | flops 5368709120 | bytes 23068672 | tf_op jit(solution)/shard_map/pallas_call | solution.py:858
  472.2 4.1 collective-permute-done.66
  479.3 17.4 %shard_map.294 = bf16[1024,768]{1,0:T(8,128)(2,1)} custom-call(s32[1024,1]{1,0:T(8,128)} %broadcast_in_dim.79.limit_ref.refs_0_, s32[1,1024]{1,0:T(1,128)} %bitcast.290, bf16[1024,256]{1,0:T(8,128)(2,1)} %fusion.41.q_ref.refs_2_, bf16[1024,512]{1,0:T(8,128)(2,1)} %fusion.38.k_ref.v_ref.refs_3_.refs_4_, bf16[1024,512]{1,0:T(8,128)(2,1)} %fusion.38.k_ref.v_ref.refs_3_.refs_4_, ...), custom_call_target="tpu_custom_call" | custom-call | flops 5368709120 | bytes 4194304 | tf_op jit(solution)/shard_map/pallas_call | solution.py:594
  496.6 2.5 fusion.127
  506.8 11.7 %collective-permute-done.69.refs_1_ = bf16[256,1024]{1,0:T(8,128)(2,1)S(1)} collective-permute-done((bf16[256,1024]{1,0:T(8,128)(2,1)S(1)}, bf16[256,1024]{1,0:T(8,128)(2,1)S(1)}, u32[]{:S(2)}, u32[]{:S(2)}) %collective-permute-start.69) | collective-permute-done | bytes 524320 | tf_op jit(solution)/shard_map/ppermute | solution.py:29
  519.3 15.0 %shard_map.295 = (f32[256,1024]{1,0:T(8,128)}, f32[4,1024]{1,0:T(4,128)}, bf16[256,512]{1,0:T(8,128)(2,1)}, bf16[256,1024]{1,0:T(8,128)(2,1)}, bf16[256,256]{1,0...) custom-call(f32[256,1024]{1,0:T(8,128)} %get-tuple-element.354.refs_0_, ...), custom_call_target="tpu_custom_call" | custom-call | flops 5368709120 | bytes 23068672 | tf_op jit(solution)/shard_map/pallas_call | solution.py:858
  535.2 5.3 shard_map.297
  558.0 19.2 %shard_map.299.refs_0_ = f32[2,1024]{1,0:T(2,128)} custom-call(s32[1024,1]{1,0:T(8,128)} %broadcast_in_dim.79.limit_ref.refs_0_, s32[1,1024]{1,0:T(1,128)} %bitcast.291, bf16[1024,768]{1,0:T(8,128)(2,1)} %fusion.32.q_ref.k_ref.v_ref.refs_2_.refs_3_.refs_4_, bf16[1024,768]{1,0:T(8,128)(2,1)} %fusion.32.q_ref.k_ref.v_ref.refs_2_.refs_3_.refs_4_, ...), custom_call_target="tpu_custom_call" | custom-call | flops 5368709120 | bytes 4194304 | tf_op jit(solution)/shard_map/pallas_call | solution.py:594
  577.2 3.4 collective-permute-done.79.refs_3_
  583.7 6.5 %collective-permute-start.84 = (bf16[64,1024]{1,0:T(8,128)(2,1)S(1)}, bf16[64,1024]{1,0:T(8,128)(2,1)S(1)}, u32[]{:S(2)}, u32[]{:S(2)}) collective-permute-start(bf16[64,1024]{1,0:T(8,128)(2,1)S(1)} %get-tuple-element.366), channel_id=1, source_target_pairs={{0,16},{4,20},{8,24},{12,28},{16,0},{20,4},{24,8},{28,12},{1,17},{... | collective-permute-start | bytes 393224 | tf_op jit(solution)/shard_map/ppermute | solution.py:29
  591.6 19.4 %shard_map.301.refs_0_ = f32[2,1024]{1,0:T(2,128)} custom-call(s32[1024,1]{1,0:T(8,128)} %bitcast.270, s32[1,1024]{1,0:T(1,128)} %bitcast.292, bf16[1024,768]{1,0:T(8,128)(2,1)} %fusion.35.q_ref.k_ref.v_ref.refs_2_.refs_3_.refs_4_, bf16[1024,768]{1,0:T(8,128)(2,1)} %fusion.35.q_ref.k_ref.v_ref.refs_2_.refs_3_.refs_4_, ...), custom_call_target="tpu_custom_call" | custom-call | flops 5368709120 | bytes 4194304 | tf_op jit(solution)/shard_map/pallas_call | solution.py:594
  613.2 2.6 shard_map.303
  622.4 2.6 collective-permute-done.89
  629.5 3.8 collective-permute-done.91
  (525 shorter events, 170.0 us)
Async XLA Ops:
  7.2 266.6 %all-gather.7.cloned.1.call-start = ((), (), s32[]{:S(2)}) async-start(), calls=%async_computation.1 | async-start | bytes 19464192 | tf_op jit(solution)/shard_map/all_gather | solution.py:630
  10.5 351.1 %all-gather.9.cloned.1.call-start = ((), (), s32[]{:S(2)}) async-start(), calls=%async_computation.2 | async-start | bytes 19464192 | tf_op jit(solution)/shard_map/all_gather | solution.py:630
  21.9 19.5 %all-to-all-start = ((bf16[4,32,2304]{2,1,0:T(8,128)(2,1)}), bf16[4,32,2304]{2,1,0:T(8,128)(2,1)S(1)}, u32[]{:S(2)}, u32[]{:S(2)}) async-start(bf16[4,32,2304]{2,1,0:T(8,128)(2,1)} %reshape.445), calls=%async_computation | async-start | bytes 1179648 | tf_op jit(solution)/shard_map/all_to_all | solution.py:1168
  25.5 15.1 %collective-permute-start = (bf16[32,1536]{1,0:T(8,128)(2,1)S(1)}, bf16[32,1536]{1,0:T(8,128)(2,1)S(1)}, u32[]{:S(2)}, u32[]{:S(2)}) collective-permute-start(bf16[32,1536]{1,0:T(8,128)(2,1)S(1)} %broadcast_select_fusion.2), channel_id=1, source_target_pairs={{0,1},{1,0},{2,3},{3,2},{4,5},{5,4},{6,7},{7,6},{8,9},{9,8},{10,11... | collective-permute-start | bytes 294920 | tf_op jit(solution)/shard_map/ppermute | solution.py:29
  45.7 51.1 %collective-permute-start.1 = (bf16[192,1536]{1,0:T(8,128)(2,1)}, bf16[192,1536]{1,0:T(8,128)(2,1)S(1)}, u32[]{:S(2)}, u32[]{:S(2)}) collective-permute-start(bf16[192,1536]{1,0:T(8,128)(2,1)} %constant_dynamic-update-slice_fusion), channel_id=1, source_target_pairs={{0,8},{4,12},{8,0},{12,4},{16,24},{20,28},{24,16},{28,20},{1,9},{5... | collective-permute-start | bytes 1769480 | tf_op jit(solution)/shard_map/ppermute | solution.py:29
  46.4 50.3 %collective-permute-start.2 = (bf16[192,1536]{1,0:T(8,128)(2,1)}, bf16[192,1536]{1,0:T(8,128)(2,1)S(1)}, u32[]{:S(2)}, u32[]{:S(2)}) collective-permute-start(bf16[192,1536]{1,0:T(8,128)(2,1)} %constant_dynamic-update-slice_fusion), channel_id=1, source_target_pairs={{0,16},{4,20},{8,24},{12,28},{16,0},{20,4},{24,8},{28,12},{1,17},{... | collective-permute-start | bytes 1769480 | tf_op jit(solution)/shard_map/ppermute | solution.py:29
  49.2 62.9 %collective-permute-start.3 = (bf16[192,1536]{1,0:T(8,128)(2,1)}, bf16[192,1536]{1,0:T(8,128)(2,1)}, u32[]{:S(2)}, u32[]{:S(2)}) collective-permute-start(bf16[192,1536]{1,0:T(8,128)(2,1)} %constant_dynamic-update-slice_fusion), channel_id=1, source_target_pairs={{0,24},{4,28},{8,16},{12,20},{16,8},{20,12},{24,0},{28,4},{1,25},{... | collective-permute-start | bytes 1769480 | tf_op jit(solution)/shard_map/ppermute | solution.py:29
  116.3 26.1 %collective-permute-start.12 = (bf16[256,1024]{1,0:T(8,128)(2,1)S(1)}, bf16[256,1024]{1,0:T(8,128)(2,1)S(1)}, u32[]{:S(2)}, u32[]{:S(2)}) collective-permute-start(bf16[256,1024]{1,0:T(8,128)(2,1)S(1)} %fusion.51), channel_id=1, source_target_pairs={{0,2},{1,3},{2,0},{3,1},{4,6},{5,7},{6,4},{7,5},{8,10},{9,11},{10,... | collective-permute-start | bytes 1572872 | tf_op jit(solution)/shard_map/ppermute | solution.py:29
  118.4 46.1 %collective-permute-start.6 = (bf16[256,1024]{1,0:T(8,128)(2,1)S(1)}, bf16[256,1024]{1,0:T(8,128)(2,1)S(1)}, u32[]{:S(2)}, u32[]{:S(2)}) collective-permute-start(bf16[256,1024]{1,0:T(8,128)(2,1)S(1)} %fusion.53), channel_id=1, source_target_pairs={{0,2},{1,3},{2,0},{3,1},{4,6},{5,7},{6,4},{7,5},{8,10},{9,11},{10,... | collective-permute-start | bytes 1572872 | tf_op jit(solution)/shard_map/ppermute | solution.py:29
  120.1 70.5 %collective-permute-start.17 = (bf16[4,128,1536]{2,1,0:T(8,128)(2,1)S(1)}, bf16[4,128,1536]{2,1,0:T(8,128)(2,1)}, u32[]{:S(2)}, u32[]{:S(2)}) collective-permute-start(bf16[4,128,1536]{2,1,0:T(8,128)(2,1)S(1)} %pad_maximum_fusion.refs_1_), channel_id=1, source_target_pairs={{0,4},{4,0},{8,12},{12,8},{16,20},{20,16},{24,28},{28,24},{1,5},{5... | collective-permute-start | bytes 4718600 | tf_op jit(solution)/shard_map/ppermute | solution.py:29
  169.2 15.8 %collective-permute-start.13 = (bf16[256,1024]{1,0:T(8,128)(2,1)}, bf16[256,1024]{1,0:T(8,128)(2,1)S(1)}, u32[]{:S(2)}, u32[]{:S(2)}) collective-permute-start(bf16[256,1024]{1,0:T(8,128)(2,1)} %get-tuple-element.346), channel_id=1, source_target_pairs={{0,2},{1,3},{2,0},{3,1},{4,6},{5,7},{6,4},{7,5},{8,10},{9,11},{10,... | collective-permute-start | bytes 1572872 | tf_op jit(solution)/shard_map/ppermute | solution.py:29
  170.7 35.2 %collective-permute-start.18 = (bf16[256,1024]{1,0:T(8,128)(2,1)}, bf16[256,1024]{1,0:T(8,128)(2,1)}, u32[]{:S(2)}, u32[]{:S(2)}) collective-permute-start(bf16[256,1024]{1,0:T(8,128)(2,1)} %get-tuple-element.346), channel_id=1, source_target_pairs={{0,1},{1,0},{2,3},{3,2},{4,5},{5,4},{6,7},{7,6},{8,9},{9,8},{10,11... | collective-permute-start | bytes 1572872 | tf_op jit(solution)/shard_map/ppermute | solution.py:29
  185.8 21.1 %collective-permute-start.19 = (bf16[256,1024]{1,0:T(8,128)(2,1)}, bf16[256,1024]{1,0:T(8,128)(2,1)S(1)}, u32[]{:S(2)}, u32[]{:S(2)}) collective-permute-start(bf16[256,1024]{1,0:T(8,128)(2,1)} %get-tuple-element.162), channel_id=1, source_target_pairs={{0,1},{1,0},{2,3},{3,2},{4,5},{5,4},{6,7},{7,6},{8,9},{9,8},{10,11... | collective-permute-start | bytes 1572872 | tf_op jit(solution)/shard_map/ppermute | solution.py:29
  186.8 38.9 %collective-permute-start.23 = (bf16[4,64,1536]{2,1,0:T(8,128)(2,1)S(1)}, bf16[4,64,1536]{2,1,0:T(8,128)(2,1)S(1)}, u32[]{:S(2)}, u32[]{:S(2)}) collective-permute-start(bf16[4,64,1536]{2,1,0:T(8,128)(2,1)S(1)} %pad_maximum_fusion.1.refs_1_), channel_id=1, source_target_pairs={{0,4},{1,3},{2,6},{3,1},{4,0},{5,7},{6,2},{7,5},{8,12},{9,11},{10,... | collective-permute-start | bytes 2359304 | tf_op jit(solution)/shard_map/ppermute | solution.py:163
  188.4 37.4 %collective-permute-start.24 = (bf16[4,64,1536]{2,1,0:T(8,128)(2,1)S(1)}, bf16[4,64,1536]{2,1,0:T(8,128)(2,1)S(1)}, u32[]{:S(2)}, u32[]{:S(2)}) collective-permute-start(bf16[4,64,1536]{2,1,0:T(8,128)(2,1)S(1)} %pad_maximum_fusion.1.refs_1_), channel_id=1, source_target_pairs={{0,2},{1,5},{2,0},{3,7},{4,6},{5,1},{6,4},{7,3},{8,10},{9,13},{10,... | collective-permute-start | bytes 2359304 | tf_op jit(solution)/shard_map/ppermute | solution.py:163
  190.6 21.9 %collective-permute-start.20 = (bf16[128,768]{1,0:T(8,128)(2,1)S(1)}, bf16[128,768]{1,0:T(8,128)(2,1)S(1)}, u32[]{:S(2)}, u32[]{:S(2)}) collective-permute-start(bf16[128,768]{1,0:T(8,128)(2,1)S(1)} %get-tuple-element.371), channel_id=1, source_target_pairs={{0,8},{4,12},{8,0},{12,4},{16,24},{20,28},{24,16},{28,20},{1,9},{5... | collective-permute-start | bytes 589832 | tf_op jit(solution)/shard_map/ppermute | solution.py:29
  205.9 19.8 %collective-permute-start.21 = (bf16[128,768]{1,0:T(8,128)(2,1)S(1)}, bf16[128,768]{1,0:T(8,128)(2,1)S(1)}, u32[]{:S(2)}, u32[]{:S(2)}) collective-permute-start(bf16[128,768]{1,0:T(8,128)(2,1)S(1)} %get-tuple-element.371), channel_id=1, source_target_pairs={{0,16},{4,20},{8,24},{12,28},{16,0},{20,4},{24,8},{28,12},{1,17},{... | collective-permute-start | bytes 589832 | tf_op jit(solution)/shard_map/ppermute | solution.py:29
  206.8 20.7 %collective-permute-start.15 = (bf16[256,1024]{1,0:T(8,128)(2,1)}, bf16[256,1024]{1,0:T(8,128)(2,1)}, u32[]{:S(2)}, u32[]{:S(2)}) collective-permute-start(bf16[256,1024]{1,0:T(8,128)(2,1)} %get-tuple-element.157), channel_id=1, source_target_pairs={{0,2},{1,3},{2,0},{3,1},{4,6},{5,7},{6,4},{7,5},{8,10},{9,11},{10,... | collective-permute-start | bytes 1572872 | tf_op jit(solution)/shard_map/ppermute | solution.py:29
  231.3 24.7 %collective-permute-start.29 = (bf16[4,64,1536]{2,1,0:T(8,128)(2,1)S(1)}, bf16[4,64,1536]{2,1,0:T(8,128)(2,1)S(1)}, u32[]{:S(2)}, u32[]{:S(2)}) collective-permute-start(bf16[4,64,1536]{2,1,0:T(8,128)(2,1)S(1)} %pad_maximum_fusion.1.refs_1_), channel_id=1, source_target_pairs={{0,1},{1,0},{2,3},{3,2},{4,5},{5,4},{6,7},{7,6},{8,9},{9,8},{10,11... | collective-permute-start | bytes 2359304 | tf_op jit(solution)/shard_map/ppermute | solution.py:29
  231.3 26.1 %collective-permute-start.30 = (bf16[4,64,1536]{2,1,0:T(8,128)(2,1)}, bf16[4,64,1536]{2,1,0:T(8,128)(2,1)S(1)}, u32[]{:S(2)}, u32[]{:S(2)}) collective-permute-start(bf16[4,64,1536]{2,1,0:T(8,128)(2,1)} %get-tuple-element.167.refs_2_), channel_id=1, source_target_pairs={{0,1},{1,0},{2,3},{3,2},{4,5},{5,4},{6,7},{7,6},{8,9},{9,8},{10,11... | collective-permute-start | bytes 2359304 | tf_op jit(solution)/shard_map/ppermute | solution.py:29
  232.5 25.0 %collective-permute-start.31 = (bf16[4,64,1536]{2,1,0:T(8,128)(2,1)S(1)}, bf16[4,64,1536]{2,1,0:T(8,128)(2,1)S(1)}, u32[]{:S(2)}, u32[]{:S(2)}) collective-permute-start(bf16[4,64,1536]{2,1,0:T(8,128)(2,1)S(1)} %copy-done.5), channel_id=1, source_target_pairs={{0,1},{1,0},{2,3},{3,2},{4,5},{5,4},{6,7},{7,6},{8,9},{9,8},{10,11... | collective-permute-start | bytes 2359304 | tf_op jit(solution)/shard_map/ppermute | solution.py:29
  239.2 19.0 %collective-permute-start.32 = (bf16[4,64,1536]{2,1,0:T(8,128)(2,1)S(1)}, bf16[4,64,1536]{2,1,0:T(8,128)(2,1)S(1)}, u32[]{:S(2)}, u32[]{:S(2)}) collective-permute-start(bf16[4,64,1536]{2,1,0:T(8,128)(2,1)S(1)} %collective-permute-done.28.refs_4_), channel_id=1, source_target_pairs={{0,1},{1,0},{2,3},{3,2},{4,5},{5,4},{6,7},{7,6},{8,9},{9,8},{10,11... | collective-permute-start | bytes 2359304 | tf_op jit(solution)/shard_map/ppermute | solution.py:29
  257.6 57.1 %collective-permute-start.36 = (bf16[4,128,768]{2,1,0:T(8,128)(2,1)S(1)}, bf16[4,128,768]{2,1,0:T(8,128)(2,1)}, u32[]{:S(2)}, u32[]{:S(2)}) collective-permute-start(bf16[4,128,768]{2,1,0:T(8,128)(2,1)S(1)} %pad_maximum_fusion.2.refs_1_), channel_id=1, source_target_pairs={{0,4},{4,0},{8,12},{12,8},{16,20},{20,16},{24,28},{28,24},{1,5},{5... | collective-permute-start | bytes 2359304 | tf_op jit(solution)/shard_map/ppermute | solution.py:29
  258.3 15.1 %collective-permute-start.37 = (bf16[256,256]{1,0:T(8,128)(2,1)S(1)}, bf16[256,256]{1,0:T(8,128)(2,1)S(1)}, u32[]{:S(2)}, u32[]{:S(2)}) collective-permute-start(bf16[256,256]{1,0:T(8,128)(2,1)S(1)} %get-tuple-element.382), channel_id=1, source_target_pairs={{0,1},{1,0},{2,3},{3,2},{4,5},{5,4},{6,7},{7,6},{8,9},{9,8},{10,11... | collective-permute-start | bytes 393224 | tf_op jit(solution)/shard_map/ppermute | solution.py:29
  272.0 17.2 %collective-permute-start.34 = (bf16[256,1024]{1,0:T(8,128)(2,1)}, bf16[256,1024]{1,0:T(8,128)(2,1)}, u32[]{:S(2)}, u32[]{:S(2)}) collective-permute-start(bf16[256,1024]{1,0:T(8,128)(2,1)} %get-tuple-element.344), channel_id=1, source_target_pairs={{0,2},{1,3},{2,0},{3,1},{4,6},{5,7},{6,4},{7,5},{8,10},{9,11},{10,... | collective-permute-start | bytes 1572872 | tf_op jit(solution)/shard_map/ppermute | solution.py:29
  288.5 26.1 %collective-permute-start.41 = (bf16[256,1024]{1,0:T(8,128)(2,1)}, bf16[256,1024]{1,0:T(8,128)(2,1)}, u32[]{:S(2)}, u32[]{:S(2)}) collective-permute-start(bf16[256,1024]{1,0:T(8,128)(2,1)} %get-tuple-element.174), channel_id=1, source_target_pairs={{0,2},{1,3},{2,0},{3,1},{4,6},{5,7},{6,4},{7,5},{8,10},{9,11},{10,... | collective-permute-start | bytes 1572872 | tf_op jit(solution)/shard_map/ppermute | solution.py:29
  289.2 29.3 %collective-permute-start.33 = (bf16[256,1024]{1,0:T(8,128)(2,1)}, bf16[256,1024]{1,0:T(8,128)(2,1)}, u32[]{:S(2)}, u32[]{:S(2)}) collective-permute-start(bf16[256,1024]{1,0:T(8,128)(2,1)} %get-tuple-element.344), channel_id=1, source_target_pairs={{0,1},{1,0},{2,3},{3,2},{4,5},{5,4},{6,7},{7,6},{8,9},{9,8},{10,11... | collective-permute-start | bytes 1572872 | tf_op jit(solution)/shard_map/ppermute | solution.py:29
  289.2 29.3 %collective-permute-start.35 = (bf16[256,1024]{1,0:T(8,128)(2,1)}, bf16[256,1024]{1,0:T(8,128)(2,1)}, u32[]{:S(2)}, u32[]{:S(2)}) collective-permute-start(bf16[256,1024]{1,0:T(8,128)(2,1)} %collective-permute-done.34), channel_id=1, source_target_pairs={{0,1},{1,0},{2,3},{3,2},{4,5},{5,4},{6,7},{7,6},{8,9},{9,8},{10,11... | collective-permute-start | bytes 1572872 | tf_op jit(solution)/shard_map/ppermute | solution.py:29
  289.7 31.8 %collective-permute-start.40 = (bf16[256,1024]{1,0:T(8,128)(2,1)}, bf16[256,1024]{1,0:T(8,128)(2,1)}, u32[]{:S(2)}, u32[]{:S(2)}) collective-permute-start(bf16[256,1024]{1,0:T(8,128)(2,1)} %get-tuple-element.174), channel_id=1, source_target_pairs={{0,1},{1,0},{2,3},{3,2},{4,5},{5,4},{6,7},{7,6},{8,9},{9,8},{10,11... | collective-permute-start | bytes 1572872 | tf_op jit(solution)/shard_map/ppermute | solution.py:29
  338.5 23.1 %collective-permute-start.43 = (bf16[256,256]{1,0:T(8,128)(2,1)}, bf16[256,256]{1,0:T(8,128)(2,1)S(1)}, u32[]{:S(2)}, u32[]{:S(2)}) collective-permute-start(bf16[256,256]{1,0:T(8,128)(2,1)} %get-tuple-element.378), channel_id=1, source_target_pairs={{0,1},{1,0},{2,3},{3,2},{4,5},{5,4},{6,7},{7,6},{8,9},{9,8},{10,11... | collective-permute-start | bytes 393224 | tf_op jit(solution)/shard_map/ppermute | solution.py:29
  338.5 23.1 %collective-permute-start.44 = (bf16[256,256]{1,0:T(8,128)(2,1)}, bf16[256,256]{1,0:T(8,128)(2,1)S(1)}, u32[]{:S(2)}, u32[]{:S(2)}) collective-permute-start(bf16[256,256]{1,0:T(8,128)(2,1)} %get-tuple-element.377), channel_id=1, source_target_pairs={{0,2},{1,3},{2,0},{3,1},{4,6},{5,7},{6,4},{7,5},{8,10},{9,11},{10,... | collective-permute-start | bytes 393224 | tf_op jit(solution)/shard_map/ppermute | solution.py:29
  339.2 22.5 %collective-permute-start.45 = (bf16[256,256]{1,0:T(8,128)(2,1)}, bf16[256,256]{1,0:T(8,128)(2,1)S(1)}, u32[]{:S(2)}, u32[]{:S(2)}) collective-permute-start(bf16[256,256]{1,0:T(8,128)(2,1)} %get-tuple-element.376), channel_id=1, source_target_pairs={{0,3},{1,2},{2,1},{3,0},{4,7},{5,6},{6,5},{7,4},{8,11},{9,10},{10,... | collective-permute-start | bytes 393224 | tf_op jit(solution)/shard_map/ppermute | solution.py:29
  342.4 34.0 %collective-permute-start.47 = (bf16[256,1024]{1,0:T(8,128)(2,1)}, bf16[256,1024]{1,0:T(8,128)(2,1)S(1)}, u32[]{:S(2)}, u32[]{:S(2)}) collective-permute-start(bf16[256,1024]{1,0:T(8,128)(2,1)} %fusion.50), channel_id=1, source_target_pairs={{0,2},{1,3},{2,0},{3,1},{4,6},{5,7},{6,4},{7,5},{8,10},{9,11},{10,... | collective-permute-start | bytes 1572872 | tf_op jit(solution)/shard_map/ppermute | solution.py:29
  377.2 14.3 %collective-permute-start.49 = (bf16[256,1024]{1,0:T(8,128)(2,1)}, bf16[256,1024]{1,0:T(8,128)(2,1)S(1)}, u32[]{:S(2)}, u32[]{:S(2)}) collective-permute-start(bf16[256,1024]{1,0:T(8,128)(2,1)} %get-tuple-element.181.refs_0_), channel_id=1, source_target_pairs={{0,2},{1,3},{2,0},{3,1},{4,6},{5,7},{6,4},{7,5},{8,10},{9,11},{10,... | collective-permute-start | bytes 1572872 | tf_op jit(solution)/shard_map/ppermute | solution.py:29
  394.2 36.3 %collective-permute-start.51 = (bf16[256,1024]{1,0:T(8,128)(2,1)}, bf16[256,1024]{1,0:T(8,128)(2,1)S(1)}, u32[]{:S(2)}, u32[]{:S(2)}) collective-permute-start(bf16[256,1024]{1,0:T(8,128)(2,1)} %get-tuple-element.194.refs_8_), channel_id=1, source_target_pairs={{0,2},{1,3},{2,0},{3,1},{4,6},{5,7},{6,4},{7,5},{8,10},{9,11},{10,... | collective-permute-start | bytes 1572872 | tf_op jit(solution)/shard_map/ppermute | solution.py:29
  395.9 34.7 %collective-permute-start.52 = (bf16[256,1024]{1,0:T(8,128)(2,1)}, bf16[256,1024]{1,0:T(8,128)(2,1)S(1)}, u32[]{:S(2)}, u32[]{:S(2)}) collective-permute-start(bf16[256,1024]{1,0:T(8,128)(2,1)} %get-tuple-element.195.refs_10_), channel_id=1, source_target_pairs={{0,2},{1,3},{2,0},{3,1},{4,6},{5,7},{6,4},{7,5},{8,10},{9,11},{10,... | collective-permute-start | bytes 1572872 | tf_op jit(solution)/shard_map/ppermute | solution.py:29
  440.8 14.0 %collective-permute-start.59 = (bf16[256,1024]{1,0:T(8,128)(2,1)}, bf16[256,1024]{1,0:T(8,128)(2,1)}, u32[]{:S(2)}, u32[]{:S(2)}) collective-permute-start(bf16[256,1024]{1,0:T(8,128)(2,1)} %get-tuple-element.212), channel_id=1, source_target_pairs={{0,2},{1,3},{2,0},{3,1},{4,6},{5,7},{6,4},{7,5},{8,10},{9,11},{10,... | collective-permute-start | bytes 1572872 | tf_op jit(solution)/shard_map/ppermute | solution.py:29
  441.2 13.6 %collective-permute-start.60 = (bf16[256,1024]{1,0:T(8,128)(2,1)}, bf16[256,1024]{1,0:T(8,128)(2,1)}, u32[]{:S(2)}, u32[]{:S(2)}) collective-permute-start(bf16[256,1024]{1,0:T(8,128)(2,1)} %get-tuple-element.213.refs_1_), channel_id=1, source_target_pairs={{0,1},{1,0},{2,3},{3,2},{4,5},{5,4},{6,7},{7,6},{8,9},{9,8},{10,11... | collective-permute-start | bytes 1572872 | tf_op jit(solution)/shard_map/ppermute | solution.py:29
  441.2 13.6 %collective-permute-start.61 = (bf16[256,1024]{1,0:T(8,128)(2,1)}, bf16[256,1024]{1,0:T(8,128)(2,1)}, u32[]{:S(2)}, u32[]{:S(2)}) collective-permute-start(bf16[256,1024]{1,0:T(8,128)(2,1)} %get-tuple-element.214.refs_3_), channel_id=1, source_target_pairs={{0,1},{1,0},{2,3},{3,2},{4,5},{5,4},{6,7},{7,6},{8,9},{9,8},{10,11... | collective-permute-start | bytes 1572872 | tf_op jit(solution)/shard_map/ppermute | solution.py:29
  441.7 13.1 %collective-permute-start.62 = (bf16[256,1024]{1,0:T(8,128)(2,1)}, bf16[256,1024]{1,0:T(8,128)(2,1)}, u32[]{:S(2)}, u32[]{:S(2)}) collective-permute-start(bf16[256,1024]{1,0:T(8,128)(2,1)} %get-tuple-element.215.refs_5_), channel_id=1, source_target_pairs={{0,1},{1,0},{2,3},{3,2},{4,5},{5,4},{6,7},{7,6},{8,9},{9,8},{10,11... | collective-permute-start | bytes 1572872 | tf_op jit(solution)/shard_map/ppermute | solution.py:29
  503.8 14.7 %collective-permute-start.69 = (bf16[256,1024]{1,0:T(8,128)(2,1)S(1)}, bf16[256,1024]{1,0:T(8,128)(2,1)S(1)}, u32[]{:S(2)}, u32[]{:S(2)}) collective-permute-start(bf16[256,1024]{1,0:T(8,128)(2,1)S(1)} %get-tuple-element.353), channel_id=1, source_target_pairs={{0,2},{1,3},{2,0},{3,1},{4,6},{5,7},{6,4},{7,5},{8,10},{9,11},{10,... | collective-permute-start | bytes 1572872 | tf_op jit(solution)/shard_map/ppermute | solution.py:29
  506.0 28.4 %collective-permute-start.71 = (bf16[256,1024]{1,0:T(8,128)(2,1)S(1)}, bf16[256,1024]{1,0:T(8,128)(2,1)S(1)}, u32[]{:S(2)}, u32[]{:S(2)}) collective-permute-start(bf16[256,1024]{1,0:T(8,128)(2,1)S(1)} %get-tuple-element.351), channel_id=1, source_target_pairs={{0,2},{1,3},{2,0},{3,1},{4,6},{5,7},{6,4},{7,5},{8,10},{9,11},{10,... | collective-permute-start | bytes 1572872 | tf_op jit(solution)/shard_map/ppermute | solution.py:29
  553.4 23.8 %collective-permute-start.77 = (bf16[4,64,1024]{2,1,0:T(8,128)(2,1)S(1)}, bf16[4,64,1024]{2,1,0:T(8,128)(2,1)S(1)}, u32[]{:S(2)}, u32[]{:S(2)}) collective-permute-start(bf16[4,64,1024]{2,1,0:T(8,128)(2,1)S(1)} %get-tuple-element.350), channel_id=1, source_target_pairs={{0,4},{1,5},{2,6},{3,7},{4,0},{5,1},{6,2},{7,3},{8,12},{9,13},{10,... | collective-permute-start | bytes 1572872 | tf_op jit(solution)/shard_map/ppermute | solution.py:137
  555.1 22.1 %collective-permute-start.78 = (bf16[4,64,1024]{2,1,0:T(8,128)(2,1)S(1)}, bf16[4,64,1024]{2,1,0:T(8,128)(2,1)S(1)}, u32[]{:S(2)}, u32[]{:S(2)}) collective-permute-start(bf16[4,64,1024]{2,1,0:T(8,128)(2,1)S(1)} %get-tuple-element.349), channel_id=1, source_target_pairs={{0,2},{1,3},{2,0},{3,1},{4,6},{5,7},{6,4},{7,5},{8,10},{9,11},{10,... | collective-permute-start | bytes 1572872 | tf_op jit(solution)/shard_map/ppermute | solution.py:137
  556.9 23.7 %collective-permute-start.79 = (bf16[4,64,1024]{2,1,0:T(8,128)(2,1)S(1)}, bf16[4,64,1024]{2,1,0:T(8,128)(2,1)S(1)}, u32[]{:S(2)}, u32[]{:S(2)}) collective-permute-start(bf16[4,64,1024]{2,1,0:T(8,128)(2,1)S(1)} %get-tuple-element.348), channel_id=1, source_target_pairs={{0,6},{1,7},{2,4},{3,5},{4,2},{5,3},{6,0},{7,1},{8,14},{9,15},{10,... | collective-permute-start | bytes 1572872 | tf_op jit(solution)/shard_map/ppermute | solution.py:137
  583.6 28.2 %collective-permute-start.83 = (bf16[64,1024]{1,0:T(8,128)(2,1)S(1)}, bf16[64,1024]{1,0:T(8,128)(2,1)S(1)}, u32[]{:S(2)}, u32[]{:S(2)}) collective-permute-start(bf16[64,1024]{1,0:T(8,128)(2,1)S(1)} %get-tuple-element.367), channel_id=1, source_target_pairs={{0,8},{4,12},{8,0},{12,4},{16,24},{20,28},{24,16},{28,20},{1,9},{5... | collective-permute-start | bytes 393224 | tf_op jit(solution)/shard_map/ppermute | solution.py:29
  583.7 28.1 %collective-permute-start.84 = (bf16[64,1024]{1,0:T(8,128)(2,1)S(1)}, bf16[64,1024]{1,0:T(8,128)(2,1)S(1)}, u32[]{:S(2)}, u32[]{:S(2)}) collective-permute-start(bf16[64,1024]{1,0:T(8,128)(2,1)S(1)} %get-tuple-element.366), channel_id=1, source_target_pairs={{0,16},{4,20},{8,24},{12,28},{16,0},{20,4},{24,8},{28,12},{1,17},{... | collective-permute-start | bytes 393224 | tf_op jit(solution)/shard_map/ppermute | solution.py:29
  590.3 21.6 %collective-permute-start.85 = (bf16[64,1024]{1,0:T(8,128)(2,1)S(1)}, bf16[64,1024]{1,0:T(8,128)(2,1)S(1)}, u32[]{:S(2)}, u32[]{:S(2)}) collective-permute-start(bf16[64,1024]{1,0:T(8,128)(2,1)S(1)} %get-tuple-element.365), channel_id=1, source_target_pairs={{0,24},{4,28},{8,16},{12,20},{16,8},{20,12},{24,0},{28,4},{1,25},{... | collective-permute-start | bytes 393224 | tf_op jit(solution)/shard_map/ppermute | solution.py:29
  (145 other events, 1162.5 us)
Sparse Core Ops, SparseCore 0:
  10.9 186.1 all-gather.6
  200.0 161.5 all-gather.8

commit v5 on v4

--- a/solution.py
+++ b/solution.py
@@ -486,20 +486,15 @@
     )(limit, spots, query, keys, keys, *after)
 
 
-def attend_back_step(limit_ref, spot_ref, q_ref, k_ref, v_ref, grad_ref, total_ref, out_ref, dk_sum, dv_sum):
+def attend_back_part(refs, start, count):
+    limit_ref, spot_ref, q_ref, k_ref, v_ref, grad_ref, total_ref, out_ref, dk_sum, dv_sum = refs
     pair, step = pl.program_id(0), pl.program_id(1)
-    pairs, steps = pl.num_programs(0), pl.num_programs(1)
     rows = q_ref.shape[0]
-
-    @pl.when(step == 0)
-    def _():
-        dk_sum[...] = jnp.zeros_like(dk_sum)
-        dv_sum[...] = jnp.zeros_like(dv_sum)
-
+    at = pl.ds(start, count)
     queries = head_parts(q_ref[...] * jnp.asarray(0.125, LOW))
     grads = head_parts(grad_ref[...])
-    key, value, totals = k_ref[...], v_ref[...], total_ref[...]
-    allowed = spot_ref[...] < limit_ref[...]
+    key, value, totals = k_ref[at, :], v_ref[at, :], total_ref[...]
+    allowed = spot_ref[:, at] < limit_ref[...]
     raw = [scores_of(query, key) for query in queries]
     grad_softs = [scores_of(grad, value) for grad in grads]
     grad_scores, soft_lows = [], []
@@ -509,13 +504,37 @@
         weighted = jnp.sum(soft * grad_soft, -1, keepdims=True)
         grad_scores.append((soft * (grad_soft - weighted)).astype(LOW))
         soft_lows.append(soft.astype(LOW))
-    dk_sum[...] += inner_rows(jnp.concatenate(grad_scores, 0), jnp.concatenate(queries, 0))
-    dv_sum[...] += inner_rows(jnp.concatenate(soft_lows, 0), jnp.concatenate(grads, 0))
+    dk_sum[at, :] += inner_rows(jnp.concatenate(grad_scores, 0), jnp.concatenate(queries, 0))
+    dv_sum[at, :] += inner_rows(jnp.concatenate(soft_lows, 0), jnp.concatenate(grads, 0))
     grad_query = head_join([jnp.dot(g, key, preferred_element_type=F32) for g in grad_scores])
     column = pl.multiple_of(pair * 128, 128)
     out_ref[pl.ds(pl.multiple_of(step * rows, rows), rows), pl.ds(column, 128)] = (
         grad_query * 0.125
     ).astype(LOW)
+
+
+def attend_back_step(refs, half=None):
+    out_ref, dk_sum, dv_sum = refs[-3:]
+    pair, step = pl.program_id(0), pl.program_id(1)
+    pairs, steps = pl.num_programs(0), pl.num_programs(1)
+    rows, length = refs[2].shape[0], refs[3].shape[0]
+
+    @pl.when(step == 0)
+    def _():
+        dk_sum[...] = jnp.zeros_like(dk_sum)
+        dv_sum[...] = jnp.zeros_like(dv_sum)
+
+    if half is None:
+        attend_back_part(refs, 0, length)
+    else:
+
+        @pl.when(step == half)
+        def _():
+            attend_back_part(refs, pl.multiple_of(half * rows, rows), rows)
+
+        @pl.when(step != half)
+        def _():
+            attend_back_part(refs, 0, length)
 
     @pl.when(step == steps - 1)
     def _():
@@ -526,10 +545,12 @@
 
 
 def attend_back_kernel(*refs):
-    attend_back_step(*refs[:7], *refs[-3:])
-
-
-def attend_sums_kernel(n_blocks, *refs):
+    attend_back_step(refs[:7] + refs[-3:])
+
+
+def attend_sums_kernel(n_blocks, causal, *refs):
+    half = refs[0][0] if causal else None
+    refs = refs[1:] if causal else refs
     *hat_refs, weight_ref, own_hat_ref, own_grad_ref = refs[7 : 10 + n_blocks]
     sums_ref, out_ref, dk_sum, dv_sum, hats, weights, sem = refs[-7:]
     rows = hat_refs[0].shape[0]
@@ -544,7 +565,7 @@
         for copy in copies:
             copy.start()
 
-    attend_back_step(*refs[:7], out_ref, dk_sum, dv_sum)
+    attend_back_step(refs[:7] + (out_ref, dk_sum, dv_sum), half)
 
     @pl.when((pair == pl.num_programs(0) - 1) & (step == pl.num_programs(1) - 1))
     def _():
@@ -567,7 +588,7 @@
 
 
 def attend_back(
-    query, keys, key_at, value_at, limit, spots, grads, totals, sum_with=None, after=()
+    query, keys, key_at, value_at, limit, spots, grads, totals, sum_with=None, after=(), half=None
 ):
     length, width = grads.shape
     pairs = width // 128
@@ -576,13 +597,15 @@
     scratch = [pltpu.VMEM((length, 128), F32), pltpu.VMEM((length, 128), F32)]
     extra = () if sum_with is None else tuple(sum_with[0]) + tuple(sum_with[1:])
     n_blocks = len(extra) - 3
+    causal = half is not None and 2 * rows == length
+    chosen = [half.reshape(1).astype(jnp.int32)] if causal else []
     if sum_with is None:
         kernel = attend_back_kernel
         out = jax.ShapeDtypeStruct((length, 3 * width), LOW)
     else:
 
         def kernel(*refs):
-            attend_sums_kernel(n_blocks, *refs)
+            attend_sums_kernel(n_blocks, causal, *refs)
 
         out = jax.ShapeDtypeStruct((2, extra[0].shape[1]), F32)
         scratch = (
@@ -595,7 +618,8 @@
         kernel,
         grid=(pairs, length // rows),
         out_shape=out,
-        in_specs=attend_specs(rows, length, key_at, value_at, 2)
+        in_specs=[pl.BlockSpec(memory_space=pltpu.SMEM)] * len(chosen)
+        + attend_specs(rows, length, key_at, value_at, 2)
         + [hbm] * len(extra[:-2])
         + [pl.BlockSpec(v.shape, lambda p, j: (0, 0)) for v in extra[-2:]]
         + [hbm] * len(after),
@@ -607,7 +631,7 @@
             bytes_accessed=16 * length * width,
             transcendentals=length * length * width // HEAD_DIM,
         ),
-    )(limit, spots, query, keys, keys, grads, totals, *extra, *after)
+    )(*chosen, limit, spots, query, keys, keys, grads, totals, *extra, *after)
 
 
 def gelu_both(values):
@@ -1317,6 +1341,7 @@
         total_decoder,
         sum_with=(decoder_hats, in_dec, decoder_hat, grad_dec),
         after=[sums_zero],
+        half=enc >> 1,
     )
     sums_three, *parts[1:] = gate([sums_three] + parts[1:])
 

time: 658 us -> 655 us (level)
  transfers between devices with their start and end apart: 96 -> 96, of which waited for: 29 -> 29; matrix products, arithmetic and copies ran while one was open for 18% -> 18% of each run, Pallas kernels for 25% -> 24%
where the time goes in v5:
time: 655 us; the launch traced here: 645 us
  Pallas kernels  201 us (31%)
  waiting for transfers between devices  184 us (28%)
  local copies, waits for them, and re-layouts  86.3 us (13%)
  starting transfers between devices  84.7 us (13%)
  other arithmetic  44.2 us (7%)
  matrix products  21 us (3%)
  between operations  17.4 us (3%)
    ppermute x84, waiting for transfers between devices, flip(): return lax.ppermute(value, axis, [(i, i ^ mask) for i in range(count)])  151 us
    ppermute x84, starting transfers between devices, flip(): return lax.ppermute(value, axis, [(i, i ^ mask) for i in range(count)])  71.5 us
    pallas_call x3, Pallas kernels, attend_back(): pl.pallas_call(kernel, grid=(pairs, length // rows), out_shape=out, in_sp...  53.1 us
    gather x3, local copies, waits for them, and re-layouts, lookup(): found = jnp.take(embedding, jnp.clip(ids, 0, entries - 1), axis=0)  36.4 us
    pallas_call x1, Pallas kernels, head(): pl.pallas_call(lambda *refs: head_kernel(count, *refs), grid=(entries //...  34.2 us
    pallas_call x2, Pallas kernels, branch_back(): pl.pallas_call(lambda *refs: branch_back_kernel(first, n_parts, len(given...  30.5 us
    pallas_call x3, Pallas kernels, attend(): pl.pallas_call(attend_kernel, grid=(pairs, length // rows), out_shape=[ja...  29.1 us
    pallas_call x2, Pallas kernels, branch(): pl.pallas_call(lambda *refs: branch_kernel(first, len(parts), *refs), out...  28 us
  transfers between devices with their start and end apart: 96, of which 29 were waited for; matrix products, arithmetic and copies ran while one was open for 18% of the time, Pallas kernels for 24%

profile of v5, /device:TPU:0, one launch (start us, length us, event | category | flops | bytes accessed | tf_op | source)
XLA Modules:
  0.0 644.9 jit_solution(3219084158606075116)
XLA Ops:
  11.4 6.2 all-gather.3
  21.9 3.5 all-to-all-start
  32.5 2.6 collective-permute-start.9
  46.4 2.7 collective-permute-start.2
  50.8 11.4 %gather_fusion.2 = bf16[1024,1024]{1,0:T(8,128)(2,1)S(1)} fusion(bf16[6400,1024]{1,0:T(8,128)(2,1)} %refs_4_.2, s32[1024]{0:T(1024)S(1)} %broadcast_clamp_fusion.2), kind=kCustom, calls=%fused_computation.clone | custom fusion | bytes 4198400 | tf_op jit(solution)/shard_map/jit(_take)/gather | solution.py:1161
  62.2 12.5 %gather_fusion.3 = bf16[1024,1024]{1,0:T(8,128)(2,1)} fusion(bf16[6400,1024]{1,0:T(8,128)(2,1)} %refs_4_.2, s32[1024]{0:T(1024)S(1)} %broadcast_clamp_fusion.1), kind=kCustom, calls=%fused_computation.1.clone | custom fusion | bytes 4198400 | tf_op jit(solution)/shard_map/jit(_take)/gather | solution.py:1161
  74.8 12.5 %gather_fusion.4 = bf16[1024,1024]{1,0:T(8,128)(2,1)} fusion(bf16[6400,1024]{1,0:T(8,128)(2,1)} %refs_4_.2, s32[1024]{0:T(1024)S(1)} %broadcast_clamp_fusion), kind=kCustom, calls=%fused_computation.2.clone | custom fusion | bytes 4198400 | tf_op jit(solution)/shard_map/jit(_take)/gather | solution.py:1161
  94.0 2.7 collective-permute-done.1.refs_3_
  96.7 15.3 %collective-permute-done.3.refs_5_ = bf16[192,1536]{1,0:T(8,128)(2,1)} collective-permute-done((bf16[192,1536]{1,0:T(8,128)(2,1)}, bf16[192,1536]{1,0:T(8,128)(2,1)}, u32[]{:S(2)}, u32[]{:S(2)}) %collective-permute-start.3) | collective-permute-done | bytes 589856 | tf_op jit(solution)/shard_map/ppermute | solution.py:29
  122.2 20.1 %collective-permute-done.12 = bf16[256,1024]{1,0:T(8,128)(2,1)S(1)} collective-permute-done((bf16[256,1024]{1,0:T(8,128)(2,1)S(1)}, bf16[256,1024]{1,0:T(8,128)(2,1)S(1)}, u32[]{:S(2)}, u32[]{:S(2)}) %collective-permute-start.12) | collective-permute-done | bytes 524320 | tf_op jit(solution)/shard_map/ppermute | solution.py:29
  142.3 22.1 %collective-permute-done.6 = bf16[256,1024]{1,0:T(8,128)(2,1)S(1)} collective-permute-done((bf16[256,1024]{1,0:T(8,128)(2,1)S(1)}, bf16[256,1024]{1,0:T(8,128)(2,1)S(1)}, u32[]{:S(2)}, u32[]{:S(2)}) %collective-permute-start.6) | collective-permute-done | bytes 524320 | tf_op jit(solution)/shard_map/ppermute | solution.py:29
  171.7 13.2 %collective-permute-done.13.refs_1_ = bf16[256,1024]{1,0:T(8,128)(2,1)S(1)} collective-permute-done((bf16[256,1024]{1,0:T(8,128)(2,1)}, bf16[256,1024]{1,0:T(8,128)(2,1)S(1)}, u32[]{:S(2)}, u32[]{:S(2)}) %collective-permute-start.13) | collective-permute-done | bytes 524320 | tf_op jit(solution)/shard_map/ppermute | solution.py:29
  190.6 9.0 %collective-permute-start.20 = (bf16[128,768]{1,0:T(8,128)(2,1)S(1)}, bf16[128,768]{1,0:T(8,128)(2,1)S(1)}, u32[]{:S(2)}, u32[]{:S(2)}) collective-permute-start(bf16[128,768]{1,0:T(8,128)(2,1)S(1)} %get-tuple-element.371), channel_id=1, source_target_pairs={{0,8},{4,12},{8,0},{12,4},{16,24},{20,28},{24,16},{28,20},{1,9},{5... | collective-permute-start | bytes 589832 | tf_op jit(solution)/shard_map/ppermute | solution.py:29
  199.5 5.1 shard_map.277
  208.3 4.2 fusion.32.q_ref.k_ref.v_ref.refs_2_.refs_3_.refs_4_
  216.2 9.5 %shard_map.278 = (bf16[1024,256]{1,0:T(8,128)(2,1)}, f32[1024,256]{1,0:T(8,128)}) custom-call(s32[1024,1]{1,0:T(8,128)} %broadcast_in_dim.79.limit_ref.refs_0_, s32[1,1024]{1,0:T(1,128)} %bitcast.288, bf16[1024,768]{1,0:T(8,128)(2,1)} %fusion.32.q_ref.k_ref.v_ref.refs_2_.refs_3_.refs_4_, bf16[1024,768]{1,0:T(8,128)(2,1)} %fusion.32.q_ref.k_ref.v_ref.refs_2_.refs_3_.refs_4_, ...), custom_call_target="tpu_custom_call" | custom-call | flops 2147483648 | bytes 2097152 | tf_op jit(solution)/shard_map/pallas_call | solution.py:470
  232.5 6.7 %collective-permute-done.28.refs_4_ = bf16[4,64,1536]{2,1,0:T(8,128)(2,1)S(1)} collective-permute-done((bf16[4,64,1536]{2,1,0:T(8,128)(2,1)}, bf16[4,64,1536]{2,1,0:T(8,128)(2,1)S(1)}, u32[]{:S(2)}, u32[]{:S(2)}) %collective-permute-start.28) | collective-permute-done | bytes 786464 | tf_op jit(solution)/shard_map/ppermute | solution.py:163
  239.2 5.0 fusion.35.q_ref.k_ref.v_ref.refs_3_.refs_4_.refs_5_
  244.2 9.7 %shard_map.280 = (bf16[1024,256]{1,0:T(8,128)(2,1)}, f32[1024,256]{1,0:T(8,128)}) custom-call(s32[1024,1]{1,0:T(8,128)} %bitcast.270, s32[1,1024]{1,0:T(1,128)} %bitcast.289, bf16[1024,768]{1,0:T(8,128)(2,1)} %fusion.35.q_ref.k_ref.v_ref.refs_3_.refs_4_.refs_5_, bf16[1024,768]{1,0:T(8,128)(2,1)} %fusion.35.q_ref.k_ref.v_ref.refs_3_.refs_4_.refs_5_, ...), custom_call_target="tpu_custom_call" | custom-call | flops 2147483648 | bytes 2097152 | tf_op jit(solution)/shard_map/pallas_call | solution.py:470
  258.5 5.1 shard_map.281
  264.5 3.5 collective-permute-done.26
  274.5 14.0 %shard_map.283 = (f32[256,1024]{1,0:T(8,128)}, bf16[256,1024]{1,0:T(8,128)(2,1)}, f32[256,4096]{1,0:T(8,128)}, bf16[256,512]{1,0:T(8,128)(2,1)}, f32[256,512]{1,...) custom-call(bf16[256,256]{1,0:T(8,128)(2,1)} %get-tuple-element.383.refs_0_, bf16[256,256]{1,0:T(8,128)(2,1)} %copy-done.68, ...), custom_call_target="tpu_custom_call" | custom-call | flops 5368709120 | bytes 23068672 | tf_op jit(solution)/shard_map/pallas_call | solution.py:788
  289.7 24.8 %collective-permute-done.41 = bf16[256,1024]{1,0:T(8,128)(2,1)} collective-permute-done((bf16[256,1024]{1,0:T(8,128)(2,1)}, bf16[256,1024]{1,0:T(8,128)(2,1)}, u32[]{:S(2)}, u32[]{:S(2)}) %collective-permute-start.41) | collective-permute-done | bytes 524320 | tf_op jit(solution)/shard_map/ppermute | solution.py:29
  314.7 3.8 shard_map.282
  318.5 3.1 fusion.41.q_ref.refs_2_
  321.6 3.6 fusion.38.k_ref.v_ref.refs_3_.refs_4_
  325.2 9.8 %shard_map.284 = (bf16[1024,256]{1,0:T(8,128)(2,1)}, f32[1024,256]{1,0:T(8,128)}) custom-call(s32[1024,1]{1,0:T(8,128)} %broadcast_in_dim.79.limit_ref.refs_0_, s32[1,1024]{1,0:T(1,128)} %bitcast.290, bf16[1024,256]{1,0:T(8,128)(2,1)} %fusion.41.q_ref.refs_2_, bf16[1024,512]{1,0:T(8,128)(2,1)} %fusion.38.k_ref.v_ref.refs_3_.refs_4_, ...), custom_call_target="tpu_custom_call" | custom-call | flops 2147483648 | bytes 2097152 | tf_op jit(solution)/shard_map/pallas_call | solution.py:470
  343.1 18.6 %all-gather.9.cloned.1.call-done = bf16[9216,1024]{1,0:T(8,128)(2,1)} async-done(((bf16[288,1024]{1,0:T(8,128)(2,1)}), bf16[9216,1024]{1,0:T(8,128)(2,1)}) %all-gather.9.cloned.1.call-update) | async-done | bytes 18874384 | tf_op jit(solution)/shard_map/all_gather | solution.py:654
  362.4 14.0 %shard_map.286 = (f32[256,1024]{1,0:T(8,128)}, bf16[256,1024]{1,0:T(8,128)(2,1)}, f32[256,4096]{1,0:T(8,128)}, bf16[256,512]{1,0:T(8,128)(2,1)}, f32[256,512]{1,...) custom-call(bf16[256,256]{1,0:T(8,128)(2,1)} %get-tuple-element.379.refs_0_, bf16[256,256]{1,0:T(8,128)(2,1)} %copy-done.71, ...), custom_call_target="tpu_custom_call" | custom-call | flops 5368709120 | bytes 23068672 | tf_op jit(solution)/shard_map/pallas_call | solution.py:788
  378.8 12.7 %collective-permute-done.49.refs_2_ = bf16[256,1024]{1,0:T(8,128)(2,1)S(1)} collective-permute-done((bf16[256,1024]{1,0:T(8,128)(2,1)}, bf16[256,1024]{1,0:T(8,128)(2,1)S(1)}, u32[]{:S(2)}, u32[]{:S(2)}) %collective-permute-start.49) | collective-permute-done | bytes 524320 | tf_op jit(solution)/shard_map/ppermute | solution.py:29
  396.3 34.2 %shard_map.289 = (bf16[256,1024]{1,0:T(8,128)(2,1)}, bf16[256,1024]{1,0:T(8,128)(2,1)}, bf16[256,1024]{1,0:T(8,128)(2,1)}, bf16[256,1024]{1,0:T(8,128)(2,1)}, f3...) custom-call(bf16[256,1024]{1,0:T(8,128)(2,1)} %get-tuple-element.182.refs_0_.refs_12_, ...), custom_call_target="tpu_custom_call" | custom-call | flops 26843545600 | bytes 13107200 | tf_op jit(solution)/shard_map/pallas_call | solution.py:1065
  444.7 2.9 fusion.80
  447.6 2.5 add_divide_fusion.refs_0_
  450.1 4.7 collective-permute-done.59.refs_0_
  454.8 15.4 %shard_map.293 = (f32[256,1024]{1,0:T(8,128)}, f32[4,1024]{1,0:T(4,128)}, bf16[256,512]{1,0:T(8,128)(2,1)}, bf16[256,1024]{1,0:T(8,128)(2,1)}, bf16[256,256]{1,0...) custom-call(f32[256,1024]{1,0:T(8,128)} %add_divide_fusion.refs_0_, ...), custom_call_target="tpu_custom_call" | custom-call | flops 5368709120 | bytes 23068672 | tf_op jit(solution)/shard_map/pallas_call | solution.py:882
  472.2 4.1 collective-permute-done.66
  479.3 17.4 %shard_map.294 = bf16[1024,768]{1,0:T(8,128)(2,1)} custom-call(s32[1024,1]{1,0:T(8,128)} %broadcast_in_dim.79.limit_ref.refs_0_, s32[1,1024]{1,0:T(1,128)} %bitcast.291, bf16[1024,256]{1,0:T(8,128)(2,1)} %fusion.41.q_ref.refs_2_, bf16[1024,512]{1,0:T(8,128)(2,1)} %fusion.38.k_ref.v_ref.refs_3_.refs_4_, bf16[1024,512]{1,0:T(8,128)(2,1)} %fusion.38.k_ref.v_ref.refs_3_.refs_4_, ...), custom_call_target="tpu_custom_call" | custom-call | flops 5368709120 | bytes 4194304 | tf_op jit(solution)/shard_map/pallas_call | solution.py:617
  496.6 2.5 fusion.127
  506.8 11.7 %collective-permute-done.69.refs_1_ = bf16[256,1024]{1,0:T(8,128)(2,1)S(1)} collective-permute-done((bf16[256,1024]{1,0:T(8,128)(2,1)S(1)}, bf16[256,1024]{1,0:T(8,128)(2,1)S(1)}, u32[]{:S(2)}, u32[]{:S(2)}) %collective-permute-start.69) | collective-permute-done | bytes 524320 | tf_op jit(solution)/shard_map/ppermute | solution.py:29
  519.3 15.0 %shard_map.295 = (f32[256,1024]{1,0:T(8,128)}, f32[4,1024]{1,0:T(4,128)}, bf16[256,512]{1,0:T(8,128)(2,1)}, bf16[256,1024]{1,0:T(8,128)(2,1)}, bf16[256,256]{1,0...) custom-call(f32[256,1024]{1,0:T(8,128)} %get-tuple-element.354.refs_0_, ...), custom_call_target="tpu_custom_call" | custom-call | flops 5368709120 | bytes 23068672 | tf_op jit(solution)/shard_map/pallas_call | solution.py:882
  535.2 5.3 shard_map.297
  558.0 19.2 %shard_map.299.refs_0_ = f32[2,1024]{1,0:T(2,128)} custom-call(s32[1024,1]{1,0:T(8,128)} %broadcast_in_dim.79.limit_ref.refs_0_, s32[1,1024]{1,0:T(1,128)} %bitcast.292, bf16[1024,768]{1,0:T(8,128)(2,1)} %fusion.32.q_ref.k_ref.v_ref.refs_2_.refs_3_.refs_4_, bf16[1024,768]{1,0:T(8,128)(2,1)} %fusion.32.q_ref.k_ref.v_ref.refs_2_.refs_3_.refs_4_, ...), custom_call_target="tpu_custom_call" | custom-call | flops 5368709120 | bytes 4194304 | tf_op jit(solution)/shard_map/pallas_call | solution.py:617
  577.2 3.4 collective-permute-done.79.refs_3_
  583.7 6.5 %collective-permute-start.84 = (bf16[64,1024]{1,0:T(8,128)(2,1)S(1)}, bf16[64,1024]{1,0:T(8,128)(2,1)S(1)}, u32[]{:S(2)}, u32[]{:S(2)}) collective-permute-start(bf16[64,1024]{1,0:T(8,128)(2,1)S(1)} %get-tuple-element.366), channel_id=1, source_target_pairs={{0,16},{4,20},{8,24},{12,28},{16,0},{20,4},{24,8},{28,12},{1,17},{... | collective-permute-start | bytes 393224 | tf_op jit(solution)/shard_map/ppermute | solution.py:29
  591.6 16.5 %shard_map.301.refs_0_ = f32[2,1024]{1,0:T(2,128)} custom-call(s32[1]{0:T(128)} %bitcast.105.refs_0_, s32[1024,1]{1,0:T(8,128)} %bitcast.271, s32[1,1024]{1,0:T(1,128)} %bitcast.293, bf16[1024,768]{1,0:T(8,128)(2,1)} %fusion.35.q_ref.k_ref.v_ref.refs_3_.refs_4_.refs_5_, bf16[1024,768]{1,0:T(8,128)(2,1)} %fusion.35.q_ref.k_ref.v_ref.refs_3_.refs_4_.refs_5_, ...), custom_call_target="tpu_custom_call" | custom-call | flops 5368709120 | bytes 4194304 | tf_op jit(solution)/shard_map/pallas_call | solution.py:617
  610.3 2.6 shard_map.303
  619.6 2.6 collective-permute-done.89
  626.7 3.8 collective-permute-done.91
  (525 shorter events, 170.0 us)
Async XLA Ops:
  7.2 266.6 %all-gather.7.cloned.1.call-start = ((), (), s32[]{:S(2)}) async-start(), calls=%async_computation.1 | async-start | bytes 19464192 | tf_op jit(solution)/shard_map/all_gather | solution.py:654
  10.5 351.1 %all-gather.9.cloned.1.call-start = ((), (), s32[]{:S(2)}) async-start(), calls=%async_computation.2 | async-start | bytes 19464192 | tf_op jit(solution)/shard_map/all_gather | solution.py:654
  21.9 19.5 %all-to-all-start = ((bf16[4,32,2304]{2,1,0:T(8,128)(2,1)}), bf16[4,32,2304]{2,1,0:T(8,128)(2,1)S(1)}, u32[]{:S(2)}, u32[]{:S(2)}) async-start(bf16[4,32,2304]{2,1,0:T(8,128)(2,1)} %reshape.448), calls=%async_computation | async-start | bytes 1179648 | tf_op jit(solution)/shard_map/all_to_all | solution.py:1192
  25.5 15.1 %collective-permute-start = (bf16[32,1536]{1,0:T(8,128)(2,1)S(1)}, bf16[32,1536]{1,0:T(8,128)(2,1)S(1)}, u32[]{:S(2)}, u32[]{:S(2)}) collective-permute-start(bf16[32,1536]{1,0:T(8,128)(2,1)S(1)} %broadcast_select_fusion.2), channel_id=1, source_target_pairs={{0,1},{1,0},{2,3},{3,2},{4,5},{5,4},{6,7},{7,6},{8,9},{9,8},{10,11... | collective-permute-start | bytes 294920 | tf_op jit(solution)/shard_map/ppermute | solution.py:29
  45.7 51.1 %collective-permute-start.1 = (bf16[192,1536]{1,0:T(8,128)(2,1)}, bf16[192,1536]{1,0:T(8,128)(2,1)S(1)}, u32[]{:S(2)}, u32[]{:S(2)}) collective-permute-start(bf16[192,1536]{1,0:T(8,128)(2,1)} %constant_dynamic-update-slice_fusion), channel_id=1, source_target_pairs={{0,8},{4,12},{8,0},{12,4},{16,24},{20,28},{24,16},{28,20},{1,9},{5... | collective-permute-start | bytes 1769480 | tf_op jit(solution)/shard_map/ppermute | solution.py:29
  46.4 50.3 %collective-permute-start.2 = (bf16[192,1536]{1,0:T(8,128)(2,1)}, bf16[192,1536]{1,0:T(8,128)(2,1)S(1)}, u32[]{:S(2)}, u32[]{:S(2)}) collective-permute-start(bf16[192,1536]{1,0:T(8,128)(2,1)} %constant_dynamic-update-slice_fusion), channel_id=1, source_target_pairs={{0,16},{4,20},{8,24},{12,28},{16,0},{20,4},{24,8},{28,12},{1,17},{... | collective-permute-start | bytes 1769480 | tf_op jit(solution)/shard_map/ppermute | solution.py:29
  49.2 62.9 %collective-permute-start.3 = (bf16[192,1536]{1,0:T(8,128)(2,1)}, bf16[192,1536]{1,0:T(8,128)(2,1)}, u32[]{:S(2)}, u32[]{:S(2)}) collective-permute-start(bf16[192,1536]{1,0:T(8,128)(2,1)} %constant_dynamic-update-slice_fusion), channel_id=1, source_target_pairs={{0,24},{4,28},{8,16},{12,20},{16,8},{20,12},{24,0},{28,4},{1,25},{... | collective-permute-start | bytes 1769480 | tf_op jit(solution)/shard_map/ppermute | solution.py:29
  116.3 26.1 %collective-permute-start.12 = (bf16[256,1024]{1,0:T(8,128)(2,1)S(1)}, bf16[256,1024]{1,0:T(8,128)(2,1)S(1)}, u32[]{:S(2)}, u32[]{:S(2)}) collective-permute-start(bf16[256,1024]{1,0:T(8,128)(2,1)S(1)} %fusion.51), channel_id=1, source_target_pairs={{0,2},{1,3},{2,0},{3,1},{4,6},{5,7},{6,4},{7,5},{8,10},{9,11},{10,... | collective-permute-start | bytes 1572872 | tf_op jit(solution)/shard_map/ppermute | solution.py:29
  118.4 46.1 %collective-permute-start.6 = (bf16[256,1024]{1,0:T(8,128)(2,1)S(1)}, bf16[256,1024]{1,0:T(8,128)(2,1)S(1)}, u32[]{:S(2)}, u32[]{:S(2)}) collective-permute-start(bf16[256,1024]{1,0:T(8,128)(2,1)S(1)} %fusion.53), channel_id=1, source_target_pairs={{0,2},{1,3},{2,0},{3,1},{4,6},{5,7},{6,4},{7,5},{8,10},{9,11},{10,... | collective-permute-start | bytes 1572872 | tf_op jit(solution)/shard_map/ppermute | solution.py:29
  120.1 70.5 %collective-permute-start.17 = (bf16[4,128,1536]{2,1,0:T(8,128)(2,1)S(1)}, bf16[4,128,1536]{2,1,0:T(8,128)(2,1)}, u32[]{:S(2)}, u32[]{:S(2)}) collective-permute-start(bf16[4,128,1536]{2,1,0:T(8,128)(2,1)S(1)} %pad_maximum_fusion.refs_1_), channel_id=1, source_target_pairs={{0,4},{4,0},{8,12},{12,8},{16,20},{20,16},{24,28},{28,24},{1,5},{5... | collective-permute-start | bytes 4718600 | tf_op jit(solution)/shard_map/ppermute | solution.py:29
  169.2 15.8 %collective-permute-start.13 = (bf16[256,1024]{1,0:T(8,128)(2,1)}, bf16[256,1024]{1,0:T(8,128)(2,1)S(1)}, u32[]{:S(2)}, u32[]{:S(2)}) collective-permute-start(bf16[256,1024]{1,0:T(8,128)(2,1)} %get-tuple-element.346), channel_id=1, source_target_pairs={{0,2},{1,3},{2,0},{3,1},{4,6},{5,7},{6,4},{7,5},{8,10},{9,11},{10,... | collective-permute-start | bytes 1572872 | tf_op jit(solution)/shard_map/ppermute | solution.py:29
  170.7 35.2 %collective-permute-start.18 = (bf16[256,1024]{1,0:T(8,128)(2,1)}, bf16[256,1024]{1,0:T(8,128)(2,1)}, u32[]{:S(2)}, u32[]{:S(2)}) collective-permute-start(bf16[256,1024]{1,0:T(8,128)(2,1)} %get-tuple-element.346), channel_id=1, source_target_pairs={{0,1},{1,0},{2,3},{3,2},{4,5},{5,4},{6,7},{7,6},{8,9},{9,8},{10,11... | collective-permute-start | bytes 1572872 | tf_op jit(solution)/shard_map/ppermute | solution.py:29
  185.8 21.1 %collective-permute-start.19 = (bf16[256,1024]{1,0:T(8,128)(2,1)}, bf16[256,1024]{1,0:T(8,128)(2,1)S(1)}, u32[]{:S(2)}, u32[]{:S(2)}) collective-permute-start(bf16[256,1024]{1,0:T(8,128)(2,1)} %get-tuple-element.162), channel_id=1, source_target_pairs={{0,1},{1,0},{2,3},{3,2},{4,5},{5,4},{6,7},{7,6},{8,9},{9,8},{10,11... | collective-permute-start | bytes 1572872 | tf_op jit(solution)/shard_map/ppermute | solution.py:29
  186.8 38.9 %collective-permute-start.23 = (bf16[4,64,1536]{2,1,0:T(8,128)(2,1)S(1)}, bf16[4,64,1536]{2,1,0:T(8,128)(2,1)S(1)}, u32[]{:S(2)}, u32[]{:S(2)}) collective-permute-start(bf16[4,64,1536]{2,1,0:T(8,128)(2,1)S(1)} %pad_maximum_fusion.1.refs_1_), channel_id=1, source_target_pairs={{0,4},{1,3},{2,6},{3,1},{4,0},{5,7},{6,2},{7,5},{8,12},{9,11},{10,... | collective-permute-start | bytes 2359304 | tf_op jit(solution)/shard_map/ppermute | solution.py:163
  188.4 37.4 %collective-permute-start.24 = (bf16[4,64,1536]{2,1,0:T(8,128)(2,1)S(1)}, bf16[4,64,1536]{2,1,0:T(8,128)(2,1)S(1)}, u32[]{:S(2)}, u32[]{:S(2)}) collective-permute-start(bf16[4,64,1536]{2,1,0:T(8,128)(2,1)S(1)} %pad_maximum_fusion.1.refs_1_), channel_id=1, source_target_pairs={{0,2},{1,5},{2,0},{3,7},{4,6},{5,1},{6,4},{7,3},{8,10},{9,13},{10,... | collective-permute-start | bytes 2359304 | tf_op jit(solution)/shard_map/ppermute | solution.py:163
  190.6 21.9 %collective-permute-start.20 = (bf16[128,768]{1,0:T(8,128)(2,1)S(1)}, bf16[128,768]{1,0:T(8,128)(2,1)S(1)}, u32[]{:S(2)}, u32[]{:S(2)}) collective-permute-start(bf16[128,768]{1,0:T(8,128)(2,1)S(1)} %get-tuple-element.371), channel_id=1, source_target_pairs={{0,8},{4,12},{8,0},{12,4},{16,24},{20,28},{24,16},{28,20},{1,9},{5... | collective-permute-start | bytes 589832 | tf_op jit(solution)/shard_map/ppermute | solution.py:29
  205.9 19.8 %collective-permute-start.21 = (bf16[128,768]{1,0:T(8,128)(2,1)S(1)}, bf16[128,768]{1,0:T(8,128)(2,1)S(1)}, u32[]{:S(2)}, u32[]{:S(2)}) collective-permute-start(bf16[128,768]{1,0:T(8,128)(2,1)S(1)} %get-tuple-element.371), channel_id=1, source_target_pairs={{0,16},{4,20},{8,24},{12,28},{16,0},{20,4},{24,8},{28,12},{1,17},{... | collective-permute-start | bytes 589832 | tf_op jit(solution)/shard_map/ppermute | solution.py:29
  206.8 20.7 %collective-permute-start.15 = (bf16[256,1024]{1,0:T(8,128)(2,1)}, bf16[256,1024]{1,0:T(8,128)(2,1)}, u32[]{:S(2)}, u32[]{:S(2)}) collective-permute-start(bf16[256,1024]{1,0:T(8,128)(2,1)} %get-tuple-element.157), channel_id=1, source_target_pairs={{0,2},{1,3},{2,0},{3,1},{4,6},{5,7},{6,4},{7,5},{8,10},{9,11},{10,... | collective-permute-start | bytes 1572872 | tf_op jit(solution)/shard_map/ppermute | solution.py:29
  231.3 24.7 %collective-permute-start.29 = (bf16[4,64,1536]{2,1,0:T(8,128)(2,1)S(1)}, bf16[4,64,1536]{2,1,0:T(8,128)(2,1)S(1)}, u32[]{:S(2)}, u32[]{:S(2)}) collective-permute-start(bf16[4,64,1536]{2,1,0:T(8,128)(2,1)S(1)} %pad_maximum_fusion.1.refs_1_), channel_id=1, source_target_pairs={{0,1},{1,0},{2,3},{3,2},{4,5},{5,4},{6,7},{7,6},{8,9},{9,8},{10,11... | collective-permute-start | bytes 2359304 | tf_op jit(solution)/shard_map/ppermute | solution.py:29
  231.3 26.1 %collective-permute-start.30 = (bf16[4,64,1536]{2,1,0:T(8,128)(2,1)}, bf16[4,64,1536]{2,1,0:T(8,128)(2,1)S(1)}, u32[]{:S(2)}, u32[]{:S(2)}) collective-permute-start(bf16[4,64,1536]{2,1,0:T(8,128)(2,1)} %get-tuple-element.167.refs_2_), channel_id=1, source_target_pairs={{0,1},{1,0},{2,3},{3,2},{4,5},{5,4},{6,7},{7,6},{8,9},{9,8},{10,11... | collective-permute-start | bytes 2359304 | tf_op jit(solution)/shard_map/ppermute | solution.py:29
  232.5 25.0 %collective-permute-start.31 = (bf16[4,64,1536]{2,1,0:T(8,128)(2,1)S(1)}, bf16[4,64,1536]{2,1,0:T(8,128)(2,1)S(1)}, u32[]{:S(2)}, u32[]{:S(2)}) collective-permute-start(bf16[4,64,1536]{2,1,0:T(8,128)(2,1)S(1)} %copy-done.5), channel_id=1, source_target_pairs={{0,1},{1,0},{2,3},{3,2},{4,5},{5,4},{6,7},{7,6},{8,9},{9,8},{10,11... | collective-permute-start | bytes 2359304 | tf_op jit(solution)/shard_map/ppermute | solution.py:29
  239.2 19.0 %collective-permute-start.32 = (bf16[4,64,1536]{2,1,0:T(8,128)(2,1)S(1)}, bf16[4,64,1536]{2,1,0:T(8,128)(2,1)S(1)}, u32[]{:S(2)}, u32[]{:S(2)}) collective-permute-start(bf16[4,64,1536]{2,1,0:T(8,128)(2,1)S(1)} %collective-permute-done.28.refs_4_), channel_id=1, source_target_pairs={{0,1},{1,0},{2,3},{3,2},{4,5},{5,4},{6,7},{7,6},{8,9},{9,8},{10,11... | collective-permute-start | bytes 2359304 | tf_op jit(solution)/shard_map/ppermute | solution.py:29
  257.6 57.1 %collective-permute-start.36 = (bf16[4,128,768]{2,1,0:T(8,128)(2,1)S(1)}, bf16[4,128,768]{2,1,0:T(8,128)(2,1)}, u32[]{:S(2)}, u32[]{:S(2)}) collective-permute-start(bf16[4,128,768]{2,1,0:T(8,128)(2,1)S(1)} %pad_maximum_fusion.2.refs_1_), channel_id=1, source_target_pairs={{0,4},{4,0},{8,12},{12,8},{16,20},{20,16},{24,28},{28,24},{1,5},{5... | collective-permute-start | bytes 2359304 | tf_op jit(solution)/shard_map/ppermute | solution.py:29
  258.3 15.1 %collective-permute-start.37 = (bf16[256,256]{1,0:T(8,128)(2,1)S(1)}, bf16[256,256]{1,0:T(8,128)(2,1)S(1)}, u32[]{:S(2)}, u32[]{:S(2)}) collective-permute-start(bf16[256,256]{1,0:T(8,128)(2,1)S(1)} %get-tuple-element.382), channel_id=1, source_target_pairs={{0,1},{1,0},{2,3},{3,2},{4,5},{5,4},{6,7},{7,6},{8,9},{9,8},{10,11... | collective-permute-start | bytes 393224 | tf_op jit(solution)/shard_map/ppermute | solution.py:29
  272.0 17.2 %collective-permute-start.34 = (bf16[256,1024]{1,0:T(8,128)(2,1)}, bf16[256,1024]{1,0:T(8,128)(2,1)}, u32[]{:S(2)}, u32[]{:S(2)}) collective-permute-start(bf16[256,1024]{1,0:T(8,128)(2,1)} %get-tuple-element.344), channel_id=1, source_target_pairs={{0,2},{1,3},{2,0},{3,1},{4,6},{5,7},{6,4},{7,5},{8,10},{9,11},{10,... | collective-permute-start | bytes 1572872 | tf_op jit(solution)/shard_map/ppermute | solution.py:29
  288.5 26.1 %collective-permute-start.41 = (bf16[256,1024]{1,0:T(8,128)(2,1)}, bf16[256,1024]{1,0:T(8,128)(2,1)}, u32[]{:S(2)}, u32[]{:S(2)}) collective-permute-start(bf16[256,1024]{1,0:T(8,128)(2,1)} %get-tuple-element.174), channel_id=1, source_target_pairs={{0,2},{1,3},{2,0},{3,1},{4,6},{5,7},{6,4},{7,5},{8,10},{9,11},{10,... | collective-permute-start | bytes 1572872 | tf_op jit(solution)/shard_map/ppermute | solution.py:29
  289.2 29.3 %collective-permute-start.33 = (bf16[256,1024]{1,0:T(8,128)(2,1)}, bf16[256,1024]{1,0:T(8,128)(2,1)}, u32[]{:S(2)}, u32[]{:S(2)}) collective-permute-start(bf16[256,1024]{1,0:T(8,128)(2,1)} %get-tuple-element.344), channel_id=1, source_target_pairs={{0,1},{1,0},{2,3},{3,2},{4,5},{5,4},{6,7},{7,6},{8,9},{9,8},{10,11... | collective-permute-start | bytes 1572872 | tf_op jit(solution)/shard_map/ppermute | solution.py:29
  289.2 29.3 %collective-permute-start.35 = (bf16[256,1024]{1,0:T(8,128)(2,1)}, bf16[256,1024]{1,0:T(8,128)(2,1)}, u32[]{:S(2)}, u32[]{:S(2)}) collective-permute-start(bf16[256,1024]{1,0:T(8,128)(2,1)} %collective-permute-done.34), channel_id=1, source_target_pairs={{0,1},{1,0},{2,3},{3,2},{4,5},{5,4},{6,7},{7,6},{8,9},{9,8},{10,11... | collective-permute-start | bytes 1572872 | tf_op jit(solution)/shard_map/ppermute | solution.py:29
  289.7 31.8 %collective-permute-start.40 = (bf16[256,1024]{1,0:T(8,128)(2,1)}, bf16[256,1024]{1,0:T(8,128)(2,1)}, u32[]{:S(2)}, u32[]{:S(2)}) collective-permute-start(bf16[256,1024]{1,0:T(8,128)(2,1)} %get-tuple-element.174), channel_id=1, source_target_pairs={{0,1},{1,0},{2,3},{3,2},{4,5},{5,4},{6,7},{7,6},{8,9},{9,8},{10,11... | collective-permute-start | bytes 1572872 | tf_op jit(solution)/shard_map/ppermute | solution.py:29
  338.5 23.1 %collective-permute-start.43 = (bf16[256,256]{1,0:T(8,128)(2,1)}, bf16[256,256]{1,0:T(8,128)(2,1)S(1)}, u32[]{:S(2)}, u32[]{:S(2)}) collective-permute-start(bf16[256,256]{1,0:T(8,128)(2,1)} %get-tuple-element.378), channel_id=1, source_target_pairs={{0,1},{1,0},{2,3},{3,2},{4,5},{5,4},{6,7},{7,6},{8,9},{9,8},{10,11... | collective-permute-start | bytes 393224 | tf_op jit(solution)/shard_map/ppermute | solution.py:29
  338.5 23.1 %collective-permute-start.44 = (bf16[256,256]{1,0:T(8,128)(2,1)}, bf16[256,256]{1,0:T(8,128)(2,1)S(1)}, u32[]{:S(2)}, u32[]{:S(2)}) collective-permute-start(bf16[256,256]{1,0:T(8,128)(2,1)} %get-tuple-element.377), channel_id=1, source_target_pairs={{0,2},{1,3},{2,0},{3,1},{4,6},{5,7},{6,4},{7,5},{8,10},{9,11},{10,... | collective-permute-start | bytes 393224 | tf_op jit(solution)/shard_map/ppermute | solution.py:29
  339.2 22.5 %collective-permute-start.45 = (bf16[256,256]{1,0:T(8,128)(2,1)}, bf16[256,256]{1,0:T(8,128)(2,1)S(1)}, u32[]{:S(2)}, u32[]{:S(2)}) collective-permute-start(bf16[256,256]{1,0:T(8,128)(2,1)} %get-tuple-element.376), channel_id=1, source_target_pairs={{0,3},{1,2},{2,1},{3,0},{4,7},{5,6},{6,5},{7,4},{8,11},{9,10},{10,... | collective-permute-start | bytes 393224 | tf_op jit(solution)/shard_map/ppermute | solution.py:29
  342.4 34.0 %collective-permute-start.47 = (bf16[256,1024]{1,0:T(8,128)(2,1)}, bf16[256,1024]{1,0:T(8,128)(2,1)S(1)}, u32[]{:S(2)}, u32[]{:S(2)}) collective-permute-start(bf16[256,1024]{1,0:T(8,128)(2,1)} %fusion.50), channel_id=1, source_target_pairs={{0,2},{1,3},{2,0},{3,1},{4,6},{5,7},{6,4},{7,5},{8,10},{9,11},{10,... | collective-permute-start | bytes 1572872 | tf_op jit(solution)/shard_map/ppermute | solution.py:29
  377.2 14.3 %collective-permute-start.49 = (bf16[256,1024]{1,0:T(8,128)(2,1)}, bf16[256,1024]{1,0:T(8,128)(2,1)S(1)}, u32[]{:S(2)}, u32[]{:S(2)}) collective-permute-start(bf16[256,1024]{1,0:T(8,128)(2,1)} %get-tuple-element.181.refs_0_), channel_id=1, source_target_pairs={{0,2},{1,3},{2,0},{3,1},{4,6},{5,7},{6,4},{7,5},{8,10},{9,11},{10,... | collective-permute-start | bytes 1572872 | tf_op jit(solution)/shard_map/ppermute | solution.py:29
  394.2 36.3 %collective-permute-start.51 = (bf16[256,1024]{1,0:T(8,128)(2,1)}, bf16[256,1024]{1,0:T(8,128)(2,1)S(1)}, u32[]{:S(2)}, u32[]{:S(2)}) collective-permute-start(bf16[256,1024]{1,0:T(8,128)(2,1)} %get-tuple-element.194.refs_8_), channel_id=1, source_target_pairs={{0,2},{1,3},{2,0},{3,1},{4,6},{5,7},{6,4},{7,5},{8,10},{9,11},{10,... | collective-permute-start | bytes 1572872 | tf_op jit(solution)/shard_map/ppermute | solution.py:29
  395.9 34.7 %collective-permute-start.52 = (bf16[256,1024]{1,0:T(8,128)(2,1)}, bf16[256,1024]{1,0:T(8,128)(2,1)S(1)}, u32[]{:S(2)}, u32[]{:S(2)}) collective-permute-start(bf16[256,1024]{1,0:T(8,128)(2,1)} %get-tuple-element.195.refs_10_), channel_id=1, source_target_pairs={{0,2},{1,3},{2,0},{3,1},{4,6},{5,7},{6,4},{7,5},{8,10},{9,11},{10,... | collective-permute-start | bytes 1572872 | tf_op jit(solution)/shard_map/ppermute | solution.py:29
  440.8 14.0 %collective-permute-start.59 = (bf16[256,1024]{1,0:T(8,128)(2,1)}, bf16[256,1024]{1,0:T(8,128)(2,1)}, u32[]{:S(2)}, u32[]{:S(2)}) collective-permute-start(bf16[256,1024]{1,0:T(8,128)(2,1)} %get-tuple-element.212), channel_id=1, source_target_pairs={{0,2},{1,3},{2,0},{3,1},{4,6},{5,7},{6,4},{7,5},{8,10},{9,11},{10,... | collective-permute-start | bytes 1572872 | tf_op jit(solution)/shard_map/ppermute | solution.py:29
  441.2 13.6 %collective-permute-start.60 = (bf16[256,1024]{1,0:T(8,128)(2,1)}, bf16[256,1024]{1,0:T(8,128)(2,1)}, u32[]{:S(2)}, u32[]{:S(2)}) collective-permute-start(bf16[256,1024]{1,0:T(8,128)(2,1)} %get-tuple-element.213.refs_1_), channel_id=1, source_target_pairs={{0,1},{1,0},{2,3},{3,2},{4,5},{5,4},{6,7},{7,6},{8,9},{9,8},{10,11... | collective-permute-start | bytes 1572872 | tf_op jit(solution)/shard_map/ppermute | solution.py:29
  441.2 13.6 %collective-permute-start.61 = (bf16[256,1024]{1,0:T(8,128)(2,1)}, bf16[256,1024]{1,0:T(8,128)(2,1)}, u32[]{:S(2)}, u32[]{:S(2)}) collective-permute-start(bf16[256,1024]{1,0:T(8,128)(2,1)} %get-tuple-element.214.refs_3_), channel_id=1, source_target_pairs={{0,1},{1,0},{2,3},{3,2},{4,5},{5,4},{6,7},{7,6},{8,9},{9,8},{10,11... | collective-permute-start | bytes 1572872 | tf_op jit(solution)/shard_map/ppermute | solution.py:29
  441.7 13.1 %collective-permute-start.62 = (bf16[256,1024]{1,0:T(8,128)(2,1)}, bf16[256,1024]{1,0:T(8,128)(2,1)}, u32[]{:S(2)}, u32[]{:S(2)}) collective-permute-start(bf16[256,1024]{1,0:T(8,128)(2,1)} %get-tuple-element.215.refs_5_), channel_id=1, source_target_pairs={{0,1},{1,0},{2,3},{3,2},{4,5},{5,4},{6,7},{7,6},{8,9},{9,8},{10,11... | collective-permute-start | bytes 1572872 | tf_op jit(solution)/shard_map/ppermute | solution.py:29
  503.8 14.7 %collective-permute-start.69 = (bf16[256,1024]{1,0:T(8,128)(2,1)S(1)}, bf16[256,1024]{1,0:T(8,128)(2,1)S(1)}, u32[]{:S(2)}, u32[]{:S(2)}) collective-permute-start(bf16[256,1024]{1,0:T(8,128)(2,1)S(1)} %get-tuple-element.353), channel_id=1, source_target_pairs={{0,2},{1,3},{2,0},{3,1},{4,6},{5,7},{6,4},{7,5},{8,10},{9,11},{10,... | collective-permute-start | bytes 1572872 | tf_op jit(solution)/shard_map/ppermute | solution.py:29
  506.0 28.4 %collective-permute-start.71 = (bf16[256,1024]{1,0:T(8,128)(2,1)S(1)}, bf16[256,1024]{1,0:T(8,128)(2,1)S(1)}, u32[]{:S(2)}, u32[]{:S(2)}) collective-permute-start(bf16[256,1024]{1,0:T(8,128)(2,1)S(1)} %get-tuple-element.351), channel_id=1, source_target_pairs={{0,2},{1,3},{2,0},{3,1},{4,6},{5,7},{6,4},{7,5},{8,10},{9,11},{10,... | collective-permute-start | bytes 1572872 | tf_op jit(solution)/shard_map/ppermute | solution.py:29
  553.4 23.8 %collective-permute-start.77 = (bf16[4,64,1024]{2,1,0:T(8,128)(2,1)S(1)}, bf16[4,64,1024]{2,1,0:T(8,128)(2,1)S(1)}, u32[]{:S(2)}, u32[]{:S(2)}) collective-permute-start(bf16[4,64,1024]{2,1,0:T(8,128)(2,1)S(1)} %get-tuple-element.350), channel_id=1, source_target_pairs={{0,4},{1,5},{2,6},{3,7},{4,0},{5,1},{6,2},{7,3},{8,12},{9,13},{10,... | collective-permute-start | bytes 1572872 | tf_op jit(solution)/shard_map/ppermute | solution.py:137
  555.1 22.1 %collective-permute-start.78 = (bf16[4,64,1024]{2,1,0:T(8,128)(2,1)S(1)}, bf16[4,64,1024]{2,1,0:T(8,128)(2,1)S(1)}, u32[]{:S(2)}, u32[]{:S(2)}) collective-permute-start(bf16[4,64,1024]{2,1,0:T(8,128)(2,1)S(1)} %get-tuple-element.349), channel_id=1, source_target_pairs={{0,2},{1,3},{2,0},{3,1},{4,6},{5,7},{6,4},{7,5},{8,10},{9,11},{10,... | collective-permute-start | bytes 1572872 | tf_op jit(solution)/shard_map/ppermute | solution.py:137
  556.9 23.7 %collective-permute-start.79 = (bf16[4,64,1024]{2,1,0:T(8,128)(2,1)S(1)}, bf16[4,64,1024]{2,1,0:T(8,128)(2,1)S(1)}, u32[]{:S(2)}, u32[]{:S(2)}) collective-permute-start(bf16[4,64,1024]{2,1,0:T(8,128)(2,1)S(1)} %get-tuple-element.348), channel_id=1, source_target_pairs={{0,6},{1,7},{2,4},{3,5},{4,2},{5,3},{6,0},{7,1},{8,14},{9,15},{10,... | collective-permute-start | bytes 1572872 | tf_op jit(solution)/shard_map/ppermute | solution.py:137
  583.6 25.3 %collective-permute-start.83 = (bf16[64,1024]{1,0:T(8,128)(2,1)S(1)}, bf16[64,1024]{1,0:T(8,128)(2,1)S(1)}, u32[]{:S(2)}, u32[]{:S(2)}) collective-permute-start(bf16[64,1024]{1,0:T(8,128)(2,1)S(1)} %get-tuple-element.367), channel_id=1, source_target_pairs={{0,8},{4,12},{8,0},{12,4},{16,24},{20,28},{24,16},{28,20},{1,9},{5... | collective-permute-start | bytes 393224 | tf_op jit(solution)/shard_map/ppermute | solution.py:29
  583.7 25.2 %collective-permute-start.84 = (bf16[64,1024]{1,0:T(8,128)(2,1)S(1)}, bf16[64,1024]{1,0:T(8,128)(2,1)S(1)}, u32[]{:S(2)}, u32[]{:S(2)}) collective-permute-start(bf16[64,1024]{1,0:T(8,128)(2,1)S(1)} %get-tuple-element.366), channel_id=1, source_target_pairs={{0,16},{4,20},{8,24},{12,28},{16,0},{20,4},{24,8},{28,12},{1,17},{... | collective-permute-start | bytes 393224 | tf_op jit(solution)/shard_map/ppermute | solution.py:29
  590.3 18.7 %collective-permute-start.85 = (bf16[64,1024]{1,0:T(8,128)(2,1)S(1)}, bf16[64,1024]{1,0:T(8,128)(2,1)S(1)}, u32[]{:S(2)}, u32[]{:S(2)}) collective-permute-start(bf16[64,1024]{1,0:T(8,128)(2,1)S(1)} %get-tuple-element.365), channel_id=1, source_target_pairs={{0,24},{4,28},{8,16},{12,20},{16,8},{20,12},{24,0},{28,4},{1,25},{... | collective-permute-start | bytes 393224 | tf_op jit(solution)/shard_map/ppermute | solution.py:29
  (145 other events, 1162.5 us)
Sparse Core Ops, SparseCore 0:
  10.9 186.1 all-gather.6
  200.0 161.5 all-gather.8

commit v6 on v5

--- a/solution.py
+++ b/solution.py
@@ -909,12 +909,16 @@
 def middle_back_kernel(first, n_parts, *refs):
     res_ref, own_ref, far_ref, va_ref, norm_ref, proj_ref = refs[:6]
     dva_ref, sums_ref = refs[6:8]
+    room, sem = refs[-2:]
+    copy = pltpu.make_async_copy(proj_ref, room, sem)
+    copy.start()
     grad = res_ref[...] + own_ref[...].astype(F32) + far_ref[...].astype(F32)
     dva, gain, shift = norm_back(grad, va_ref[...], norm_ref[first : first + 1, :])
     dva_ref[...] = dva
     sums_ref[0:1, :] = gain
     sums_ref[1:2, :] = shift
-    spread = dense_back(dva.astype(LOW), proj_ref[...]).astype(LOW)
+    copy.wait()
+    spread = dense_back(dva.astype(LOW), room[...]).astype(LOW)
     share = spread.shape[1] // n_parts
     for j in range(n_parts):
         refs[8 + j][...] = spread[:, j * share : (j + 1) * share]
@@ -930,9 +934,10 @@
             jax.ShapeDtypeStruct((2, width), F32),
         ]
         + [jax.ShapeDtypeStruct((rows, width // n_parts), LOW)] * n_parts,
-        in_specs=[vmem] * 6,
+        in_specs=[vmem] * 5 + [pl.BlockSpec(memory_space=pl.ANY)],
         out_specs=[vmem] * (2 + n_parts),
-        compiler_params=pltpu.CompilerParams(vmem_limit_bytes=32 * MIB),
+        scratch_shapes=[pltpu.VMEM(proj.shape, LOW), pltpu.SemaphoreType.DMA],
+        compiler_params=pltpu.CompilerParams(vmem_limit_bytes=52 * MIB),
         cost_estimate=pl.CostEstimate(
             flops=0, bytes_accessed=0, transcendentals=0
         ),

time: 655 us -> 651 us (level)
  transfers between devices with their start and end apart: 96 -> 96, of which waited for: 29 -> 29; matrix products, arithmetic and copies ran while one was open for 18% -> 18% of each run, Pallas kernels for 24% -> 25%
where the time goes in v6:
time: 651 us; the launch traced here: 641 us
  Pallas kernels  205 us (31%)
  waiting for transfers between devices  183 us (28%)
  starting transfers between devices  83.5 us (13%)
  local copies, waits for them, and re-layouts  83.1 us (13%)
  other arithmetic  42.3 us (6%)
  matrix products  20.8 us (3%)
  between operations  17 us (3%)
    ppermute x84, waiting for transfers between devices, flip(): return lax.ppermute(value, axis, [(i, i ^ mask) for i in range(count)])  151 us
    ppermute x84, starting transfers between devices, flip(): return lax.ppermute(value, axis, [(i, i ^ mask) for i in range(count)])  70.2 us
    pallas_call x3, Pallas kernels, attend_back(): pl.pallas_call(kernel, grid=(pairs, length // rows), out_shape=out, in_sp...  53.1 us
    gather x3, local copies, waits for them, and re-layouts, lookup(): found = jnp.take(embedding, jnp.clip(ids, 0, entries - 1), axis=0)  36.3 us
    pallas_call x1, Pallas kernels, head(): pl.pallas_call(lambda *refs: head_kernel(count, *refs), grid=(entries //...  34.2 us
    pallas_call x2, Pallas kernels, branch_back(): pl.pallas_call(lambda *refs: branch_back_kernel(first, n_parts, len(given...  30.5 us
    pallas_call x3, Pallas kernels, attend(): pl.pallas_call(attend_kernel, grid=(pairs, length // rows), out_shape=[ja...  29 us
    pallas_call x2, Pallas kernels, branch(): pl.pallas_call(lambda *refs: branch_kernel(first, len(parts), *refs), out...  27.9 us
  transfers between devices with their start and end apart: 96, of which 29 were waited for; matrix products, arithmetic and copies ran while one was open for 18% of the time, Pallas kernels for 25%

profile of v6, /device:TPU:0, one launch (start us, length us, event | category | flops | bytes accessed | tf_op | source)
XLA Modules:
  0.0 640.8 jit_solution(6736253078765659557)
XLA Ops:
  11.4 6.2 all-gather.3
  21.9 3.5 all-to-all-start
  32.5 2.6 collective-permute-start.9
  46.5 2.8 collective-permute-start.2
  50.8 11.4 %gather_fusion.2 = bf16[1024,1024]{1,0:T(8,128)(2,1)S(1)} fusion(bf16[6400,1024]{1,0:T(8,128)(2,1)} %refs_4_.2, s32[1024]{0:T(1024)S(1)} %broadcast_clamp_fusion.2), kind=kCustom, calls=%fused_computation.clone | custom fusion | bytes 4198400 | tf_op jit(solution)/shard_map/jit(_take)/gather | solution.py:1166
  62.2 12.4 %gather_fusion.3 = bf16[1024,1024]{1,0:T(8,128)(2,1)} fusion(bf16[6400,1024]{1,0:T(8,128)(2,1)} %refs_4_.2, s32[1024]{0:T(1024)S(1)} %broadcast_clamp_fusion.1), kind=kCustom, calls=%fused_computation.1.clone | custom fusion | bytes 4198400 | tf_op jit(solution)/shard_map/jit(_take)/gather | solution.py:1166
  74.7 12.5 %gather_fusion.4 = bf16[1024,1024]{1,0:T(8,128)(2,1)} fusion(bf16[6400,1024]{1,0:T(8,128)(2,1)} %refs_4_.2, s32[1024]{0:T(1024)S(1)} %broadcast_clamp_fusion), kind=kCustom, calls=%fused_computation.2.clone | custom fusion | bytes 4198400 | tf_op jit(solution)/shard_map/jit(_take)/gather | solution.py:1166
  93.9 2.8 collective-permute-done.1.refs_3_
  96.7 15.3 %collective-permute-done.3.refs_5_ = bf16[192,1536]{1,0:T(8,128)(2,1)} collective-permute-done((bf16[192,1536]{1,0:T(8,128)(2,1)}, bf16[192,1536]{1,0:T(8,128)(2,1)}, u32[]{:S(2)}, u32[]{:S(2)}) %collective-permute-start.3) | collective-permute-done | bytes 589856 | tf_op jit(solution)/shard_map/ppermute | solution.py:29
  122.9 19.4 %collective-permute-done.12 = bf16[256,1024]{1,0:T(8,128)(2,1)S(1)} collective-permute-done((bf16[256,1024]{1,0:T(8,128)(2,1)S(1)}, bf16[256,1024]{1,0:T(8,128)(2,1)S(1)}, u32[]{:S(2)}, u32[]{:S(2)}) %collective-permute-start.12) | collective-permute-done | bytes 524320 | tf_op jit(solution)/shard_map/ppermute | solution.py:29
  142.3 22.1 %collective-permute-done.6 = bf16[256,1024]{1,0:T(8,128)(2,1)S(1)} collective-permute-done((bf16[256,1024]{1,0:T(8,128)(2,1)S(1)}, bf16[256,1024]{1,0:T(8,128)(2,1)S(1)}, u32[]{:S(2)}, u32[]{:S(2)}) %collective-permute-start.6) | collective-permute-done | bytes 524320 | tf_op jit(solution)/shard_map/ppermute | solution.py:29
  171.7 13.4 %collective-permute-done.13.refs_1_ = bf16[256,1024]{1,0:T(8,128)(2,1)S(1)} collective-permute-done((bf16[256,1024]{1,0:T(8,128)(2,1)}, bf16[256,1024]{1,0:T(8,128)(2,1)S(1)}, u32[]{:S(2)}, u32[]{:S(2)}) %collective-permute-start.13) | collective-permute-done | bytes 524320 | tf_op jit(solution)/shard_map/ppermute | solution.py:29
  190.8 8.9 %collective-permute-start.20 = (bf16[128,768]{1,0:T(8,128)(2,1)S(1)}, bf16[128,768]{1,0:T(8,128)(2,1)S(1)}, u32[]{:S(2)}, u32[]{:S(2)}) collective-permute-start(bf16[128,768]{1,0:T(8,128)(2,1)S(1)} %get-tuple-element.371), channel_id=1, source_target_pairs={{0,8},{4,12},{8,0},{12,4},{16,24},{20,28},{24,16},{28,20},{1,9},{5... | collective-permute-start | bytes 589832 | tf_op jit(solution)/shard_map/ppermute | solution.py:29
  199.7 5.1 shard_map.277
  208.4 4.2 fusion.32.q_ref.k_ref.v_ref.refs_2_.refs_3_.refs_4_
  216.3 9.5 %shard_map.278 = (bf16[1024,256]{1,0:T(8,128)(2,1)}, f32[1024,256]{1,0:T(8,128)}) custom-call(s32[1024,1]{1,0:T(8,128)} %broadcast_in_dim.79.limit_ref.refs_0_, s32[1,1024]{1,0:T(1,128)} %bitcast.290, bf16[1024,768]{1,0:T(8,128)(2,1)} %fusion.32.q_ref.k_ref.v_ref.refs_2_.refs_3_.refs_4_, bf16[1024,768]{1,0:T(8,128)(2,1)} %fusion.32.q_ref.k_ref.v_ref.refs_2_.refs_3_.refs_4_, ...), custom_call_target="tpu_custom_call" | custom-call | flops 2147483648 | bytes 2097152 | tf_op jit(solution)/shard_map/pallas_call | solution.py:470
  232.6 6.6 %collective-permute-done.28.refs_4_ = bf16[4,64,1536]{2,1,0:T(8,128)(2,1)S(1)} collective-permute-done((bf16[4,64,1536]{2,1,0:T(8,128)(2,1)}, bf16[4,64,1536]{2,1,0:T(8,128)(2,1)S(1)}, u32[]{:S(2)}, u32[]{:S(2)}) %collective-permute-start.28) | collective-permute-done | bytes 786464 | tf_op jit(solution)/shard_map/ppermute | solution.py:163
  239.3 5.0 fusion.35.q_ref.k_ref.v_ref.refs_3_.refs_4_.refs_5_
  244.3 9.7 %shard_map.280 = (bf16[1024,256]{1,0:T(8,128)(2,1)}, f32[1024,256]{1,0:T(8,128)}) custom-call(s32[1024,1]{1,0:T(8,128)} %bitcast.272, s32[1,1024]{1,0:T(1,128)} %bitcast.291, bf16[1024,768]{1,0:T(8,128)(2,1)} %fusion.35.q_ref.k_ref.v_ref.refs_3_.refs_4_.refs_5_, bf16[1024,768]{1,0:T(8,128)(2,1)} %fusion.35.q_ref.k_ref.v_ref.refs_3_.refs_4_.refs_5_, ...), custom_call_target="tpu_custom_call" | custom-call | flops 2147483648 | bytes 2097152 | tf_op jit(solution)/shard_map/pallas_call | solution.py:470
  258.6 5.1 shard_map.281
  264.6 3.6 collective-permute-done.26
  274.6 13.9 %shard_map.283 = (f32[256,1024]{1,0:T(8,128)}, bf16[256,1024]{1,0:T(8,128)(2,1)}, f32[256,4096]{1,0:T(8,128)}, bf16[256,512]{1,0:T(8,128)(2,1)}, f32[256,512]{1,...) custom-call(bf16[256,256]{1,0:T(8,128)(2,1)} %get-tuple-element.383.refs_0_, bf16[256,256]{1,0:T(8,128)(2,1)} %copy-done.68, ...), custom_call_target="tpu_custom_call" | custom-call | flops 5368709120 | bytes 23068672 | tf_op jit(solution)/shard_map/pallas_call | solution.py:788
  289.8 24.9 %collective-permute-done.41 = bf16[256,1024]{1,0:T(8,128)(2,1)} collective-permute-done((bf16[256,1024]{1,0:T(8,128)(2,1)}, bf16[256,1024]{1,0:T(8,128)(2,1)}, u32[]{:S(2)}, u32[]{:S(2)}) %collective-permute-start.41) | collective-permute-done | bytes 524320 | tf_op jit(solution)/shard_map/ppermute | solution.py:29
  314.8 3.8 shard_map.282
  318.6 2.9 fusion.41.q_ref.refs_2_
  321.6 3.6 fusion.38.k_ref.v_ref.refs_3_.refs_4_
  325.1 9.8 %shard_map.284 = (bf16[1024,256]{1,0:T(8,128)(2,1)}, f32[1024,256]{1,0:T(8,128)}) custom-call(s32[1024,1]{1,0:T(8,128)} %broadcast_in_dim.79.limit_ref.refs_0_, s32[1,1024]{1,0:T(1,128)} %bitcast.292, bf16[1024,256]{1,0:T(8,128)(2,1)} %fusion.41.q_ref.refs_2_, bf16[1024,512]{1,0:T(8,128)(2,1)} %fusion.38.k_ref.v_ref.refs_3_.refs_4_, ...), custom_call_target="tpu_custom_call" | custom-call | flops 2147483648 | bytes 2097152 | tf_op jit(solution)/shard_map/pallas_call | solution.py:470
  342.2 17.2 %all-gather.9.cloned.1.call-done = bf16[9216,1024]{1,0:T(8,128)(2,1)} async-done(((bf16[288,1024]{1,0:T(8,128)(2,1)}), bf16[9216,1024]{1,0:T(8,128)(2,1)}) %all-gather.9.cloned.1.call-update) | async-done | bytes 18874384 | tf_op jit(solution)/shard_map/all_gather | solution.py:654
  360.1 14.0 %shard_map.286 = (f32[256,1024]{1,0:T(8,128)}, bf16[256,1024]{1,0:T(8,128)(2,1)}, f32[256,4096]{1,0:T(8,128)}, bf16[256,512]{1,0:T(8,128)(2,1)}, f32[256,512]{1,...) custom-call(bf16[256,256]{1,0:T(8,128)(2,1)} %get-tuple-element.379.refs_0_, bf16[256,256]{1,0:T(8,128)(2,1)} %copy-done.71, ...), custom_call_target="tpu_custom_call" | custom-call | flops 5368709120 | bytes 23068672 | tf_op jit(solution)/shard_map/pallas_call | solution.py:788
  376.5 12.7 %collective-permute-done.49.refs_2_ = bf16[256,1024]{1,0:T(8,128)(2,1)S(1)} collective-permute-done((bf16[256,1024]{1,0:T(8,128)(2,1)}, bf16[256,1024]{1,0:T(8,128)(2,1)S(1)}, u32[]{:S(2)}, u32[]{:S(2)}) %collective-permute-start.49) | collective-permute-done | bytes 524320 | tf_op jit(solution)/shard_map/ppermute | solution.py:29
  393.9 34.2 %shard_map.289 = (bf16[256,1024]{1,0:T(8,128)(2,1)}, bf16[256,1024]{1,0:T(8,128)(2,1)}, bf16[256,1024]{1,0:T(8,128)(2,1)}, bf16[256,1024]{1,0:T(8,128)(2,1)}, f3...) custom-call(bf16[256,1024]{1,0:T(8,128)(2,1)} %get-tuple-element.182.refs_0_.refs_12_, ...), custom_call_target="tpu_custom_call" | custom-call | flops 26843545600 | bytes 13107200 | tf_op jit(solution)/shard_map/pallas_call | solution.py:1070
  442.0 2.9 fusion.80
  447.3 3.9 collective-permute-done.59.refs_0_
  452.0 15.4 %shard_map.293 = (f32[256,1024]{1,0:T(8,128)}, f32[4,1024]{1,0:T(4,128)}, bf16[256,512]{1,0:T(8,128)(2,1)}, bf16[256,1024]{1,0:T(8,128)(2,1)}, bf16[256,256]{1,0...) custom-call(f32[256,1024]{1,0:T(8,128)} %add_divide_fusion.refs_0_, ...), custom_call_target="tpu_custom_call" | custom-call | flops 5368709120 | bytes 23068672 | tf_op jit(solution)/shard_map/pallas_call | solution.py:882
  469.4 4.1 collective-permute-done.66
  476.6 17.3 %shard_map.294 = bf16[1024,768]{1,0:T(8,128)(2,1)} custom-call(s32[1024,1]{1,0:T(8,128)} %broadcast_in_dim.79.limit_ref.refs_0_, s32[1,1024]{1,0:T(1,128)} %bitcast.293, bf16[1024,256]{1,0:T(8,128)(2,1)} %fusion.41.q_ref.refs_2_, bf16[1024,512]{1,0:T(8,128)(2,1)} %fusion.38.k_ref.v_ref.refs_3_.refs_4_, bf16[1024,512]{1,0:T(8,128)(2,1)} %fusion.38.k_ref.v_ref.refs_3_.refs_4_, ...), custom_call_target="tpu_custom_call" | custom-call | flops 5368709120 | bytes 4194304 | tf_op jit(solution)/shard_map/pallas_call | solution.py:617
  493.9 2.5 fusion.127
  505.0 10.8 %collective-permute-done.69.refs_1_ = bf16[256,1024]{1,0:T(8,128)(2,1)S(1)} collective-permute-done((bf16[256,1024]{1,0:T(8,128)(2,1)S(1)}, bf16[256,1024]{1,0:T(8,128)(2,1)S(1)}, u32[]{:S(2)}, u32[]{:S(2)}) %collective-permute-start.69) | collective-permute-done | bytes 524320 | tf_op jit(solution)/shard_map/ppermute | solution.py:29
  516.5 15.1 %shard_map.295 = (f32[256,1024]{1,0:T(8,128)}, f32[4,1024]{1,0:T(4,128)}, bf16[256,512]{1,0:T(8,128)(2,1)}, bf16[256,1024]{1,0:T(8,128)(2,1)}, bf16[256,256]{1,0...) custom-call(f32[256,1024]{1,0:T(8,128)} %get-tuple-element.354.refs_0_, ...), custom_call_target="tpu_custom_call" | custom-call | flops 5368709120 | bytes 23068672 | tf_op jit(solution)/shard_map/pallas_call | solution.py:882
  532.5 5.4 shard_map.297
  540.9 6.1 shard_map.298
  556.8 19.2 %shard_map.299.refs_0_ = f32[2,1024]{1,0:T(2,128)} custom-call(s32[1024,1]{1,0:T(8,128)} %broadcast_in_dim.79.limit_ref.refs_0_, s32[1,1024]{1,0:T(1,128)} %bitcast.294, bf16[1024,768]{1,0:T(8,128)(2,1)} %fusion.32.q_ref.k_ref.v_ref.refs_2_.refs_3_.refs_4_, bf16[1024,768]{1,0:T(8,128)(2,1)} %fusion.32.q_ref.k_ref.v_ref.refs_2_.refs_3_.refs_4_, ...), custom_call_target="tpu_custom_call" | custom-call | flops 5368709120 | bytes 4194304 | tf_op jit(solution)/shard_map/pallas_call | solution.py:617
  576.0 3.4 collective-permute-done.79.refs_3_
  582.5 4.7 collective-permute-start.84
  588.5 16.5 %shard_map.301.refs_0_ = f32[2,1024]{1,0:T(2,128)} custom-call(s32[1]{0:T(128)} %bitcast.105.refs_0_, s32[1024,1]{1,0:T(8,128)} %bitcast.273, s32[1,1024]{1,0:T(1,128)} %bitcast.295, bf16[1024,768]{1,0:T(8,128)(2,1)} %fusion.35.q_ref.k_ref.v_ref.refs_3_.refs_4_.refs_5_, bf16[1024,768]{1,0:T(8,128)(2,1)} %fusion.35.q_ref.k_ref.v_ref.refs_3_.refs_4_.refs_5_, ...), custom_call_target="tpu_custom_call" | custom-call | flops 5368709120 | bytes 4194304 | tf_op jit(solution)/shard_map/pallas_call | solution.py:617
  607.1 2.6 shard_map.303
  622.8 3.1 collective-permute-done.91
  628.1 2.4 shard_map.304
  (525 shorter events, 168.9 us)
Async XLA Ops:
  7.2 266.8 %all-gather.7.cloned.1.call-start = ((), (), s32[]{:S(2)}) async-start(), calls=%async_computation.1 | async-start | bytes 19464192 | tf_op jit(solution)/shard_map/all_gather | solution.py:654
  10.5 348.8 %all-gather.9.cloned.1.call-start = ((), (), s32[]{:S(2)}) async-start(), calls=%async_computation.2 | async-start | bytes 19464192 | tf_op jit(solution)/shard_map/all_gather | solution.py:654
  21.9 19.5 %all-to-all-start = ((bf16[4,32,2304]{2,1,0:T(8,128)(2,1)}), bf16[4,32,2304]{2,1,0:T(8,128)(2,1)S(1)}, u32[]{:S(2)}, u32[]{:S(2)}) async-start(bf16[4,32,2304]{2,1,0:T(8,128)(2,1)} %reshape.448), calls=%async_computation | async-start | bytes 1179648 | tf_op jit(solution)/shard_map/all_to_all | solution.py:1197
  25.5 15.1 %collective-permute-start = (bf16[32,1536]{1,0:T(8,128)(2,1)S(1)}, bf16[32,1536]{1,0:T(8,128)(2,1)S(1)}, u32[]{:S(2)}, u32[]{:S(2)}) collective-permute-start(bf16[32,1536]{1,0:T(8,128)(2,1)S(1)} %broadcast_select_fusion.2), channel_id=1, source_target_pairs={{0,1},{1,0},{2,3},{3,2},{4,5},{5,4},{6,7},{7,6},{8,9},{9,8},{10,11... | collective-permute-start | bytes 294920 | tf_op jit(solution)/shard_map/ppermute | solution.py:29
  45.6 51.1 %collective-permute-start.1 = (bf16[192,1536]{1,0:T(8,128)(2,1)}, bf16[192,1536]{1,0:T(8,128)(2,1)S(1)}, u32[]{:S(2)}, u32[]{:S(2)}) collective-permute-start(bf16[192,1536]{1,0:T(8,128)(2,1)} %constant_dynamic-update-slice_fusion), channel_id=1, source_target_pairs={{0,8},{4,12},{8,0},{12,4},{16,24},{20,28},{24,16},{28,20},{1,9},{5... | collective-permute-start | bytes 1769480 | tf_op jit(solution)/shard_map/ppermute | solution.py:29
  46.5 50.3 %collective-permute-start.2 = (bf16[192,1536]{1,0:T(8,128)(2,1)}, bf16[192,1536]{1,0:T(8,128)(2,1)S(1)}, u32[]{:S(2)}, u32[]{:S(2)}) collective-permute-start(bf16[192,1536]{1,0:T(8,128)(2,1)} %constant_dynamic-update-slice_fusion), channel_id=1, source_target_pairs={{0,16},{4,20},{8,24},{12,28},{16,0},{20,4},{24,8},{28,12},{1,17},{... | collective-permute-start | bytes 1769480 | tf_op jit(solution)/shard_map/ppermute | solution.py:29
  49.2 62.9 %collective-permute-start.3 = (bf16[192,1536]{1,0:T(8,128)(2,1)}, bf16[192,1536]{1,0:T(8,128)(2,1)}, u32[]{:S(2)}, u32[]{:S(2)}) collective-permute-start(bf16[192,1536]{1,0:T(8,128)(2,1)} %constant_dynamic-update-slice_fusion), channel_id=1, source_target_pairs={{0,24},{4,28},{8,16},{12,20},{16,8},{20,12},{24,0},{28,4},{1,25},{... | collective-permute-start | bytes 1769480 | tf_op jit(solution)/shard_map/ppermute | solution.py:29
  116.3 26.0 %collective-permute-start.12 = (bf16[256,1024]{1,0:T(8,128)(2,1)S(1)}, bf16[256,1024]{1,0:T(8,128)(2,1)S(1)}, u32[]{:S(2)}, u32[]{:S(2)}) collective-permute-start(bf16[256,1024]{1,0:T(8,128)(2,1)S(1)} %fusion.51), channel_id=1, source_target_pairs={{0,2},{1,3},{2,0},{3,1},{4,6},{5,7},{6,4},{7,5},{8,10},{9,11},{10,... | collective-permute-start | bytes 1572872 | tf_op jit(solution)/shard_map/ppermute | solution.py:29
  118.4 46.0 %collective-permute-start.6 = (bf16[256,1024]{1,0:T(8,128)(2,1)S(1)}, bf16[256,1024]{1,0:T(8,128)(2,1)S(1)}, u32[]{:S(2)}, u32[]{:S(2)}) collective-permute-start(bf16[256,1024]{1,0:T(8,128)(2,1)S(1)} %fusion.53), channel_id=1, source_target_pairs={{0,2},{1,3},{2,0},{3,1},{4,6},{5,7},{6,4},{7,5},{8,10},{9,11},{10,... | collective-permute-start | bytes 1572872 | tf_op jit(solution)/shard_map/ppermute | solution.py:29
  120.2 70.6 %collective-permute-start.17 = (bf16[4,128,1536]{2,1,0:T(8,128)(2,1)S(1)}, bf16[4,128,1536]{2,1,0:T(8,128)(2,1)}, u32[]{:S(2)}, u32[]{:S(2)}) collective-permute-start(bf16[4,128,1536]{2,1,0:T(8,128)(2,1)S(1)} %pad_maximum_fusion.refs_1_), channel_id=1, source_target_pairs={{0,4},{4,0},{8,12},{12,8},{16,20},{20,16},{24,28},{28,24},{1,5},{5... | collective-permute-start | bytes 4718600 | tf_op jit(solution)/shard_map/ppermute | solution.py:29
  169.1 16.1 %collective-permute-start.13 = (bf16[256,1024]{1,0:T(8,128)(2,1)}, bf16[256,1024]{1,0:T(8,128)(2,1)S(1)}, u32[]{:S(2)}, u32[]{:S(2)}) collective-permute-start(bf16[256,1024]{1,0:T(8,128)(2,1)} %get-tuple-element.346), channel_id=1, source_target_pairs={{0,2},{1,3},{2,0},{3,1},{4,6},{5,7},{6,4},{7,5},{8,10},{9,11},{10,... | collective-permute-start | bytes 1572872 | tf_op jit(solution)/shard_map/ppermute | solution.py:29
  170.7 35.4 %collective-permute-start.18 = (bf16[256,1024]{1,0:T(8,128)(2,1)}, bf16[256,1024]{1,0:T(8,128)(2,1)}, u32[]{:S(2)}, u32[]{:S(2)}) collective-permute-start(bf16[256,1024]{1,0:T(8,128)(2,1)} %get-tuple-element.346), channel_id=1, source_target_pairs={{0,1},{1,0},{2,3},{3,2},{4,5},{5,4},{6,7},{7,6},{8,9},{9,8},{10,11... | collective-permute-start | bytes 1572872 | tf_op jit(solution)/shard_map/ppermute | solution.py:29
  186.0 21.0 %collective-permute-start.19 = (bf16[256,1024]{1,0:T(8,128)(2,1)}, bf16[256,1024]{1,0:T(8,128)(2,1)S(1)}, u32[]{:S(2)}, u32[]{:S(2)}) collective-permute-start(bf16[256,1024]{1,0:T(8,128)(2,1)} %get-tuple-element.162), channel_id=1, source_target_pairs={{0,1},{1,0},{2,3},{3,2},{4,5},{5,4},{6,7},{7,6},{8,9},{9,8},{10,11... | collective-permute-start | bytes 1572872 | tf_op jit(solution)/shard_map/ppermute | solution.py:29
  187.0 38.8 %collective-permute-start.23 = (bf16[4,64,1536]{2,1,0:T(8,128)(2,1)S(1)}, bf16[4,64,1536]{2,1,0:T(8,128)(2,1)S(1)}, u32[]{:S(2)}, u32[]{:S(2)}) collective-permute-start(bf16[4,64,1536]{2,1,0:T(8,128)(2,1)S(1)} %pad_maximum_fusion.1.refs_1_), channel_id=1, source_target_pairs={{0,4},{1,3},{2,6},{3,1},{4,0},{5,7},{6,2},{7,5},{8,12},{9,11},{10,... | collective-permute-start | bytes 2359304 | tf_op jit(solution)/shard_map/ppermute | solution.py:163
  188.6 37.3 %collective-permute-start.24 = (bf16[4,64,1536]{2,1,0:T(8,128)(2,1)S(1)}, bf16[4,64,1536]{2,1,0:T(8,128)(2,1)S(1)}, u32[]{:S(2)}, u32[]{:S(2)}) collective-permute-start(bf16[4,64,1536]{2,1,0:T(8,128)(2,1)S(1)} %pad_maximum_fusion.1.refs_1_), channel_id=1, source_target_pairs={{0,2},{1,5},{2,0},{3,7},{4,6},{5,1},{6,4},{7,3},{8,10},{9,13},{10,... | collective-permute-start | bytes 2359304 | tf_op jit(solution)/shard_map/ppermute | solution.py:163
  190.8 21.8 %collective-permute-start.20 = (bf16[128,768]{1,0:T(8,128)(2,1)S(1)}, bf16[128,768]{1,0:T(8,128)(2,1)S(1)}, u32[]{:S(2)}, u32[]{:S(2)}) collective-permute-start(bf16[128,768]{1,0:T(8,128)(2,1)S(1)} %get-tuple-element.371), channel_id=1, source_target_pairs={{0,8},{4,12},{8,0},{12,4},{16,24},{20,28},{24,16},{28,20},{1,9},{5... | collective-permute-start | bytes 589832 | tf_op jit(solution)/shard_map/ppermute | solution.py:29
  206.1 19.7 %collective-permute-start.21 = (bf16[128,768]{1,0:T(8,128)(2,1)S(1)}, bf16[128,768]{1,0:T(8,128)(2,1)S(1)}, u32[]{:S(2)}, u32[]{:S(2)}) collective-permute-start(bf16[128,768]{1,0:T(8,128)(2,1)S(1)} %get-tuple-element.371), channel_id=1, source_target_pairs={{0,16},{4,20},{8,24},{12,28},{16,0},{20,4},{24,8},{28,12},{1,17},{... | collective-permute-start | bytes 589832 | tf_op jit(solution)/shard_map/ppermute | solution.py:29
  206.9 20.7 %collective-permute-start.15 = (bf16[256,1024]{1,0:T(8,128)(2,1)}, bf16[256,1024]{1,0:T(8,128)(2,1)}, u32[]{:S(2)}, u32[]{:S(2)}) collective-permute-start(bf16[256,1024]{1,0:T(8,128)(2,1)} %get-tuple-element.157), channel_id=1, source_target_pairs={{0,2},{1,3},{2,0},{3,1},{4,6},{5,7},{6,4},{7,5},{8,10},{9,11},{10,... | collective-permute-start | bytes 1572872 | tf_op jit(solution)/shard_map/ppermute | solution.py:29
  231.4 24.7 %collective-permute-start.29 = (bf16[4,64,1536]{2,1,0:T(8,128)(2,1)S(1)}, bf16[4,64,1536]{2,1,0:T(8,128)(2,1)S(1)}, u32[]{:S(2)}, u32[]{:S(2)}) collective-permute-start(bf16[4,64,1536]{2,1,0:T(8,128)(2,1)S(1)} %pad_maximum_fusion.1.refs_1_), channel_id=1, source_target_pairs={{0,1},{1,0},{2,3},{3,2},{4,5},{5,4},{6,7},{7,6},{8,9},{9,8},{10,11... | collective-permute-start | bytes 2359304 | tf_op jit(solution)/shard_map/ppermute | solution.py:29
  231.4 26.0 %collective-permute-start.30 = (bf16[4,64,1536]{2,1,0:T(8,128)(2,1)}, bf16[4,64,1536]{2,1,0:T(8,128)(2,1)S(1)}, u32[]{:S(2)}, u32[]{:S(2)}) collective-permute-start(bf16[4,64,1536]{2,1,0:T(8,128)(2,1)} %get-tuple-element.167.refs_2_), channel_id=1, source_target_pairs={{0,1},{1,0},{2,3},{3,2},{4,5},{5,4},{6,7},{7,6},{8,9},{9,8},{10,11... | collective-permute-start | bytes 2359304 | tf_op jit(solution)/shard_map/ppermute | solution.py:29
  232.6 25.0 %collective-permute-start.31 = (bf16[4,64,1536]{2,1,0:T(8,128)(2,1)S(1)}, bf16[4,64,1536]{2,1,0:T(8,128)(2,1)S(1)}, u32[]{:S(2)}, u32[]{:S(2)}) collective-permute-start(bf16[4,64,1536]{2,1,0:T(8,128)(2,1)S(1)} %copy-done.5), channel_id=1, source_target_pairs={{0,1},{1,0},{2,3},{3,2},{4,5},{5,4},{6,7},{7,6},{8,9},{9,8},{10,11... | collective-permute-start | bytes 2359304 | tf_op jit(solution)/shard_map/ppermute | solution.py:29
  239.3 19.1 %collective-permute-start.32 = (bf16[4,64,1536]{2,1,0:T(8,128)(2,1)S(1)}, bf16[4,64,1536]{2,1,0:T(8,128)(2,1)S(1)}, u32[]{:S(2)}, u32[]{:S(2)}) collective-permute-start(bf16[4,64,1536]{2,1,0:T(8,128)(2,1)S(1)} %collective-permute-done.28.refs_4_), channel_id=1, source_target_pairs={{0,1},{1,0},{2,3},{3,2},{4,5},{5,4},{6,7},{7,6},{8,9},{9,8},{10,11... | collective-permute-start | bytes 2359304 | tf_op jit(solution)/shard_map/ppermute | solution.py:29
  257.6 57.2 %collective-permute-start.36 = (bf16[4,128,768]{2,1,0:T(8,128)(2,1)S(1)}, bf16[4,128,768]{2,1,0:T(8,128)(2,1)}, u32[]{:S(2)}, u32[]{:S(2)}) collective-permute-start(bf16[4,128,768]{2,1,0:T(8,128)(2,1)S(1)} %pad_maximum_fusion.2.refs_1_), channel_id=1, source_target_pairs={{0,4},{4,0},{8,12},{12,8},{16,20},{20,16},{24,28},{28,24},{1,5},{5... | collective-permute-start | bytes 2359304 | tf_op jit(solution)/shard_map/ppermute | solution.py:29
  258.4 14.5 %collective-permute-start.37 = (bf16[256,256]{1,0:T(8,128)(2,1)S(1)}, bf16[256,256]{1,0:T(8,128)(2,1)S(1)}, u32[]{:S(2)}, u32[]{:S(2)}) collective-permute-start(bf16[256,256]{1,0:T(8,128)(2,1)S(1)} %get-tuple-element.382), channel_id=1, source_target_pairs={{0,1},{1,0},{2,3},{3,2},{4,5},{5,4},{6,7},{7,6},{8,9},{9,8},{10,11... | collective-permute-start | bytes 393224 | tf_op jit(solution)/shard_map/ppermute | solution.py:29
  271.4 17.9 %collective-permute-start.34 = (bf16[256,1024]{1,0:T(8,128)(2,1)S(1)}, bf16[256,1024]{1,0:T(8,128)(2,1)}, u32[]{:S(2)}, u32[]{:S(2)}) collective-permute-start(bf16[256,1024]{1,0:T(8,128)(2,1)S(1)} %get-tuple-element.344), channel_id=1, source_target_pairs={{0,2},{1,3},{2,0},{3,1},{4,6},{5,7},{6,4},{7,5},{8,10},{9,11},{10,... | collective-permute-start | bytes 1572872 | tf_op jit(solution)/shard_map/ppermute | solution.py:29
  288.6 26.1 %collective-permute-start.41 = (bf16[256,1024]{1,0:T(8,128)(2,1)}, bf16[256,1024]{1,0:T(8,128)(2,1)}, u32[]{:S(2)}, u32[]{:S(2)}) collective-permute-start(bf16[256,1024]{1,0:T(8,128)(2,1)} %get-tuple-element.174), channel_id=1, source_target_pairs={{0,2},{1,3},{2,0},{3,1},{4,6},{5,7},{6,4},{7,5},{8,10},{9,11},{10,... | collective-permute-start | bytes 1572872 | tf_op jit(solution)/shard_map/ppermute | solution.py:29
  289.2 29.3 %collective-permute-start.33 = (bf16[256,1024]{1,0:T(8,128)(2,1)S(1)}, bf16[256,1024]{1,0:T(8,128)(2,1)}, u32[]{:S(2)}, u32[]{:S(2)}) collective-permute-start(bf16[256,1024]{1,0:T(8,128)(2,1)S(1)} %get-tuple-element.344), channel_id=1, source_target_pairs={{0,1},{1,0},{2,3},{3,2},{4,5},{5,4},{6,7},{7,6},{8,9},{9,8},{10,11... | collective-permute-start | bytes 1572872 | tf_op jit(solution)/shard_map/ppermute | solution.py:29
  289.3 29.3 %collective-permute-start.35 = (bf16[256,1024]{1,0:T(8,128)(2,1)}, bf16[256,1024]{1,0:T(8,128)(2,1)}, u32[]{:S(2)}, u32[]{:S(2)}) collective-permute-start(bf16[256,1024]{1,0:T(8,128)(2,1)} %collective-permute-done.34), channel_id=1, source_target_pairs={{0,1},{1,0},{2,3},{3,2},{4,5},{5,4},{6,7},{7,6},{8,9},{9,8},{10,11... | collective-permute-start | bytes 1572872 | tf_op jit(solution)/shard_map/ppermute | solution.py:29
  289.7 31.8 %collective-permute-start.40 = (bf16[256,1024]{1,0:T(8,128)(2,1)}, bf16[256,1024]{1,0:T(8,128)(2,1)}, u32[]{:S(2)}, u32[]{:S(2)}) collective-permute-start(bf16[256,1024]{1,0:T(8,128)(2,1)} %get-tuple-element.174), channel_id=1, source_target_pairs={{0,1},{1,0},{2,3},{3,2},{4,5},{5,4},{6,7},{7,6},{8,9},{9,8},{10,11... | collective-permute-start | bytes 1572872 | tf_op jit(solution)/shard_map/ppermute | solution.py:29
  338.3 21.0 %collective-permute-start.43 = (bf16[256,256]{1,0:T(8,128)(2,1)S(1)}, bf16[256,256]{1,0:T(8,128)(2,1)S(1)}, u32[]{:S(2)}, u32[]{:S(2)}) collective-permute-start(bf16[256,256]{1,0:T(8,128)(2,1)S(1)} %get-tuple-element.378), channel_id=1, source_target_pairs={{0,1},{1,0},{2,3},{3,2},{4,5},{5,4},{6,7},{7,6},{8,9},{9,8},{10,11... | collective-permute-start | bytes 393224 | tf_op jit(solution)/shard_map/ppermute | solution.py:29
  338.3 21.0 %collective-permute-start.44 = (bf16[256,256]{1,0:T(8,128)(2,1)S(1)}, bf16[256,256]{1,0:T(8,128)(2,1)S(1)}, u32[]{:S(2)}, u32[]{:S(2)}) collective-permute-start(bf16[256,256]{1,0:T(8,128)(2,1)S(1)} %get-tuple-element.377), channel_id=1, source_target_pairs={{0,2},{1,3},{2,0},{3,1},{4,6},{5,7},{6,4},{7,5},{8,10},{9,11},{10,... | collective-permute-start | bytes 393224 | tf_op jit(solution)/shard_map/ppermute | solution.py:29
  339.0 20.4 %collective-permute-start.45 = (bf16[256,256]{1,0:T(8,128)(2,1)S(1)}, bf16[256,256]{1,0:T(8,128)(2,1)S(1)}, u32[]{:S(2)}, u32[]{:S(2)}) collective-permute-start(bf16[256,256]{1,0:T(8,128)(2,1)S(1)} %get-tuple-element.376), channel_id=1, source_target_pairs={{0,3},{1,2},{2,1},{3,0},{4,7},{5,6},{6,5},{7,4},{8,11},{9,10},{10,... | collective-permute-start | bytes 393224 | tf_op jit(solution)/shard_map/ppermute | solution.py:29
  341.4 32.6 %collective-permute-start.47 = (bf16[256,1024]{1,0:T(8,128)(2,1)S(1)}, bf16[256,1024]{1,0:T(8,128)(2,1)S(1)}, u32[]{:S(2)}, u32[]{:S(2)}) collective-permute-start(bf16[256,1024]{1,0:T(8,128)(2,1)S(1)} %fusion.50), channel_id=1, source_target_pairs={{0,2},{1,3},{2,0},{3,1},{4,6},{5,7},{6,4},{7,5},{8,10},{9,11},{10,... | collective-permute-start | bytes 1572872 | tf_op jit(solution)/shard_map/ppermute | solution.py:29
  374.9 14.3 %collective-permute-start.49 = (bf16[256,1024]{1,0:T(8,128)(2,1)}, bf16[256,1024]{1,0:T(8,128)(2,1)S(1)}, u32[]{:S(2)}, u32[]{:S(2)}) collective-permute-start(bf16[256,1024]{1,0:T(8,128)(2,1)} %get-tuple-element.181.refs_0_), channel_id=1, source_target_pairs={{0,2},{1,3},{2,0},{3,1},{4,6},{5,7},{6,4},{7,5},{8,10},{9,11},{10,... | collective-permute-start | bytes 1572872 | tf_op jit(solution)/shard_map/ppermute | solution.py:29
  376.5 12.7 %collective-permute-start.48 = (bf16[256,1024]{1,0:T(8,128)(2,1)}, bf16[256,1024]{1,0:T(8,128)(2,1)S(1)}, u32[]{:S(2)}, u32[]{:S(2)}) collective-permute-start(bf16[256,1024]{1,0:T(8,128)(2,1)} %get-tuple-element.181.refs_0_), channel_id=1, source_target_pairs={{0,1},{1,0},{2,3},{3,2},{4,5},{5,4},{6,7},{7,6},{8,9},{9,8},{10,11... | collective-permute-start | bytes 1572872 | tf_op jit(solution)/shard_map/ppermute | solution.py:29
  391.9 36.3 %collective-permute-start.51 = (bf16[256,1024]{1,0:T(8,128)(2,1)}, bf16[256,1024]{1,0:T(8,128)(2,1)S(1)}, u32[]{:S(2)}, u32[]{:S(2)}) collective-permute-start(bf16[256,1024]{1,0:T(8,128)(2,1)} %get-tuple-element.194.refs_8_), channel_id=1, source_target_pairs={{0,2},{1,3},{2,0},{3,1},{4,6},{5,7},{6,4},{7,5},{8,10},{9,11},{10,... | collective-permute-start | bytes 1572872 | tf_op jit(solution)/shard_map/ppermute | solution.py:29
  393.5 34.7 %collective-permute-start.52 = (bf16[256,1024]{1,0:T(8,128)(2,1)}, bf16[256,1024]{1,0:T(8,128)(2,1)S(1)}, u32[]{:S(2)}, u32[]{:S(2)}) collective-permute-start(bf16[256,1024]{1,0:T(8,128)(2,1)} %get-tuple-element.195.refs_10_), channel_id=1, source_target_pairs={{0,2},{1,3},{2,0},{3,1},{4,6},{5,7},{6,4},{7,5},{8,10},{9,11},{10,... | collective-permute-start | bytes 1572872 | tf_op jit(solution)/shard_map/ppermute | solution.py:29
  437.3 13.9 %collective-permute-start.59 = (bf16[256,1024]{1,0:T(8,128)(2,1)}, bf16[256,1024]{1,0:T(8,128)(2,1)S(1)}, u32[]{:S(2)}, u32[]{:S(2)}) collective-permute-start(bf16[256,1024]{1,0:T(8,128)(2,1)} %get-tuple-element.212), channel_id=1, source_target_pairs={{0,2},{1,3},{2,0},{3,1},{4,6},{5,7},{6,4},{7,5},{8,10},{9,11},{10,... | collective-permute-start | bytes 1572872 | tf_op jit(solution)/shard_map/ppermute | solution.py:29
  437.8 13.4 %collective-permute-start.60 = (bf16[256,1024]{1,0:T(8,128)(2,1)}, bf16[256,1024]{1,0:T(8,128)(2,1)}, u32[]{:S(2)}, u32[]{:S(2)}) collective-permute-start(bf16[256,1024]{1,0:T(8,128)(2,1)} %get-tuple-element.213.refs_1_), channel_id=1, source_target_pairs={{0,1},{1,0},{2,3},{3,2},{4,5},{5,4},{6,7},{7,6},{8,9},{9,8},{10,11... | collective-permute-start | bytes 1572872 | tf_op jit(solution)/shard_map/ppermute | solution.py:29
  437.8 13.4 %collective-permute-start.61 = (bf16[256,1024]{1,0:T(8,128)(2,1)}, bf16[256,1024]{1,0:T(8,128)(2,1)}, u32[]{:S(2)}, u32[]{:S(2)}) collective-permute-start(bf16[256,1024]{1,0:T(8,128)(2,1)} %get-tuple-element.214.refs_3_), channel_id=1, source_target_pairs={{0,1},{1,0},{2,3},{3,2},{4,5},{5,4},{6,7},{7,6},{8,9},{9,8},{10,11... | collective-permute-start | bytes 1572872 | tf_op jit(solution)/shard_map/ppermute | solution.py:29
  501.0 14.7 %collective-permute-start.69 = (bf16[256,1024]{1,0:T(8,128)(2,1)S(1)}, bf16[256,1024]{1,0:T(8,128)(2,1)S(1)}, u32[]{:S(2)}, u32[]{:S(2)}) collective-permute-start(bf16[256,1024]{1,0:T(8,128)(2,1)S(1)} %get-tuple-element.353), channel_id=1, source_target_pairs={{0,2},{1,3},{2,0},{3,1},{4,6},{5,7},{6,4},{7,5},{8,10},{9,11},{10,... | collective-permute-start | bytes 1572872 | tf_op jit(solution)/shard_map/ppermute | solution.py:29
  504.2 27.5 %collective-permute-start.71 = (bf16[256,1024]{1,0:T(8,128)(2,1)S(1)}, bf16[256,1024]{1,0:T(8,128)(2,1)S(1)}, u32[]{:S(2)}, u32[]{:S(2)}) collective-permute-start(bf16[256,1024]{1,0:T(8,128)(2,1)S(1)} %get-tuple-element.351), channel_id=1, source_target_pairs={{0,2},{1,3},{2,0},{3,1},{4,6},{5,7},{6,4},{7,5},{8,10},{9,11},{10,... | collective-permute-start | bytes 1572872 | tf_op jit(solution)/shard_map/ppermute | solution.py:29
  551.4 24.5 %collective-permute-start.77 = (bf16[4,64,1024]{2,1,0:T(8,128)(2,1)S(1)}, bf16[4,64,1024]{2,1,0:T(8,128)(2,1)S(1)}, u32[]{:S(2)}, u32[]{:S(2)}) collective-permute-start(bf16[4,64,1024]{2,1,0:T(8,128)(2,1)S(1)} %get-tuple-element.350), channel_id=1, source_target_pairs={{0,4},{1,5},{2,6},{3,7},{4,0},{5,1},{6,2},{7,3},{8,12},{9,13},{10,... | collective-permute-start | bytes 1572872 | tf_op jit(solution)/shard_map/ppermute | solution.py:137
  553.2 22.8 %collective-permute-start.78 = (bf16[4,64,1024]{2,1,0:T(8,128)(2,1)S(1)}, bf16[4,64,1024]{2,1,0:T(8,128)(2,1)S(1)}, u32[]{:S(2)}, u32[]{:S(2)}) collective-permute-start(bf16[4,64,1024]{2,1,0:T(8,128)(2,1)S(1)} %get-tuple-element.349), channel_id=1, source_target_pairs={{0,2},{1,3},{2,0},{3,1},{4,6},{5,7},{6,4},{7,5},{8,10},{9,11},{10,... | collective-permute-start | bytes 1572872 | tf_op jit(solution)/shard_map/ppermute | solution.py:137
  554.4 25.1 %collective-permute-start.79 = (bf16[4,64,1024]{2,1,0:T(8,128)(2,1)S(1)}, bf16[4,64,1024]{2,1,0:T(8,128)(2,1)S(1)}, u32[]{:S(2)}, u32[]{:S(2)}) collective-permute-start(bf16[4,64,1024]{2,1,0:T(8,128)(2,1)S(1)} %get-tuple-element.348), channel_id=1, source_target_pairs={{0,6},{1,7},{2,4},{3,5},{4,2},{5,3},{6,0},{7,1},{8,14},{9,15},{10,... | collective-permute-start | bytes 1572872 | tf_op jit(solution)/shard_map/ppermute | solution.py:137
  582.4 23.4 %collective-permute-start.83 = (bf16[64,1024]{1,0:T(8,128)(2,1)S(1)}, bf16[64,1024]{1,0:T(8,128)(2,1)S(1)}, u32[]{:S(2)}, u32[]{:S(2)}) collective-permute-start(bf16[64,1024]{1,0:T(8,128)(2,1)S(1)} %get-tuple-element.367), channel_id=1, source_target_pairs={{0,8},{4,12},{8,0},{12,4},{16,24},{20,28},{24,16},{28,20},{1,9},{5... | collective-permute-start | bytes 393224 | tf_op jit(solution)/shard_map/ppermute | solution.py:29
  582.5 23.3 %collective-permute-start.84 = (bf16[64,1024]{1,0:T(8,128)(2,1)S(1)}, bf16[64,1024]{1,0:T(8,128)(2,1)S(1)}, u32[]{:S(2)}, u32[]{:S(2)}) collective-permute-start(bf16[64,1024]{1,0:T(8,128)(2,1)S(1)} %get-tuple-element.366), channel_id=1, source_target_pairs={{0,16},{4,20},{8,24},{12,28},{16,0},{20,4},{24,8},{28,12},{1,17},{... | collective-permute-start | bytes 393224 | tf_op jit(solution)/shard_map/ppermute | solution.py:29
  587.2 18.6 %collective-permute-start.85 = (bf16[64,1024]{1,0:T(8,128)(2,1)S(1)}, bf16[64,1024]{1,0:T(8,128)(2,1)S(1)}, u32[]{:S(2)}, u32[]{:S(2)}) collective-permute-start(bf16[64,1024]{1,0:T(8,128)(2,1)S(1)} %get-tuple-element.365), channel_id=1, source_target_pairs={{0,24},{4,28},{8,16},{12,20},{16,8},{20,12},{24,0},{28,4},{1,25},{... | collective-permute-start | bytes 393224 | tf_op jit(solution)/shard_map/ppermute | solution.py:29
  (145 other events, 1174.9 us)
Sparse Core Ops, SparseCore 0:
  10.9 186.4 all-gather.6
  200.3 158.9 all-gather.8
